TPU v7x, 32 devices: a whole 2x2x4 slice. The times are simulated.
32 devices in a mesh: parts: 2 (over x), expert: 16 (over z, y, core).
Axes of the slice: x: 2, y: 2, z: 4, core: 2. Of those that a mesh axis runs over, the one named last changes fastest.
Arguments:
- tokens: bfloat16 [4096, 1536], P(('parts', 'expert')), parts along dimension 0, may hold values from -6 to 6
- out_grad: bfloat16 [4096, 1536], P(('parts', 'expert')), parts along dimension 0, may hold values from -6 to 6
- gate: float32 [4096], P(('parts', 'expert')), parts along dimension 0, may hold values from 0.2 to 1
- expert_id: int32 [4096], P(('parts', 'expert')), parts along dimension 0, may hold values from 0 to 1, as said below
- dropped: int32 [4096], P(('parts', 'expert')), parts along dimension 0, may hold values from 0 to 1, as said below
- slot: int32 [4096], P(('parts', 'expert')), parts along dimension 0, may hold values from 0 to 79, as said below
- saved_hidden: bfloat16 [2560, 12288], P('parts', 'expert'), parts along dimension 0, may hold values from -6 to 6
- w_in: bfloat16 [1536, 12288], P(None, 'expert'), may hold values from -0.15625 to 0.15625
- w_out: bfloat16 [12288, 1536], P('expert'), may hold values from -0.078125 to 0.078125
Outputs:
- token_grad: bfloat16 [4096, 1536], P(('parts', 'expert')), parts along dimension 0
- gate_grad: float32 [4096], P(('parts', 'expert')), parts along dimension 0
- w_in_grad: bfloat16 [3072, 12288], P('parts', 'expert'), parts along dimension 0
- w_out_grad: bfloat16 [24576, 1536], P(('parts', 'expert')), parts along dimension 0
There are 2 independent parts, one for each index of `parts`. A program takes and returns all parts, laid end to end along the dimension named above; an argument that names none is the same for every part. Nothing has to cross between parts.
Inputs may be any that keep to these rules, and one draw needn't show every extreme that they name: `expert_id`: each device's tokens name experts; one expert, the same for every device of a part, is chosen by more than 80 tokens of every device. Among one device's tokens that name one expert, in token order, the first 80 are kept and the others are dropped. A kept token's slot is its rank in token order among the device's tokens that name the same expert; a dropped token's slot is 0.
All inputs are finite; a program needn't handle non-finite values.
Results may differ from a plain program's by a relative error of at most 0.0085.
Values may be sent and summed in bfloat16 or wider, within the bound.
No kernel may reach another device: no remote copies, remote signals or barrier semaphores. Data moves between devices by JAX's collectives and lax.ppermute only.
A program may use at most 128 MiB of HBM per device.

v0:
```python
import jax
import jax.numpy as jnp
from jax import lax
from jax.sharding import PartitionSpec as P

SPLIT = 8


def normal_parts(hidden):
    normal_cdf = 0.5 * (1.0 + jax.scipy.special.erf(hidden * 0.7071067811865476))
    density = jnp.exp(-0.5 * hidden * hidden) * 0.3989422804014327
    return (normal_cdf, density)


def body(tokens, out_grad, gate, expert_id, dropped, slot, saved_hidden, w_in, w_out):
    sources = lax.axis_size("expert")
    experts = sources // SPLIT
    slots = saved_hidden.shape[0] // sources
    width = tokens.shape[1]
    slot_rows = sources * slots
    scaled = (gate[:, None] * out_grad.astype(jnp.float32)).astype(jnp.bfloat16)
    place = expert_id * slots + slot
    target = jnp.where(dropped == 1, experts * slots, place)
    token_buffer = (
        jnp.zeros((experts * slots, width), jnp.bfloat16).at[target].set(tokens, mode="drop")
    )
    grad_buffer = (
        jnp.zeros((experts * slots, width), jnp.bfloat16).at[target].set(scaled, mode="drop")
    )
    token_copies = jnp.broadcast_to(
        token_buffer.reshape(experts, 1, slots, width), (experts, SPLIT, slots, width)
    ).reshape(sources, slots, width)
    grad_copies = jnp.broadcast_to(
        grad_buffer.reshape(experts, 1, slots, width), (experts, SPLIT, slots, width)
    ).reshape(sources, slots, width)
    got_tokens, got_grads = (
        lax.all_to_all(token_copies, "expert", split_axis=0, concat_axis=0, tiled=True),
        lax.all_to_all(grad_copies, "expert", split_axis=0, concat_axis=0, tiled=True),
    )
    routed = got_tokens.reshape(slot_rows, width)
    routed_grad = got_grads.reshape(slot_rows, width)
    hidden = saved_hidden.astype(jnp.float32)
    normal_cdf, density = normal_parts(hidden)
    activated = hidden * normal_cdf
    grad_act = lax.dot_general(
        routed_grad, w_out, (((1,), (1,)), ((), ())), preferred_element_type=jnp.float32
    )
    activated_b = activated.astype(jnp.bfloat16)
    hidden_grad = (grad_act * (normal_cdf + hidden * density)).astype(jnp.bfloat16)
    w_out_grad = lax.dot_general(
        activated_b, routed_grad, (((0,), (0,)), ((), ())), preferred_element_type=jnp.float32
    ).astype(jnp.bfloat16)
    w_in_grad = lax.dot_general(
        routed, hidden_grad, (((0,), (0,)), ((), ())), preferred_element_type=jnp.float32
    ).astype(jnp.bfloat16)
    partial_grad = lax.dot_general(
        hidden_grad, w_in, (((1,), (1,)), ((), ())), preferred_element_type=jnp.float32
    ).astype(jnp.bfloat16)
    gate_part = jnp.sum(grad_act * activated, axis=1).astype(jnp.bfloat16)
    returned, gate_back = (
        lax.all_to_all(
            partial_grad.reshape(sources, slots, width),
            "expert",
            split_axis=0,
            concat_axis=0,
            tiled=True,
        ),
        lax.all_to_all(
            gate_part.reshape(sources, slots), "expert", split_axis=0, concat_axis=0, tiled=True
        ),
    )
    summed = jnp.sum(
        returned.astype(jnp.float32).reshape(experts, SPLIT, slots, width), axis=1
    ).reshape(experts * slots, width)
    gate_sum = jnp.sum(
        gate_back.astype(jnp.float32).reshape(experts, SPLIT, slots), axis=1
    ).reshape(experts * slots)
    index_back = jnp.where(dropped == 1, 0, place)
    token_grad = jnp.where(dropped[:, None] == 1, jnp.float32(0.0), summed[index_back]).astype(
        jnp.bfloat16
    )
    gate_grad = jnp.where(dropped == 1, jnp.float32(0.0), gate_sum[index_back] / gate)
    return (token_grad, gate_grad, w_in_grad, w_out_grad)


def solution(mesh):
    in_specs = (
        P(("parts", "expert"), None),
        P(("parts", "expert"), None),
        P(("parts", "expert")),
        P(("parts", "expert")),
        P(("parts", "expert")),
        P(("parts", "expert")),
        P("parts", "expert"),
        P(None, "expert"),
        P("expert", None),
    )
    out_specs = (
        P(("parts", "expert"), None),
        P(("parts", "expert")),
        P("parts", "expert"),
        P(("parts", "expert"), None),
    )
    return jax.shard_map(body, mesh=mesh, in_specs=in_specs, out_specs=out_specs, check_vma=False)
```

profile of v0, /device:TPU:13, one launch (start us, length us, event | category | flops | bytes accessed | tf_op | source)
XLA Modules:
  0.0 301.9 jit_solution(2849933979414946801)
XLA Ops:
  0.6 0.0 copy-start
  0.6 0.8 compare_select_fusion
  1.5 1.9 scatter_custom_fusion
  3.4 2.3 broadcast_in_dim.50
  5.7 6.6 %all-to-all-start = ((bf16[16,80,1536]{2,1,0:T(8,128)(2,1)}), bf16[16,80,1536]{2,1,0:T(8,128)(2,1)}, u32[]{:S(2)}, u32[]{:S(2)}) async-start(bf16[16,80,1536]{2,1,0:T(8,128)(2,1)} %bitcast.25), calls=%async_computation | async-start | bytes 7864320 | tf_op jit(solution)/shard_map/all_to_all | solution.py:38
  12.2 1.8 scatter_custom_fusion.1
  14.0 85.0 %all-to-all-done = bf16[16,80,1536]{2,1,0:T(8,128)(2,1)} async-done(((bf16[16,80,1536]{2,1,0:T(8,128)(2,1)}), bf16[16,80,1536]{2,1,0:T(8,128)(2,1)}, u32[]{:S(2)}, u32[]{:S(2)}) %all-to-all-start) | async-done | bytes 3932192 | tf_op jit(solution)/shard_map/all_to_all | solution.py:38
  99.1 2.3 broadcast_in_dim.54
  101.3 4.9 %all-to-all-start.3 = ((bf16[16,80,1536]{2,1,0:T(8,128)(2,1)}), bf16[16,80,1536]{2,1,0:T(8,128)(2,1)}, u32[]{:S(2)}, u32[]{:S(2)}) async-start(bf16[16,80,1536]{2,1,0:T(8,128)(2,1)} %bitcast.24), calls=%async_computation.3 | async-start | bytes 7864320 | tf_op jit(solution)/shard_map/all_to_all | solution.py:37
  106.3 4.0 %copy.15 = bf16[1280,768]{0,1:T(8,128)(2,1)} copy(bf16[1280,768]{1,0:T(8,128)(2,1)} %param.15) | data formatting | bytes 3932160 | tf_op args[6]
  110.2 8.5 %multiply_reduce_fusion = (bf16[1280]{0:T(1024)(128)(2,1)S(1)}, bf16[1280,768]{0,1:T(8,128)(2,1)}) fusion(bf16[1280,768]{0,1:T(8,128)(2,1)} %copy.15, bf16[1280,1536]{1,0:T(8,128)(2,1)} %bitcast.2, bf16[768,1536]{1,0:T(8,128)(2,1)} %param.17), kind=kOutput, calls=%fused_computation.19 | convolution fusion | flops 3033660160 | bytes 10226176 | tf_op jit(solution)/shard_map/dot_general | solution.py:45
  118.8 0.7 convert_element_type.67
  119.5 73.6 %all-to-all-done.3 = bf16[16,80,1536]{2,1,0:T(8,128)(2,1)} async-done(((bf16[16,80,1536]{2,1,0:T(8,128)(2,1)}), bf16[16,80,1536]{2,1,0:T(8,128)(2,1)}, u32[]{:S(2)}, u32[]{:S(2)}) %all-to-all-start.3) | async-done | bytes 3932192 | tf_op jit(solution)/shard_map/all_to_all | solution.py:37
  193.1 4.9 %all-to-all-start.2 = ((bf16[16,1,80]{2,1,0:T(2,128)(2,1)}), bf16[16,1,80]{2,1,0:T(2,128)(2,1)S(1)}, u32[]{:S(2)}, u32[]{:S(2)}) async-start(bf16[16,1,80]{2,1,0:T(2,128)(2,1)} %convert_element_type.67), calls=%async_computation.2 | async-start | bytes 16384 | tf_op jit(solution)/shard_map/all_to_all | solution.py:68
  198.0 0.0 copy-done
  198.0 6.4 %convolution_convert_fusion = bf16[1280,1536]{1,0:T(8,128)(2,1)} fusion(bf16[1280,768]{0,1:T(8,128)(2,1)} %get-tuple-element.5, bf16[1536,768]{1,0:T(8,128)(2,1)S(1)} %copy-done), kind=kOutput, calls=%fused_computation.10 | convolution fusion | flops 3021864960 | bytes 8257536 | tf_op jit(solution)/shard_map/dot_general | solution.py:56
  204.4 0.0 all-to-all-done.2
  204.4 0.0 copy-start.3
  204.4 6.2 %all-to-all-start.1 = ((bf16[16,80,1536]{2,1,0:T(8,128)(2,1)}), bf16[16,80,1536]{2,1,0:T(8,128)(2,1)}, u32[]{:S(2)}, u32[]{:S(2)}) async-start(bf16[16,80,1536]{2,1,0:T(8,128)(2,1)} %bitcast.26), calls=%async_computation.1 | async-start | bytes 7864320 | tf_op jit(solution)/shard_map/all_to_all | solution.py:61
  210.6 0.0 copy-done.3
  210.6 0.0 copy-start.1
  210.6 7.6 %convolution_convert_fusion.2 = bf16[1536,768]{1,0:T(8,128)(2,1)} fusion(bf16[1280,1536]{1,0:T(8,128)(2,1)} %bitcast.9, bf16[1280,768]{0,1:T(8,128)(2,1)} %get-tuple-element.5), kind=kOutput, calls=%fused_computation.21 | convolution fusion | flops 3021078528 | bytes 8257536 | tf_op jit(solution)/shard_map/dot_general | solution.py:53
  218.2 0.0 copy-done.1
  218.2 0.0 copy-start.2
  218.2 6.6 %convolution_convert_fusion.1 = bf16[768,1536]{1,0:T(8,128)(2,1)} fusion(bf16[1280,1536]{1,0:T(8,128)(2,1)} %bitcast.2, bf16[1280,768]{0,1:T(8,128)(2,1)S(1)} %copy-done.1), kind=kOutput, calls=%fused_computation.20 | convolution fusion | flops 3026976768 | bytes 8257536 | tf_op jit(solution)/shard_map/dot_general | solution.py:50
  224.8 0.1 reshape.67
  224.9 1.3 gather_fusion.1
  226.1 0.0 copy-done.2
  226.2 0.5 divide_select_fusion
  226.7 70.8 %all-to-all-done.1 = bf16[16,80,1536]{2,1,0:T(8,128)(2,1)} async-done(((bf16[16,80,1536]{2,1,0:T(8,128)(2,1)}), bf16[16,80,1536]{2,1,0:T(8,128)(2,1)}, u32[]{:S(2)}, u32[]{:S(2)}) %all-to-all-start.1) | async-done | bytes 3932192 | tf_op jit(solution)/shard_map/all_to_all | solution.py:61
  297.4 2.6 convert_reduce_fusion
  300.1 0.9 gather_fusion
  301.0 0.9 select_convert_fusion
  (4 shorter events, 0.0 us)
Async XLA Ops:
  0.6 197.4 %copy-start = (bf16[1536,768]{1,0:T(8,128)(2,1)S(1)}, bf16[1536,768]{1,0:T(8,128)(2,1)}, u32[]{:S(2)}) copy-start(bf16[1536,768]{1,0:T(8,128)(2,1)} %param.16) | copy-start | bytes 7077892
  5.7 93.4 %all-to-all-start = ((bf16[16,80,1536]{2,1,0:T(8,128)(2,1)}), bf16[16,80,1536]{2,1,0:T(8,128)(2,1)}, u32[]{:S(2)}, u32[]{:S(2)}) async-start(bf16[16,80,1536]{2,1,0:T(8,128)(2,1)} %bitcast.25), calls=%async_computation | async-start | bytes 7864320 | tf_op jit(solution)/shard_map/all_to_all | solution.py:38
  101.3 91.8 %all-to-all-start.3 = ((bf16[16,80,1536]{2,1,0:T(8,128)(2,1)}), bf16[16,80,1536]{2,1,0:T(8,128)(2,1)}, u32[]{:S(2)}, u32[]{:S(2)}) async-start(bf16[16,80,1536]{2,1,0:T(8,128)(2,1)} %bitcast.24), calls=%async_computation.3 | async-start | bytes 7864320 | tf_op jit(solution)/shard_map/all_to_all | solution.py:37
  193.1 11.3 %all-to-all-start.2 = ((bf16[16,1,80]{2,1,0:T(2,128)(2,1)}), bf16[16,1,80]{2,1,0:T(2,128)(2,1)S(1)}, u32[]{:S(2)}, u32[]{:S(2)}) async-start(bf16[16,1,80]{2,1,0:T(2,128)(2,1)} %convert_element_type.67), calls=%async_computation.2 | async-start | bytes 16384 | tf_op jit(solution)/shard_map/all_to_all | solution.py:68
  204.4 6.2 %copy-start.3 = (s32[128]{0:T(128)S(1)}, s32[128]{0:T(128)}, u32[]{:S(2)}) copy-start(s32[128]{0:T(128)} %param.13) | copy-start | bytes 1540
  204.4 93.0 %all-to-all-start.1 = ((bf16[16,80,1536]{2,1,0:T(8,128)(2,1)}), bf16[16,80,1536]{2,1,0:T(8,128)(2,1)}, u32[]{:S(2)}, u32[]{:S(2)}) async-start(bf16[16,80,1536]{2,1,0:T(8,128)(2,1)} %bitcast.26), calls=%async_computation.1 | async-start | bytes 7864320 | tf_op jit(solution)/shard_map/all_to_all | solution.py:61
  210.6 7.6 %copy-start.1 = (bf16[1280,768]{0,1:T(8,128)(2,1)S(1)}, bf16[1280,768]{0,1:T(8,128)(2,1)}, u32[]{:S(2)}) copy-start(bf16[1280,768]{0,1:T(8,128)(2,1)} %copy.15) | copy-start | bytes 5898244
  218.2 8.0 %copy-start.2 = (f32[128]{0:T(128)S(1)}, f32[128]{0:T(128)}, u32[]{:S(2)}) copy-start(f32[128]{0:T(128)} %param.11) | copy-start | bytes 1540
where the time goes:
time: 302 us
  waiting for transfers between devices  229 us (76%)
  matrix products  29.1 us (10%)
  starting transfers between devices  22.5 us (7%)
  local copies, waits for them, and re-layouts  13.3 us (4%)
  other arithmetic  6.79 us (2%)
    all_to_all x1, waiting for transfers between devices, body(): lax.all_to_all(grad_copies, 'expert', split_axis=0, concat_axis=0, tiled=...  85 us
    all_to_all x1, waiting for transfers between devices, body(): lax.all_to_all(token_copies, 'expert', split_axis=0, concat_axis=0, tiled...  73.6 us
    all_to_all x1, waiting for transfers between devices, body(): lax.all_to_all(partial_grad.reshape(sources, slots, width), 'expert', spl...  70.8 us
    dot_general x1, matrix products, body(): lax.dot_general(routed_grad, w_out, (((1,), (1,)), ((), ())), preferred_e...  8.54 us
    dot_general x1, matrix products, body(): lax.dot_general(routed, hidden_grad, (((0,), (0,)), ((), ())), preferred_...  7.56 us
    dot_general x1, matrix products, body(): lax.dot_general(activated_b, routed_grad, (((0,), (0,)), ((), ())), prefe...  6.57 us
    all_to_all x1, starting transfers between devices, body(): lax.all_to_all(grad_copies, 'expert', split_axis=0, concat_axis=0, tiled=...  6.55 us
    dot_general x1, matrix products, body(): lax.dot_general(hidden_grad, w_in, (((1,), (1,)), ((), ())), preferred_el...  6.41 us
  transfers between devices with their start and end apart: 4, of which 3 were waited for; matrix products, arithmetic and copies ran while one was open for 12% of the time, Pallas kernels for 0%

commit v1 on v0

v1 whole, which is shorter than its diff:
```python
import jax
import jax.numpy as jnp
from jax import lax
from jax.sharding import PartitionSpec as P

SPLIT = 8
CORE, LOW, HIGH = 1, 2, 4


def normal_parts(hidden):
    normal_cdf = 0.5 * (1.0 + jax.scipy.special.erf(hidden * 0.7071067811865476))
    density = jnp.exp(-0.5 * hidden * hidden) * 0.3989422804014327
    return (normal_cdf, density)


def bits(core):
    return (HIGH, LOW, CORE) if core == 0 else (LOW, HIGH, CORE)


def pairs(devices, step):
    return [(i, i ^ bits(i % 2)[step]) for i in range(devices)]


def gather_rows(rows, devices):
    for step in range(3):
        rows = jnp.concatenate([rows, lax.ppermute(rows, "expert", pairs(devices, step))])
    return rows


def scatter_sum(rows, devices):
    for step in (2, 1, 0):
        half = rows.shape[0] // 2
        got = lax.ppermute(rows[half:], "expert", pairs(devices, step))
        total = rows[:half].astype(jnp.float32) + got.astype(jnp.float32)
        rows = total.astype(rows.dtype) if step else total
    return rows


def shift(devices, by):
    return [(i, (i + by * SPLIT) % devices) for i in range(devices)]


def body(tokens, out_grad, gate, expert_id, dropped, slot, saved_hidden, w_in, w_out):
    devices = lax.axis_size("expert")
    experts = devices // SPLIT
    slots = saved_hidden.shape[0] // devices
    hidden_units = saved_hidden.shape[1]
    me = lax.axis_index("expert")
    my_expert, my_place = me // SPLIT, me % SPLIT

    scaled = (gate[:, None] * out_grad.astype(jnp.float32)).astype(jnp.bfloat16)
    ahead = lax.rem(expert_id - my_expert + experts, experts)
    place = jnp.where(dropped == 1, -1, ahead * slots + slot)
    chosen = lax.broadcasted_iota(jnp.int32, (experts * slots, place.shape[0]), 0) == place[None, :]
    onehot = chosen.astype(jnp.bfloat16)

    def to_slots(values):
        return jnp.dot(onehot, values, preferred_element_type=jnp.float32).astype(jnp.bfloat16)

    def dispatch(values):
        buffer = to_slots(values)
        far = jnp.concatenate(
            [
                lax.ppermute(buffer[s * slots : (s + 1) * slots], "expert", shift(devices, s))
                for s in range(1, experts)
            ]
        )
        return gather_rows(buffer[:slots], devices), gather_rows(far, devices)

    core = me % 2
    near_masks = []
    for i in range(SPLIT):
        swapped = core ^ (i >> 2)
        first, second = jnp.where(swapped, LOW, HIGH), jnp.where(swapped, HIGH, LOW)
        near_masks.append((i & 1) * first + ((i >> 1) & 1) * second + (i >> 2) * CORE)
    near_order = jnp.stack([my_expert * SPLIT + (my_place ^ m) for m in near_masks])
    far_order = jnp.stack(
        [
            lax.rem(my_expert - s + experts, experts) * SPLIT + (my_place ^ m)
            for m in near_masks
            for s in range(1, experts)
        ]
    )
    by_source = saved_hidden.reshape(devices, slots, hidden_units)
    grads = dispatch(scaled)
    routed = dispatch(tokens)

    returned, gate_parts = [], []
    w_out_grad = w_in_grad = jnp.float32(0.0)
    for order, rows, routed_grad in zip((near_order, far_order), routed, grads):
        hidden = by_source[order].reshape(rows.shape[0], hidden_units).astype(jnp.float32)
        normal_cdf, density = normal_parts(hidden)
        activated = hidden * normal_cdf
        activated_b = activated.astype(jnp.bfloat16)
        grad_act = lax.dot_general(
            routed_grad, w_out, (((1,), (1,)), ((), ())), preferred_element_type=jnp.float32
        )
        hidden_grad = (grad_act * (normal_cdf + hidden * density)).astype(jnp.bfloat16)
        partial_grad = lax.dot_general(
            hidden_grad, w_in, (((1,), (1,)), ((), ())), preferred_element_type=jnp.float32
        ).astype(jnp.bfloat16)
        gate_parts.append(jnp.sum(grad_act * activated, axis=1).reshape(SPLIT, -1))
        w_out_grad += lax.dot_general(
            activated_b, routed_grad, (((0,), (0,)), ((), ())), preferred_element_type=jnp.float32
        )
        w_in_grad += lax.dot_general(
            rows, hidden_grad, (((0,), (0,)), ((), ())), preferred_element_type=jnp.float32
        )
        returned.append(scatter_sum(partial_grad, devices))

    def home(own, far):
        back = [
            lax.ppermute(far[(s - 1) * slots : s * slots], "expert", shift(devices, -s))
            for s in range(1, experts)
        ]
        return jnp.concatenate([own] + back)

    summed = home(returned[0].astype(jnp.bfloat16), returned[1].astype(jnp.bfloat16))
    gate_sum = scatter_sum(jnp.concatenate(gate_parts, axis=1), devices).reshape(-1)
    gate_sum = home(gate_sum[:slots], gate_sum[slots:])
    token_grad = lax.dot_general(
        onehot, summed, (((0,), (0,)), ((), ())), preferred_element_type=jnp.float32
    ).astype(jnp.bfloat16)
    slot_gate = jnp.sum(jnp.where(chosen, gate_sum[:, None], 0.0), axis=0)
    gate_grad = jnp.where(dropped == 1, jnp.float32(0.0), slot_gate / gate)
    return (token_grad, gate_grad, w_in_grad.astype(jnp.bfloat16), w_out_grad.astype(jnp.bfloat16))


def solution(mesh):
    in_specs = (
        P(("parts", "expert"), None),
        P(("parts", "expert"), None),
        P(("parts", "expert")),
        P(("parts", "expert")),
        P(("parts", "expert")),
        P(("parts", "expert")),
        P("parts", "expert"),
        P(None, "expert"),
        P("expert", None),
    )
    out_specs = (
        P(("parts", "expert"), None),
        P(("parts", "expert")),
        P("parts", "expert"),
        P(("parts", "expert"), None),
    )
    return jax.shard_map(body, mesh=mesh, in_specs=in_specs, out_specs=out_specs, check_vma=False)
```

time: 302 us -> 137 us (0.45)
  the two profiles are of different devices: /device:TPU:13 before, /device:TPU:0 now
where the time goes in v1:
time: 137 us
  waiting for transfers between devices  40.7 us (30%)
  matrix products  36 us (26%)
  starting transfers between devices  23.6 us (17%)
  other arithmetic  20.3 us (15%)
  local copies, waits for them, and re-layouts  15 us (11%)
    ppermute x9, waiting for transfers between devices, scatter_sum(): got = lax.ppermute(rows[half:], 'expert', pairs(devices, step))  22.6 us
    concatenate x8, other arithmetic, gather_rows(): jnp.concatenate([rows, lax.ppermute(rows, 'expert', pairs(devices, step))])  11.9 us
    ppermute x12, waiting for transfers between devices, gather_rows(): lax.ppermute(rows, 'expert', pairs(devices, step))  11.3 us
    dot_general x2, matrix products, body(): lax.dot_general(activated_b, routed_grad, (((0,), (0,)), ((), ())), prefe...  10.8 us
    ppermute x12, starting transfers between devices, gather_rows(): lax.ppermute(rows, 'expert', pairs(devices, step))  10.7 us
    dot_general x2, matrix products, body(): lax.dot_general(routed_grad, w_out, (((1,), (1,)), ((), ())), preferred_e...  8.65 us
    dot_general x2, matrix products, body(): lax.dot_general(rows, hidden_grad, (((0,), (0,)), ((), ())), preferred_el...  8.3 us
    dot_general x2, matrix products, body(): lax.dot_general(hidden_grad, w_in, (((1,), (1,)), ((), ())), preferred_el...  5.55 us
  transfers between devices with their start and end apart: 25, of which 10 were waited for; matrix products, arithmetic and copies ran while one was open for 48% of the time, Pallas kernels for 0%

profile of v1, /device:TPU:0, one launch (start us, length us, event | category | flops | bytes accessed | tf_op | source)
XLA Modules:
  0.0 136.6 jit_solution(9052411774569650671)
XLA Ops:
  0.7 0.9 compare_select_fusion.5
  1.5 1.4 convolution_convert_fusion.3
  2.9 0.8 fusion.59
  3.7 4.0 %collective-permute-start.6 = (bf16[80,1536]{1,0:T(8,128)(2,1)}, bf16[80,1536]{1,0:T(8,128)(2,1)}, u32[]{:S(2)}, u32[]{:S(2)}) collective-permute-start(bf16[80,1536]{1,0:T(8,128)(2,1)} %get-tuple-element.11), channel_id=1, source_target_pairs={{0,8},{1,9},{2,10},{3,11},{4,12},{5,13},{6,14},{7,15},{8,0},{9,1},... | collective-permute-start | bytes 737288 | tf_op jit(solution)/shard_map/ppermute | solution.py:64
  7.8 1.6 %collective-permute-start = (bf16[80,1536]{1,0:T(8,128)(2,1)}, bf16[80,1536]{1,0:T(8,128)(2,1)}, u32[]{:S(2)}, u32[]{:S(2)}) collective-permute-start(bf16[80,1536]{1,0:T(8,128)(2,1)} %get-tuple-element.10), channel_id=1, source_target_pairs={{0,4},{1,3},{2,6},{3,1},{4,0},{5,7},{6,2},{7,5},{8,12},{9,11},{10,... | collective-permute-start | bytes 737288 | tf_op jit(solution)/shard_map/ppermute | solution.py:26
  9.3 0.3 convolution_convert_fusion.2
  9.6 0.8 fusion.58
  10.4 0.3 collective-permute-start.21
  10.8 0.1 collective-permute-start.18
  11.1 3.1 %gather_fusion.1 = bf16[8,80,768]{2,1,0:T(8,128)(2,1)} fusion(bf16[16,80,768]{2,1,0:T(8,128)(2,1)} %bitcast.50, s32[1024]{0:T(1024)S(1)} %pad_clamp_fusion), kind=kCustom, calls=%fused_computation.1 | custom fusion | bytes 1966112 | tf_op jit(solution)/shard_map/gather | solution.py:91
  14.2 2.2 %gather_fusion = bf16[8,80,768]{2,1,0:T(8,128)(2,1)S(1)} fusion(bf16[16,80,768]{2,1,0:T(8,128)(2,1)} %bitcast.51, s32[1024]{0:T(1024)S(1)} %pad_clamp_fusion.1), kind=kCustom, calls=%fused_computation | custom fusion | bytes 1966112 | tf_op jit(solution)/shard_map/gather | solution.py:91
  16.4 2.3 %collective-permute-done = bf16[80,1536]{1,0:T(8,128)(2,1)} collective-permute-done((bf16[80,1536]{1,0:T(8,128)(2,1)}, bf16[80,1536]{1,0:T(8,128)(2,1)}, u32[]{:S(2)}, u32[]{:S(2)}) %collective-permute-start) | collective-permute-done | bytes 245792 | tf_op jit(solution)/shard_map/ppermute | solution.py:26
  18.7 1.1 pad_maximum_fusion.5
  19.8 1.6 %collective-permute-start.1 = (bf16[160,1536]{1,0:T(8,128)(2,1)S(1)}, bf16[160,1536]{1,0:T(8,128)(2,1)S(1)}, u32[]{:S(2)}, u32[]{:S(2)}) collective-permute-start(bf16[160,1536]{1,0:T(8,128)(2,1)S(1)} %pad_maximum_fusion.5), channel_id=1, source_target_pairs={{0,2},{1,5},{2,0},{3,7},{4,6},{5,1},{6,4},{7,3},{8,10},{9,13},{10,... | collective-permute-start | bytes 1474568 | tf_op jit(solution)/shard_map/ppermute | solution.py:26
  21.4 4.1 %collective-permute-done.6 = bf16[80,1536]{1,0:T(8,128)(2,1)} collective-permute-done((bf16[80,1536]{1,0:T(8,128)(2,1)}, bf16[80,1536]{1,0:T(8,128)(2,1)}, u32[]{:S(2)}, u32[]{:S(2)}) %collective-permute-start.6) | collective-permute-done | bytes 245792 | tf_op jit(solution)/shard_map/ppermute | solution.py:64
  25.5 3.8 %collective-permute-done.18 = bf16[80,1536]{1,0:T(8,128)(2,1)} collective-permute-done((bf16[80,1536]{1,0:T(8,128)(2,1)}, bf16[80,1536]{1,0:T(8,128)(2,1)}, u32[]{:S(2)}, u32[]{:S(2)}) %collective-permute-start.18) | collective-permute-done | bytes 245792 | tf_op jit(solution)/shard_map/ppermute | solution.py:26
  29.2 1.1 pad_maximum_fusion.7
  30.3 1.6 %collective-permute-start.19 = (bf16[160,1536]{1,0:T(8,128)(2,1)S(1)}, bf16[160,1536]{1,0:T(8,128)(2,1)S(1)}, u32[]{:S(2)}, u32[]{:S(2)}) collective-permute-start(bf16[160,1536]{1,0:T(8,128)(2,1)S(1)} %pad_maximum_fusion.7), channel_id=1, source_target_pairs={{0,2},{1,5},{2,0},{3,7},{4,6},{5,1},{6,4},{7,3},{8,10},{9,13},{10,... | collective-permute-start | bytes 1474568 | tf_op jit(solution)/shard_map/ppermute | solution.py:26
  31.9 2.5 %collective-permute-start.22 = (bf16[80,1536]{1,0:T(8,128)(2,1)}, bf16[80,1536]{1,0:T(8,128)(2,1)S(1)}, u32[]{:S(2)}, u32[]{:S(2)}) collective-permute-start(bf16[80,1536]{1,0:T(8,128)(2,1)} %collective-permute-done.21), channel_id=1, source_target_pairs={{0,4},{1,3},{2,6},{3,1},{4,0},{5,7},{6,2},{7,5},{8,12},{9,11},{10,... | collective-permute-start | bytes 737288 | tf_op jit(solution)/shard_map/ppermute | solution.py:26
  34.4 1.7 %constant_dynamic-update-slice_fusion.3 = bf16[640,1536]{1,0:T(8,128)(2,1)} fusion(bf16[80,1536]{1,0:T(8,128)(2,1)} %collective-permute-done.6), kind=kLoop, calls=%fused_computation.84 | loop fusion | bytes 491520
  36.1 1.0 pad_maximum_fusion.6
  37.0 0.7 collective-permute-start.8
  37.8 3.7 %collective-permute-done.22 = bf16[80,1536]{1,0:T(8,128)(2,1)S(1)} collective-permute-done((bf16[80,1536]{1,0:T(8,128)(2,1)}, bf16[80,1536]{1,0:T(8,128)(2,1)S(1)}, u32[]{:S(2)}, u32[]{:S(2)}) %collective-permute-start.22) | collective-permute-done | bytes 245792 | tf_op jit(solution)/shard_map/ppermute | solution.py:26
  41.5 1.1 pad_maximum_fusion.8
  42.6 0.5 collective-permute-start.23
  43.1 0.7 constant_dynamic-update-slice_fusion.2
  43.8 1.3 pad_maximum_fusion.1
  45.2 2.3 %pad_maximum_fusion.3 = bf16[320,1536]{1,0:T(8,128)(2,1)} fusion(bf16[160,1536]{1,0:T(8,128)(2,1)S(1)} %collective-permute-done.19, bf16[80,1536]{1,0:T(8,128)(2,1)} %collective-permute-done.18, bf16[80,1536]{1,0:T(8,128)(2,1)} %get-tuple-element.8), kind=kLoop, calls=%fused_computation.60 | loop fusion | flops 2949120 | bytes 1966080 | tf_op jit(solution)/shard_map/concatenate | solution.py:26
  47.6 0.5 collective-permute-start.20
  48.1 1.9 %pad_maximum_fusion.2 = bf16[320,1536]{1,0:T(8,128)(2,1)} fusion(bf16[160,1536]{1,0:T(8,128)(2,1)S(1)} %collective-permute-done.8, bf16[80,1536]{1,0:T(8,128)(2,1)S(1)} %collective-permute-done.7, bf16[80,1536]{1,0:T(8,128)(2,1)} %collective-permute-done.6), kind=kLoop, calls=%fused_computation.59 | loop fusion | flops 2949120 | bytes 1966080 | tf_op jit(solution)/shard_map/concatenate | solution.py:26
  50.0 1.4 %collective-permute-done.23 = bf16[160,1536]{1,0:T(8,128)(2,1)S(1)} collective-permute-done((bf16[160,1536]{1,0:T(8,128)(2,1)S(1)}, bf16[160,1536]{1,0:T(8,128)(2,1)S(1)}, u32[]{:S(2)}, u32[]{:S(2)}) %collective-permute-start.23) | collective-permute-done | bytes 491552 | tf_op jit(solution)/shard_map/ppermute | solution.py:26
  51.5 2.1 %pad_maximum_fusion.4 = bf16[320,1536]{1,0:T(8,128)(2,1)} fusion(bf16[160,1536]{1,0:T(8,128)(2,1)S(1)} %collective-permute-done.23, bf16[80,1536]{1,0:T(8,128)(2,1)S(1)} %collective-permute-done.22, bf16[80,1536]{1,0:T(8,128)(2,1)} %collective-permute-done.21), kind=kLoop, calls=%fused_computation.61 | loop fusion | flops 2949120 | bytes 1966080 | tf_op jit(solution)/shard_map/concatenate | solution.py:26
  53.6 1.5 %collective-permute-start.24 = (bf16[320,1536]{1,0:T(8,128)(2,1)}, bf16[320,1536]{1,0:T(8,128)(2,1)}, u32[]{:S(2)}, u32[]{:S(2)}) collective-permute-start(bf16[320,1536]{1,0:T(8,128)(2,1)} %pad_maximum_fusion.4), channel_id=1, source_target_pairs={{0,1},{1,0},{2,3},{3,2},{4,5},{5,4},{6,7},{7,6},{8,9},{9,8},{10,11... | collective-permute-start | bytes 2949128 | tf_op jit(solution)/shard_map/ppermute | solution.py:26
  55.1 0.8 constant_dynamic-update-slice_fusion.1
  56.0 5.1 %multiply_reduce_fusion.1 = (f32[640]{0:T(1024)S(1)}, f32[640,768]{1,0:T(8,128)}, f32[640,768]{1,0:T(8,128)}) fusion(bf16[8,80,768]{2,1,0:T(8,128)(2,1)S(1)} %gather_fusion, bf16[768,1536]{1,0:T(8,128)(2,1)S(1)} %copy-done, bf16[320,1536]{1,0:T(8,128)(2,1)S(1)} %collective-permute-done.2, bf16[160,1536]{1,0:T(8,128)(2,1)S(1)} %collective-permute-done.1, ...), kind=kOutput, calls=%fused_computation.52 | convolution fusion | flops 1521253760 | bytes 9243136 | tf_op jit(solution)/shard_map/dot_general | solution.py:95
  61.2 2.9 %fusion.7 = bf16[640,768]{1,0:T(8,128)(2,1)S(1)} fusion(f32[640,768]{1,0:T(8,128)} %get-tuple-element.15, f32[640,768]{1,0:T(8,128)} %get-tuple-element.5, bf16[8,80,768]{2,1,0:T(8,128)(2,1)S(1)} %gather_fusion), kind=kLoop, calls=%fused_computation.26 | loop fusion | flops 3932160 | bytes 5898240 | tf_op jit(solution)/shard_map/convert_element_type | solution.py:98
  64.1 1.7 %convolution_convert_fusion.1 = bf16[640,1536]{1,0:T(8,128)(2,1)S(1)} fusion(bf16[640,768]{1,0:T(8,128)(2,1)S(1)} %fusion.7, bf16[1536,768]{1,0:T(8,128)(2,1)S(1)} %copy-done.22), kind=kOutput, calls=%fused_computation.15 | convolution fusion | flops 1510932480 | bytes 5308416 | tf_op jit(solution)/shard_map/dot_general | solution.py:99
  65.9 1.0 slice.110
  66.9 0.6 copy-done.4
  67.5 2.2 %constant_dynamic-update-slice_fusion = bf16[640,1536]{1,0:T(8,128)(2,1)} fusion(bf16[640,1536]{1,0:T(8,128)(2,1)} %constant_dynamic-update-slice_fusion.1, bf16[320,1536]{1,0:T(8,128)(2,1)} %collective-permute-done.9), kind=kLoop, calls=%fused_computation.81 | loop fusion | bytes 1966080 | tf_op jit(solution)/shard_map/concatenate | solution.py:26
  69.7 3.5 %multiply_reduce_fusion = (f32[640]{0:T(1024)S(1)}, f32[640,768]{1,0:T(8,128)S(1)}, f32[640,768]{1,0:T(8,128)S(1)}) fusion(bf16[8,80,768]{2,1,0:T(8,128)(2,1)S(1)} %copy-done.2, bf16[640,1536]{1,0:T(8,128)(2,1)} %constant_dynamic-update-slice_fusion, bf16[768,1536]{1,0:T(8,128)(2,1)S(1)} %copy-done), kind=kOutput, calls=%fused_computation.51 | convolution fusion | flops 1513389440 | bytes 9243136 | tf_op jit(solution)/shard_map/dot_general | solution.py:95
  73.2 5.8 %fusion.33 = f32[768,1536]{1,0:T(8,128)} fusion(bf16[640,1536]{1,0:T(8,128)(2,1)} %constant_dynamic-update-slice_fusion, f32[640,768]{1,0:T(8,128)S(1)} %get-tuple-element.7, bf16[640,768]{1,0:T(8,128)(2,1)S(1)} %bitcast.49), kind=kOutput, calls=%fused_computation.57 | convolution fusion | flops 1511424000 | bytes 9633792 | tf_op jit(solution)/shard_map/dot_general | solution.py:103
  79.0 1.7 %fusion.15 = bf16[640,768]{1,0:T(8,128)(2,1)} fusion(f32[640,768]{1,0:T(8,128)S(1)} %get-tuple-element.14, f32[640,768]{1,0:T(8,128)S(1)} %get-tuple-element.7, bf16[8,80,768]{2,1,0:T(8,128)(2,1)S(1)} %copy-done.2), kind=kLoop, calls=%fused_computation.34 | loop fusion | flops 3932160 | bytes 5898240 | tf_op jit(solution)/shard_map/convert_element_type | solution.py:98
  80.9 3.8 %convolution_convert_fusion = bf16[640,1536]{1,0:T(8,128)(2,1)S(1)} fusion(bf16[640,768]{1,0:T(8,128)(2,1)} %fusion.15, bf16[1536,768]{1,0:T(8,128)(2,1)} %param.16), kind=kOutput, calls=%fused_computation.14 | convolution fusion | flops 1510932480 | bytes 5308416 | tf_op jit(solution)/shard_map/dot_general | solution.py:99
  84.8 0.5 collective-permute-start.10
  85.4 1.8 %collective-permute-start.15 = (f32[2,160]{1,0:T(2,128)S(1)}, f32[2,160]{1,0:T(2,128)S(1)}, u32[]{:S(2)}, u32[]{:S(2)}) collective-permute-start(f32[2,160]{1,0:T(2,128)S(1)} %slice.125), channel_id=1, source_target_pairs={{0,2},{1,5},{2,0},{3,7},{4,6},{5,1},{6,4},{7,3},{8,10},{9,13},{10,... | collective-permute-start | bytes 3848 | tf_op jit(solution)/shard_map/ppermute | solution.py:33
  87.3 5.0 %add_convert_fusion = bf16[768,1536]{1,0:T(8,128)(2,1)} fusion(f32[768,1536]{1,0:T(8,128)S(1)} %copy-done.1, f32[640,768]{1,0:T(8,128)S(1)} %copy-done.3, bf16[640,768]{1,0:T(8,128)(2,1)S(1)} %bitcast.48, bf16[320,1536]{1,0:T(8,128)(2,1)S(1)} %copy-done.11, bf16[160,1536]{1,0:T(8,128)(2,1)S(1)} %copy-done.7, bf16[80,1536]{1,0:T(8,128)(2,1)} %collective-permute-done, ...), kind=kOutput, calls=%fused_computation.2 | convolution fusion | flops 1521647616 | bytes 11993088 | tf_op jit(solution)/shard_map/dot_general | solution.py:103
  92.4 3.4 %fusion.23 = f32[1536,768]{1,0:T(8,128)S(1)} fusion(bf16[640,768]{1,0:T(8,128)(2,1)S(1)} %copy-done.12, bf16[320,1536]{1,0:T(8,128)(2,1)} %collective-permute-done.24, bf16[160,1536]{1,0:T(8,128)(2,1)S(1)} %copy-done.18, bf16[80,1536]{1,0:T(8,128)(2,1)S(1)} %copy-done.14, bf16[80,1536]{1,0:T(8,128)(2,1)} %collective-permute-done.21), kind=kOutput, calls=%fused_computation.43 | convolution fusion | flops 1517813760 | bytes 7667712 | tf_op jit(solution)/shard_map/dot_general | solution.py:106
  96.0 3.9 %collective-permute-start.17 = (f32[80]{0:T(128)S(1)}, f32[80]{0:T(128)S(1)}, u32[]{:S(2)}, u32[]{:S(2)}) collective-permute-start(f32[80]{0:T(128)S(1)} %get-tuple-element.13), channel_id=1, source_target_pairs={{0,8},{1,9},{2,10},{3,11},{4,12},{5,13},{6,14},{7,15},{8,0},{9,1},... | collective-permute-start | bytes 968 | tf_op jit(solution)/shard_map/ppermute | solution.py:113
  99.9 4.9 %add_convert_fusion.1 = bf16[1536,768]{1,0:T(8,128)(2,1)} fusion(f32[1536,768]{1,0:T(8,128)S(1)} %fusion.23, bf16[640,768]{1,0:T(8,128)(2,1)S(1)} %copy-done.9, bf16[320,1536]{1,0:T(8,128)(2,1)} %collective-permute-done.20, bf16[160,1536]{1,0:T(8,128)(2,1)S(1)} %copy-done.16, bf16[80,1536]{1,0:T(8,128)(2,1)} %collective-permute-done.18, ...), kind=kOutput, calls=%fused_computation.3 | convolution fusion | flops 1520173056 | bytes 10027008 | tf_op jit(solution)/shard_map/dot_general | solution.py:106
  105.0 0.5 compare_select_fusion.4
  105.6 0.2 add_convert_fusion.2
  105.8 0.9 collective-permute-start.11
  106.7 0.4 copy-done.5
  107.1 1.4 %add_convert_fusion.3 = bf16[320,1536]{1,0:T(8,128)(2,1)S(1)} fusion(bf16[320,1536]{1,0:T(8,128)(2,1)} %collective-permute-done.3, bf16[640,1536]{1,0:T(8,128)(2,1)S(1)} %copy-done.5), kind=kLoop, calls=%fused_computation.54 | loop fusion | flops 1966080 | bytes 2949120 | tf_op jit(solution)/shard_map/convert_element_type | solution.py:35
  108.6 0.9 collective-permute-start.4
  109.5 5.2 %collective-permute-done.11 = bf16[160,1536]{1,0:T(8,128)(2,1)S(1)} collective-permute-done((bf16[160,1536]{1,0:T(8,128)(2,1)S(1)}, bf16[160,1536]{1,0:T(8,128)(2,1)S(1)}, u32[]{:S(2)}, u32[]{:S(2)}) %collective-permute-start.11) | collective-permute-done | bytes 491552 | tf_op jit(solution)/shard_map/ppermute | solution.py:33
  114.7 0.1 add_convert_fusion.4
  114.9 0.3 collective-permute-start.12
  115.1 8.9 %collective-permute-done.4 = bf16[160,1536]{1,0:T(8,128)(2,1)S(1)} collective-permute-done((bf16[160,1536]{1,0:T(8,128)(2,1)S(1)}, bf16[160,1536]{1,0:T(8,128)(2,1)S(1)}, u32[]{:S(2)}, u32[]{:S(2)}) %collective-permute-start.4) | collective-permute-done | bytes 491552 | tf_op jit(solution)/shard_map/ppermute | solution.py:33
  124.1 0.1 add_convert_fusion.5
  124.4 8.3 %collective-permute-done.5 = bf16[80,1536]{1,0:T(8,128)(2,1)S(1)} collective-permute-done((bf16[80,1536]{1,0:T(8,128)(2,1)S(1)}, bf16[80,1536]{1,0:T(8,128)(2,1)S(1)}, u32[]{:S(2)}, u32[]{:S(2)}) %collective-permute-start.5) | collective-permute-done | bytes 245792 | tf_op jit(solution)/shard_map/ppermute | solution.py:33
  132.8 2.7 %collective-permute-done.13 = bf16[80,1536]{1,0:T(8,128)(2,1)S(1)} collective-permute-done((bf16[80,1536]{1,0:T(8,128)(2,1)S(1)}, bf16[80,1536]{1,0:T(8,128)(2,1)S(1)}, u32[]{:S(2)}, u32[]{:S(2)}) %collective-permute-start.13) | collective-permute-done | bytes 245792 | tf_op jit(solution)/shard_map/ppermute | solution.py:113
  135.5 1.1 convolution_convert_fusion.4
  (92 shorter events, 1.7 us)
Async XLA Ops:
  0.6 55.3 %copy-start = (bf16[768,1536]{1,0:T(8,128)(2,1)S(1)}, bf16[768,1536]{1,0:T(8,128)(2,1)}, u32[]{:S(2)}) copy-start(bf16[768,1536]{1,0:T(8,128)(2,1)} %param.17) | copy-start | bytes 7077892
  0.6 8.7 %copy-start.19 = (bf16[128,1536]{1,0:T(8,128)(2,1)S(1)}, bf16[128,1536]{1,0:T(8,128)(2,1)}, u32[]{:S(2)}) copy-start(bf16[128,1536]{1,0:T(8,128)(2,1)} %param.9) | copy-start | bytes 1179652
  3.7 21.8 %collective-permute-start.6 = (bf16[80,1536]{1,0:T(8,128)(2,1)}, bf16[80,1536]{1,0:T(8,128)(2,1)}, u32[]{:S(2)}, u32[]{:S(2)}) collective-permute-start(bf16[80,1536]{1,0:T(8,128)(2,1)} %get-tuple-element.11), channel_id=1, source_target_pairs={{0,8},{1,9},{2,10},{3,11},{4,12},{5,13},{6,14},{7,15},{8,0},{9,1},... | collective-permute-start | bytes 737288 | tf_op jit(solution)/shard_map/ppermute | solution.py:64
  7.8 11.0 %collective-permute-start = (bf16[80,1536]{1,0:T(8,128)(2,1)}, bf16[80,1536]{1,0:T(8,128)(2,1)}, u32[]{:S(2)}, u32[]{:S(2)}) collective-permute-start(bf16[80,1536]{1,0:T(8,128)(2,1)} %get-tuple-element.10), channel_id=1, source_target_pairs={{0,4},{1,3},{2,6},{3,1},{4,0},{5,7},{6,2},{7,5},{8,12},{9,11},{10,... | collective-permute-start | bytes 737288 | tf_op jit(solution)/shard_map/ppermute | solution.py:26
  10.4 21.5 %collective-permute-start.21 = (bf16[80,1536]{1,0:T(8,128)(2,1)}, bf16[80,1536]{1,0:T(8,128)(2,1)}, u32[]{:S(2)}, u32[]{:S(2)}) collective-permute-start(bf16[80,1536]{1,0:T(8,128)(2,1)} %get-tuple-element.9), channel_id=1, source_target_pairs={{0,8},{1,9},{2,10},{3,11},{4,12},{5,13},{6,14},{7,15},{8,0},{9,1},... | collective-permute-start | bytes 737288 | tf_op jit(solution)/shard_map/ppermute | solution.py:64
  10.8 18.5 %collective-permute-start.18 = (bf16[80,1536]{1,0:T(8,128)(2,1)}, bf16[80,1536]{1,0:T(8,128)(2,1)}, u32[]{:S(2)}, u32[]{:S(2)}) collective-permute-start(bf16[80,1536]{1,0:T(8,128)(2,1)} %get-tuple-element.8), channel_id=1, source_target_pairs={{0,4},{1,3},{2,6},{3,1},{4,0},{5,7},{6,2},{7,5},{8,12},{9,11},{10,... | collective-permute-start | bytes 737288 | tf_op jit(solution)/shard_map/ppermute | solution.py:26
  19.8 24.0 %collective-permute-start.1 = (bf16[160,1536]{1,0:T(8,128)(2,1)S(1)}, bf16[160,1536]{1,0:T(8,128)(2,1)S(1)}, u32[]{:S(2)}, u32[]{:S(2)}) collective-permute-start(bf16[160,1536]{1,0:T(8,128)(2,1)S(1)} %pad_maximum_fusion.5), channel_id=1, source_target_pairs={{0,2},{1,5},{2,0},{3,7},{4,6},{5,1},{6,4},{7,3},{8,10},{9,13},{10,... | collective-permute-start | bytes 1474568 | tf_op jit(solution)/shard_map/ppermute | solution.py:26
  25.5 10.6 %collective-permute-start.7 = (bf16[80,1536]{1,0:T(8,128)(2,1)}, bf16[80,1536]{1,0:T(8,128)(2,1)S(1)}, u32[]{:S(2)}, u32[]{:S(2)}) collective-permute-start(bf16[80,1536]{1,0:T(8,128)(2,1)} %collective-permute-done.6), channel_id=1, source_target_pairs={{0,4},{1,3},{2,6},{3,1},{4,0},{5,7},{6,2},{7,5},{8,12},{9,11},{10,... | collective-permute-start | bytes 737288 | tf_op jit(solution)/shard_map/ppermute | solution.py:26
  30.3 14.9 %collective-permute-start.19 = (bf16[160,1536]{1,0:T(8,128)(2,1)S(1)}, bf16[160,1536]{1,0:T(8,128)(2,1)S(1)}, u32[]{:S(2)}, u32[]{:S(2)}) collective-permute-start(bf16[160,1536]{1,0:T(8,128)(2,1)S(1)} %pad_maximum_fusion.7), channel_id=1, source_target_pairs={{0,2},{1,5},{2,0},{3,7},{4,6},{5,1},{6,4},{7,3},{8,10},{9,13},{10,... | collective-permute-start | bytes 1474568 | tf_op jit(solution)/shard_map/ppermute | solution.py:26
  31.9 9.6 %collective-permute-start.22 = (bf16[80,1536]{1,0:T(8,128)(2,1)}, bf16[80,1536]{1,0:T(8,128)(2,1)S(1)}, u32[]{:S(2)}, u32[]{:S(2)}) collective-permute-start(bf16[80,1536]{1,0:T(8,128)(2,1)} %collective-permute-done.21), channel_id=1, source_target_pairs={{0,4},{1,3},{2,6},{3,1},{4,0},{5,7},{6,2},{7,5},{8,12},{9,11},{10,... | collective-permute-start | bytes 737288 | tf_op jit(solution)/shard_map/ppermute | solution.py:26
  37.0 11.0 %collective-permute-start.8 = (bf16[160,1536]{1,0:T(8,128)(2,1)S(1)}, bf16[160,1536]{1,0:T(8,128)(2,1)S(1)}, u32[]{:S(2)}, u32[]{:S(2)}) collective-permute-start(bf16[160,1536]{1,0:T(8,128)(2,1)S(1)} %pad_maximum_fusion.6), channel_id=1, source_target_pairs={{0,2},{1,5},{2,0},{3,7},{4,6},{5,1},{6,4},{7,3},{8,10},{9,13},{10,... | collective-permute-start | bytes 1474568 | tf_op jit(solution)/shard_map/ppermute | solution.py:26
  41.5 10.0 %copy-start.13 = (bf16[80,1536]{1,0:T(8,128)(2,1)}, bf16[80,1536]{1,0:T(8,128)(2,1)S(1)}, u32[]{:S(2)}) copy-start(bf16[80,1536]{1,0:T(8,128)(2,1)S(1)} %collective-permute-done.22) | copy-start | bytes 737284
  42.6 8.9 %collective-permute-start.23 = (bf16[160,1536]{1,0:T(8,128)(2,1)S(1)}, bf16[160,1536]{1,0:T(8,128)(2,1)S(1)}, u32[]{:S(2)}, u32[]{:S(2)}) collective-permute-start(bf16[160,1536]{1,0:T(8,128)(2,1)S(1)} %pad_maximum_fusion.8), channel_id=1, source_target_pairs={{0,2},{1,5},{2,0},{3,7},{4,6},{5,1},{6,4},{7,3},{8,10},{9,13},{10,... | collective-permute-start | bytes 1474568 | tf_op jit(solution)/shard_map/ppermute | solution.py:26
  43.8 12.1 %copy-start.6 = (bf16[160,1536]{1,0:T(8,128)(2,1)}, bf16[160,1536]{1,0:T(8,128)(2,1)S(1)}, u32[]{:S(2)}) copy-start(bf16[160,1536]{1,0:T(8,128)(2,1)S(1)} %collective-permute-done.1) | copy-start | bytes 1474564
  45.1 10.8 %collective-permute-start.2 = (bf16[320,1536]{1,0:T(8,128)(2,1)S(1)}, bf16[320,1536]{1,0:T(8,128)(2,1)S(1)}, u32[]{:S(2)}, u32[]{:S(2)}) collective-permute-start(bf16[320,1536]{1,0:T(8,128)(2,1)S(1)} %pad_maximum_fusion.1), channel_id=1, source_target_pairs={{0,1},{1,0},{2,3},{3,2},{4,5},{5,4},{6,7},{7,6},{8,9},{9,8},{10,11... | collective-permute-start | bytes 2949128 | tf_op jit(solution)/shard_map/ppermute | solution.py:26
  45.2 4.8 %copy-start.15 = (bf16[160,1536]{1,0:T(8,128)(2,1)}, bf16[160,1536]{1,0:T(8,128)(2,1)S(1)}, u32[]{:S(2)}) copy-start(bf16[160,1536]{1,0:T(8,128)(2,1)S(1)} %collective-permute-done.19) | copy-start | bytes 1474564
  47.6 52.4 %collective-permute-start.20 = (bf16[320,1536]{1,0:T(8,128)(2,1)}, bf16[320,1536]{1,0:T(8,128)(2,1)}, u32[]{:S(2)}, u32[]{:S(2)}) collective-permute-start(bf16[320,1536]{1,0:T(8,128)(2,1)} %pad_maximum_fusion.3), channel_id=1, source_target_pairs={{0,1},{1,0},{2,3},{3,2},{4,5},{5,4},{6,7},{7,6},{8,9},{9,8},{10,11... | collective-permute-start | bytes 2949128 | tf_op jit(solution)/shard_map/ppermute | solution.py:26
  50.0 16.9 %collective-permute-start.9 = (bf16[320,1536]{1,0:T(8,128)(2,1)}, bf16[320,1536]{1,0:T(8,128)(2,1)}, u32[]{:S(2)}, u32[]{:S(2)}) collective-permute-start(bf16[320,1536]{1,0:T(8,128)(2,1)} %pad_maximum_fusion.2), channel_id=1, source_target_pairs={{0,1},{1,0},{2,3},{3,2},{4,5},{5,4},{6,7},{7,6},{8,9},{9,8},{10,11... | collective-permute-start | bytes 2949128 | tf_op jit(solution)/shard_map/ppermute | solution.py:26
  51.5 4.5 %copy-start.17 = (bf16[160,1536]{1,0:T(8,128)(2,1)}, bf16[160,1536]{1,0:T(8,128)(2,1)S(1)}, u32[]{:S(2)}) copy-start(bf16[160,1536]{1,0:T(8,128)(2,1)S(1)} %collective-permute-done.23) | copy-start | bytes 1474564
  53.6 38.8 %collective-permute-start.24 = (bf16[320,1536]{1,0:T(8,128)(2,1)}, bf16[320,1536]{1,0:T(8,128)(2,1)}, u32[]{:S(2)}, u32[]{:S(2)}) collective-permute-start(bf16[320,1536]{1,0:T(8,128)(2,1)} %pad_maximum_fusion.4), channel_id=1, source_target_pairs={{0,1},{1,0},{2,3},{3,2},{4,5},{5,4},{6,7},{7,6},{8,9},{9,8},{10,11... | collective-permute-start | bytes 2949128 | tf_op jit(solution)/shard_map/ppermute | solution.py:26
  55.9 5.2 %copy-start.10 = (bf16[320,1536]{1,0:T(8,128)(2,1)}, bf16[320,1536]{1,0:T(8,128)(2,1)S(1)}, u32[]{:S(2)}) copy-start(bf16[320,1536]{1,0:T(8,128)(2,1)S(1)} %collective-permute-done.2) | copy-start | bytes 2949124
  61.2 2.9 %copy-start.22 = (bf16[1536,768]{1,0:T(8,128)(2,1)S(1)}, bf16[1536,768]{1,0:T(8,128)(2,1)}, u32[]{:S(2)}) copy-start(bf16[1536,768]{1,0:T(8,128)(2,1)} %param.16) | copy-start | bytes 7077892
  64.1 1.7 %copy-start.8 = (bf16[640,768]{1,0:T(8,128)(2,1)}, bf16[640,768]{1,0:T(8,128)(2,1)S(1)}, u32[]{:S(2)}) copy-start(bf16[640,768]{1,0:T(8,128)(2,1)S(1)} %fusion.7) | copy-start | bytes 2949124
  65.8 1.6 %copy-start.4 = (bf16[640,1536]{1,0:T(8,128)(2,1)}, bf16[640,1536]{1,0:T(8,128)(2,1)S(1)}, u32[]{:S(2)}) copy-start(bf16[640,1536]{1,0:T(8,128)(2,1)S(1)} %convolution_convert_fusion.1) | copy-start | bytes 5898244
  65.8 3.9 %copy-start.2 = (bf16[8,80,768]{2,1,0:T(8,128)(2,1)S(1)}, bf16[8,80,768]{2,1,0:T(8,128)(2,1)}, u32[]{:S(2)}) copy-start(bf16[8,80,768]{2,1,0:T(8,128)(2,1)} %gather_fusion.1) | copy-start | bytes 2949124
  66.9 39.8 %collective-permute-start.3 = (bf16[320,1536]{1,0:T(8,128)(2,1)}, bf16[320,1536]{1,0:T(8,128)(2,1)}, u32[]{:S(2)}, u32[]{:S(2)}) collective-permute-start(bf16[320,1536]{1,0:T(8,128)(2,1)} %slice.110), channel_id=1, source_target_pairs={{0,1},{1,0},{2,3},{3,2},{4,5},{5,4},{6,7},{7,6},{8,9},{9,8},{10,11... | collective-permute-start | bytes 2949128 | tf_op jit(solution)/shard_map/ppermute | solution.py:33
  80.8 4.5 %collective-permute-start.14 = (f32[4,160]{1,0:T(4,128)S(1)}, f32[4,160]{1,0:T(4,128)S(1)}, u32[]{:S(2)}, u32[]{:S(2)}) collective-permute-start(f32[4,160]{1,0:T(4,128)S(1)} %pad_maximum_fusion.11), channel_id=1, source_target_pairs={{0,1},{1,0},{2,3},{3,2},{4,5},{5,4},{6,7},{7,6},{8,9},{9,8},{10,11... | collective-permute-start | bytes 7688 | tf_op jit(solution)/shard_map/ppermute | solution.py:33
  80.8 6.4 %copy-start.1 = (f32[768,1536]{1,0:T(8,128)S(1)}, f32[768,1536]{1,0:T(8,128)}, u32[]{:S(2)}) copy-start(f32[768,1536]{1,0:T(8,128)} %fusion.33) | copy-start | bytes 14155780
  80.8 6.4 %copy-start.7 = (bf16[160,1536]{1,0:T(8,128)(2,1)S(1)}, bf16[160,1536]{1,0:T(8,128)(2,1)}, u32[]{:S(2)}) copy-start(bf16[160,1536]{1,0:T(8,128)(2,1)} %copy-done.6) | copy-start | bytes 1474564
  80.8 6.4 %copy-start.11 = (bf16[320,1536]{1,0:T(8,128)(2,1)S(1)}, bf16[320,1536]{1,0:T(8,128)(2,1)}, u32[]{:S(2)}) copy-start(bf16[320,1536]{1,0:T(8,128)(2,1)} %copy-done.10) | copy-start | bytes 2949124
  84.7 2.6 %copy-start.3 = (f32[640,768]{1,0:T(8,128)S(1)}, f32[640,768]{1,0:T(8,128)}, u32[]{:S(2)}) copy-start(f32[640,768]{1,0:T(8,128)} %get-tuple-element.5) | copy-start | bytes 5898244
  84.8 20.8 %collective-permute-start.10 = (bf16[320,1536]{1,0:T(8,128)(2,1)S(1)}, bf16[320,1536]{1,0:T(8,128)(2,1)S(1)}, u32[]{:S(2)}, u32[]{:S(2)}) collective-permute-start(bf16[320,1536]{1,0:T(8,128)(2,1)S(1)} %slice.117), channel_id=1, source_target_pairs={{0,1},{1,0},{2,3},{3,2},{4,5},{5,4},{6,7},{7,6},{8,9},{9,8},{10,11... | collective-permute-start | bytes 2949128 | tf_op jit(solution)/shard_map/ppermute | solution.py:33
  85.4 6.9 %collective-permute-start.15 = (f32[2,160]{1,0:T(2,128)S(1)}, f32[2,160]{1,0:T(2,128)S(1)}, u32[]{:S(2)}, u32[]{:S(2)}) collective-permute-start(f32[2,160]{1,0:T(2,128)S(1)} %slice.125), channel_id=1, source_target_pairs={{0,2},{1,5},{2,0},{3,7},{4,6},{5,1},{6,4},{7,3},{8,10},{9,13},{10,... | collective-permute-start | bytes 3848 | tf_op jit(solution)/shard_map/ppermute | solution.py:33
  87.3 5.2 %copy-start.12 = (bf16[640,768]{1,0:T(8,128)(2,1)S(1)}, bf16[640,768]{1,0:T(8,128)(2,1)}, u32[]{:S(2)}) copy-start(bf16[640,768]{1,0:T(8,128)(2,1)} %fusion.15) | copy-start | bytes 2949124
  87.3 5.2 %copy-start.14 = (bf16[80,1536]{1,0:T(8,128)(2,1)S(1)}, bf16[80,1536]{1,0:T(8,128)(2,1)}, u32[]{:S(2)}) copy-start(bf16[80,1536]{1,0:T(8,128)(2,1)} %copy-done.13) | copy-start | bytes 737284
  87.3 5.2 %copy-start.18 = (bf16[160,1536]{1,0:T(8,128)(2,1)S(1)}, bf16[160,1536]{1,0:T(8,128)(2,1)}, u32[]{:S(2)}) copy-start(bf16[160,1536]{1,0:T(8,128)(2,1)} %copy-done.17) | copy-start | bytes 1474564
  92.3 7.6 %copy-start.9 = (bf16[640,768]{1,0:T(8,128)(2,1)S(1)}, bf16[640,768]{1,0:T(8,128)(2,1)}, u32[]{:S(2)}) copy-start(bf16[640,768]{1,0:T(8,128)(2,1)} %copy-done.8) | copy-start | bytes 2949124
  92.3 7.6 %copy-start.16 = (bf16[160,1536]{1,0:T(8,128)(2,1)S(1)}, bf16[160,1536]{1,0:T(8,128)(2,1)}, u32[]{:S(2)}) copy-start(bf16[160,1536]{1,0:T(8,128)(2,1)} %copy-done.15) | copy-start | bytes 1474564
  92.3 3.6 %collective-permute-start.16 = (f32[1,160]{1,0:T(1,128)S(1)}, f32[1,160]{1,0:T(1,128)S(1)}, u32[]{:S(2)}, u32[]{:S(2)}) collective-permute-start(f32[1,160]{1,0:T(1,128)S(1)} %slice.127), channel_id=1, source_target_pairs={{0,4},{1,3},{2,6},{3,1},{4,0},{5,7},{6,2},{7,5},{8,12},{9,11},{10,... | collective-permute-start | bytes 1928 | tf_op jit(solution)/shard_map/ppermute | solution.py:33
  96.0 9.0 %copy-start.20 = (f32[128]{0:T(128)S(1)}, f32[128]{0:T(128)}, u32[]{:S(2)}) copy-start(f32[128]{0:T(128)} %param.11) | copy-start | bytes 1540
  96.0 9.0 %copy-start.21 = (s32[128]{0:T(128)S(1)}, s32[128]{0:T(128)}, u32[]{:S(2)}) copy-start(s32[128]{0:T(128)} %param.13) | copy-start | bytes 1540
  96.0 8.8 %collective-permute-start.17 = (f32[80]{0:T(128)S(1)}, f32[80]{0:T(128)S(1)}, u32[]{:S(2)}, u32[]{:S(2)}) collective-permute-start(f32[80]{0:T(128)S(1)} %get-tuple-element.13), channel_id=1, source_target_pairs={{0,8},{1,9},{2,10},{3,11},{4,12},{5,13},{6,14},{7,15},{8,0},{9,1},... | collective-permute-start | bytes 968 | tf_op jit(solution)/shard_map/ppermute | solution.py:113
  105.6 1.5 %copy-start.5 = (bf16[640,1536]{1,0:T(8,128)(2,1)S(1)}, bf16[640,1536]{1,0:T(8,128)(2,1)}, u32[]{:S(2)}) copy-start(bf16[640,1536]{1,0:T(8,128)(2,1)} %copy-done.4) | copy-start | bytes 5898244
  105.8 8.9 %collective-permute-start.11 = (bf16[160,1536]{1,0:T(8,128)(2,1)S(1)}, bf16[160,1536]{1,0:T(8,128)(2,1)S(1)}, u32[]{:S(2)}, u32[]{:S(2)}) collective-permute-start(bf16[160,1536]{1,0:T(8,128)(2,1)S(1)} %slice.119), channel_id=1, source_target_pairs={{0,2},{1,5},{2,0},{3,7},{4,6},{5,1},{6,4},{7,3},{8,10},{9,13},{10,... | collective-permute-start | bytes 1474568 | tf_op jit(solution)/shard_map/ppermute | solution.py:33
  108.6 15.5 %collective-permute-start.4 = (bf16[160,1536]{1,0:T(8,128)(2,1)S(1)}, bf16[160,1536]{1,0:T(8,128)(2,1)S(1)}, u32[]{:S(2)}, u32[]{:S(2)}) collective-permute-start(bf16[160,1536]{1,0:T(8,128)(2,1)S(1)} %slice.112), channel_id=1, source_target_pairs={{0,2},{1,5},{2,0},{3,7},{4,6},{5,1},{6,4},{7,3},{8,10},{9,13},{10,... | collective-permute-start | bytes 1474568 | tf_op jit(solution)/shard_map/ppermute | solution.py:33
  114.9 9.4 %collective-permute-start.12 = (bf16[80,1536]{1,0:T(8,128)(2,1)S(1)}, bf16[80,1536]{1,0:T(8,128)(2,1)S(1)}, u32[]{:S(2)}, u32[]{:S(2)}) collective-permute-start(bf16[80,1536]{1,0:T(8,128)(2,1)S(1)} %slice.121), channel_id=1, source_target_pairs={{0,4},{1,3},{2,6},{3,1},{4,0},{5,7},{6,2},{7,5},{8,12},{9,11},{10,... | collective-permute-start | bytes 737288 | tf_op jit(solution)/shard_map/ppermute | solution.py:33
  124.2 8.5 %collective-permute-start.5 = (bf16[80,1536]{1,0:T(8,128)(2,1)S(1)}, bf16[80,1536]{1,0:T(8,128)(2,1)S(1)}, u32[]{:S(2)}, u32[]{:S(2)}) collective-permute-start(bf16[80,1536]{1,0:T(8,128)(2,1)S(1)} %slice.114), channel_id=1, source_target_pairs={{0,4},{1,3},{2,6},{3,1},{4,0},{5,7},{6,2},{7,5},{8,12},{9,11},{10,... | collective-permute-start | bytes 737288 | tf_op jit(solution)/shard_map/ppermute | solution.py:33
  124.4 11.2 %collective-permute-start.13 = (bf16[80,1536]{1,0:T(8,128)(2,1)S(1)}, bf16[80,1536]{1,0:T(8,128)(2,1)S(1)}, u32[]{:S(2)}, u32[]{:S(2)}) collective-permute-start(bf16[80,1536]{1,0:T(8,128)(2,1)S(1)} %add_convert_fusion.6), channel_id=1, source_target_pairs={{0,8},{1,9},{2,10},{3,11},{4,12},{5,13},{6,14},{7,15},{8,0},{9,1},... | collective-permute-start | bytes 737288 | tf_op jit(solution)/shard_map/ppermute | solution.py:113

commit v2 on v1

--- a/solution.py
+++ b/solution.py
@@ -4,7 +4,6 @@
 from jax.sharding import PartitionSpec as P
 
 SPLIT = 8
-CORE, LOW, HIGH = 1, 2, 4
 
 
 def normal_parts(hidden):
@@ -13,27 +12,20 @@
     return (normal_cdf, density)
 
 
-def bits(core):
-    return (HIGH, LOW, CORE) if core == 0 else (LOW, HIGH, CORE)
-
-
-def pairs(devices, step):
-    return [(i, i ^ bits(i % 2)[step]) for i in range(devices)]
+def groups(devices):
+    return [list(range(e, e + SPLIT)) for e in range(0, devices, SPLIT)]
 
 
 def gather_rows(rows, devices):
-    for step in range(3):
-        rows = jnp.concatenate([rows, lax.ppermute(rows, "expert", pairs(devices, step))])
-    return rows
+    return lax.all_gather(
+        rows, "expert", axis_index_groups=groups(devices), axis=0, tiled=True
+    )
 
 
 def scatter_sum(rows, devices):
-    for step in (2, 1, 0):
-        half = rows.shape[0] // 2
-        got = lax.ppermute(rows[half:], "expert", pairs(devices, step))
-        total = rows[:half].astype(jnp.float32) + got.astype(jnp.float32)
-        rows = total.astype(rows.dtype) if step else total
-    return rows
+    return lax.psum_scatter(
+        rows, "expert", axis_index_groups=groups(devices), scatter_dimension=0, tiled=True
+    )
 
 
 def shift(devices, by):
@@ -46,7 +38,7 @@
     slots = saved_hidden.shape[0] // devices
     hidden_units = saved_hidden.shape[1]
     me = lax.axis_index("expert")
-    my_expert, my_place = me // SPLIT, me % SPLIT
+    my_expert = me // SPLIT
 
     scaled = (gate[:, None] * out_grad.astype(jnp.float32)).astype(jnp.bfloat16)
     ahead = lax.rem(expert_id - my_expert + experts, experts)
@@ -67,17 +59,11 @@
         )
         return gather_rows(buffer[:slots], devices), gather_rows(far, devices)
 
-    core = me % 2
-    near_masks = []
-    for i in range(SPLIT):
-        swapped = core ^ (i >> 2)
-        first, second = jnp.where(swapped, LOW, HIGH), jnp.where(swapped, HIGH, LOW)
-        near_masks.append((i & 1) * first + ((i >> 1) & 1) * second + (i >> 2) * CORE)
-    near_order = jnp.stack([my_expert * SPLIT + (my_place ^ m) for m in near_masks])
+    near_order = my_expert * SPLIT + jnp.arange(SPLIT)
     far_order = jnp.stack(
         [
-            lax.rem(my_expert - s + experts, experts) * SPLIT + (my_place ^ m)
-            for m in near_masks
+            lax.rem(my_expert - s + experts, experts) * SPLIT + i
+            for i in range(SPLIT)
             for s in range(1, experts)
         ]
     )

time: 137 us -> 199 us (1.45)
  waiting for transfers between devices: 40.7 us -> 103 us
  other arithmetic: 20.3 us -> 3.1 us
  starting transfers between devices: 23.6 us -> 9.08 us
  blocking collectives: 0 us -> 13.8 us
  between operations: 1.1 us -> 14.3 us
  matrix products: 36 us -> 41.1 us
    reduce_scatter x0 -> x2, waiting for transfers between devices: none -> 47.7 us  [scatter_sum(): lax.psum_scatter(rows, 'expert', axis_index_groups=groups(devices), scatt...]
    ppermute x21 -> x0, waiting for transfers between devices: 33.8 us -> none  [the longest x9 22.6 us: scatter_sum(): got = lax.ppermute(rows[half:], 'expert', pairs(devices, step))]
    all_gather x0 -> x4, waiting for transfers between devices: none -> 29.7 us  [gather_rows(): lax.all_gather(rows, 'expert', axis_index_groups=groups(devices), axis=0,...]
    ppermute x2, waiting for transfers between devices: 4.09 us -> 24.6 us  [dispatch(): lax.ppermute(buffer[s * slots:(s + 1) * slots], 'expert', shift(devices, s))]
    ppermute x21 -> x0, starting transfers between devices: 15.3 us -> none  [the longest x12 10.7 us: gather_rows(): lax.ppermute(rows, 'expert', pairs(devices, step))]
    unnamed x0 -> x1, blocking collectives: none -> 13.8 us
    concatenate x8 -> x0, other arithmetic: 11.9 us -> none  [gather_rows(): jnp.concatenate([rows, lax.ppermute(rows, 'expert', pairs(devices, step))])]
    dot_general x2, matrix products: 8.3 us -> 12.9 us  [body(): lax.dot_general(rows, hidden_grad, (((0,), (0,)), ((), ())), preferred_el...]
  transfers between devices with their start and end apart: 25 -> 10, of which waited for: 10 -> 7; matrix products, arithmetic and copies ran while one was open for 48% -> 24% of each run, Pallas kernels for 0% -> 0%
where the time goes in v2:
time: 199 us
  waiting for transfers between devices  103 us (52%)
  matrix products  41.1 us (21%)
  local copies, waits for them, and re-layouts  14.4 us (7%)
  between operations  14.3 us (7%)
  blocking collectives  13.8 us (7%)
  starting transfers between devices  9.08 us (5%)
  other arithmetic  3.1 us (2%)
    reduce_scatter x2, waiting for transfers between devices, scatter_sum(): lax.psum_scatter(rows, 'expert', axis_index_groups=groups(devices), scatt...  47.7 us
    all_gather x4, waiting for transfers between devices, gather_rows(): lax.all_gather(rows, 'expert', axis_index_groups=groups(devices), axis=0,...  29.7 us
    ppermute x2, waiting for transfers between devices, dispatch(): lax.ppermute(buffer[s * slots:(s + 1) * slots], 'expert', shift(devices, s))  24.6 us
    unnamed x1, blocking collectives  13.8 us
    dot_general x2, matrix products, body(): lax.dot_general(rows, hidden_grad, (((0,), (0,)), ((), ())), preferred_el...  12.9 us
    dot_general x2, matrix products, body(): lax.dot_general(activated_b, routed_grad, (((0,), (0,)), ((), ())), prefe...  11.2 us
    dot_general x2, matrix products, body(): lax.dot_general(routed_grad, w_out, (((1,), (1,)), ((), ())), preferred_e...  7.35 us
    unnamed x35, local copies, waits for them, and re-layouts  6.67 us
  transfers between devices with their start and end apart: 10, of which 7 were waited for; matrix products, arithmetic and copies ran while one was open for 24% of the time, Pallas kernels for 0%

profile of v2, /device:TPU:0, one launch (start us, length us, event | category | flops | bytes accessed | tf_op | source)
XLA Modules:
  0.0 198.6 jit_solution(15658351367831842143)
XLA Ops:
  7.2 0.0 copy-start
  7.2 0.0 all-gather.7.cloned.1.call-start
  7.3 0.9 compare_select_fusion.5
  8.1 1.4 convolution_convert_fusion.3
  9.5 0.7 fusion.37
  10.2 4.0 %collective-permute-start = (bf16[80,1536]{1,0:T(8,128)(2,1)S(1)}, bf16[80,1536]{1,0:T(8,128)(2,1)S(1)}, u32[]{:S(2)}, u32[]{:S(2)}) collective-permute-start(bf16[80,1536]{1,0:T(8,128)(2,1)S(1)} %get-tuple-element.11), channel_id=1, source_target_pairs={{0,8},{1,9},{2,10},{3,11},{4,12},{5,13},{6,14},{7,15},{8,0},{9,1},... | collective-permute-start | bytes 737288 | tf_op jit(solution)/shard_map/ppermute | solution.py:56
  14.3 11.2 %collective-permute-done = bf16[80,1536]{1,0:T(8,128)(2,1)S(1)} collective-permute-done((bf16[80,1536]{1,0:T(8,128)(2,1)S(1)}, bf16[80,1536]{1,0:T(8,128)(2,1)S(1)}, u32[]{:S(2)}, u32[]{:S(2)}) %collective-permute-start) | collective-permute-done | bytes 245792 | tf_op jit(solution)/shard_map/ppermute | solution.py:56
  25.5 0.7 copy-done.11
  26.2 0.0 all-gather.7.cloned.1.call-update
  26.2 0.0 all-gather.5.cloned.1.call-start
  26.3 0.7 all-gather.5.cloned.1.call-update
  27.0 0.0 all-gather.9.cloned.1.call-start
  27.0 0.3 convolution_convert_fusion.2
  27.3 0.8 fusion.36
  28.1 0.0 all-gather.9.cloned.1.call-update
  28.1 0.0 all-gather.11.cloned.1.call-start
  28.1 0.1 collective-permute-start.3
  28.2 13.4 %collective-permute-done.3 = bf16[80,1536]{1,0:T(8,128)(2,1)S(1)} collective-permute-done((bf16[80,1536]{1,0:T(8,128)(2,1)S(1)}, bf16[80,1536]{1,0:T(8,128)(2,1)S(1)}, u32[]{:S(2)}, u32[]{:S(2)}) %collective-permute-start.3) | collective-permute-done | bytes 245792 | tf_op jit(solution)/shard_map/ppermute | solution.py:56
  41.6 0.7 copy-done.10
  42.3 0.0 all-gather.11.cloned.1.call-update
  42.3 0.0 reduce-scatter.5.cloned.1.call-start
  42.4 0.1 stack.35
  42.5 2.2 %gather_fusion.1 = bf16[8,80,768]{2,1,0:T(8,128)(2,1)S(1)} fusion(bf16[16,80,768]{2,1,0:T(8,128)(2,1)} %bitcast.47, s32[1024]{0:T(1024)S(1)} %pad_clamp_fusion), kind=kCustom, calls=%fused_computation.1 | custom fusion | bytes 1966112 | tf_op jit(solution)/shard_map/gather | solution.py:77
  44.7 7.5 %all-gather.7.cloned.1.call-done = bf16[640,1536]{1,0:T(8,128)(2,1)} async-done(((bf16[80,1536]{1,0:T(8,128)(2,1)}), bf16[640,1536]{1,0:T(8,128)(2,1)}) %all-gather.7.cloned.1.call-update) | async-done | bytes 1966096 | tf_op jit(solution)/shard_map/all_gather | solution.py:20
  52.2 3.5 %multiply_reduce_fusion = (f32[640]{0:T(1024)S(1)}, f32[640,768]{1,0:T(8,128)S(1)}, f32[640,768]{1,0:T(8,128)S(1)}) fusion(bf16[8,80,768]{2,1,0:T(8,128)(2,1)S(1)} %gather_fusion.1, bf16[640,1536]{1,0:T(8,128)(2,1)} %all-gather.7.cloned.1.call-done, bf16[768,1536]{1,0:T(8,128)(2,1)S(1)} %copy-done), kind=kOutput, calls=%fused_computation.35 | convolution fusion | flops 1513389440 | bytes 9243136 | tf_op jit(solution)/shard_map/dot_general | solution.py:81
  55.7 0.0 copy-start.14
  55.8 0.7 fusion.15
  56.5 0.5 copy-done.1
  57.0 1.0 copy-done.7
  58.0 0.5 copy-done.14
  58.5 3.0 %convolution_convert_fusion = bf16[640,1536]{1,0:T(8,128)(2,1)} fusion(bf16[640,768]{1,0:T(8,128)(2,1)S(1)} %fusion.15, bf16[1536,768]{1,0:T(8,128)(2,1)S(1)} %copy-done.14), kind=kOutput, calls=%fused_computation.14 | convolution fusion | flops 1510932480 | bytes 5308416 | tf_op jit(solution)/shard_map/dot_general | solution.py:85
  61.5 0.0 reduce-scatter.5.cloned.1.call-update
  61.5 0.0 reduce-scatter.3.cloned.1.call-start
  61.6 3.1 %gather_fusion = bf16[8,80,768]{2,1,0:T(8,128)(2,1)} fusion(bf16[16,80,768]{2,1,0:T(8,128)(2,1)} %bitcast.48, s32[1024]{0:T(1024)S(1)} %pad_clamp_fusion.1), kind=kCustom, calls=%fused_computation | custom fusion | bytes 1966112 | tf_op jit(solution)/shard_map/gather | solution.py:77
  64.7 9.9 %all-gather.5.cloned.1.call-done = bf16[640,1536]{1,0:T(8,128)(2,1)} async-done(((bf16[80,1536]{1,0:T(8,128)(2,1)}), bf16[640,1536]{1,0:T(8,128)(2,1)}) %all-gather.5.cloned.1.call-update) | async-done | bytes 1966096 | tf_op jit(solution)/shard_map/all_gather | solution.py:20
  74.6 3.8 %multiply_reduce_fusion.1 = (f32[640]{0:T(1024)S(1)}, f32[640,768]{1,0:T(8,128)S(1)}, f32[640,768]{1,0:T(8,128)S(1)}) fusion(bf16[8,80,768]{2,1,0:T(8,128)(2,1)} %gather_fusion, bf16[640,1536]{1,0:T(8,128)(2,1)} %all-gather.5.cloned.1.call-done, bf16[768,1536]{1,0:T(8,128)(2,1)S(1)} %copy-done), kind=kOutput, calls=%fused_computation.36 | convolution fusion | flops 1513389440 | bytes 9243136 | tf_op jit(solution)/shard_map/dot_general | solution.py:81
  78.5 0.0 copy-start.4
  78.5 0.0 copy-start.15
  78.5 0.7 fusion.7
  79.2 0.5 copy-done.4
  79.7 0.9 copy-done.8
  80.7 0.5 copy-done.15
  81.2 3.0 %convolution_convert_fusion.1 = bf16[640,1536]{1,0:T(8,128)(2,1)} fusion(bf16[640,768]{1,0:T(8,128)(2,1)S(1)} %fusion.7, bf16[1536,768]{1,0:T(8,128)(2,1)S(1)} %copy-done.15), kind=kOutput, calls=%fused_computation.15 | convolution fusion | flops 1510932480 | bytes 5308416 | tf_op jit(solution)/shard_map/dot_general | solution.py:85
  84.2 0.0 reduce-scatter.3.cloned.1.call-update
  84.2 0.6 copy-done.16
  84.8 0.6 dynamic-slice
  85.4 0.1 reshape.359
  85.5 12.3 %all-gather.9.cloned.1.call-done = bf16[640,1536]{1,0:T(8,128)(2,1)} async-done(((bf16[80,1536]{1,0:T(8,128)(2,1)}), bf16[640,1536]{1,0:T(8,128)(2,1)}) %all-gather.9.cloned.1.call-update) | async-done | bytes 1966096 | tf_op jit(solution)/shard_map/all_gather | solution.py:20
  97.8 6.1 %fusion.38 = f32[1536,768]{1,0:T(8,128)} fusion(bf16[640,1536]{1,0:T(8,128)(2,1)} %all-gather.9.cloned.1.call-done, bf16[640,768]{1,0:T(8,128)(2,1)} %copy-done.8), kind=kOutput, calls=%fused_computation.70 | convolution fusion | flops 1509949440 | bytes 7667712 | tf_op jit(solution)/shard_map/dot_general | solution.py:92
  103.9 4.2 %fusion.19 = f32[768,1536]{1,0:T(8,128)} fusion(bf16[640,1536]{1,0:T(8,128)(2,1)S(1)} %copy-done.6, f32[640,768]{1,0:T(8,128)S(1)} %copy-done.5, bf16[640,768]{1,0:T(8,128)(2,1)S(1)} %bitcast.46), kind=kOutput, calls=%fused_computation.39 | convolution fusion | flops 1511424000 | bytes 9633792 | tf_op jit(solution)/shard_map/dot_general | solution.py:89
  108.2 0.1 reshape.360
  108.2 0.1 pad_maximum_fusion
  108.3 13.8 %all-reduce = f32[8,160]{1,0:T(8,128)S(1)} all-reduce(f32[8,160]{1,0:T(8,128)S(1)} %pad_maximum_fusion), channel_id=4, replica_groups={{0,1,2,3,4,5,6,7},{8,9,10,11,12,13,14,15},{16,17,18,19,20,21,22,23},{24..., use_global_device_ids=true, to_apply=%region_4.5.clone | all-reduce | flops 1280 | bytes 10240
  122.1 0.7 dynamic-slice_bitcast_fusion.1
  122.8 2.4 %collective-permute-start.2 = (f32[80]{0:T(128)S(1)}, f32[80]{0:T(128)S(1)}, u32[]{:S(2)}, u32[]{:S(2)}) collective-permute-start(f32[80]{0:T(128)S(1)} %get-tuple-element.13), channel_id=1, source_target_pairs={{0,8},{1,9},{2,10},{3,11},{4,12},{5,13},{6,14},{7,15},{8,0},{9,1},... | collective-permute-start | bytes 968 | tf_op jit(solution)/shard_map/ppermute | solution.py:99
  125.2 7.0 %add_convert_fusion = bf16[768,1536]{1,0:T(8,128)(2,1)} fusion(f32[768,1536]{1,0:T(8,128)} %fusion.19, bf16[640,1536]{1,0:T(8,128)(2,1)} %all-gather.7.cloned.1.call-done, f32[640,768]{1,0:T(8,128)} %copy-done.1, bf16[640,768]{1,0:T(8,128)(2,1)S(1)} %bitcast.45), kind=kOutput, calls=%fused_computation.2 | convolution fusion | flops 1513783296 | bytes 11993088 | tf_op jit(solution)/shard_map/dot_general | solution.py:89
  132.2 6.8 %add_convert_fusion.1 = bf16[1536,768]{1,0:T(8,128)(2,1)} fusion(f32[1536,768]{1,0:T(8,128)} %fusion.38, bf16[640,1536]{1,0:T(8,128)(2,1)} %all-gather.11.cloned.1.call-done, bf16[640,768]{1,0:T(8,128)(2,1)} %copy-done.7), kind=kOutput, calls=%fused_computation.3 | convolution fusion | flops 1512308736 | bytes 10027008 | tf_op jit(solution)/shard_map/dot_general | solution.py:92
  139.0 0.1 pad_maximum_fusion.1
  139.0 14.4 %reduce-scatter.5.cloned.1.call-done = bf16[80,1536]{1,0:T(8,128)(2,1)} async-done(((bf16[640,1536]{1,0:T(8,128)(2,1)}), bf16[80,1536]{1,0:T(8,128)(2,1)}) %reduce-scatter.5.cloned.1.call-update) | async-done | bytes 245776 | tf_op jit(solution)/shard_map/reduce_scatter | solution.py:26
  153.4 2.4 %collective-permute-start.1 = (bf16[80,1536]{1,0:T(8,128)(2,1)}, bf16[80,1536]{1,0:T(8,128)(2,1)S(1)}, u32[]{:S(2)}, u32[]{:S(2)}) collective-permute-start(bf16[80,1536]{1,0:T(8,128)(2,1)} %reduce-scatter.5.cloned.1.call-done), channel_id=1, source_target_pairs={{0,8},{1,9},{2,10},{3,11},{4,12},{5,13},{6,14},{7,15},{8,0},{9,1},... | collective-permute-start | bytes 737288 | tf_op jit(solution)/shard_map/ppermute | solution.py:99
  155.8 0.1 select_reduce_fusion
  155.9 0.5 compare_select_fusion.4
  156.4 33.3 %reduce-scatter.3.cloned.1.call-done = bf16[80,1536]{1,0:T(8,128)(2,1)} async-done(((bf16[640,1536]{1,0:T(8,128)(2,1)}), bf16[80,1536]{1,0:T(8,128)(2,1)}) %reduce-scatter.3.cloned.1.call-update) | async-done | bytes 245776 | tf_op jit(solution)/shard_map/reduce_scatter | solution.py:26
  189.8 2.0 %convolution_convert_fusion.4 = bf16[128,1536]{1,0:T(8,128)(2,1)} fusion(bf16[80,1536]{1,0:T(8,128)(2,1)S(1)} %collective-permute-done.1, bf16[80,1536]{1,0:T(8,128)(2,1)} %reduce-scatter.3.cloned.1.call-done, s32[128]{0:T(128)S(1)} %compare_select_fusion.5), kind=kOutput, calls=%fused_computation.18 | convolution fusion | flops 64114688 | bytes 885248 | tf_op jit(solution)/shard_map/dot_general | solution.py:107
  (28 shorter events, 0.1 us)
Async XLA Ops:
  7.2 45.1 %copy-start = (bf16[768,1536]{1,0:T(8,128)(2,1)S(1)}, bf16[768,1536]{1,0:T(8,128)(2,1)}, u32[]{:S(2)}) copy-start(bf16[768,1536]{1,0:T(8,128)(2,1)} %param.17) | copy-start | bytes 7077892
  7.2 19.8 %copy-start.9 = (bf16[128,1536]{1,0:T(8,128)(2,1)S(1)}, bf16[128,1536]{1,0:T(8,128)(2,1)}, u32[]{:S(2)}) copy-start(bf16[128,1536]{1,0:T(8,128)(2,1)} %param.9) | copy-start | bytes 1179652
  7.2 45.0 %all-gather.7.cloned.1.call-start = ((), (), s32[]{:S(2)}) async-start(), calls=%async_computation.4 | async-start | bytes 2211840 | tf_op jit(solution)/shard_map/all_gather | solution.py:20
  10.2 15.3 %collective-permute-start = (bf16[80,1536]{1,0:T(8,128)(2,1)S(1)}, bf16[80,1536]{1,0:T(8,128)(2,1)S(1)}, u32[]{:S(2)}, u32[]{:S(2)}) collective-permute-start(bf16[80,1536]{1,0:T(8,128)(2,1)S(1)} %get-tuple-element.11), channel_id=1, source_target_pairs={{0,8},{1,9},{2,10},{3,11},{4,12},{5,13},{6,14},{7,15},{8,0},{9,1},... | collective-permute-start | bytes 737288 | tf_op jit(solution)/shard_map/ppermute | solution.py:56
  25.5 0.7 copy-start.11
  26.2 48.4 %all-gather.5.cloned.1.call-start = ((), (), s32[]{:S(2)}) async-start(), calls=%async_computation.2 | async-start | bytes 2211840 | tf_op jit(solution)/shard_map/all_gather | solution.py:20
  27.0 70.8 %all-gather.9.cloned.1.call-start = ((), (), s32[]{:S(2)}) async-start(), calls=%async_computation.6 | async-start | bytes 2211840 | tf_op jit(solution)/shard_map/all_gather | solution.py:20
  28.1 104.1 %all-gather.11.cloned.1.call-start = ((), (), s32[]{:S(2)}) async-start(), calls=%async_computation.7 | async-start | bytes 2211840 | tf_op jit(solution)/shard_map/all_gather | solution.py:20
  28.1 13.5 %collective-permute-start.3 = (bf16[80,1536]{1,0:T(8,128)(2,1)S(1)}, bf16[80,1536]{1,0:T(8,128)(2,1)S(1)}, u32[]{:S(2)}, u32[]{:S(2)}) collective-permute-start(bf16[80,1536]{1,0:T(8,128)(2,1)S(1)} %get-tuple-element.8), channel_id=1, source_target_pairs={{0,8},{1,9},{2,10},{3,11},{4,12},{5,13},{6,14},{7,15},{8,0},{9,1},... | collective-permute-start | bytes 737288 | tf_op jit(solution)/shard_map/ppermute | solution.py:56
  41.6 0.7 copy-start.10
  42.3 111.1 %reduce-scatter.5.cloned.1.call-start = ((), (), s32[]{:S(2)}) async-start(), calls=%async_computation.5 | async-start | bytes 2211840 | tf_op jit(solution)/shard_map/reduce_scatter | solution.py:26
  55.7 1.3 copy-start.1
  55.7 2.7 %copy-start.14 = (bf16[1536,768]{1,0:T(8,128)(2,1)S(1)}, bf16[1536,768]{1,0:T(8,128)(2,1)}, u32[]{:S(2)}) copy-start(bf16[1536,768]{1,0:T(8,128)(2,1)} %param.16) | copy-start | bytes 7077892
  57.0 1.0 copy-start.7
  61.5 128.3 %reduce-scatter.3.cloned.1.call-start = ((), (), s32[]{:S(2)}) async-start(), calls=%async_computation.3 | async-start | bytes 2211840 | tf_op jit(solution)/shard_map/reduce_scatter | solution.py:26
  74.6 3.9 %copy-start.2 = (bf16[8,80,768]{2,1,0:T(8,128)(2,1)S(1)}, bf16[8,80,768]{2,1,0:T(8,128)(2,1)}, u32[]{:S(2)}) copy-start(bf16[8,80,768]{2,1,0:T(8,128)(2,1)} %gather_fusion) | copy-start | bytes 2949124
  78.5 1.3 copy-start.4
  78.5 2.7 %copy-start.15 = (bf16[1536,768]{1,0:T(8,128)(2,1)S(1)}, bf16[1536,768]{1,0:T(8,128)(2,1)}, u32[]{:S(2)}) copy-start(bf16[1536,768]{1,0:T(8,128)(2,1)} %param.16) | copy-start | bytes 7077892
  79.7 1.0 copy-start.8
  84.2 0.7 copy-start.16
  97.8 6.1 %copy-start.3 = (bf16[8,80,768]{2,1,0:T(8,128)(2,1)S(1)}, bf16[8,80,768]{2,1,0:T(8,128)(2,1)}, u32[]{:S(2)}) copy-start(bf16[8,80,768]{2,1,0:T(8,128)(2,1)} %gather_fusion) | copy-start | bytes 2949124
  97.8 6.1 %copy-start.5 = (f32[640,768]{1,0:T(8,128)S(1)}, f32[640,768]{1,0:T(8,128)}, u32[]{:S(2)}) copy-start(f32[640,768]{1,0:T(8,128)} %copy-done.4) | copy-start | bytes 5898244
  97.8 6.1 %copy-start.6 = (bf16[640,1536]{1,0:T(8,128)(2,1)S(1)}, bf16[640,1536]{1,0:T(8,128)(2,1)}, u32[]{:S(2)}) copy-start(bf16[640,1536]{1,0:T(8,128)(2,1)} %all-gather.5.cloned.1.call-done) | copy-start | bytes 5898244
  122.8 16.1 %collective-permute-start.2 = (f32[80]{0:T(128)S(1)}, f32[80]{0:T(128)S(1)}, u32[]{:S(2)}, u32[]{:S(2)}) collective-permute-start(f32[80]{0:T(128)S(1)} %get-tuple-element.13), channel_id=1, source_target_pairs={{0,8},{1,9},{2,10},{3,11},{4,12},{5,13},{6,14},{7,15},{8,0},{9,1},... | collective-permute-start | bytes 968 | tf_op jit(solution)/shard_map/ppermute | solution.py:99
  132.2 23.7 %copy-start.12 = (f32[128]{0:T(128)S(1)}, f32[128]{0:T(128)}, u32[]{:S(2)}) copy-start(f32[128]{0:T(128)} %param.11) | copy-start | bytes 1540
  132.2 23.7 %copy-start.13 = (s32[128]{0:T(128)S(1)}, s32[128]{0:T(128)}, u32[]{:S(2)}) copy-start(s32[128]{0:T(128)} %param.13) | copy-start | bytes 1540
  153.4 36.3 %collective-permute-start.1 = (bf16[80,1536]{1,0:T(8,128)(2,1)}, bf16[80,1536]{1,0:T(8,128)(2,1)S(1)}, u32[]{:S(2)}, u32[]{:S(2)}) collective-permute-start(bf16[80,1536]{1,0:T(8,128)(2,1)} %reduce-scatter.5.cloned.1.call-done), channel_id=1, source_target_pairs={{0,8},{1,9},{2,10},{3,11},{4,12},{5,13},{6,14},{7,15},{8,0},{9,1},... | collective-permute-start | bytes 737288 | tf_op jit(solution)/shard_map/ppermute | solution.py:99
Sparse Core Ops, SparseCore 0:
  26.3 25.8 all-gather.6
  54.4 20.1 all-gather.4
  76.3 21.4 all-gather.8
  99.3 21.6 all-gather.10
  123.2 30.2 reduce-scatter.4
  155.7 33.9 reduce-scatter.2

commit v3 on v0

v3 whole, which is shorter than its diff:
```python
import functools

import jax
import jax.numpy as jnp
from jax import lax
from jax.experimental import pallas as pl
from jax.experimental.pallas import tpu as pltpu
from jax.sharding import PartitionSpec as P

SPLIT = 8
CORE, LOW, HIGH = 1, 2, 4
TILE = 256
LANES = 128
VMEM = pl.BlockSpec(memory_space=pltpu.VMEM)
ANY = pl.BlockSpec(memory_space=pl.ANY)
F32, BF16 = jnp.float32, jnp.bfloat16


def params():
    return pltpu.CompilerParams(vmem_limit_bytes=48 * 1024 * 1024)


def cost(flops, moved, exps=0):
    return pl.CostEstimate(flops=flops, bytes_accessed=moved, transcendentals=exps)


def bits(core):
    return (HIGH, LOW, CORE) if core == 0 else (LOW, HIGH, CORE)


def meet(rows, step):
    devices = lax.axis_size("expert")
    return lax.ppermute(rows, "expert", [(i, i ^ bits(i % 2)[step]) for i in range(devices)])


def shift(rows, by):
    devices = lax.axis_size("expert")
    pairs = [(i, (i + by * SPLIT) % devices) for i in range(devices)]
    return lax.ppermute(rows, "expert", pairs)


def cross(rows, sign):
    experts = lax.axis_size("expert") // SPLIT
    if experts == 2:
        return shift(rows, sign)
    slots = rows.shape[0] // (experts - 1)
    return jnp.concatenate(
        [shift(rows[(s - 1) * slots : s * slots], sign * s) for s in range(1, experts)]
    )


def gather_pieces(rows, *beside):
    got = meet(rows, 0)
    two = jnp.concatenate([rows, after(got, *beside) if beside else got])
    more = meet(two, 1)
    pieces = [two, more, meet(two, 2), meet(more, 2)]
    if two.shape[0] % 16:
        return [jnp.concatenate(pieces)]
    return pieces


def after(value, *earlier):
    return lax.optimization_barrier((value, *earlier))[0]


def sources_met(me, experts):
    block = jnp.arange(SPLIT * (experts - 1), dtype=jnp.int32)

    def place(i):
        first = jnp.where(((me ^ (i >> 2)) & 1) == 1, LOW, HIGH)
        second = (LOW + HIGH) - first
        mask = (i & 1) * first + ((i >> 1) & 1) * second + (i >> 2) * CORE
        return (me & (SPLIT - 1)) ^ mask

    my_expert = me >> 3
    from_expert = my_expert - 1 - block % (experts - 1)
    from_expert = jnp.where(from_expert < 0, from_expert + experts, from_expert)
    near = my_expert * SPLIT + place(block[:SPLIT])
    return near, from_expert * SPLIT + place(block // (experts - 1))


def slot_places(expert_id, dropped, slot, slots):
    devices = lax.axis_size("expert")
    ahead = expert_id - lax.axis_index("expert") // SPLIT
    ahead = jnp.where(ahead < 0, ahead + devices // SPLIT, ahead)
    return jnp.where(dropped == 1, -1, ahead * slots + slot)


def chosen(place, first, count):
    rows = lax.broadcasted_iota(jnp.int32, (count, place.shape[1]), 0) + first
    return rows == place


def place_kernel(slots, scale, expert_id, dropped, slot, gate, values, near, far):
    place = slot_places(expert_id[...], dropped[...], slot[...], slots)
    rows = values[...]
    if scale:
        count = rows.shape[0]
        across = lax.broadcasted_iota(jnp.int32, (count, count), 1)
        down = lax.broadcasted_iota(jnp.int32, (count, count), 0)
        column = jnp.sum(jnp.where(across == down, gate[...], 0.0), axis=1, keepdims=True)
        rows = (column * rows.astype(F32)).astype(BF16)
    for first, out in ((0, near), (slots, far)):
        onehot = chosen(place, first, out.shape[0]).astype(F32).astype(BF16)
        out[...] = jnp.dot(onehot, rows, preferred_element_type=F32).astype(BF16)


def to_slots(slots, scale, expert_id, dropped, slot, gate, values):
    experts = lax.axis_size("expert") // SPLIT
    width = values.shape[1]
    return pl.pallas_call(
        functools.partial(place_kernel, slots, scale),
        out_shape=(
            jax.ShapeDtypeStruct((slots, width), BF16),
            jax.ShapeDtypeStruct(((experts - 1) * slots, width), BF16),
        ),
        in_specs=[VMEM] * 5,
        out_specs=(VMEM, VMEM),
        compiler_params=params(),
        cost_estimate=cost(2 * experts * slots * values.size, 6 * values.size),
        name="rows_to_slots",
    )(expert_id, dropped, slot, gate, values)


def home_kernel(slots, expert_id, dropped, slot, gate, kept, got, back, token_grad, gate_grad):
    place = slot_places(expert_id[...], dropped[...], slot[...], slots)
    width = token_grad.shape[1]
    near = kept[...].astype(F32) + got[...].astype(F32)
    total = jnp.zeros(token_grad.shape, F32)
    gates = jnp.zeros(gate_grad.shape, F32)
    for first, rows in ((0, near), (slots, back[...].astype(F32))):
        picks = chosen(place, first, rows.shape[0])
        total += lax.dot_general(
            picks.astype(F32).astype(BF16),
            rows[:, :width].astype(BF16),
            (((0,), (0,)), ((), ())),
            preferred_element_type=F32,
        )
        column = rows[:, width : width + 1]
        gates += jnp.sum(jnp.where(picks, column, 0.0), axis=0, keepdims=True)
    token_grad[...] = total.astype(BF16)
    gate_grad[...] = jnp.where(dropped[...] == 1, 0.0, gates / gate[...])


def to_tokens(slots, expert_id, dropped, slot, gate, kept, got, back):
    count, width = expert_id.shape[1], kept.shape[1] - LANES
    return pl.pallas_call(
        functools.partial(home_kernel, slots),
        out_shape=(
            jax.ShapeDtypeStruct((count, width), BF16),
            jax.ShapeDtypeStruct((1, count), F32),
        ),
        in_specs=[VMEM] * 7,
        out_specs=(VMEM, VMEM),
        compiler_params=params(),
        name="slots_to_tokens",
    )(expert_id, dropped, slot, gate, kept, got, back)


def activation_kernel(order, hidden, activated, slope):
    rows = hidden.shape[1]
    step = 16 if rows % 16 == 0 else rows

    def chunk(i, carry):
        at = pl.ds(i * step, step) if rows > step else slice(None)
        h = hidden[0, at, :].astype(F32)
        cdf = 0.5 * (1.0 + lax.erf(h * 0.7071067811865476))
        density = jnp.exp(-0.5 * h * h) * 0.3989422804014327
        activated[0, at, :] = (h * cdf).astype(BF16)
        slope[0, at, :] = cdf + h * density
        return carry

    lax.fori_loop(0, rows // step, chunk, 0)


def activation(by_source, order):
    _, slots, units = by_source.shape
    block = (1, slots, units)
    shape = (order.shape[0], slots, units)
    size = order.shape[0] * slots * units
    act, slope = pl.pallas_call(
        activation_kernel,
        grid_spec=pltpu.PrefetchScalarGridSpec(
            num_scalar_prefetch=1,
            grid=(order.shape[0],),
            in_specs=[pl.BlockSpec(block, lambda i, order: (order[i], 0, 0))],
            out_specs=[pl.BlockSpec(block, lambda i, order: (i, 0, 0))] * 2,
        ),
        out_shape=(jax.ShapeDtypeStruct(shape, BF16), jax.ShapeDtypeStruct(shape, F32)),
        compiler_params=params(),
        cost_estimate=cost(60 * size, 8 * size, 2 * size),
        name="activation",
    )(order, by_source)
    return act.reshape(-1, units), slope.reshape(-1, units)


def copies(pairs, sem):
    made = [pltpu.make_async_copy(src, dst, sem.at[i]) for i, (src, dst) in enumerate(pairs)]
    for copy in made:
        copy.start()
    return made


def row_blocks(refs, buffer):
    pairs, first = [], 0
    for ref in refs:
        count = ref.shape[0]
        pairs.append((ref, buffer.at[pl.ds(first, count)]))
        first += count
    return pairs


def slot_grad_kernel(pieces, *refs):
    grads = refs[:pieces]
    w_out, w_in, act, slope, hidden_grad, kept, sent = refs[pieces : pieces + 7]
    g, wo, wi, a, s, hg, part, in_sem, out_sem = refs[pieces + 7 :]
    rows, units = hg.shape
    width = g.shape[1]
    half = rows // 2
    wo_tiles, wi_tiles = units // TILE, width // TILE
    pairs = row_blocks(grads, g)
    pairs += [(w_out.at[pl.ds(j * TILE, TILE)], wo.at[pl.ds(j * TILE, TILE)]) for j in range(wo_tiles)]
    pairs += [(act, a), (slope, s)]
    pairs += [(w_in.at[pl.ds(j * TILE, TILE)], wi.at[pl.ds(j * TILE, TILE)]) for j in range(wi_tiles)]
    loads = copies(pairs, in_sem)
    for copy in loads[:pieces]:
        copy.wait()
    loads = loads[pieces:]
    stores = []

    def store(src, dst):
        copy = pltpu.make_async_copy(src, dst, out_sem.at[len(stores)])
        copy.start()
        stores.append(copy)

    gates = jnp.zeros((rows, 1), F32)
    for j in range(wo_tiles):
        at = slice(j * TILE, (j + 1) * TILE)
        loads[j].wait()
        grad_act = lax.dot_general(
            g[...], wo[at, :], (((1,), (1,)), ((), ())), preferred_element_type=F32
        )
        if j == 0:
            loads[wo_tiles].wait()
            loads[wo_tiles + 1].wait()
        hg[:, at] = (grad_act * s[:, at]).astype(BF16)
        gates += jnp.sum(grad_act * a[:, at].astype(F32), axis=1, keepdims=True)
    store(hg, hidden_grad)
    part[:, width:] = jnp.broadcast_to(gates, (rows, LANES)).astype(BF16)
    loads = loads[wo_tiles + 2 :]

    def store_columns(at):
        store(part.at[pl.ds(half, half), at], sent.at[:, at])
        store(part.at[pl.ds(0, half), at], kept.at[:, at])

    store_columns(pl.ds(width, LANES))
    for j in range(wi_tiles):
        loads[j].wait()
        at = slice(j * TILE, (j + 1) * TILE)
        part[:, at] = lax.dot_general(
            hg[...], wi[at, :], (((1,), (1,)), ((), ())), preferred_element_type=F32
        ).astype(BF16)
        store_columns(pl.ds(j * TILE, TILE))
    for copy in stores:
        copy.wait()


def slot_grads(grads, w_out, w_in, act, slope):
    rows, units = act.shape
    width = w_in.shape[0]
    tiles = units // TILE, width // TILE
    wide = width + LANES
    return pl.pallas_call(
        functools.partial(slot_grad_kernel, len(grads)),
        out_shape=(
            jax.ShapeDtypeStruct((rows, units), BF16),
            jax.ShapeDtypeStruct((rows // 2, wide), BF16),
            jax.ShapeDtypeStruct((rows // 2, wide), BF16),
        ),
        in_specs=[ANY] * (len(grads) + 4),
        out_specs=(ANY, ANY, ANY),
        scratch_shapes=[
            pltpu.VMEM((rows, width), BF16),
            pltpu.VMEM((units, width), BF16),
            pltpu.VMEM((width, units), BF16),
            pltpu.VMEM((rows, units), BF16),
            pltpu.VMEM((rows, units), F32),
            pltpu.VMEM((rows, units), BF16),
            pltpu.VMEM((rows, wide), BF16),
            pltpu.SemaphoreType.DMA((len(grads) + 2 + sum(tiles),)),
            pltpu.SemaphoreType.DMA((3 + 2 * tiles[1],)),
        ],
        compiler_params=params(),
        cost_estimate=cost(4 * rows * units * width, 4 * units * width + 4 * rows * wide),
        name="slot_grads",
    )(*grads, w_out, w_in, act, slope)


def weight_kernel(left_count, right_count, *refs):
    lefts = refs[:left_count]
    rights = refs[left_count : left_count + right_count]
    out, left, right, result, in_sem, out_sem = refs[left_count + right_count :]
    loads = copies(row_blocks(lefts, left) + row_blocks(rights, right), in_sem)
    for copy in loads:
        copy.wait()
    stores = []
    for j in range(left.shape[1] // TILE):
        at = slice(j * TILE, (j + 1) * TILE)
        result[at, :] = lax.dot_general(
            left[:, at], right[...], (((0,), (0,)), ((), ())), preferred_element_type=F32
        ).astype(BF16)
        rows = pl.ds(j * TILE, TILE)
        copy = pltpu.make_async_copy(result.at[rows], out.at[rows], out_sem.at[j])
        copy.start()
        stores.append(copy)
    for copy in stores:
        copy.wait()


def weight_grad(lefts, rights, name):
    rows = sum(x.shape[0] for x in lefts)
    m, n = lefts[0].shape[1], rights[0].shape[1]
    return pl.pallas_call(
        functools.partial(weight_kernel, len(lefts), len(rights)),
        out_shape=jax.ShapeDtypeStruct((m, n), BF16),
        in_specs=[ANY] * (len(lefts) + len(rights)),
        out_specs=ANY,
        scratch_shapes=[
            pltpu.VMEM((rows, m), BF16),
            pltpu.VMEM((rows, n), BF16),
            pltpu.VMEM((m, n), BF16),
            pltpu.SemaphoreType.DMA((len(lefts) + len(rights),)),
            pltpu.SemaphoreType.DMA((m // TILE,)),
        ],
        compiler_params=params(),
        cost_estimate=cost(2 * rows * m * n, 2 * (rows * m + rows * n + m * n)),
        name=name,
    )(*lefts, *rights)


def add(a, b):
    return (a.astype(F32) + b.astype(F32)).astype(BF16)


def sum_pieces(kept, sent):
    for step in (2, 1):
        got = meet(sent, step)
        half = kept.shape[0] // 2
        sent = add(kept[half:], got[half:])
        kept = add(kept[:half], got[:half])
    return kept, meet(sent, 0)


def body(tokens, out_grad, gate, expert_id, dropped, slot, saved_hidden, w_in, w_out):
    devices = lax.axis_size("expert")
    experts = devices // SPLIT
    slots = saved_hidden.shape[0] // devices
    units = saved_hidden.shape[1]
    me = lax.axis_index("expert")
    row = lambda x: x.reshape(1, -1)
    gate, routing = row(gate), (row(expert_id), row(dropped), row(slot))

    near_order, far_order = sources_met(me, experts)
    by_source = saved_hidden.reshape(devices, slots, units)

    near_grad, far_grad = to_slots(slots, True, *routing, gate, out_grad)
    near_act, near_slope = activation(by_source, near_order)
    far_act, far_slope = activation(by_source, far_order)
    near_rows, far_rows = to_slots(slots, False, *routing, gate, tokens)

    near_grads = gather_pieces(near_grad, near_act)
    far_grad = after(cross(far_grad, 1), far_act, near_grads[0])
    far_rows = cross(after(far_rows, far_grad), 1)
    far_grads = gather_pieces(far_grad)
    near_grads[0] = after(near_grads[0], far_grads[0])

    near_hg, near_kept, near_sent = slot_grads(near_grads, w_out, w_in, near_act, near_slope)
    near_rows = gather_pieces(after(near_rows, far_grads[-3:][0]))
    near_kept, near_got = sum_pieces(near_kept, near_sent)
    far_hg, far_kept, far_sent = slot_grads(far_grads, w_out, w_in, far_act, far_slope)
    far_rows = gather_pieces(far_rows)
    far_kept, far_got = sum_pieces(far_kept, far_sent)
    far_sum = add(far_kept, far_got)
    near_act = after(near_act, far_sum)

    w_out_grad = weight_grad([near_act, far_act], near_grads + far_grads, "w_out_grad")
    w_in_grad = weight_grad(near_rows + far_rows, [near_hg, far_hg], "w_in_grad")
    back = after(cross(far_sum, -1), w_out_grad, w_in_grad)
    token_grad, gate_grad = to_tokens(slots, *routing, gate, near_kept, near_got, back)
    return (token_grad, gate_grad.reshape(-1), w_in_grad, w_out_grad)


def solution(mesh):
    in_specs = (
        P(("parts", "expert"), None),
        P(("parts", "expert"), None),
        P(("parts", "expert")),
        P(("parts", "expert")),
        P(("parts", "expert")),
        P(("parts", "expert")),
        P("parts", "expert"),
        P(None, "expert"),
        P("expert", None),
    )
    out_specs = (
        P(("parts", "expert"), None),
        P(("parts", "expert")),
        P("parts", "expert"),
        P(("parts", "expert"), None),
    )
    return jax.shard_map(body, mesh=mesh, in_specs=in_specs, out_specs=out_specs, check_vma=False)
```

time: 302 us -> 120 us (0.40)
  the two profiles are of different devices: /device:TPU:13 before, /device:TPU:0 now
where the time goes in v3:
time: 120 us
  waiting for transfers between devices  44.4 us (37%)
  Pallas kernels  43.1 us (36%)
  starting transfers between devices  21.6 us (18%)
  local copies, waits for them, and re-layouts  6.88 us (6%)
  other arithmetic  3.04 us (3%)
    ppermute x22, waiting for transfers between devices, meet(): lax.ppermute(rows, 'expert', [(i, i ^ bits(i % 2)[step]) for i in range(d...  31.9 us
    pallas_call x2, Pallas kernels, slot_grads(): pl.pallas_call(functools.partial(slot_grad_kernel, len(grads)), out_shape...  22.6 us
    pallas_call x2, Pallas kernels, weight_grad(): pl.pallas_call(functools.partial(weight_kernel, len(lefts), len(rights)),...  14.8 us
    ppermute x22, starting transfers between devices, meet(): lax.ppermute(rows, 'expert', [(i, i ^ bits(i % 2)[step]) for i in range(d...  13.8 us
    ppermute x3, waiting for transfers between devices, shift(): return lax.ppermute(rows, 'expert', pairs)  12.6 us
    ppermute x3, starting transfers between devices, shift(): return lax.ppermute(rows, 'expert', pairs)  7.76 us
    unnamed x38, local copies, waits for them, and re-layouts  6.82 us
    pallas_call x2, Pallas kernels, activation(): pl.pallas_call(activation_kernel, grid_spec=pltpu.PrefetchScalarGridSpec(...  3.89 us
  transfers between devices with their start and end apart: 25, of which 8 were waited for; matrix products, arithmetic and copies ran while one was open for 3% of the time, Pallas kernels for 35%

profile of v3, /device:TPU:0, one launch (start us, length us, event | category | flops | bytes accessed | tf_op | source)
XLA Modules:
  0.0 120.0 jit_solution(5022633835826308349)
XLA Ops:
  0.6 1.0 copy-done.2
  1.6 0.7 copy-done.4
  2.3 0.7 copy-done.6
  2.9 0.7 copy-done.8
  3.6 0.7 copy-done.10
  4.3 0.4 rows_to_slots.2
  4.6 3.1 %collective-permute-start = (bf16[80,1536]{1,0:T(8,128)(2,1)S(1)}, bf16[80,1536]{1,0:T(8,128)(2,1)S(1)}, u32[]{:S(2)}, u32[]{:S(2)}) collective-permute-start(bf16[80,1536]{1,0:T(8,128)(2,1)S(1)} %get-tuple-element.27), channel_id=1, source_target_pairs={{0,4},{1,3},{2,6},{3,1},{4,0},{5,7},{6,2},{7,5},{8,12},{9,11},{10,... | collective-permute-start | bytes 737288 | tf_op jit(solution)/shard_map/ppermute | solution.py:33
  7.7 2.6 %collective-permute-start.1 = (bf16[80,1536]{1,0:T(8,128)(2,1)S(1)}, bf16[80,1536]{1,0:T(8,128)(2,1)S(1)}, u32[]{:S(2)}, u32[]{:S(2)}) collective-permute-start(bf16[80,1536]{1,0:T(8,128)(2,1)S(1)} %get-tuple-element.30), channel_id=1, source_target_pairs={{0,8},{1,9},{2,10},{3,11},{4,12},{5,13},{6,14},{7,15},{8,0},{9,1},... | collective-permute-start | bytes 737288 | tf_op jit(solution)/shard_map/ppermute | solution.py:39
  10.3 0.0 copy-start
  10.4 1.5 %copy-done = bf16[1280,768]{1,0:T(8,128)(2,1)S(1)} copy-done((bf16[1280,768]{1,0:T(8,128)(2,1)S(1)}, bf16[1280,768]{1,0:T(8,128)(2,1)}, u32[]{:S(2)}) %copy-start) | copy-done | bytes 1966104
  11.9 1.9 %activation.2 = (bf16[8,80,768]{2,1,0:T(8,128)(2,1)S(1)}, f32[8,80,768]{2,1,0:T(8,128)S(1)}) custom-call(s32[8]{0:T(128)S(1)} %get-tuple-element.57.order, bf16[16,80,768]{2,1,0:T(8,128)(2,1)S(1)} %bitcast.10), custom_call_target="tpu_custom_call" | custom-call | flops 29491200 | bytes 3932160 | tf_op jit(solution)/shard_map/activation/pallas_call | solution.py:181
  13.8 0.0 copy-start.12
  13.9 1.3 %copy-done.12 = f32[8,80,768]{2,1,0:T(8,128)} copy-done((f32[8,80,768]{2,1,0:T(8,128)}, f32[8,80,768]{2,1,0:T(8,128)S(1)}, u32[]{:S(2)}) %copy-start.12) | copy-done | bytes 1966104
  15.1 1.9 %activation.3 = (bf16[8,80,768]{2,1,0:T(8,128)(2,1)S(1)}, f32[8,80,768]{2,1,0:T(8,128)S(1)}) custom-call(s32[8]{0:T(128)S(1)} %get-tuple-element.56.order, bf16[16,80,768]{2,1,0:T(8,128)(2,1)S(1)} %bitcast.11), custom_call_target="tpu_custom_call" | custom-call | flops 29491200 | bytes 3932160 | tf_op jit(solution)/shard_map/activation/pallas_call | solution.py:181
  17.1 0.0 copy-start.13
  17.1 0.0 copy-start.3
  17.1 0.0 copy-start.5
  17.1 0.0 copy-start.7
  17.1 0.0 copy-start.9
  17.1 0.0 copy-start.11
  17.2 0.0 collective-permute-done
  17.2 4.1 %collective-permute-done.1 = bf16[80,1536]{1,0:T(8,128)(2,1)S(1)} collective-permute-done((bf16[80,1536]{1,0:T(8,128)(2,1)S(1)}, bf16[80,1536]{1,0:T(8,128)(2,1)S(1)}, u32[]{:S(2)}, u32[]{:S(2)}) %collective-permute-start.1) | collective-permute-done | bytes 245792 | tf_op jit(solution)/shard_map/ppermute | solution.py:39
  21.3 0.7 collective-permute-start.2
  22.0 5.5 %collective-permute-done.2 = bf16[80,1536]{1,0:T(8,128)(2,1)S(1)} collective-permute-done((bf16[80,1536]{1,0:T(8,128)(2,1)S(1)}, bf16[80,1536]{1,0:T(8,128)(2,1)S(1)}, u32[]{:S(2)}, u32[]{:S(2)}) %collective-permute-start.2) | collective-permute-done | bytes 245792 | tf_op jit(solution)/shard_map/ppermute | solution.py:33
  27.5 0.5 collective-permute-start.9
  28.0 0.3 rows_to_slots.3
  28.3 2.2 %collective-permute-start.20 = (bf16[80,1536]{1,0:T(8,128)(2,1)S(1)}, bf16[80,1536]{1,0:T(8,128)(2,1)S(1)}, u32[]{:S(2)}, u32[]{:S(2)}) collective-permute-start(bf16[80,1536]{1,0:T(8,128)(2,1)S(1)} %get-tuple-element.44), channel_id=1, source_target_pairs={{0,8},{1,9},{2,10},{3,11},{4,12},{5,13},{6,14},{7,15},{8,0},{9,1},... | collective-permute-start | bytes 737288 | tf_op jit(solution)/shard_map/ppermute | solution.py:39
  30.5 1.5 %collective-permute-start.3 = (bf16[160,1536]{1,0:T(8,128)(2,1)S(1)}, bf16[160,1536]{1,0:T(8,128)(2,1)S(1)}, u32[]{:S(2)}, u32[]{:S(2)}) collective-permute-start(bf16[160,1536]{1,0:T(8,128)(2,1)S(1)} %constant_dynamic-update-slice_fusion.refs_0_.refs_2_), channel_id=1, source_target_pairs={{0,2},{1,5},{2,0},{3,7},{4,6},{5,1},{6,4},{7,3},{8,10},{9,13},{10,... | collective-permute-start | bytes 1474568 | tf_op jit(solution)/shard_map/ppermute | solution.py:33
  32.0 0.0 collective-permute-start.10
  32.0 4.4 %collective-permute-done.9.refs_1_.refs_7_ = bf16[160,1536]{1,0:T(8,128)(2,1)S(1)} collective-permute-done((bf16[160,1536]{1,0:T(8,128)(2,1)S(1)}, bf16[160,1536]{1,0:T(8,128)(2,1)S(1)}, u32[]{:S(2)}, u32[]{:S(2)}) %collective-permute-start.9) | collective-permute-done | bytes 491552 | tf_op jit(solution)/shard_map/ppermute | solution.py:33
  36.4 0.8 collective-permute-start.11
  37.2 5.2 %collective-permute-done.20 = bf16[80,1536]{1,0:T(8,128)(2,1)S(1)} collective-permute-done((bf16[80,1536]{1,0:T(8,128)(2,1)S(1)}, bf16[80,1536]{1,0:T(8,128)(2,1)S(1)}, u32[]{:S(2)}, u32[]{:S(2)}) %collective-permute-start.20) | collective-permute-done | bytes 245792 | tf_op jit(solution)/shard_map/ppermute | solution.py:39
  42.4 6.3 %collective-permute-done.21 = bf16[80,1536]{1,0:T(8,128)(2,1)S(1)} collective-permute-done((bf16[80,1536]{1,0:T(8,128)(2,1)S(1)}, bf16[80,1536]{1,0:T(8,128)(2,1)S(1)}, u32[]{:S(2)}, u32[]{:S(2)}) %collective-permute-start.21) | collective-permute-done | bytes 245792 | tf_op jit(solution)/shard_map/ppermute | solution.py:33
  48.8 0.3 collective-permute-start.22
  49.1 0.0 collective-permute-done.10.refs_2_.refs_8_
  49.1 11.3 %slot_grads.3 = (bf16[640,768]{1,0:T(8,128)(2,1)S(1)}, bf16[320,1664]{1,0:T(8,128)(2,1)S(1)}, bf16[320,1664]{1,0:T(8,128)(2,1)S(1)}) custom-call(bf16[160,1536]{1,0:T(8,128)(2,1)S(1)} %constant_dynamic-update-slice_fusion.2.refs_0_.refs_6_, bf16[160,1536]{1,0:T(8,128)(2,1)S(1)} %collective-permute-done.9.refs_1_.refs_7_, ...), custom_call_target="tpu_custom_call" | custom-call | flops 3019898880 | bytes 8978432 | tf_op jit(solution)/shard_map/slot_grads/pallas_call | solution.py:273
  60.4 0.6 collective-permute-start.12
  61.0 0.1 collective-permute-start.16
  61.1 11.3 %slot_grads.2 = (bf16[640,768]{1,0:T(8,128)(2,1)S(1)}, bf16[320,1664]{1,0:T(8,128)(2,1)S(1)}, bf16[320,1664]{1,0:T(8,128)(2,1)S(1)}) custom-call(bf16[160,1536]{1,0:T(8,128)(2,1)S(1)} %constant_dynamic-update-slice_fusion.refs_0_.refs_2_, bf16[160,1536]{1,0:T(8,128)(2,1)S(1)} %collective-permute-done.3.refs_1_.refs_3_, ...), custom_call_target="tpu_custom_call" | custom-call | flops 3019898880 | bytes 8978432 | tf_op jit(solution)/shard_map/slot_grads/pallas_call | solution.py:273
  72.4 1.5 %collective-permute-start.6 = (bf16[320,1664]{1,0:T(8,128)(2,1)S(1)}, bf16[320,1664]{1,0:T(8,128)(2,1)S(1)}, u32[]{:S(2)}, u32[]{:S(2)}) collective-permute-start(bf16[320,1664]{1,0:T(8,128)(2,1)S(1)} %get-tuple-element.36), channel_id=1, source_target_pairs={{0,1},{1,0},{2,3},{3,2},{4,5},{5,4},{6,7},{7,6},{8,9},{9,8},{10,11... | collective-permute-start | bytes 3194888 | tf_op jit(solution)/shard_map/ppermute | solution.py:33
  73.9 0.0 collective-permute-done.16
  73.9 0.4 collective-permute-start.17
  74.3 0.5 collective-permute-start.23
  74.8 0.0 collective-permute-done.22.refs_5_
  74.8 0.1 collective-permute-start.18
  74.8 8.0 %collective-permute-done.17.refs_1_ = bf16[160,1536]{1,0:T(8,128)(2,1)S(1)} collective-permute-done((bf16[160,1536]{1,0:T(8,128)(2,1)S(1)}, bf16[160,1536]{1,0:T(8,128)(2,1)S(1)}, u32[]{:S(2)}, u32[]{:S(2)}) %collective-permute-start.17) | collective-permute-done | bytes 491552 | tf_op jit(solution)/shard_map/ppermute | solution.py:33
  82.8 0.5 collective-permute-start.19
  83.3 2.4 %add_convert_fusion.1 = (bf16[160,1664]{1,0:T(8,128)(2,1)}, bf16[160,1664]{1,0:T(8,128)(2,1)}) fusion(bf16[320,1664]{1,0:T(8,128)(2,1)} %collective-permute-done.12, bf16[320,1664]{1,0:T(8,128)(2,1)S(1)} %get-tuple-element.38), kind=kLoop, calls=%fused_computation.1 | loop fusion | flops 2129920 | bytes 3194880 | tf_op jit(solution)/shard_map/convert_element_type | solution.py:342
  85.8 0.3 collective-permute-start.13
  86.1 0.3 add_convert_fusion.3
  86.4 1.8 %collective-permute-start.7 = (bf16[160,1664]{1,0:T(8,128)(2,1)S(1)}, bf16[160,1664]{1,0:T(8,128)(2,1)S(1)}, u32[]{:S(2)}, u32[]{:S(2)}) collective-permute-start(bf16[160,1664]{1,0:T(8,128)(2,1)S(1)} %get-tuple-element.53), channel_id=1, source_target_pairs={{0,2},{1,5},{2,0},{3,7},{4,6},{5,1},{6,4},{7,3},{8,10},{9,13},{10,... | collective-permute-start | bytes 1597448 | tf_op jit(solution)/shard_map/ppermute | solution.py:33
  88.2 0.0 copy-start.14
  88.2 7.4 %w_in_grad.1 = bf16[1536,768]{1,0:T(8,128)(2,1)} custom-call(bf16[160,1536]{1,0:T(8,128)(2,1)S(1)} %constant_dynamic-update-slice_fusion.4.refs_0_, bf16[160,1536]{1,0:T(8,128)(2,1)S(1)} %collective-permute-done.17.refs_1_, bf16[160,1536]{1,0:T(8,128)(2,1)S(1)} %collective-permute-done.18.refs_2_, bf16[160,1536]{1,0:T(8,128)(2,1)S(1)} %collective-permute-done.19.refs_3_, ...), custom_call_target="tpu_custom_call" | custom-call | flops 3019898880 | bytes 8257536 | tf_op jit(solution)/shard_map/w_in_grad/pallas_call | solution.py:323
  95.7 0.1 add_convert_fusion.5
  95.7 0.6 collective-permute-start.14
  96.4 7.6 %collective-permute-done.7 = bf16[160,1664]{1,0:T(8,128)(2,1)S(1)} collective-permute-done((bf16[160,1664]{1,0:T(8,128)(2,1)S(1)}, bf16[160,1664]{1,0:T(8,128)(2,1)S(1)}, u32[]{:S(2)}, u32[]{:S(2)}) %collective-permute-start.7) | collective-permute-done | bytes 532512 | tf_op jit(solution)/shard_map/ppermute | solution.py:33
  104.0 0.1 add_convert_fusion.7
  104.2 0.6 collective-permute-start.8
  104.8 0.3 copy-done.16
  105.1 0.1 add_convert_fusion.4
  105.2 3.0 %collective-permute-start.15 = (bf16[80,1664]{1,0:T(8,128)(2,1)S(1)}, bf16[80,1664]{1,0:T(8,128)(2,1)S(1)}, u32[]{:S(2)}, u32[]{:S(2)}) collective-permute-start(bf16[80,1664]{1,0:T(8,128)(2,1)S(1)} %add_convert_fusion.4), channel_id=1, source_target_pairs={{0,8},{1,9},{2,10},{3,11},{4,12},{5,13},{6,14},{7,15},{8,0},{9,1},... | collective-permute-start | bytes 798728 | tf_op jit(solution)/shard_map/ppermute | solution.py:39
  108.2 7.4 %w_out_grad.1 = bf16[768,1536]{1,0:T(8,128)(2,1)} custom-call(bf16[640,768]{1,0:T(8,128)(2,1)S(1)} %bitcast.27, bf16[640,768]{1,0:T(8,128)(2,1)S(1)} %bitcast.29, bf16[160,1536]{1,0:T(8,128)(2,1)S(1)} %constant_dynamic-update-slice_fusion.refs_0_.refs_2_, bf16[160,1536]{1,0:T(8,128)(2,1)S(1)} %collective-permute-done.3.refs_1_.refs_3_, ...), custom_call_target="tpu_custom_call" | custom-call | flops 3019898880 | bytes 8257536 | tf_op jit(solution)/shard_map/w_out_grad/pallas_call | solution.py:323
  115.5 3.3 %collective-permute-done.15.back = bf16[80,1664]{1,0:T(8,128)(2,1)S(1)} collective-permute-done((bf16[80,1664]{1,0:T(8,128)(2,1)S(1)}, bf16[80,1664]{1,0:T(8,128)(2,1)S(1)}, u32[]{:S(2)}, u32[]{:S(2)}) %collective-permute-start.15) | collective-permute-done | bytes 266272 | tf_op jit(solution)/shard_map/ppermute | solution.py:39
  118.8 1.2 slots_to_tokens.1
  (43 shorter events, 0.2 us)
Async XLA Ops:
  0.6 1.0 copy-start.2
  1.6 0.7 copy-start.4
  2.3 0.7 copy-start.6
  2.9 0.7 copy-start.8
  3.6 0.7 copy-start.10
  4.6 12.5 %collective-permute-start = (bf16[80,1536]{1,0:T(8,128)(2,1)S(1)}, bf16[80,1536]{1,0:T(8,128)(2,1)S(1)}, u32[]{:S(2)}, u32[]{:S(2)}) collective-permute-start(bf16[80,1536]{1,0:T(8,128)(2,1)S(1)} %get-tuple-element.27), channel_id=1, source_target_pairs={{0,4},{1,3},{2,6},{3,1},{4,0},{5,7},{6,2},{7,5},{8,12},{9,11},{10,... | collective-permute-start | bytes 737288 | tf_op jit(solution)/shard_map/ppermute | solution.py:33
  7.7 13.6 %collective-permute-start.1 = (bf16[80,1536]{1,0:T(8,128)(2,1)S(1)}, bf16[80,1536]{1,0:T(8,128)(2,1)S(1)}, u32[]{:S(2)}, u32[]{:S(2)}) collective-permute-start(bf16[80,1536]{1,0:T(8,128)(2,1)S(1)} %get-tuple-element.30), channel_id=1, source_target_pairs={{0,8},{1,9},{2,10},{3,11},{4,12},{5,13},{6,14},{7,15},{8,0},{9,1},... | collective-permute-start | bytes 737288 | tf_op jit(solution)/shard_map/ppermute | solution.py:39
  10.3 1.5 %copy-start = (bf16[1280,768]{1,0:T(8,128)(2,1)S(1)}, bf16[1280,768]{1,0:T(8,128)(2,1)}, u32[]{:S(2)}) copy-start(bf16[1280,768]{1,0:T(8,128)(2,1)} %param.15) | copy-start | bytes 5898244
  11.9 3.2 %copy-start.1 = (bf16[1280,768]{1,0:T(8,128)(2,1)S(1)}, bf16[1280,768]{1,0:T(8,128)(2,1)}, u32[]{:S(2)}) copy-start(bf16[1280,768]{1,0:T(8,128)(2,1)} %param.15) | copy-start | bytes 5898244
  13.8 1.3 %copy-start.12 = (f32[8,80,768]{2,1,0:T(8,128)}, f32[8,80,768]{2,1,0:T(8,128)S(1)}, u32[]{:S(2)}) copy-start(f32[8,80,768]{2,1,0:T(8,128)S(1)} %get-tuple-element.34) | copy-start | bytes 5898244
  17.1 25.3 %copy-start.13 = (f32[8,80,768]{2,1,0:T(8,128)}, f32[8,80,768]{2,1,0:T(8,128)S(1)}, u32[]{:S(2)}) copy-start(f32[8,80,768]{2,1,0:T(8,128)S(1)} %get-tuple-element.37) | copy-start | bytes 5898244
  17.1 10.9 %copy-start.3 = (bf16[128,1536]{1,0:T(8,128)(2,1)S(1)}, bf16[128,1536]{1,0:T(8,128)(2,1)}, u32[]{:S(2)}) copy-start(bf16[128,1536]{1,0:T(8,128)(2,1)} %values.3) | copy-start | bytes 1179652
  17.1 10.9 %copy-start.5 = (s32[128]{0:T(128)S(1)}, s32[128]{0:T(128)}, u32[]{:S(2)}) copy-start(s32[128]{0:T(128)} %param.12) | copy-start | bytes 1540
  17.1 10.9 %copy-start.7 = (s32[128]{0:T(128)S(1)}, s32[128]{0:T(128)}, u32[]{:S(2)}) copy-start(s32[128]{0:T(128)} %param.13) | copy-start | bytes 1540
  17.1 10.9 %copy-start.9 = (s32[128]{0:T(128)S(1)}, s32[128]{0:T(128)}, u32[]{:S(2)}) copy-start(s32[128]{0:T(128)} %param.14) | copy-start | bytes 1540
  17.1 10.9 %copy-start.11 = (f32[128]{0:T(128)S(1)}, f32[128]{0:T(128)}, u32[]{:S(2)}) copy-start(f32[128]{0:T(128)} %param.11) | copy-start | bytes 1540
  21.3 6.2 %collective-permute-start.2 = (bf16[80,1536]{1,0:T(8,128)(2,1)S(1)}, bf16[80,1536]{1,0:T(8,128)(2,1)S(1)}, u32[]{:S(2)}, u32[]{:S(2)}) collective-permute-start(bf16[80,1536]{1,0:T(8,128)(2,1)S(1)} %collective-permute-done.1), channel_id=1, source_target_pairs={{0,4},{1,3},{2,6},{3,1},{4,0},{5,7},{6,2},{7,5},{8,12},{9,11},{10,... | collective-permute-start | bytes 737288 | tf_op jit(solution)/shard_map/ppermute | solution.py:33
  27.5 8.9 %collective-permute-start.9 = (bf16[160,1536]{1,0:T(8,128)(2,1)S(1)}, bf16[160,1536]{1,0:T(8,128)(2,1)S(1)}, u32[]{:S(2)}, u32[]{:S(2)}) collective-permute-start(bf16[160,1536]{1,0:T(8,128)(2,1)S(1)} %constant_dynamic-update-slice_fusion.2.refs_0_.refs_6_), channel_id=1, source_target_pairs={{0,2},{1,5},{2,0},{3,7},{4,6},{5,1},{6,4},{7,3},{8,10},{9,13},{10,... | collective-permute-start | bytes 1474568 | tf_op jit(solution)/shard_map/ppermute | solution.py:33
  28.3 14.1 %collective-permute-start.20 = (bf16[80,1536]{1,0:T(8,128)(2,1)S(1)}, bf16[80,1536]{1,0:T(8,128)(2,1)S(1)}, u32[]{:S(2)}, u32[]{:S(2)}) collective-permute-start(bf16[80,1536]{1,0:T(8,128)(2,1)S(1)} %get-tuple-element.44), channel_id=1, source_target_pairs={{0,8},{1,9},{2,10},{3,11},{4,12},{5,13},{6,14},{7,15},{8,0},{9,1},... | collective-permute-start | bytes 737288 | tf_op jit(solution)/shard_map/ppermute | solution.py:39
  30.5 18.6 %collective-permute-start.3 = (bf16[160,1536]{1,0:T(8,128)(2,1)S(1)}, bf16[160,1536]{1,0:T(8,128)(2,1)S(1)}, u32[]{:S(2)}, u32[]{:S(2)}) collective-permute-start(bf16[160,1536]{1,0:T(8,128)(2,1)S(1)} %constant_dynamic-update-slice_fusion.refs_0_.refs_2_), channel_id=1, source_target_pairs={{0,2},{1,5},{2,0},{3,7},{4,6},{5,1},{6,4},{7,3},{8,10},{9,13},{10,... | collective-permute-start | bytes 1474568 | tf_op jit(solution)/shard_map/ppermute | solution.py:33
  32.0 17.1 %collective-permute-start.10 = (bf16[160,1536]{1,0:T(8,128)(2,1)S(1)}, bf16[160,1536]{1,0:T(8,128)(2,1)S(1)}, u32[]{:S(2)}, u32[]{:S(2)}) collective-permute-start(bf16[160,1536]{1,0:T(8,128)(2,1)S(1)} %constant_dynamic-update-slice_fusion.2.refs_0_.refs_6_), channel_id=1, source_target_pairs={{0,1},{1,0},{2,3},{3,2},{4,5},{5,4},{6,7},{7,6},{8,9},{9,8},{10,11... | collective-permute-start | bytes 1474568 | tf_op jit(solution)/shard_map/ppermute | solution.py:33
  36.4 12.7 %collective-permute-start.11 = (bf16[160,1536]{1,0:T(8,128)(2,1)S(1)}, bf16[160,1536]{1,0:T(8,128)(2,1)S(1)}, u32[]{:S(2)}, u32[]{:S(2)}) collective-permute-start(bf16[160,1536]{1,0:T(8,128)(2,1)S(1)} %collective-permute-done.9.refs_1_.refs_7_), channel_id=1, source_target_pairs={{0,1},{1,0},{2,3},{3,2},{4,5},{5,4},{6,7},{7,6},{8,9},{9,8},{10,11... | collective-permute-start | bytes 1474568 | tf_op jit(solution)/shard_map/ppermute | solution.py:33
  42.4 6.4 %collective-permute-start.21 = (bf16[80,1536]{1,0:T(8,128)(2,1)S(1)}, bf16[80,1536]{1,0:T(8,128)(2,1)S(1)}, u32[]{:S(2)}, u32[]{:S(2)}) collective-permute-start(bf16[80,1536]{1,0:T(8,128)(2,1)S(1)} %collective-permute-done.20), channel_id=1, source_target_pairs={{0,4},{1,3},{2,6},{3,1},{4,0},{5,7},{6,2},{7,5},{8,12},{9,11},{10,... | collective-permute-start | bytes 737288 | tf_op jit(solution)/shard_map/ppermute | solution.py:33
  42.4 18.7 %collective-permute-start.4 = (bf16[160,1536]{1,0:T(8,128)(2,1)S(1)}, bf16[160,1536]{1,0:T(8,128)(2,1)S(1)}, u32[]{:S(2)}, u32[]{:S(2)}) collective-permute-start(bf16[160,1536]{1,0:T(8,128)(2,1)S(1)} %constant_dynamic-update-slice_fusion.refs_0_.refs_2_), channel_id=1, source_target_pairs={{0,1},{1,0},{2,3},{3,2},{4,5},{5,4},{6,7},{7,6},{8,9},{9,8},{10,11... | collective-permute-start | bytes 1474568 | tf_op jit(solution)/shard_map/ppermute | solution.py:33
  48.8 26.0 %collective-permute-start.22 = (bf16[160,1536]{1,0:T(8,128)(2,1)S(1)}, bf16[160,1536]{1,0:T(8,128)(2,1)S(1)}, u32[]{:S(2)}, u32[]{:S(2)}) collective-permute-start(bf16[160,1536]{1,0:T(8,128)(2,1)S(1)} %constant_dynamic-update-slice_fusion.6.refs_4_), channel_id=1, source_target_pairs={{0,2},{1,5},{2,0},{3,7},{4,6},{5,1},{6,4},{7,3},{8,10},{9,13},{10,... | collective-permute-start | bytes 1474568 | tf_op jit(solution)/shard_map/ppermute | solution.py:33
  49.1 12.0 %collective-permute-start.5 = (bf16[160,1536]{1,0:T(8,128)(2,1)S(1)}, bf16[160,1536]{1,0:T(8,128)(2,1)S(1)}, u32[]{:S(2)}, u32[]{:S(2)}) collective-permute-start(bf16[160,1536]{1,0:T(8,128)(2,1)S(1)} %collective-permute-done.3.refs_1_.refs_3_), channel_id=1, source_target_pairs={{0,1},{1,0},{2,3},{3,2},{4,5},{5,4},{6,7},{7,6},{8,9},{9,8},{10,11... | collective-permute-start | bytes 1474568 | tf_op jit(solution)/shard_map/ppermute | solution.py:33
  60.4 22.4 %collective-permute-start.12 = (bf16[320,1664]{1,0:T(8,128)(2,1)S(1)}, bf16[320,1664]{1,0:T(8,128)(2,1)}, u32[]{:S(2)}, u32[]{:S(2)}) collective-permute-start(bf16[320,1664]{1,0:T(8,128)(2,1)S(1)} %get-tuple-element.39), channel_id=1, source_target_pairs={{0,1},{1,0},{2,3},{3,2},{4,5},{5,4},{6,7},{7,6},{8,9},{9,8},{10,11... | collective-permute-start | bytes 3194888 | tf_op jit(solution)/shard_map/ppermute | solution.py:33
  61.0 12.9 %collective-permute-start.16 = (bf16[80,1536]{1,0:T(8,128)(2,1)S(1)}, bf16[80,1536]{1,0:T(8,128)(2,1)S(1)}, u32[]{:S(2)}, u32[]{:S(2)}) collective-permute-start(bf16[80,1536]{1,0:T(8,128)(2,1)S(1)} %get-tuple-element.42), channel_id=1, source_target_pairs={{0,4},{1,3},{2,6},{3,1},{4,0},{5,7},{6,2},{7,5},{8,12},{9,11},{10,... | collective-permute-start | bytes 737288 | tf_op jit(solution)/shard_map/ppermute | solution.py:33
  72.4 13.4 %collective-permute-start.6 = (bf16[320,1664]{1,0:T(8,128)(2,1)S(1)}, bf16[320,1664]{1,0:T(8,128)(2,1)S(1)}, u32[]{:S(2)}, u32[]{:S(2)}) collective-permute-start(bf16[320,1664]{1,0:T(8,128)(2,1)S(1)} %get-tuple-element.36), channel_id=1, source_target_pairs={{0,1},{1,0},{2,3},{3,2},{4,5},{5,4},{6,7},{7,6},{8,9},{9,8},{10,11... | collective-permute-start | bytes 3194888 | tf_op jit(solution)/shard_map/ppermute | solution.py:33
  73.9 8.9 %collective-permute-start.17 = (bf16[160,1536]{1,0:T(8,128)(2,1)S(1)}, bf16[160,1536]{1,0:T(8,128)(2,1)S(1)}, u32[]{:S(2)}, u32[]{:S(2)}) collective-permute-start(bf16[160,1536]{1,0:T(8,128)(2,1)S(1)} %constant_dynamic-update-slice_fusion.4.refs_0_), channel_id=1, source_target_pairs={{0,2},{1,5},{2,0},{3,7},{4,6},{5,1},{6,4},{7,3},{8,10},{9,13},{10,... | collective-permute-start | bytes 1474568 | tf_op jit(solution)/shard_map/ppermute | solution.py:33
  74.3 12.1 %collective-permute-start.23 = (bf16[160,1536]{1,0:T(8,128)(2,1)S(1)}, bf16[160,1536]{1,0:T(8,128)(2,1)S(1)}, u32[]{:S(2)}, u32[]{:S(2)}) collective-permute-start(bf16[160,1536]{1,0:T(8,128)(2,1)S(1)} %constant_dynamic-update-slice_fusion.6.refs_4_), channel_id=1, source_target_pairs={{0,1},{1,0},{2,3},{3,2},{4,5},{5,4},{6,7},{7,6},{8,9},{9,8},{10,11... | collective-permute-start | bytes 1474568 | tf_op jit(solution)/shard_map/ppermute | solution.py:33
  74.8 13.4 %collective-permute-start.18 = (bf16[160,1536]{1,0:T(8,128)(2,1)S(1)}, bf16[160,1536]{1,0:T(8,128)(2,1)S(1)}, u32[]{:S(2)}, u32[]{:S(2)}) collective-permute-start(bf16[160,1536]{1,0:T(8,128)(2,1)S(1)} %constant_dynamic-update-slice_fusion.4.refs_0_), channel_id=1, source_target_pairs={{0,1},{1,0},{2,3},{3,2},{4,5},{5,4},{6,7},{7,6},{8,9},{9,8},{10,11... | collective-permute-start | bytes 1474568 | tf_op jit(solution)/shard_map/ppermute | solution.py:33
  82.8 5.3 %collective-permute-start.24 = (bf16[160,1536]{1,0:T(8,128)(2,1)S(1)}, bf16[160,1536]{1,0:T(8,128)(2,1)S(1)}, u32[]{:S(2)}, u32[]{:S(2)}) collective-permute-start(bf16[160,1536]{1,0:T(8,128)(2,1)S(1)} %collective-permute-done.22.refs_5_), channel_id=1, source_target_pairs={{0,1},{1,0},{2,3},{3,2},{4,5},{5,4},{6,7},{7,6},{8,9},{9,8},{10,11... | collective-permute-start | bytes 1474568 | tf_op jit(solution)/shard_map/ppermute | solution.py:33
  82.8 5.3 %collective-permute-start.19 = (bf16[160,1536]{1,0:T(8,128)(2,1)S(1)}, bf16[160,1536]{1,0:T(8,128)(2,1)S(1)}, u32[]{:S(2)}, u32[]{:S(2)}) collective-permute-start(bf16[160,1536]{1,0:T(8,128)(2,1)S(1)} %collective-permute-done.17.refs_1_), channel_id=1, source_target_pairs={{0,1},{1,0},{2,3},{3,2},{4,5},{5,4},{6,7},{7,6},{8,9},{9,8},{10,11... | collective-permute-start | bytes 1474568 | tf_op jit(solution)/shard_map/ppermute | solution.py:33
  85.8 9.9 %collective-permute-start.13 = (bf16[160,1664]{1,0:T(8,128)(2,1)}, bf16[160,1664]{1,0:T(8,128)(2,1)S(1)}, u32[]{:S(2)}, u32[]{:S(2)}) collective-permute-start(bf16[160,1664]{1,0:T(8,128)(2,1)} %get-tuple-element.51), channel_id=1, source_target_pairs={{0,2},{1,5},{2,0},{3,7},{4,6},{5,1},{6,4},{7,3},{8,10},{9,13},{10,... | collective-permute-start | bytes 1597448 | tf_op jit(solution)/shard_map/ppermute | solution.py:33
  86.4 17.6 %collective-permute-start.7 = (bf16[160,1664]{1,0:T(8,128)(2,1)S(1)}, bf16[160,1664]{1,0:T(8,128)(2,1)S(1)}, u32[]{:S(2)}, u32[]{:S(2)}) collective-permute-start(bf16[160,1664]{1,0:T(8,128)(2,1)S(1)} %get-tuple-element.53), channel_id=1, source_target_pairs={{0,2},{1,5},{2,0},{3,7},{4,6},{5,1},{6,4},{7,3},{8,10},{9,13},{10,... | collective-permute-start | bytes 1597448 | tf_op jit(solution)/shard_map/ppermute | solution.py:33
  88.2 7.5 %copy-start.14 = (bf16[160,1664]{1,0:T(8,128)(2,1)S(1)}, bf16[160,1664]{1,0:T(8,128)(2,1)}, u32[]{:S(2)}) copy-start(bf16[160,1664]{1,0:T(8,128)(2,1)} %get-tuple-element.50) | copy-start | bytes 1597444
  95.7 8.4 %copy-start.15 = (bf16[160,1664]{1,0:T(8,128)(2,1)}, bf16[160,1664]{1,0:T(8,128)(2,1)S(1)}, u32[]{:S(2)}) copy-start(bf16[160,1664]{1,0:T(8,128)(2,1)S(1)} %collective-permute-done.13) | copy-start | bytes 1597444
  95.7 9.1 %collective-permute-start.14 = (bf16[80,1664]{1,0:T(8,128)(2,1)S(1)}, bf16[80,1664]{1,0:T(8,128)(2,1)S(1)}, u32[]{:S(2)}, u32[]{:S(2)}) collective-permute-start(bf16[80,1664]{1,0:T(8,128)(2,1)S(1)} %add_convert_fusion.5), channel_id=1, source_target_pairs={{0,4},{1,3},{2,6},{3,1},{4,0},{5,7},{6,2},{7,5},{8,12},{9,11},{10,... | collective-permute-start | bytes 798728 | tf_op jit(solution)/shard_map/ppermute | solution.py:33
  104.0 1.0 copy-start.16
  104.2 14.7 %collective-permute-start.8 = (bf16[80,1664]{1,0:T(8,128)(2,1)S(1)}, bf16[80,1664]{1,0:T(8,128)(2,1)S(1)}, u32[]{:S(2)}, u32[]{:S(2)}) collective-permute-start(bf16[80,1664]{1,0:T(8,128)(2,1)S(1)} %get-tuple-element.54), channel_id=1, source_target_pairs={{0,4},{1,3},{2,6},{3,1},{4,0},{5,7},{6,2},{7,5},{8,12},{9,11},{10,... | collective-permute-start | bytes 798728 | tf_op jit(solution)/shard_map/ppermute | solution.py:33
  105.2 13.6 %collective-permute-start.15 = (bf16[80,1664]{1,0:T(8,128)(2,1)S(1)}, bf16[80,1664]{1,0:T(8,128)(2,1)S(1)}, u32[]{:S(2)}, u32[]{:S(2)}) collective-permute-start(bf16[80,1664]{1,0:T(8,128)(2,1)S(1)} %add_convert_fusion.4), channel_id=1, source_target_pairs={{0,8},{1,9},{2,10},{3,11},{4,12},{5,13},{6,14},{7,15},{8,0},{9,1},... | collective-permute-start | bytes 798728 | tf_op jit(solution)/shard_map/ppermute | solution.py:39

commit v4 on v3

v4 whole, which is shorter than its diff:
```python
import functools

import jax
import jax.numpy as jnp
from jax import lax
from jax.experimental import pallas as pl
from jax.experimental.pallas import tpu as pltpu
from jax.sharding import PartitionSpec as P

SPLIT = 8
CORE, LOW, HIGH = 1, 2, 4
LANES = 128
VMEM = pl.BlockSpec(memory_space=pltpu.VMEM)
F32, BF16 = jnp.float32, jnp.bfloat16


def params():
    return pltpu.CompilerParams(vmem_limit_bytes=48 * 1024 * 1024)


def cost(flops, moved, exps=0):
    return pl.CostEstimate(flops=flops, bytes_accessed=moved, transcendentals=exps)


def bits(core):
    return (HIGH, LOW, CORE) if core == 0 else (LOW, HIGH, CORE)


def meet(rows, step):
    devices = lax.axis_size("expert")
    return lax.ppermute(rows, "expert", [(i, i ^ bits(i % 2)[step]) for i in range(devices)])


def shift(rows, by):
    devices = lax.axis_size("expert")
    pairs = [(i, (i + by * SPLIT) % devices) for i in range(devices)]
    return lax.ppermute(rows, "expert", pairs)


def cross(rows, sign):
    experts = lax.axis_size("expert") // SPLIT
    if experts == 2:
        return shift(rows, sign)
    slots = rows.shape[0] // (experts - 1)
    return jnp.concatenate(
        [shift(rows[(s - 1) * slots : s * slots], sign * s) for s in range(1, experts)]
    )


def after(value, *earlier):
    return lax.optimization_barrier((value, *earlier))[0]


def sources_met(me, experts):
    block = jnp.arange(SPLIT * (experts - 1), dtype=jnp.int32)

    def place(i):
        first = jnp.where(((me ^ (i >> 2)) & 1) == 1, LOW, HIGH)
        second = (LOW + HIGH) - first
        mask = (i & 1) * first + ((i >> 1) & 1) * second + (i >> 2) * CORE
        return (me & (SPLIT - 1)) ^ mask

    my_expert = me >> 3
    from_expert = my_expert - 1 - block % (experts - 1)
    from_expert = jnp.where(from_expert < 0, from_expert + experts, from_expert)
    near = my_expert * SPLIT + place(block[:SPLIT])
    return near, from_expert * SPLIT + place(block // (experts - 1))


def slot_places(expert_id, dropped, slot, slots):
    devices = lax.axis_size("expert")
    ahead = expert_id - lax.axis_index("expert") // SPLIT
    ahead = jnp.where(ahead < 0, ahead + devices // SPLIT, ahead)
    return jnp.where(dropped == 1, -1, ahead * slots + slot)


def chosen(place, first, count):
    rows = lax.broadcasted_iota(jnp.int32, (count, place.shape[1]), 0) + first
    return rows == place


def copies(sources, buffers, sem):
    made = [
        pltpu.make_async_copy(src, dst, sem.at[i]) for i, (src, dst) in enumerate(zip(sources, buffers))
    ]
    for copy in made:
        copy.start()
    for copy in made:
        copy.wait()


def place_kernel(slots, scale, *refs):
    near, far = refs[5:7]
    expert_id, dropped, slot, gate, values = refs[7:12]
    copies(refs[:5], refs[7:12], refs[12])
    place = slot_places(expert_id[...], dropped[...], slot[...], slots)
    rows = values[...]
    if scale:
        count = rows.shape[0]
        across = lax.broadcasted_iota(jnp.int32, (count, count), 1)
        down = lax.broadcasted_iota(jnp.int32, (count, count), 0)
        column = jnp.sum(jnp.where(across == down, gate[...], 0.0), axis=1, keepdims=True)
        rows = (column * rows.astype(F32)).astype(BF16)
    for first, out in ((0, near), (slots, far)):
        onehot = chosen(place, first, out.shape[0]).astype(F32).astype(BF16)
        out[...] = jnp.dot(onehot, rows, preferred_element_type=F32).astype(BF16)


def to_slots(slots, scale, *inputs):
    experts = lax.axis_size("expert") // SPLIT
    width = inputs[-1].shape[1]
    return pl.pallas_call(
        functools.partial(place_kernel, slots, scale),
        out_shape=(
            jax.ShapeDtypeStruct((slots, width), BF16),
            jax.ShapeDtypeStruct(((experts - 1) * slots, width), BF16),
        ),
        in_specs=[pl.BlockSpec(memory_space=pltpu.HBM)] * 5,
        out_specs=(VMEM, VMEM),
        scratch_shapes=[pltpu.VMEM(x.shape, x.dtype) for x in inputs]
        + [pltpu.SemaphoreType.DMA((5,))],
        compiler_params=params(),
        cost_estimate=cost(2 * experts * slots * inputs[-1].size, 6 * inputs[-1].size),
        name="rows_to_slots",
    )(*inputs)


def home_kernel(slots, expert_id, dropped, slot, gate, kept, got, back, token_grad, gate_grad):
    place = slot_places(expert_id[...], dropped[...], slot[...], slots)
    width = token_grad.shape[1]
    near = kept[...].astype(F32) + got[...].astype(F32)
    total = jnp.zeros(token_grad.shape, F32)
    gates = jnp.zeros(gate_grad.shape, F32)
    for first, rows in ((0, near), (slots, back[...].astype(F32))):
        picks = chosen(place, first, rows.shape[0])
        total += lax.dot_general(
            picks.astype(F32).astype(BF16),
            rows[:, :width].astype(BF16),
            (((0,), (0,)), ((), ())),
            preferred_element_type=F32,
        )
        column = rows[:, width : width + 1]
        gates += jnp.sum(jnp.where(picks, column, 0.0), axis=0, keepdims=True)
    token_grad[...] = total.astype(BF16)
    gate_grad[...] = jnp.where(dropped[...] == 1, 0.0, gates / gate[...])


def to_tokens(slots, expert_id, dropped, slot, gate, kept, got, back):
    count, width = expert_id.shape[1], kept.shape[1] - LANES
    return pl.pallas_call(
        functools.partial(home_kernel, slots),
        out_shape=(
            jax.ShapeDtypeStruct((count, width), BF16),
            jax.ShapeDtypeStruct((1, count), F32),
        ),
        in_specs=[VMEM] * 7,
        out_specs=(VMEM, VMEM),
        compiler_params=params(),
        name="slots_to_tokens",
    )(expert_id, dropped, slot, gate, kept, got, back)


def activation_kernel(order, hidden, activated, slope):
    rows = hidden.shape[1]
    step = 16 if rows % 16 == 0 else rows

    def chunk(i, carry):
        at = pl.ds(i * step, step) if rows > step else slice(None)
        h = hidden[0, at, :].astype(F32)
        cdf = 0.5 * (1.0 + lax.erf(h * 0.7071067811865476))
        density = jnp.exp(-0.5 * h * h) * 0.3989422804014327
        activated[0, at, :] = (h * cdf).astype(BF16)
        slope[0, at, :] = cdf + h * density
        return carry

    lax.fori_loop(0, rows // step, chunk, 0)


def activation(by_source, order):
    _, slots, units = by_source.shape
    block = (1, slots, units)
    shape = (order.shape[0], slots, units)
    size = order.shape[0] * slots * units
    act, slope = pl.pallas_call(
        activation_kernel,
        grid_spec=pltpu.PrefetchScalarGridSpec(
            num_scalar_prefetch=1,
            grid=(order.shape[0],),
            in_specs=[pl.BlockSpec(block, lambda i, order: (order[i], 0, 0))],
            out_specs=[pl.BlockSpec(block, lambda i, order: (i, 0, 0))] * 2,
        ),
        out_shape=(jax.ShapeDtypeStruct(shape, BF16), jax.ShapeDtypeStruct(shape, F32)),
        compiler_params=params(),
        cost_estimate=cost(60 * size, 8 * size, 2 * size),
        name="activation",
    )(order, by_source)
    return act.reshape(-1, units), slope.reshape(-1, units)


def add(a, b):
    return (a.astype(F32) + b.astype(F32)).astype(BF16)


def halves(x):
    half = x.shape[0] // 2
    return x[:half], x[half:]


def add_halves(kept, got):
    kept, got = halves(kept), halves(got)
    return add(kept[0], got[0]), add(kept[1], got[1])


def product(a, b, dims):
    return lax.dot_general(a, b, (dims, ((), ())), preferred_element_type=F32)


def hidden_part(grads, w_out, act, slope):
    grad_act = product(grads, w_out, ((1,), (1,)))
    gates = jnp.sum(grad_act * act.astype(F32), axis=1, keepdims=True)
    return (grad_act * slope).astype(BF16), gates


def slot_part(hidden_grad, gates, w_in):
    part = product(hidden_grad, w_in, ((1,), (1,))).astype(BF16)
    gates = jnp.broadcast_to(gates, (gates.shape[0], LANES)).astype(BF16)
    return halves(jnp.concatenate([part, gates], axis=1))


def body(tokens, out_grad, gate, expert_id, dropped, slot, saved_hidden, w_in, w_out):
    devices = lax.axis_size("expert")
    experts = devices // SPLIT
    slots = saved_hidden.shape[0] // devices
    units = saved_hidden.shape[1]
    me = lax.axis_index("expert")
    row = lambda x: x.reshape(1, -1)
    routing = (row(expert_id), row(dropped), row(slot), row(gate))
    near_order, far_order = sources_met(me, experts)
    by_source = saved_hidden.reshape(devices, slots, units)
    join = jnp.concatenate

    near_grad, far_grad = to_slots(slots, True, *routing, out_grad)
    near_row, far_row = to_slots(slots, False, *routing, tokens)

    far_grad = cross(far_grad, 1)
    got = meet(near_grad, 0)
    near_act, near_slope = activation(by_source, near_order)
    got = after(got, near_act, near_row)
    near_two = join([near_grad, got])
    near_more = meet(near_two, 1)
    far_act, far_slope = activation(by_source, after(far_order, near_two))
    near_more = after(near_more, far_act)
    near_last = meet(near_two, 2), meet(near_more, 2)

    far_grad = after(far_grad, near_more)
    got = meet(far_grad, 0)
    near_grads = join([near_two, near_more, *near_last])
    near_hg, near_gates = hidden_part(near_grads, w_out, near_act, near_slope)
    got = after(got, near_hg)
    far_two = join([far_grad, got])
    far_more = meet(far_two, 1)
    near_kept, near_sent = slot_part(after(near_hg, far_two), near_gates, w_in)
    far_more = after(far_more, near_sent)
    far_last = meet(far_two, 2), meet(far_more, 2)
    near_got = meet(near_sent, 2)

    near_row, far_row = after(near_row, far_more), after(far_row, far_more)
    far_row = cross(far_row, 1)
    got = meet(near_row, 0)
    far_grads = join([far_two, far_more, *far_last])
    far_hg, far_gates = hidden_part(far_grads, w_out, far_act, far_slope)
    got = after(got, far_hg)
    near_row2 = join([near_row, got])
    near_row4 = meet(near_row2, 1)
    far_kept, far_sent = slot_part(after(far_hg, near_row2), far_gates, w_in)

    far_got = meet(far_sent, 2)
    far_kept, far_sent = add_halves(far_kept, far_got)
    far_got = meet(far_sent, 1)
    near_kept, near_sent = add_halves(near_kept, after(near_got, far_sent))
    near_got = meet(near_sent, 1)
    act = join([near_act, far_act])
    w_out_grad = product(after(act, far_sent), join([near_grads, far_grads]), ((0,), (0,))).astype(BF16)
    far_row_got = meet(far_row, 0)
    far_got = after(far_got, w_out_grad, far_row)
    far_kept, far_sent = add_halves(far_kept, far_got)
    far_got = meet(far_sent, 0)
    near_row4 = after(near_row4, far_sent)
    near_rows = join([near_row2, near_row4, meet(near_row2, 2), meet(near_row4, 2)])
    far_row2 = join([far_row, far_row_got])
    far_row4 = meet(far_row2, 1)
    far_got = after(far_got, far_row2, near_row4)
    far_sum = add(far_kept, far_got)
    back = cross(far_sum, -1)
    near_kept, near_sent = add_halves(near_kept, after(near_got, far_sum))
    near_got = meet(near_sent, 0)
    far_rows = join([far_row2, far_row4, meet(far_row2, 2), meet(far_row4, 2)])
    w_in_grad = product(
        join([near_rows, far_rows]), join([near_hg, far_hg]), ((0,), (0,))
    ).astype(BF16)
    back = after(back, w_in_grad)
    token_grad, gate_grad = to_tokens(slots, *routing, near_kept, near_got, back)
    return (token_grad, gate_grad.reshape(-1), w_in_grad, w_out_grad)


def solution(mesh):
    in_specs = (
        P(("parts", "expert"), None),
        P(("parts", "expert"), None),
        P(("parts", "expert")),
        P(("parts", "expert")),
        P(("parts", "expert")),
        P(("parts", "expert")),
        P("parts", "expert"),
        P(None, "expert"),
        P("expert", None),
    )
    out_specs = (
        P(("parts", "expert"), None),
        P(("parts", "expert")),
        P("parts", "expert"),
        P(("parts", "expert"), None),
    )
    return jax.shard_map(body, mesh=mesh, in_specs=in_specs, out_specs=out_specs, check_vma=False)
```

time: 120 us -> 117 us (0.975)
  Pallas kernels: 43.1 us -> 6.18 us
  matrix products: 0 us -> 16.3 us
  waiting for transfers between devices: 44.4 us -> 52.2 us
  local copies, waits for them, and re-layouts: 6.88 us -> 14.3 us
  starting transfers between devices: 21.6 us -> 25.3 us
  other arithmetic: 3.04 us -> 1.15 us
    pallas_call x4 -> x0, Pallas kernels: 37.4 us -> none  [the longest x2 22.6 us: slot_grads(): pl.pallas_call(functools.partial(slot_grad_kernel, len(grads)), out_shape...]
    dot_general x0 -> x6, matrix products: none -> 16.3 us  [product(): return lax.dot_general(a, b, (dims, ((), ())), preferred_element_type=F32)]
    unnamed x38 -> x56, local copies, waits for them, and re-layouts: 6.82 us -> 13.9 us
    ppermute x22, starting transfers between devices: 13.8 us -> 19.8 us  [meet(): lax.ppermute(rows, 'expert', [(i, i ^ bits(i % 2)[step]) for i in range(d...]
    ppermute x22, waiting for transfers between devices: 31.9 us -> 37.5 us  [meet(): lax.ppermute(rows, 'expert', [(i, i ^ bits(i % 2)[step]) for i in range(d...]
    ppermute x3, starting transfers between devices: 7.76 us -> 5.45 us  [shift(): return lax.ppermute(rows, 'expert', pairs)]
    convert_element_type x5, other arithmetic: 3.02 us -> 0.84 us  [add(): return (a.astype(F32) + b.astype(F32)).astype(BF16)]
    ppermute x3, waiting for transfers between devices: 12.6 us -> 14.7 us  [shift(): return lax.ppermute(rows, 'expert', pairs)]
  transfers between devices with their start and end apart: 25 -> 25, of which waited for: 8 -> 12; matrix products, arithmetic and copies ran while one was open for 3% -> 17% of each run, Pallas kernels for 35% -> 4%
where the time goes in v4:
time: 117 us; the launch traced here: 116 us
  waiting for transfers between devices  52.2 us (45%)
  starting transfers between devices  25.3 us (22%)
  matrix products  16.3 us (14%)
  local copies, waits for them, and re-layouts  14.3 us (12%)
  Pallas kernels  6.18 us (5%)
    ppermute x22, waiting for transfers between devices, meet(): lax.ppermute(rows, 'expert', [(i, i ^ bits(i % 2)[step]) for i in range(d...  37.5 us
    ppermute x22, starting transfers between devices, meet(): lax.ppermute(rows, 'expert', [(i, i ^ bits(i % 2)[step]) for i in range(d...  19.8 us
    dot_general x6, matrix products, product(): return lax.dot_general(a, b, (dims, ((), ())), preferred_element_type=F32)  16.3 us
    ppermute x3, waiting for transfers between devices, shift(): return lax.ppermute(rows, 'expert', pairs)  14.7 us
    unnamed x56, local copies, waits for them, and re-layouts  13.9 us
    ppermute x3, starting transfers between devices, shift(): return lax.ppermute(rows, 'expert', pairs)  5.45 us
    pallas_call x2, Pallas kernels, activation(): pl.pallas_call(activation_kernel, grid_spec=pltpu.PrefetchScalarGridSpec(...  3.89 us
  transfers between devices with their start and end apart: 25, of which 12 were waited for; matrix products, arithmetic and copies ran while one was open for 17% of the time, Pallas kernels for 4%

profile of v4, /device:TPU:0, one launch (start us, length us, event | category | flops | bytes accessed | tf_op | source)
XLA Modules:
  0.0 116.4 jit_solution(16841750854133281272)
XLA Ops:
  0.7 1.1 copy-done.3
  1.8 0.7 copy-done.5
  2.5 0.7 copy-done.8
  3.1 0.7 copy-done.11
  3.8 0.7 copy-done.14
  4.4 0.6 rows_to_slots.2
  5.0 3.1 %collective-permute-start = (bf16[80,1536]{1,0:T(8,128)(2,1)S(1)}, bf16[80,1536]{1,0:T(8,128)(2,1)S(1)}, u32[]{:S(2)}, u32[]{:S(2)}) collective-permute-start(bf16[80,1536]{1,0:T(8,128)(2,1)S(1)} %get-tuple-element.32), channel_id=1, source_target_pairs={{0,4},{1,3},{2,6},{3,1},{4,0},{5,7},{6,2},{7,5},{8,12},{9,11},{10,... | collective-permute-start | bytes 737288 | tf_op jit(solution)/shard_map/ppermute | solution.py:31
  8.1 1.0 copy-done.4
  9.1 0.7 copy-done.6
  9.8 0.7 copy-done.9
  10.4 0.7 copy-done.12
  11.1 0.7 copy-done.15
  11.7 0.5 rows_to_slots.3
  12.3 1.5 %copy-done.1 = bf16[1280,768]{1,0:T(8,128)(2,1)S(1)} copy-done((bf16[1280,768]{1,0:T(8,128)(2,1)S(1)}, bf16[1280,768]{1,0:T(8,128)(2,1)}, u32[]{:S(2)}) %copy-start.1) | copy-done | bytes 1966104
  13.8 1.9 %activation.2 = (bf16[8,80,768]{2,1,0:T(8,128)(2,1)S(1)}, f32[8,80,768]{2,1,0:T(8,128)S(1)}) custom-call(s32[8]{0:T(128)S(1)} %get-tuple-element.103.order, bf16[16,80,768]{2,1,0:T(8,128)(2,1)S(1)} %bitcast.29), custom_call_target="tpu_custom_call" | custom-call | flops 29491200 | bytes 3932160 | tf_op jit(solution)/shard_map/activation/pallas_call | solution.py:184
  15.8 0.8 constant_dynamic-update-slice_fusion.25
  16.6 0.8 constant_dynamic-update-slice_fusion.24
  17.3 1.5 %collective-permute-start.1 = (bf16[160,1536]{1,0:T(8,128)(2,1)S(1)}, bf16[160,1536]{1,0:T(8,128)(2,1)S(1)}, u32[]{:S(2)}, u32[]{:S(2)}) collective-permute-start(bf16[160,1536]{1,0:T(8,128)(2,1)S(1)} %get-tuple-element.98), channel_id=1, source_target_pairs={{0,2},{1,5},{2,0},{3,7},{4,6},{5,1},{6,4},{7,3},{8,10},{9,13},{10,... | collective-permute-start | bytes 1474568 | tf_op jit(solution)/shard_map/ppermute | solution.py:31
  18.8 2.6 %collective-permute-start.4 = (bf16[80,1536]{1,0:T(8,128)(2,1)S(1)}, bf16[80,1536]{1,0:T(8,128)(2,1)S(1)}, u32[]{:S(2)}, u32[]{:S(2)}) collective-permute-start(bf16[80,1536]{1,0:T(8,128)(2,1)S(1)} %get-tuple-element.40), channel_id=1, source_target_pairs={{0,8},{1,9},{2,10},{3,11},{4,12},{5,13},{6,14},{7,15},{8,0},{9,1},... | collective-permute-start | bytes 737288 | tf_op jit(solution)/shard_map/ppermute | solution.py:37
  21.4 1.9 %activation.3 = (bf16[8,80,768]{2,1,0:T(8,128)(2,1)S(1)}, f32[8,80,768]{2,1,0:T(8,128)S(1)}) custom-call(s32[8]{0:T(128)S(1)} %get-tuple-element.36.order, bf16[16,80,768]{2,1,0:T(8,128)(2,1)S(1)} %bitcast.30), custom_call_target="tpu_custom_call" | custom-call | flops 29491200 | bytes 3932160 | tf_op jit(solution)/shard_map/activation/pallas_call | solution.py:184
  23.4 2.8 %collective-permute-done.1 = bf16[160,1536]{1,0:T(8,128)(2,1)S(1)} collective-permute-done((bf16[160,1536]{1,0:T(8,128)(2,1)S(1)}, bf16[160,1536]{1,0:T(8,128)(2,1)S(1)}, u32[]{:S(2)}, u32[]{:S(2)}) %collective-permute-start.1) | collective-permute-done | bytes 491552 | tf_op jit(solution)/shard_map/ppermute | solution.py:31
  26.2 3.8 %collective-permute-start.3 = (bf16[160,1536]{1,0:T(8,128)(2,1)S(1)}, bf16[160,1536]{1,0:T(8,128)(2,1)S(1)}, u32[]{:S(2)}, u32[]{:S(2)}) collective-permute-start(bf16[160,1536]{1,0:T(8,128)(2,1)S(1)} %collective-permute-done.1), channel_id=1, source_target_pairs={{0,1},{1,0},{2,3},{3,2},{4,5},{5,4},{6,7},{7,6},{8,9},{9,8},{10,11... | collective-permute-start | bytes 1474568 | tf_op jit(solution)/shard_map/ppermute | solution.py:31
  30.0 2.2 %collective-permute-done.4 = bf16[80,1536]{1,0:T(8,128)(2,1)S(1)} collective-permute-done((bf16[80,1536]{1,0:T(8,128)(2,1)S(1)}, bf16[80,1536]{1,0:T(8,128)(2,1)S(1)}, u32[]{:S(2)}, u32[]{:S(2)}) %collective-permute-start.4) | collective-permute-done | bytes 245792 | tf_op jit(solution)/shard_map/ppermute | solution.py:37
  32.2 0.9 constant_dynamic-update-slice_fusion.23
  33.1 0.9 constant_dynamic-update-slice_fusion.22
  33.9 0.9 constant_dynamic-update-slice_fusion.21
  34.8 1.8 %fusion.4 = (bf16[640,768]{1,0:T(8,128)(2,1)S(1)}, bf16[640]{0:T(1024)(128)(2,1)S(1)}) fusion(f32[8,80,768]{2,1,0:T(8,128)S(1)} %get-tuple-element.39, bf16[8,80,768]{2,1,0:T(8,128)(2,1)S(1)} %get-tuple-element.33, bf16[640,1536]{1,0:T(8,128)(2,1)S(1)} %get-tuple-element.77, bf16[768,1536]{1,0:T(8,128)(2,1)S(1)} %copy-done.18), kind=kOutput, calls=%fused_computation.15 | convolution fusion | flops 1512406400 | bytes 8258816 | tf_op jit(solution)/shard_map/dot_general | solution.py:215
  36.6 0.3 copy-done.17
  37.0 1.4 %collective-permute-done.5 = bf16[80,1536]{1,0:T(8,128)(2,1)S(1)} collective-permute-done((bf16[80,1536]{1,0:T(8,128)(2,1)S(1)}, bf16[80,1536]{1,0:T(8,128)(2,1)S(1)}, u32[]{:S(2)}, u32[]{:S(2)}) %collective-permute-start.5) | collective-permute-done | bytes 245792 | tf_op jit(solution)/shard_map/ppermute | solution.py:31
  38.5 0.6 collective-permute-start.7
  39.0 1.7 %convolution_convert_fusion.3 = bf16[640,1536]{1,0:T(8,128)(2,1)S(1)} fusion(bf16[640,768]{1,0:T(8,128)(2,1)S(1)} %get-tuple-element.43, bf16[1536,768]{1,0:T(8,128)(2,1)S(1)} %copy-done), kind=kOutput, calls=%fused_computation.3 | convolution fusion | flops 1510932480 | bytes 5308416 | tf_op jit(solution)/shard_map/dot_general | solution.py:215
  40.8 0.1 broadcast_in_dim.21
  40.9 0.1 fusion.6
  41.0 6.3 %collective-permute-done.7 = bf16[160,1536]{1,0:T(8,128)(2,1)S(1)} collective-permute-done((bf16[160,1536]{1,0:T(8,128)(2,1)S(1)}, bf16[160,1536]{1,0:T(8,128)(2,1)S(1)}, u32[]{:S(2)}, u32[]{:S(2)}) %collective-permute-start.7) | collective-permute-done | bytes 491552 | tf_op jit(solution)/shard_map/ppermute | solution.py:31
  47.3 0.6 collective-permute-start.10
  48.2 1.0 collective-permute-done.9
  49.3 1.9 %multiply_reduce_fusion = (bf16[640]{0:T(1024)(128)(2,1)S(1)}, bf16[640,768]{1,0:T(8,128)(2,1)S(1)}) fusion(bf16[8,80,768]{2,1,0:T(8,128)(2,1)S(1)} %get-tuple-element.37, f32[8,80,768]{2,1,0:T(8,128)S(1)} %get-tuple-element.45, bf16[640,1536]{1,0:T(8,128)(2,1)S(1)} %get-tuple-element.71, bf16[768,1536]{1,0:T(8,128)(2,1)S(1)} %copy-done.18), kind=kOutput, calls=%fused_computation.16 | convolution fusion | flops 1512406400 | bytes 8258816 | tf_op jit(solution)/shard_map/dot_general | solution.py:215
  51.1 2.4 %collective-permute-done.10 = bf16[80,1536]{1,0:T(8,128)(2,1)S(1)} collective-permute-done((bf16[80,1536]{1,0:T(8,128)(2,1)S(1)}, bf16[80,1536]{1,0:T(8,128)(2,1)S(1)}, u32[]{:S(2)}, u32[]{:S(2)}) %collective-permute-start.10) | collective-permute-done | bytes 245792 | tf_op jit(solution)/shard_map/ppermute | solution.py:31
  53.6 1.7 %convolution_convert_fusion.2 = bf16[640,1536]{1,0:T(8,128)(2,1)S(1)} fusion(bf16[640,768]{1,0:T(8,128)(2,1)S(1)} %get-tuple-element.48, bf16[1536,768]{1,0:T(8,128)(2,1)S(1)} %copy-done), kind=kOutput, calls=%fused_computation.2 | convolution fusion | flops 1510932480 | bytes 5308416 | tf_op jit(solution)/shard_map/dot_general | solution.py:215
  55.3 0.1 broadcast_in_dim.22
  55.5 0.1 fusion.5
  55.6 1.7 %collective-permute-start.14 = (bf16[80,1536]{1,0:T(8,128)(2,1)S(1)}, bf16[80,1536]{1,0:T(8,128)(2,1)S(1)}, u32[]{:S(2)}, u32[]{:S(2)}) collective-permute-start(bf16[80,1536]{1,0:T(8,128)(2,1)S(1)} %get-tuple-element.52), channel_id=1, source_target_pairs={{0,8},{1,9},{2,10},{3,11},{4,12},{5,13},{6,14},{7,15},{8,0},{9,1},... | collective-permute-start | bytes 737288 | tf_op jit(solution)/shard_map/ppermute | solution.py:37
  57.3 0.1 pad_maximum_fusion
  57.4 0.2 collective-permute-start.6
  57.7 12.5 %collective-permute-done.14 = bf16[80,1536]{1,0:T(8,128)(2,1)S(1)} collective-permute-done((bf16[80,1536]{1,0:T(8,128)(2,1)S(1)}, bf16[80,1536]{1,0:T(8,128)(2,1)S(1)}, u32[]{:S(2)}, u32[]{:S(2)}) %collective-permute-start.14) | collective-permute-done | bytes 245792 | tf_op jit(solution)/shard_map/ppermute | solution.py:37
  70.2 0.5 collective-permute-start.17
  70.7 0.3 add_convert_fusion
  70.9 1.6 %collective-permute-start.13 = (bf16[160,1664]{1,0:T(8,128)(2,1)S(1)}, bf16[160,1664]{1,0:T(8,128)(2,1)S(1)}, u32[]{:S(2)}, u32[]{:S(2)}) collective-permute-start(bf16[160,1664]{1,0:T(8,128)(2,1)S(1)} %get-tuple-element.61), channel_id=1, source_target_pairs={{0,2},{1,5},{2,0},{3,7},{4,6},{5,1},{6,4},{7,3},{8,10},{9,13},{10,... | collective-permute-start | bytes 1597448 | tf_op jit(solution)/shard_map/ppermute | solution.py:31
  72.5 4.6 %convolution_convert_fusion.1 = bf16[768,1536]{1,0:T(8,128)(2,1)} fusion(bf16[1280,768]{1,0:T(8,128)(2,1)S(1)} %pad_maximum_fusion, bf16[1280,1536]{1,0:T(8,128)(2,1)S(1)} %get-tuple-element.70), kind=kOutput, calls=%fused_computation.1 | convolution fusion | flops 3021078528 | bytes 8257536 | tf_op jit(solution)/shard_map/dot_general | solution.py:215
  77.1 8.9 %collective-permute-done.13 = bf16[160,1664]{1,0:T(8,128)(2,1)S(1)} collective-permute-done((bf16[160,1664]{1,0:T(8,128)(2,1)S(1)}, bf16[160,1664]{1,0:T(8,128)(2,1)S(1)}, u32[]{:S(2)}, u32[]{:S(2)}) %collective-permute-start.13) | collective-permute-done | bytes 532512 | tf_op jit(solution)/shard_map/ppermute | solution.py:31
  86.1 0.4 collective-permute-start.21
  86.5 0.3 add_convert_fusion.1
  86.8 1.3 %collective-permute-start.12 = (bf16[160,1664]{1,0:T(8,128)(2,1)S(1)}, bf16[160,1664]{1,0:T(8,128)(2,1)S(1)}, u32[]{:S(2)}, u32[]{:S(2)}) collective-permute-start(bf16[160,1664]{1,0:T(8,128)(2,1)S(1)} %get-tuple-element.62), channel_id=1, source_target_pairs={{0,2},{1,5},{2,0},{3,7},{4,6},{5,1},{6,4},{7,3},{8,10},{9,13},{10,... | collective-permute-start | bytes 1597448 | tf_op jit(solution)/shard_map/ppermute | solution.py:31
  88.4 1.3 %collective-permute-start.22 = (bf16[160,1536]{1,0:T(8,128)(2,1)S(1)}, bf16[160,1536]{1,0:T(8,128)(2,1)S(1)}, u32[]{:S(2)}, u32[]{:S(2)}) collective-permute-start(bf16[160,1536]{1,0:T(8,128)(2,1)S(1)} %get-tuple-element.83), channel_id=1, source_target_pairs={{0,2},{1,5},{2,0},{3,7},{4,6},{5,1},{6,4},{7,3},{8,10},{9,13},{10,... | collective-permute-start | bytes 1474568 | tf_op jit(solution)/shard_map/ppermute | solution.py:31
  89.7 7.8 %collective-permute-done.15 = bf16[80,1664]{1,0:T(8,128)(2,1)S(1)} collective-permute-done((bf16[80,1664]{1,0:T(8,128)(2,1)S(1)}, bf16[80,1664]{1,0:T(8,128)(2,1)S(1)}, u32[]{:S(2)}, u32[]{:S(2)}) %collective-permute-start.15) | collective-permute-done | bytes 266272 | tf_op jit(solution)/shard_map/ppermute | solution.py:31
  97.4 0.1 add_convert_fusion.6
  97.5 1.2 %collective-permute-start.19 = (bf16[80,1664]{1,0:T(8,128)(2,1)S(1)}, bf16[80,1664]{1,0:T(8,128)(2,1)S(1)}, u32[]{:S(2)}, u32[]{:S(2)}) collective-permute-start(bf16[80,1664]{1,0:T(8,128)(2,1)S(1)} %add_convert_fusion.6), channel_id=1, source_target_pairs={{0,8},{1,9},{2,10},{3,11},{4,12},{5,13},{6,14},{7,15},{8,0},{9,1},... | collective-permute-start | bytes 798728 | tf_op jit(solution)/shard_map/ppermute | solution.py:37
  98.7 5.2 %collective-permute-done.22 = bf16[160,1536]{1,0:T(8,128)(2,1)S(1)} collective-permute-done((bf16[160,1536]{1,0:T(8,128)(2,1)S(1)}, bf16[160,1536]{1,0:T(8,128)(2,1)S(1)}, u32[]{:S(2)}, u32[]{:S(2)}) %collective-permute-start.22) | collective-permute-done | bytes 491552 | tf_op jit(solution)/shard_map/ppermute | solution.py:31
  103.9 4.7 %collective-permute-start.24 = (bf16[160,1536]{1,0:T(8,128)(2,1)S(1)}, bf16[160,1536]{1,0:T(8,128)(2,1)S(1)}, u32[]{:S(2)}, u32[]{:S(2)}) collective-permute-start(bf16[160,1536]{1,0:T(8,128)(2,1)S(1)} %collective-permute-done.22), channel_id=1, source_target_pairs={{0,1},{1,0},{2,3},{3,2},{4,5},{5,4},{6,7},{7,6},{8,9},{9,8},{10,11... | collective-permute-start | bytes 1474568 | tf_op jit(solution)/shard_map/ppermute | solution.py:31
  108.6 0.1 add_convert_fusion.4
  108.9 1.2 %collective-permute-done.24 = bf16[160,1536]{1,0:T(8,128)(2,1)S(1)} collective-permute-done((bf16[160,1536]{1,0:T(8,128)(2,1)S(1)}, bf16[160,1536]{1,0:T(8,128)(2,1)S(1)}, u32[]{:S(2)}, u32[]{:S(2)}) %collective-permute-start.24) | collective-permute-done | bytes 491552 | tf_op jit(solution)/shard_map/ppermute | solution.py:31
  110.2 4.6 %convolution_convert_fusion = bf16[1536,768]{1,0:T(8,128)(2,1)} fusion(bf16[1280,1536]{1,0:T(8,128)(2,1)S(1)} %constant_dynamic-update-slice_fusion.28, bf16[640,768]{1,0:T(8,128)(2,1)S(1)} %get-tuple-element.48, bf16[640,768]{1,0:T(8,128)(2,1)S(1)} %get-tuple-element.43), kind=kOutput, calls=%fused_computation | convolution fusion | flops 3025010688 | bytes 8257536 | tf_op jit(solution)/shard_map/dot_general | solution.py:215
  114.8 0.5 collective-permute-done.18.got
  115.3 1.2 %slots_to_tokens.1 = (bf16[128,1536]{1,0:T(8,128)(2,1)}, f32[1,128]{1,0:T(1,128)}) custom-call(s32[1,128]{1,0:T(1,128)S(1)} %bitcast.35, s32[1,128]{1,0:T(1,128)S(1)} %bitcast.38, s32[1,128]{1,0:T(1,128)S(1)} %bitcast.41, f32[1,128]{1,0:T(1,128)S(1)} %bitcast.44, bf16[80,1664]{1,0:T(8,128)(2,1)S(1)} %get-tuple-element.69.kept, ...), custom_call_target="tpu_custom_call" | custom-call | tf_op jit(solution)/shard_map/slots_to_tokens/pallas_call | solution.py:150
  (66 shorter events, 1.1 us)
Async XLA Ops:
  0.6 38.4 %copy-start = (bf16[1536,768]{1,0:T(8,128)(2,1)S(1)}, bf16[1536,768]{1,0:T(8,128)(2,1)}, u32[]{:S(2)}) copy-start(bf16[1536,768]{1,0:T(8,128)(2,1)} %param.16) | copy-start | bytes 7077892
  0.6 1.1 copy-start.3
  1.8 0.7 copy-start.5
  2.4 0.7 copy-start.8
  3.1 0.7 copy-start.11
  3.8 0.7 copy-start.14
  5.0 11.5 %collective-permute-start = (bf16[80,1536]{1,0:T(8,128)(2,1)S(1)}, bf16[80,1536]{1,0:T(8,128)(2,1)S(1)}, u32[]{:S(2)}, u32[]{:S(2)}) collective-permute-start(bf16[80,1536]{1,0:T(8,128)(2,1)S(1)} %get-tuple-element.32), channel_id=1, source_target_pairs={{0,4},{1,3},{2,6},{3,1},{4,0},{5,7},{6,2},{7,5},{8,12},{9,11},{10,... | collective-permute-start | bytes 737288 | tf_op jit(solution)/shard_map/ppermute | solution.py:31
  8.1 1.0 copy-start.4
  9.1 0.7 copy-start.6
  9.8 0.7 copy-start.9
  10.4 0.7 copy-start.12
  11.1 0.7 copy-start.15
  12.3 1.5 %copy-start.1 = (bf16[1280,768]{1,0:T(8,128)(2,1)S(1)}, bf16[1280,768]{1,0:T(8,128)(2,1)}, u32[]{:S(2)}) copy-start(bf16[1280,768]{1,0:T(8,128)(2,1)} %param.15) | copy-start | bytes 5898244
  13.8 7.6 %copy-start.2 = (bf16[1280,768]{1,0:T(8,128)(2,1)S(1)}, bf16[1280,768]{1,0:T(8,128)(2,1)}, u32[]{:S(2)}) copy-start(bf16[1280,768]{1,0:T(8,128)(2,1)} %param.15) | copy-start | bytes 5898244
  17.3 8.8 %collective-permute-start.1 = (bf16[160,1536]{1,0:T(8,128)(2,1)S(1)}, bf16[160,1536]{1,0:T(8,128)(2,1)S(1)}, u32[]{:S(2)}, u32[]{:S(2)}) collective-permute-start(bf16[160,1536]{1,0:T(8,128)(2,1)S(1)} %get-tuple-element.98), channel_id=1, source_target_pairs={{0,2},{1,5},{2,0},{3,7},{4,6},{5,1},{6,4},{7,3},{8,10},{9,13},{10,... | collective-permute-start | bytes 1474568 | tf_op jit(solution)/shard_map/ppermute | solution.py:31
  18.8 13.4 %collective-permute-start.4 = (bf16[80,1536]{1,0:T(8,128)(2,1)S(1)}, bf16[80,1536]{1,0:T(8,128)(2,1)S(1)}, u32[]{:S(2)}, u32[]{:S(2)}) collective-permute-start(bf16[80,1536]{1,0:T(8,128)(2,1)S(1)} %get-tuple-element.40), channel_id=1, source_target_pairs={{0,8},{1,9},{2,10},{3,11},{4,12},{5,13},{6,14},{7,15},{8,0},{9,1},... | collective-permute-start | bytes 737288 | tf_op jit(solution)/shard_map/ppermute | solution.py:37
  21.4 11.6 %collective-permute-start.2 = (bf16[160,1536]{1,0:T(8,128)(2,1)S(1)}, bf16[160,1536]{1,0:T(8,128)(2,1)S(1)}, u32[]{:S(2)}, u32[]{:S(2)}) collective-permute-start(bf16[160,1536]{1,0:T(8,128)(2,1)S(1)} %get-tuple-element.98), channel_id=1, source_target_pairs={{0,1},{1,0},{2,3},{3,2},{4,5},{5,4},{6,7},{7,6},{8,9},{9,8},{10,11... | collective-permute-start | bytes 1474568 | tf_op jit(solution)/shard_map/ppermute | solution.py:31
  26.2 7.8 %collective-permute-start.3 = (bf16[160,1536]{1,0:T(8,128)(2,1)S(1)}, bf16[160,1536]{1,0:T(8,128)(2,1)S(1)}, u32[]{:S(2)}, u32[]{:S(2)}) collective-permute-start(bf16[160,1536]{1,0:T(8,128)(2,1)S(1)} %collective-permute-done.1), channel_id=1, source_target_pairs={{0,1},{1,0},{2,3},{3,2},{4,5},{5,4},{6,7},{7,6},{8,9},{9,8},{10,11... | collective-permute-start | bytes 1474568 | tf_op jit(solution)/shard_map/ppermute | solution.py:31
  32.2 6.2 %collective-permute-start.5 = (bf16[80,1536]{1,0:T(8,128)(2,1)S(1)}, bf16[80,1536]{1,0:T(8,128)(2,1)S(1)}, u32[]{:S(2)}, u32[]{:S(2)}) collective-permute-start(bf16[80,1536]{1,0:T(8,128)(2,1)S(1)} %collective-permute-done.4), channel_id=1, source_target_pairs={{0,4},{1,3},{2,6},{3,1},{4,0},{5,7},{6,2},{7,5},{8,12},{9,11},{10,... | collective-permute-start | bytes 737288 | tf_op jit(solution)/shard_map/ppermute | solution.py:31
  32.2 2.6 %copy-start.18 = (bf16[768,1536]{1,0:T(8,128)(2,1)S(1)}, bf16[768,1536]{1,0:T(8,128)(2,1)}, u32[]{:S(2)}) copy-start(bf16[768,1536]{1,0:T(8,128)(2,1)} %param.17) | copy-start | bytes 7077892
  34.8 2.1 %copy-start.17 = (bf16[1280,1536]{1,0:T(8,128)(2,1)S(1)}, bf16[1280,1536]{1,0:T(8,128)(2,1)}, u32[]{:S(2)}) copy-start(bf16[1280,1536]{1,0:T(8,128)(2,1)} %get-tuple-element.76) | copy-start | bytes 11796484
  38.5 8.9 %collective-permute-start.7 = (bf16[160,1536]{1,0:T(8,128)(2,1)S(1)}, bf16[160,1536]{1,0:T(8,128)(2,1)S(1)}, u32[]{:S(2)}, u32[]{:S(2)}) collective-permute-start(bf16[160,1536]{1,0:T(8,128)(2,1)S(1)} %get-tuple-element.92), channel_id=1, source_target_pairs={{0,2},{1,5},{2,0},{3,7},{4,6},{5,1},{6,4},{7,3},{8,10},{9,13},{10,... | collective-permute-start | bytes 1474568 | tf_op jit(solution)/shard_map/ppermute | solution.py:31
  39.0 9.1 %collective-permute-start.8 = (bf16[160,1536]{1,0:T(8,128)(2,1)S(1)}, bf16[160,1536]{1,0:T(8,128)(2,1)S(1)}, u32[]{:S(2)}, u32[]{:S(2)}) collective-permute-start(bf16[160,1536]{1,0:T(8,128)(2,1)S(1)} %get-tuple-element.92), channel_id=1, source_target_pairs={{0,1},{1,0},{2,3},{3,2},{4,5},{5,4},{6,7},{7,6},{8,9},{9,8},{10,11... | collective-permute-start | bytes 1474568 | tf_op jit(solution)/shard_map/ppermute | solution.py:31
  47.3 1.9 %collective-permute-start.9 = (bf16[160,1536]{1,0:T(8,128)(2,1)S(1)}, bf16[160,1536]{1,0:T(8,128)(2,1)S(1)}, u32[]{:S(2)}, u32[]{:S(2)}) collective-permute-start(bf16[160,1536]{1,0:T(8,128)(2,1)S(1)} %collective-permute-done.7), channel_id=1, source_target_pairs={{0,1},{1,0},{2,3},{3,2},{4,5},{5,4},{6,7},{7,6},{8,9},{9,8},{10,11... | collective-permute-start | bytes 1474568 | tf_op jit(solution)/shard_map/ppermute | solution.py:31
  47.3 6.2 %collective-permute-start.10 = (bf16[80,1536]{1,0:T(8,128)(2,1)S(1)}, bf16[80,1536]{1,0:T(8,128)(2,1)S(1)}, u32[]{:S(2)}, u32[]{:S(2)}) collective-permute-start(bf16[80,1536]{1,0:T(8,128)(2,1)S(1)} %get-tuple-element.46), channel_id=1, source_target_pairs={{0,4},{1,3},{2,6},{3,1},{4,0},{5,7},{6,2},{7,5},{8,12},{9,11},{10,... | collective-permute-start | bytes 737288 | tf_op jit(solution)/shard_map/ppermute | solution.py:31
  55.6 15.1 %collective-permute-start.11 = (bf16[320,1664]{1,0:T(8,128)(2,1)S(1)}, bf16[320,1664]{1,0:T(8,128)(2,1)S(1)}, u32[]{:S(2)}, u32[]{:S(2)}) collective-permute-start(bf16[320,1664]{1,0:T(8,128)(2,1)S(1)} %fusion.5), channel_id=1, source_target_pairs={{0,1},{1,0},{2,3},{3,2},{4,5},{5,4},{6,7},{7,6},{8,9},{9,8},{10,11... | collective-permute-start | bytes 3194888 | tf_op jit(solution)/shard_map/ppermute | solution.py:31
  55.6 14.5 %collective-permute-start.14 = (bf16[80,1536]{1,0:T(8,128)(2,1)S(1)}, bf16[80,1536]{1,0:T(8,128)(2,1)S(1)}, u32[]{:S(2)}, u32[]{:S(2)}) collective-permute-start(bf16[80,1536]{1,0:T(8,128)(2,1)S(1)} %get-tuple-element.52), channel_id=1, source_target_pairs={{0,8},{1,9},{2,10},{3,11},{4,12},{5,13},{6,14},{7,15},{8,0},{9,1},... | collective-permute-start | bytes 737288 | tf_op jit(solution)/shard_map/ppermute | solution.py:37
  57.4 19.7 %collective-permute-start.6 = (bf16[320,1664]{1,0:T(8,128)(2,1)S(1)}, bf16[320,1664]{1,0:T(8,128)(2,1)S(1)}, u32[]{:S(2)}, u32[]{:S(2)}) collective-permute-start(bf16[320,1664]{1,0:T(8,128)(2,1)S(1)} %fusion.6), channel_id=1, source_target_pairs={{0,1},{1,0},{2,3},{3,2},{4,5},{5,4},{6,7},{7,6},{8,9},{9,8},{10,11... | collective-permute-start | bytes 3194888 | tf_op jit(solution)/shard_map/ppermute | solution.py:31
  70.2 18.2 %collective-permute-start.16 = (bf16[80,1536]{1,0:T(8,128)(2,1)S(1)}, bf16[80,1536]{1,0:T(8,128)(2,1)S(1)}, u32[]{:S(2)}, u32[]{:S(2)}) collective-permute-start(bf16[80,1536]{1,0:T(8,128)(2,1)S(1)} %collective-permute-done.14), channel_id=1, source_target_pairs={{0,4},{1,3},{2,6},{3,1},{4,0},{5,7},{6,2},{7,5},{8,12},{9,11},{10,... | collective-permute-start | bytes 737288 | tf_op jit(solution)/shard_map/ppermute | solution.py:31
  70.2 15.9 %collective-permute-start.17 = (bf16[160,1536]{1,0:T(8,128)(2,1)S(1)}, bf16[160,1536]{1,0:T(8,128)(2,1)S(1)}, u32[]{:S(2)}, u32[]{:S(2)}) collective-permute-start(bf16[160,1536]{1,0:T(8,128)(2,1)S(1)} %get-tuple-element.87), channel_id=1, source_target_pairs={{0,2},{1,5},{2,0},{3,7},{4,6},{5,1},{6,4},{7,3},{8,10},{9,13},{10,... | collective-permute-start | bytes 1474568 | tf_op jit(solution)/shard_map/ppermute | solution.py:31
  70.7 17.5 %collective-permute-start.20 = (bf16[160,1536]{1,0:T(8,128)(2,1)S(1)}, bf16[160,1536]{1,0:T(8,128)(2,1)S(1)}, u32[]{:S(2)}, u32[]{:S(2)}) collective-permute-start(bf16[160,1536]{1,0:T(8,128)(2,1)S(1)} %get-tuple-element.87), channel_id=1, source_target_pairs={{0,1},{1,0},{2,3},{3,2},{4,5},{5,4},{6,7},{7,6},{8,9},{9,8},{10,11... | collective-permute-start | bytes 1474568 | tf_op jit(solution)/shard_map/ppermute | solution.py:31
  70.9 15.1 %collective-permute-start.13 = (bf16[160,1664]{1,0:T(8,128)(2,1)S(1)}, bf16[160,1664]{1,0:T(8,128)(2,1)S(1)}, u32[]{:S(2)}, u32[]{:S(2)}) collective-permute-start(bf16[160,1664]{1,0:T(8,128)(2,1)S(1)} %get-tuple-element.61), channel_id=1, source_target_pairs={{0,2},{1,5},{2,0},{3,7},{4,6},{5,1},{6,4},{7,3},{8,10},{9,13},{10,... | collective-permute-start | bytes 1597448 | tf_op jit(solution)/shard_map/ppermute | solution.py:31
  86.1 2.1 %collective-permute-start.21 = (bf16[160,1536]{1,0:T(8,128)(2,1)S(1)}, bf16[160,1536]{1,0:T(8,128)(2,1)S(1)}, u32[]{:S(2)}, u32[]{:S(2)}) collective-permute-start(bf16[160,1536]{1,0:T(8,128)(2,1)S(1)} %collective-permute-done.17), channel_id=1, source_target_pairs={{0,1},{1,0},{2,3},{3,2},{4,5},{5,4},{6,7},{7,6},{8,9},{9,8},{10,11... | collective-permute-start | bytes 1474568 | tf_op jit(solution)/shard_map/ppermute | solution.py:31
  86.8 11.9 %collective-permute-start.12 = (bf16[160,1664]{1,0:T(8,128)(2,1)S(1)}, bf16[160,1664]{1,0:T(8,128)(2,1)S(1)}, u32[]{:S(2)}, u32[]{:S(2)}) collective-permute-start(bf16[160,1664]{1,0:T(8,128)(2,1)S(1)} %get-tuple-element.62), channel_id=1, source_target_pairs={{0,2},{1,5},{2,0},{3,7},{4,6},{5,1},{6,4},{7,3},{8,10},{9,13},{10,... | collective-permute-start | bytes 1597448 | tf_op jit(solution)/shard_map/ppermute | solution.py:31
  88.1 9.3 %collective-permute-start.15 = (bf16[80,1664]{1,0:T(8,128)(2,1)S(1)}, bf16[80,1664]{1,0:T(8,128)(2,1)S(1)}, u32[]{:S(2)}, u32[]{:S(2)}) collective-permute-start(bf16[80,1664]{1,0:T(8,128)(2,1)S(1)} %add_convert_fusion.7), channel_id=1, source_target_pairs={{0,4},{1,3},{2,6},{3,1},{4,0},{5,7},{6,2},{7,5},{8,12},{9,11},{10,... | collective-permute-start | bytes 798728 | tf_op jit(solution)/shard_map/ppermute | solution.py:31
  88.4 15.5 %collective-permute-start.22 = (bf16[160,1536]{1,0:T(8,128)(2,1)S(1)}, bf16[160,1536]{1,0:T(8,128)(2,1)S(1)}, u32[]{:S(2)}, u32[]{:S(2)}) collective-permute-start(bf16[160,1536]{1,0:T(8,128)(2,1)S(1)} %get-tuple-element.83), channel_id=1, source_target_pairs={{0,2},{1,5},{2,0},{3,7},{4,6},{5,1},{6,4},{7,3},{8,10},{9,13},{10,... | collective-permute-start | bytes 1474568 | tf_op jit(solution)/shard_map/ppermute | solution.py:31
  89.7 19.2 %collective-permute-start.23 = (bf16[160,1536]{1,0:T(8,128)(2,1)S(1)}, bf16[160,1536]{1,0:T(8,128)(2,1)S(1)}, u32[]{:S(2)}, u32[]{:S(2)}) collective-permute-start(bf16[160,1536]{1,0:T(8,128)(2,1)S(1)} %get-tuple-element.83), channel_id=1, source_target_pairs={{0,1},{1,0},{2,3},{3,2},{4,5},{5,4},{6,7},{7,6},{8,9},{9,8},{10,11... | collective-permute-start | bytes 1474568 | tf_op jit(solution)/shard_map/ppermute | solution.py:31
  97.5 17.2 %collective-permute-start.19 = (bf16[80,1664]{1,0:T(8,128)(2,1)S(1)}, bf16[80,1664]{1,0:T(8,128)(2,1)S(1)}, u32[]{:S(2)}, u32[]{:S(2)}) collective-permute-start(bf16[80,1664]{1,0:T(8,128)(2,1)S(1)} %add_convert_fusion.6), channel_id=1, source_target_pairs={{0,8},{1,9},{2,10},{3,11},{4,12},{5,13},{6,14},{7,15},{8,0},{9,1},... | collective-permute-start | bytes 798728 | tf_op jit(solution)/shard_map/ppermute | solution.py:37
  103.9 6.2 %collective-permute-start.24 = (bf16[160,1536]{1,0:T(8,128)(2,1)S(1)}, bf16[160,1536]{1,0:T(8,128)(2,1)S(1)}, u32[]{:S(2)}, u32[]{:S(2)}) collective-permute-start(bf16[160,1536]{1,0:T(8,128)(2,1)S(1)} %collective-permute-done.22), channel_id=1, source_target_pairs={{0,1},{1,0},{2,3},{3,2},{4,5},{5,4},{6,7},{7,6},{8,9},{9,8},{10,11... | collective-permute-start | bytes 1474568 | tf_op jit(solution)/shard_map/ppermute | solution.py:31
  108.8 6.5 %collective-permute-start.18 = (bf16[80,1664]{1,0:T(8,128)(2,1)S(1)}, bf16[80,1664]{1,0:T(8,128)(2,1)S(1)}, u32[]{:S(2)}, u32[]{:S(2)}) collective-permute-start(bf16[80,1664]{1,0:T(8,128)(2,1)S(1)} %get-tuple-element.68), channel_id=1, source_target_pairs={{0,4},{1,3},{2,6},{3,1},{4,0},{5,7},{6,2},{7,5},{8,12},{9,11},{10,... | collective-permute-start | bytes 798728 | tf_op jit(solution)/shard_map/ppermute | solution.py:31
  110.2 5.1 %copy-start.7 = (s32[128]{0:T(128)S(1)}, s32[128]{0:T(128)}, u32[]{:S(2)}) copy-start(s32[128]{0:T(128)} %param.12) | copy-start | bytes 1540
  110.2 5.1 %copy-start.10 = (s32[128]{0:T(128)S(1)}, s32[128]{0:T(128)}, u32[]{:S(2)}) copy-start(s32[128]{0:T(128)} %param.13) | copy-start | bytes 1540
  110.2 5.1 %copy-start.13 = (s32[128]{0:T(128)S(1)}, s32[128]{0:T(128)}, u32[]{:S(2)}) copy-start(s32[128]{0:T(128)} %param.14) | copy-start | bytes 1540
  110.2 5.1 %copy-start.16 = (f32[128]{0:T(128)S(1)}, f32[128]{0:T(128)}, u32[]{:S(2)}) copy-start(f32[128]{0:T(128)} %param.11) | copy-start | bytes 1540

commit v5 on v4

--- a/solution.py
+++ b/solution.py
@@ -67,11 +67,12 @@
     return near, from_expert * SPLIT + place(block // (experts - 1))
 
 
-def slot_places(expert_id, dropped, slot, slots):
+def pack_routing(expert_id, dropped, slot, gate, slots):
     devices = lax.axis_size("expert")
-    ahead = expert_id - lax.axis_index("expert") // SPLIT
+    ahead = expert_id - (lax.axis_index("expert") >> 3)
     ahead = jnp.where(ahead < 0, ahead + devices // SPLIT, ahead)
-    return jnp.where(dropped == 1, -1, ahead * slots + slot)
+    place = jnp.where(dropped == 1, -1, ahead * slots + slot)
+    return jnp.stack([place.astype(F32), gate])
 
 
 def chosen(place, first, count):
@@ -79,54 +80,40 @@
     return rows == place
 
 
-def copies(sources, buffers, sem):
-    made = [
-        pltpu.make_async_copy(src, dst, sem.at[i]) for i, (src, dst) in enumerate(zip(sources, buffers))
-    ]
-    for copy in made:
-        copy.start()
-    for copy in made:
-        copy.wait()
-
-
-def place_kernel(slots, scale, *refs):
-    near, far = refs[5:7]
-    expert_id, dropped, slot, gate, values = refs[7:12]
-    copies(refs[:5], refs[7:12], refs[12])
-    place = slot_places(expert_id[...], dropped[...], slot[...], slots)
+def place_kernel(slots, scale, routing, values, near, far):
+    place = routing[0:1, :].astype(jnp.int32)
     rows = values[...]
     if scale:
         count = rows.shape[0]
         across = lax.broadcasted_iota(jnp.int32, (count, count), 1)
         down = lax.broadcasted_iota(jnp.int32, (count, count), 0)
-        column = jnp.sum(jnp.where(across == down, gate[...], 0.0), axis=1, keepdims=True)
+        gates = jnp.where(across == down, routing[1:2, :], 0.0)
+        column = jnp.sum(gates, axis=1, keepdims=True)
         rows = (column * rows.astype(F32)).astype(BF16)
     for first, out in ((0, near), (slots, far)):
         onehot = chosen(place, first, out.shape[0]).astype(F32).astype(BF16)
         out[...] = jnp.dot(onehot, rows, preferred_element_type=F32).astype(BF16)
 
 
-def to_slots(slots, scale, *inputs):
+def to_slots(slots, scale, routing, values):
     experts = lax.axis_size("expert") // SPLIT
-    width = inputs[-1].shape[1]
+    width = values.shape[1]
     return pl.pallas_call(
         functools.partial(place_kernel, slots, scale),
         out_shape=(
             jax.ShapeDtypeStruct((slots, width), BF16),
             jax.ShapeDtypeStruct(((experts - 1) * slots, width), BF16),
         ),
-        in_specs=[pl.BlockSpec(memory_space=pltpu.HBM)] * 5,
+        in_specs=[VMEM] * 2,
         out_specs=(VMEM, VMEM),
-        scratch_shapes=[pltpu.VMEM(x.shape, x.dtype) for x in inputs]
-        + [pltpu.SemaphoreType.DMA((5,))],
         compiler_params=params(),
-        cost_estimate=cost(2 * experts * slots * inputs[-1].size, 6 * inputs[-1].size),
+        cost_estimate=cost(values.size, values.size),
         name="rows_to_slots",
-    )(*inputs)
-
-
-def home_kernel(slots, expert_id, dropped, slot, gate, kept, got, back, token_grad, gate_grad):
-    place = slot_places(expert_id[...], dropped[...], slot[...], slots)
+    )(routing, values)
+
+
+def home_kernel(slots, routing, kept, got, back, token_grad, gate_grad):
+    place = routing[0:1, :].astype(jnp.int32)
     width = token_grad.shape[1]
     near = kept[...].astype(F32) + got[...].astype(F32)
     total = jnp.zeros(token_grad.shape, F32)
@@ -142,22 +129,22 @@
         column = rows[:, width : width + 1]
         gates += jnp.sum(jnp.where(picks, column, 0.0), axis=0, keepdims=True)
     token_grad[...] = total.astype(BF16)
-    gate_grad[...] = jnp.where(dropped[...] == 1, 0.0, gates / gate[...])
-
-
-def to_tokens(slots, expert_id, dropped, slot, gate, kept, got, back):
-    count, width = expert_id.shape[1], kept.shape[1] - LANES
+    gate_grad[...] = jnp.where(place < 0, 0.0, gates / routing[1:2, :])
+
+
+def to_tokens(slots, routing, kept, got, back):
+    count, width = routing.shape[1], kept.shape[1] - LANES
     return pl.pallas_call(
         functools.partial(home_kernel, slots),
         out_shape=(
             jax.ShapeDtypeStruct((count, width), BF16),
             jax.ShapeDtypeStruct((1, count), F32),
         ),
-        in_specs=[VMEM] * 7,
+        in_specs=[VMEM] * 4,
         out_specs=(VMEM, VMEM),
         compiler_params=params(),
         name="slots_to_tokens",
-    )(expert_id, dropped, slot, gate, kept, got, back)
+    )(routing, kept, got, back)
 
 
 def activation_kernel(order, hidden, activated, slope):
@@ -191,7 +178,7 @@
         ),
         out_shape=(jax.ShapeDtypeStruct(shape, BF16), jax.ShapeDtypeStruct(shape, F32)),
         compiler_params=params(),
-        cost_estimate=cost(60 * size, 8 * size, 2 * size),
+        cost_estimate=cost(size, size),
         name="activation",
     )(order, by_source)
     return act.reshape(-1, units), slope.reshape(-1, units)
@@ -209,6 +196,16 @@
 def add_halves(kept, got):
     kept, got = halves(kept), halves(got)
     return add(kept[0], got[0]), add(kept[1], got[1])
+
+
+def split_slots(rows, experts):
+    rows = rows.reshape(experts - 1, 2, -1, rows.shape[1])
+    return [rows[:, i].reshape(-1, rows.shape[3]) for i in range(2)]
+
+
+def join_slots(a, b, experts):
+    a, b = [x.reshape(experts - 1, -1, x.shape[1]) for x in (a, b)]
+    return jnp.concatenate([a, b], axis=1).reshape(-1, a.shape[2])
 
 
 def product(a, b, dims):
@@ -233,73 +230,79 @@
     slots = saved_hidden.shape[0] // devices
     units = saved_hidden.shape[1]
     me = lax.axis_index("expert")
-    row = lambda x: x.reshape(1, -1)
-    routing = (row(expert_id), row(dropped), row(slot), row(gate))
+    routing = pack_routing(expert_id, dropped, slot, gate, slots)
     near_order, far_order = sources_met(me, experts)
     by_source = saved_hidden.reshape(devices, slots, units)
     join = jnp.concatenate
 
-    near_grad, far_grad = to_slots(slots, True, *routing, out_grad)
-    near_row, far_row = to_slots(slots, False, *routing, tokens)
-
-    far_grad = cross(far_grad, 1)
+    near_grad, far_grad = to_slots(slots, True, routing, out_grad)
+    near_row, far_row = to_slots(slots, False, routing, tokens)
+
+    far_grad_a, far_grad_b = split_slots(far_grad, experts)
+    far_grad_a = cross(far_grad_a, 1)
     got = meet(near_grad, 0)
     near_act, near_slope = activation(by_source, near_order)
-    got = after(got, near_act, near_row)
+    far_grad_a = after(far_grad_a, near_act, near_row)
+    far_grad_b = cross(after(far_grad_b, far_grad_a), 1)
+    got = after(got, far_grad_a)
     near_two = join([near_grad, got])
     near_more = meet(near_two, 1)
+    near_last = meet(near_two, 2)
+    near_row_got = meet(after(near_row, near_two), 0)
     far_act, far_slope = activation(by_source, after(far_order, near_two))
-    near_more = after(near_more, far_act)
-    near_last = meet(near_two, 2), meet(near_more, 2)
-
-    far_grad = after(far_grad, near_more)
-    got = meet(far_grad, 0)
+    far_grad = join_slots(far_grad_a, after(far_grad_b, far_act), experts)
+    far_got = meet(far_grad, 0)
+    far_row_a, far_row_b = split_slots(far_row, experts)
+    far_row_a = cross(after(far_row_a, far_grad), 1)
+    near_more = after(near_more, far_grad)
+    near_last = near_last, meet(near_more, 2)
+    near_row2 = join([near_row, after(near_row_got, near_more)])
+    near_row4 = meet(near_row2, 1)
+
     near_grads = join([near_two, near_more, *near_last])
+    near_grads = after(near_grads, near_row2)
     near_hg, near_gates = hidden_part(near_grads, w_out, near_act, near_slope)
-    got = after(got, near_hg)
-    far_two = join([far_grad, got])
+    far_two = join([far_grad, after(far_got, near_hg)])
     far_more = meet(far_two, 1)
+    far_last = meet(far_two, 2)
     near_kept, near_sent = slot_part(after(near_hg, far_two), near_gates, w_in)
-    far_more = after(far_more, near_sent)
-    far_last = meet(far_two, 2), meet(far_more, 2)
     near_got = meet(near_sent, 2)
-
-    near_row, far_row = after(near_row, far_more), after(far_row, far_more)
-    far_row = cross(far_row, 1)
-    got = meet(near_row, 0)
+    far_row_a = after(far_row_a, near_sent)
+    far_more = after(far_more, far_row_a)
+    far_last = far_last, meet(far_more, 2)
+    far_row_b = cross(after(far_row_b, far_row_a), 1)
+    near_row4 = after(near_row4, far_more)
+    near_rows = join([near_row2, near_row4, meet(near_row2, 2), meet(near_row4, 2)])
+    near_kept, near_sent = add_halves(near_kept, after(near_got, far_row_a))
+    near_got = meet(near_sent, 1)
+
     far_grads = join([far_two, far_more, *far_last])
+    far_grads = after(far_grads, near_sent)
     far_hg, far_gates = hidden_part(far_grads, w_out, far_act, far_slope)
-    got = after(got, far_hg)
-    near_row2 = join([near_row, got])
-    near_row4 = meet(near_row2, 1)
-    far_kept, far_sent = slot_part(after(far_hg, near_row2), far_gates, w_in)
-
-    far_got = meet(far_sent, 2)
-    far_kept, far_sent = add_halves(far_kept, far_got)
+    far_kept, far_sent = slot_part(far_hg, far_gates, w_in)
+    far_kept, far_sent = add_halves(far_kept, meet(far_sent, 2))
     far_got = meet(far_sent, 1)
+    far_row = join_slots(far_row_a, after(far_row_b, far_sent), experts)
+    far_row_got = meet(far_row, 0)
+    near_act, near_grads = after(near_act, far_row), after(near_grads, far_row)
+    w_out_grad = product(
+        join([near_act, far_act]), join([near_grads, far_grads]), ((0,), (0,))
+    ).astype(BF16)
+    far_row2 = join([far_row, after(far_row_got, w_out_grad)])
+    far_row4 = meet(far_row2, 1)
+    far_kept, far_sent = add_halves(far_kept, after(far_got, far_row2))
+    far_got = meet(far_sent, 0)
     near_kept, near_sent = add_halves(near_kept, after(near_got, far_sent))
-    near_got = meet(near_sent, 1)
-    act = join([near_act, far_act])
-    w_out_grad = product(after(act, far_sent), join([near_grads, far_grads]), ((0,), (0,))).astype(BF16)
-    far_row_got = meet(far_row, 0)
-    far_got = after(far_got, w_out_grad, far_row)
-    far_kept, far_sent = add_halves(far_kept, far_got)
-    far_got = meet(far_sent, 0)
-    near_row4 = after(near_row4, far_sent)
-    near_rows = join([near_row2, near_row4, meet(near_row2, 2), meet(near_row4, 2)])
-    far_row2 = join([far_row, far_row_got])
-    far_row4 = meet(far_row2, 1)
-    far_got = after(far_got, far_row2, near_row4)
-    far_sum = add(far_kept, far_got)
+    near_got = meet(near_sent, 0)
+    far_sum = add(far_kept, after(far_got, near_sent))
     back = cross(far_sum, -1)
-    near_kept, near_sent = add_halves(near_kept, after(near_got, far_sum))
-    near_got = meet(near_sent, 0)
+    far_row4 = after(far_row4, far_sum)
     far_rows = join([far_row2, far_row4, meet(far_row2, 2), meet(far_row4, 2)])
     w_in_grad = product(
         join([near_rows, far_rows]), join([near_hg, far_hg]), ((0,), (0,))
     ).astype(BF16)
-    back = after(back, w_in_grad)
-    token_grad, gate_grad = to_tokens(slots, *routing, near_kept, near_got, back)
+    near_got, back = after(near_got, w_in_grad), after(back, w_in_grad)
+    token_grad, gate_grad = to_tokens(slots, routing, near_kept, near_got, back)
     return (token_grad, gate_grad.reshape(-1), w_in_grad, w_out_grad)
 
 

time: 117 us -> 102 us (0.87)
  waiting for transfers between devices: 52.2 us -> 41.4 us
  local copies, waits for them, and re-layouts: 14.3 us -> 9.54 us
  starting transfers between devices: 25.3 us -> 21.7 us
  matrix products: 16.3 us -> 19.6 us
  other arithmetic: 1.15 us -> 2.68 us
    ppermute x22, waiting for transfers between devices: 37.5 us -> 29.1 us  [meet(): lax.ppermute(rows, 'expert', [(i, i ^ bits(i % 2)[step]) for i in range(d...]
    unnamed x56 -> x28, local copies, waits for them, and re-layouts: 13.9 us -> 7.61 us
    ppermute x22, starting transfers between devices: 19.8 us -> 14.8 us  [meet(): lax.ppermute(rows, 'expert', [(i, i ^ bits(i % 2)[step]) for i in range(d...]
    dot_general x6, matrix products: 16.3 us -> 19.6 us  [product(): return lax.dot_general(a, b, (dims, ((), ())), preferred_element_type=F32)]
    ppermute x3 -> x5, waiting for transfers between devices: 14.7 us -> 12.3 us  [shift(): return lax.ppermute(rows, 'expert', pairs)]
    another operation x0 -> x2, other arithmetic: none -> 1.51 us  [pack_routing(): return jnp.stack([place.astype(F32), gate])]
    concatenate x1 -> x3, local copies, waits for them, and re-layouts: 0.07 us -> 1.57 us  [the longest x1 0.81 us: body(): near_grads = join([near_two, near_more, *near_last])]
    ppermute x3 -> x5, starting transfers between devices: 5.45 us -> 6.89 us  [shift(): return lax.ppermute(rows, 'expert', pairs)]
  transfers between devices with their start and end apart: 25 -> 27, of which waited for: 12 -> 13; matrix products, arithmetic and copies ran while one was open for 17% -> 26% of each run, Pallas kernels for 4% -> 4%
where the time goes in v5:
time: 102 us
  waiting for transfers between devices  41.4 us (41%)
  starting transfers between devices  21.7 us (21%)
  matrix products  19.6 us (19%)
  local copies, waits for them, and re-layouts  9.54 us (9%)
  Pallas kernels  5.69 us (6%)
  other arithmetic  2.68 us (3%)
    ppermute x22, waiting for transfers between devices, meet(): lax.ppermute(rows, 'expert', [(i, i ^ bits(i % 2)[step]) for i in range(d...  29.1 us
    dot_general x6, matrix products, product(): return lax.dot_general(a, b, (dims, ((), ())), preferred_element_type=F32)  19.6 us
    ppermute x22, starting transfers between devices, meet(): lax.ppermute(rows, 'expert', [(i, i ^ bits(i % 2)[step]) for i in range(d...  14.8 us
    ppermute x5, waiting for transfers between devices, shift(): return lax.ppermute(rows, 'expert', pairs)  12.3 us
    unnamed x28, local copies, waits for them, and re-layouts  7.61 us
    ppermute x5, starting transfers between devices, shift(): return lax.ppermute(rows, 'expert', pairs)  6.89 us
    pallas_call x2, Pallas kernels, activation(): pl.pallas_call(activation_kernel, grid_spec=pltpu.PrefetchScalarGridSpec(...  3.89 us
  transfers between devices with their start and end apart: 27, of which 13 were waited for; matrix products, arithmetic and copies ran while one was open for 26% of the time, Pallas kernels for 4%

profile of v5, /device:TPU:0, one launch (start us, length us, event | category | flops | bytes accessed | tf_op | source)
XLA Modules:
  0.0 101.6 jit_solution(13434559502286694550)
XLA Ops:
  0.7 0.8 fusion.18
  1.5 0.7 pad_maximum_fusion.4.routing
  2.2 1.0 copy-done.3
  3.2 0.4 rows_to_slots.2
  3.5 3.1 %collective-permute-start = (bf16[80,1536]{1,0:T(8,128)(2,1)S(1)}, bf16[80,1536]{1,0:T(8,128)(2,1)S(1)}, u32[]{:S(2)}, u32[]{:S(2)}) collective-permute-start(bf16[80,1536]{1,0:T(8,128)(2,1)S(1)} %get-tuple-element.42), channel_id=1, source_target_pairs={{0,4},{1,3},{2,6},{3,1},{4,0},{5,7},{6,2},{7,5},{8,12},{9,11},{10,... | collective-permute-start | bytes 737288 | tf_op jit(solution)/shard_map/ppermute | solution.py:31
  6.6 2.7 %collective-permute-start.1 = (bf16[40,1536]{1,0:T(8,128)(2,1)S(1)}, bf16[40,1536]{1,0:T(8,128)(2,1)S(1)}, u32[]{:S(2)}, u32[]{:S(2)}) collective-permute-start(bf16[40,1536]{1,0:T(8,128)(2,1)S(1)} %get-tuple-element.97), channel_id=1, source_target_pairs={{0,8},{1,9},{2,10},{3,11},{4,12},{5,13},{6,14},{7,15},{8,0},{9,1},... | collective-permute-start | bytes 368648 | tf_op jit(solution)/shard_map/ppermute | solution.py:37
  9.3 1.0 copy-done.4
  10.3 0.3 rows_to_slots.3
  10.6 1.5 %copy-done.1 = bf16[1280,768]{1,0:T(8,128)(2,1)S(1)} copy-done((bf16[1280,768]{1,0:T(8,128)(2,1)S(1)}, bf16[1280,768]{1,0:T(8,128)(2,1)}, u32[]{:S(2)}) %copy-start.1) | copy-done | bytes 1966104
  12.2 1.9 %activation.2 = (bf16[8,80,768]{2,1,0:T(8,128)(2,1)S(1)}, f32[8,80,768]{2,1,0:T(8,128)S(1)}) custom-call(s32[8]{0:T(128)S(1)} %get-tuple-element.103.order, bf16[16,80,768]{2,1,0:T(8,128)(2,1)S(1)} %bitcast.48), custom_call_target="tpu_custom_call" | custom-call | flops 491520 | bytes 491520 | tf_op jit(solution)/shard_map/activation/pallas_call | solution.py:171
  14.1 0.7 constant_dynamic-update-slice_fusion.1
  14.8 0.7 constant_dynamic-update-slice_fusion
  15.6 1.5 %collective-permute-start.2 = (bf16[160,1536]{1,0:T(8,128)(2,1)S(1)}, bf16[160,1536]{1,0:T(8,128)(2,1)S(1)}, u32[]{:S(2)}, u32[]{:S(2)}) collective-permute-start(bf16[160,1536]{1,0:T(8,128)(2,1)S(1)} %get-tuple-element.98), channel_id=1, source_target_pairs={{0,2},{1,5},{2,0},{3,7},{4,6},{5,1},{6,4},{7,3},{8,10},{9,13},{10,... | collective-permute-start | bytes 1474568 | tf_op jit(solution)/shard_map/ppermute | solution.py:31
  17.1 1.7 %collective-permute-start.3 = (bf16[40,1536]{1,0:T(8,128)(2,1)S(1)}, bf16[40,1536]{1,0:T(8,128)(2,1)S(1)}, u32[]{:S(2)}, u32[]{:S(2)}) collective-permute-start(bf16[40,1536]{1,0:T(8,128)(2,1)S(1)} %get-tuple-element.48), channel_id=1, source_target_pairs={{0,8},{1,9},{2,10},{3,11},{4,12},{5,13},{6,14},{7,15},{8,0},{9,1},... | collective-permute-start | bytes 368648 | tf_op jit(solution)/shard_map/ppermute | solution.py:37
  18.8 0.7 constant_dynamic-update-slice_fusion.23
  19.5 0.5 collective-permute-start.4
  20.0 1.9 %activation.3 = (bf16[8,80,768]{2,1,0:T(8,128)(2,1)S(1)}, f32[8,80,768]{2,1,0:T(8,128)S(1)}) custom-call(s32[8]{0:T(128)S(1)} %get-tuple-element.49.order, bf16[16,80,768]{2,1,0:T(8,128)(2,1)S(1)} %bitcast.49), custom_call_target="tpu_custom_call" | custom-call | flops 491520 | bytes 491520 | tf_op jit(solution)/shard_map/activation/pallas_call | solution.py:171
  22.0 2.4 %collective-permute-done.3 = bf16[40,1536]{1,0:T(8,128)(2,1)S(1)} collective-permute-done((bf16[40,1536]{1,0:T(8,128)(2,1)S(1)}, bf16[40,1536]{1,0:T(8,128)(2,1)S(1)}, u32[]{:S(2)}, u32[]{:S(2)}) %collective-permute-start.3) | collective-permute-done | bytes 122912 | tf_op jit(solution)/shard_map/ppermute | solution.py:37
  24.4 0.7 collective-permute-start.6
  25.1 1.4 %collective-permute-start.7 = (bf16[80,1536]{1,0:T(8,128)(2,1)S(1)}, bf16[80,1536]{1,0:T(8,128)(2,1)S(1)}, u32[]{:S(2)}, u32[]{:S(2)}) collective-permute-start(bf16[80,1536]{1,0:T(8,128)(2,1)S(1)} %maximum_bitcast_fusion), channel_id=1, source_target_pairs={{0,4},{1,3},{2,6},{3,1},{4,0},{5,7},{6,2},{7,5},{8,12},{9,11},{10,... | collective-permute-start | bytes 737288 | tf_op jit(solution)/shard_map/ppermute | solution.py:31
  26.5 1.6 %collective-permute-start.9 = (bf16[40,1536]{1,0:T(8,128)(2,1)S(1)}, bf16[40,1536]{1,0:T(8,128)(2,1)S(1)}, u32[]{:S(2)}, u32[]{:S(2)}) collective-permute-start(bf16[40,1536]{1,0:T(8,128)(2,1)S(1)} %get-tuple-element.60), channel_id=1, source_target_pairs={{0,8},{1,9},{2,10},{3,11},{4,12},{5,13},{6,14},{7,15},{8,0},{9,1},... | collective-permute-start | bytes 368648 | tf_op jit(solution)/shard_map/ppermute | solution.py:37
  28.1 0.8 collective-permute-start.5
  28.9 0.8 constant_dynamic-update-slice_fusion.4
  29.7 3.5 %collective-permute-done.6 = bf16[80,1536]{1,0:T(8,128)(2,1)S(1)} collective-permute-done((bf16[80,1536]{1,0:T(8,128)(2,1)S(1)}, bf16[80,1536]{1,0:T(8,128)(2,1)S(1)}, u32[]{:S(2)}, u32[]{:S(2)}) %collective-permute-start.6) | collective-permute-done | bytes 245792 | tf_op jit(solution)/shard_map/ppermute | solution.py:31
  33.2 0.7 constant_dynamic-update-slice_fusion.22
  33.9 0.8 constant_dynamic-update-slice_fusion.3
  34.7 0.8 constant_dynamic-update-slice_fusion.2
  35.5 3.4 %fusion.14 = (bf16[640,768]{1,0:T(8,128)(2,1)S(1)}, bf16[640]{0:T(1024)(128)(2,1)S(1)}) fusion(f32[8,80,768]{2,1,0:T(8,128)S(1)} %get-tuple-element.56, bf16[8,80,768]{2,1,0:T(8,128)(2,1)S(1)} %get-tuple-element.44, bf16[640,1536]{1,0:T(8,128)(2,1)} %constant_dynamic-update-slice_fusion.2, bf16[768,1536]{1,0:T(8,128)(2,1)S(1)} %copy-done.6), kind=kOutput, calls=%fused_computation.21 | convolution fusion | flops 1512406400 | bytes 8258816 | tf_op jit(solution)/shard_map/dot_general | solution.py:212
  39.1 0.2 collective-permute-start.12
  39.3 1.7 %convolution_convert_fusion.2 = bf16[640,1536]{1,0:T(8,128)(2,1)S(1)} fusion(bf16[640,768]{1,0:T(8,128)(2,1)S(1)} %get-tuple-element.58, bf16[1536,768]{1,0:T(8,128)(2,1)S(1)} %copy-done), kind=kOutput, calls=%fused_computation.7 | convolution fusion | flops 1510932480 | bytes 5308416 | tf_op jit(solution)/shard_map/dot_general | solution.py:212
  41.0 0.1 broadcast_in_dim.26
  41.1 0.1 fusion.16
  41.2 0.4 collective-permute-start.8
  41.7 2.0 %collective-permute-start.19 = (bf16[160,1536]{1,0:T(8,128)(2,1)S(1)}, bf16[160,1536]{1,0:T(8,128)(2,1)S(1)}, u32[]{:S(2)}, u32[]{:S(2)}) collective-permute-start(bf16[160,1536]{1,0:T(8,128)(2,1)S(1)} %get-tuple-element.91), channel_id=1, source_target_pairs={{0,2},{1,5},{2,0},{3,7},{4,6},{5,1},{6,4},{7,3},{8,10},{9,13},{10,... | collective-permute-start | bytes 1474568 | tf_op jit(solution)/shard_map/ppermute | solution.py:31
  43.7 4.2 %collective-permute-done.11 = bf16[160,1536]{1,0:T(8,128)(2,1)S(1)} collective-permute-done((bf16[160,1536]{1,0:T(8,128)(2,1)S(1)}, bf16[160,1536]{1,0:T(8,128)(2,1)S(1)}, u32[]{:S(2)}, u32[]{:S(2)}) %collective-permute-start.11) | collective-permute-done | bytes 491552 | tf_op jit(solution)/shard_map/ppermute | solution.py:31
  48.0 1.7 %collective-permute-done.13 = bf16[160,1536]{1,0:T(8,128)(2,1)S(1)} collective-permute-done((bf16[160,1536]{1,0:T(8,128)(2,1)S(1)}, bf16[160,1536]{1,0:T(8,128)(2,1)S(1)}, u32[]{:S(2)}, u32[]{:S(2)}) %collective-permute-start.13) | collective-permute-done | bytes 491552 | tf_op jit(solution)/shard_map/ppermute | solution.py:31
  49.8 0.3 add_convert_fusion.2
  50.1 1.9 %multiply_reduce_fusion = (bf16[640]{0:T(1024)(128)(2,1)S(1)}, bf16[640,768]{1,0:T(8,128)(2,1)S(1)}) fusion(bf16[8,80,768]{2,1,0:T(8,128)(2,1)S(1)} %get-tuple-element.50, f32[8,80,768]{2,1,0:T(8,128)S(1)} %get-tuple-element.65, bf16[640,1536]{1,0:T(8,128)(2,1)S(1)} %constant_dynamic-update-slice_fusion.9, bf16[768,1536]{1,0:T(8,128)(2,1)S(1)} %copy-done.6), kind=kOutput, calls=%fused_computation.22 | convolution fusion | flops 1512406400 | bytes 8258816 | tf_op jit(solution)/shard_map/dot_general | solution.py:212
  52.0 1.7 %convolution_convert_fusion.1 = bf16[640,1536]{1,0:T(8,128)(2,1)S(1)} fusion(bf16[640,768]{1,0:T(8,128)(2,1)S(1)} %get-tuple-element.85, bf16[1536,768]{1,0:T(8,128)(2,1)S(1)} %copy-done), kind=kOutput, calls=%fused_computation.6 | convolution fusion | flops 1510932480 | bytes 5308416 | tf_op jit(solution)/shard_map/dot_general | solution.py:212
  53.7 0.1 broadcast_in_dim.27
  53.8 0.1 fusion.15
  53.9 0.2 collective-permute-start.14
  54.1 0.4 collective-permute-start.20
  54.5 0.1 collective-permute-start.21
  54.7 2.7 %collective-permute-done.20 = bf16[160,1536]{1,0:T(8,128)(2,1)S(1)} collective-permute-done((bf16[160,1536]{1,0:T(8,128)(2,1)S(1)}, bf16[160,1536]{1,0:T(8,128)(2,1)S(1)}, u32[]{:S(2)}, u32[]{:S(2)}) %collective-permute-start.20) | collective-permute-done | bytes 491552 | tf_op jit(solution)/shard_map/ppermute | solution.py:31
  57.4 0.7 collective-permute-done.21
  58.1 0.1 collective-permute-start.10
  58.2 0.3 add_convert_fusion
  58.5 2.1 %collective-permute-start.15 = (bf16[160,1664]{1,0:T(8,128)(2,1)S(1)}, bf16[160,1664]{1,0:T(8,128)(2,1)S(1)}, u32[]{:S(2)}, u32[]{:S(2)}) collective-permute-start(bf16[160,1664]{1,0:T(8,128)(2,1)S(1)} %get-tuple-element.80), channel_id=1, source_target_pairs={{0,2},{1,5},{2,0},{3,7},{4,6},{5,1},{6,4},{7,3},{8,10},{9,13},{10,... | collective-permute-start | bytes 1597448 | tf_op jit(solution)/shard_map/ppermute | solution.py:31
  60.6 2.3 %collective-permute-done.16 = bf16[40,1536]{1,0:T(8,128)(2,1)S(1)} collective-permute-done((bf16[40,1536]{1,0:T(8,128)(2,1)S(1)}, bf16[40,1536]{1,0:T(8,128)(2,1)S(1)}, u32[]{:S(2)}, u32[]{:S(2)}) %collective-permute-start.16) | collective-permute-done | bytes 122912 | tf_op jit(solution)/shard_map/ppermute | solution.py:37
  63.0 6.3 %fusion.4 = bf16[768,1536]{1,0:T(8,128)(2,1)} fusion(bf16[640,1536]{1,0:T(8,128)(2,1)S(1)} %constant_dynamic-update-slice_fusion.9, bf16[640,1536]{1,0:T(8,128)(2,1)} %constant_dynamic-update-slice_fusion.2, bf16[640,768]{1,0:T(8,128)(2,1)S(1)} %bitcast.53, bf16[640,768]{1,0:T(8,128)(2,1)S(1)} %bitcast.52), kind=kOutput, calls=%fused_computation.4 | convolution fusion | flops 3032875008 | bytes 8257536 | tf_op jit(solution)/shard_map/dot_general | solution.py:212
  69.3 2.6 %collective-permute-done.17 = bf16[80,1536]{1,0:T(8,128)(2,1)S(1)} collective-permute-done((bf16[80,1536]{1,0:T(8,128)(2,1)S(1)}, bf16[80,1536]{1,0:T(8,128)(2,1)S(1)}, u32[]{:S(2)}, u32[]{:S(2)}) %collective-permute-start.17) | collective-permute-done | bytes 245792 | tf_op jit(solution)/shard_map/ppermute | solution.py:31
  71.9 0.9 collective-permute-start.22
  72.8 3.0 %collective-permute-done.15 = bf16[160,1664]{1,0:T(8,128)(2,1)S(1)} collective-permute-done((bf16[160,1664]{1,0:T(8,128)(2,1)S(1)}, bf16[160,1664]{1,0:T(8,128)(2,1)S(1)}, u32[]{:S(2)}, u32[]{:S(2)}) %collective-permute-start.15) | collective-permute-done | bytes 532512 | tf_op jit(solution)/shard_map/ppermute | solution.py:31
  75.8 0.1 add_convert_fusion.8
  76.0 0.1 add_convert_fusion.6
  76.1 8.9 %collective-permute-done.23 = bf16[80,1664]{1,0:T(8,128)(2,1)S(1)} collective-permute-done((bf16[80,1664]{1,0:T(8,128)(2,1)S(1)}, bf16[80,1664]{1,0:T(8,128)(2,1)S(1)}, u32[]{:S(2)}, u32[]{:S(2)}) %collective-permute-start.23) | collective-permute-done | bytes 266272 | tf_op jit(solution)/shard_map/ppermute | solution.py:31
  85.0 0.1 add_convert_fusion.4
  85.3 1.0 collective-permute-start.26
  86.3 0.7 collective-permute-done.25
  87.1 4.6 %convolution_convert_fusion = bf16[1536,768]{1,0:T(8,128)(2,1)} fusion(bf16[1280,1536]{1,0:T(8,128)(2,1)S(1)} %constant_dynamic-update-slice_fusion.14, bf16[640,768]{1,0:T(8,128)(2,1)S(1)} %get-tuple-element.85, bf16[640,768]{1,0:T(8,128)(2,1)S(1)} %get-tuple-element.58), kind=kOutput, calls=%fused_computation.5 | convolution fusion | flops 3025010688 | bytes 8257536 | tf_op jit(solution)/shard_map/dot_general | solution.py:212
  91.6 1.2 %collective-permute-done.18.got = bf16[80,1664]{1,0:T(8,128)(2,1)S(1)} collective-permute-done((bf16[80,1664]{1,0:T(8,128)(2,1)S(1)}, bf16[80,1664]{1,0:T(8,128)(2,1)S(1)}, u32[]{:S(2)}, u32[]{:S(2)}) %collective-permute-start.18) | collective-permute-done | bytes 266272 | tf_op jit(solution)/shard_map/ppermute | solution.py:31
  92.8 7.6 %collective-permute-done.26.back = bf16[80,1664]{1,0:T(8,128)(2,1)S(1)} collective-permute-done((bf16[80,1664]{1,0:T(8,128)(2,1)S(1)}, bf16[80,1664]{1,0:T(8,128)(2,1)S(1)}, u32[]{:S(2)}, u32[]{:S(2)}) %collective-permute-start.26) | collective-permute-done | bytes 266272 | tf_op jit(solution)/shard_map/ppermute | solution.py:37
  100.4 1.2 %slots_to_tokens.1 = (bf16[128,1536]{1,0:T(8,128)(2,1)}, f32[1,128]{1,0:T(1,128)}) custom-call(f32[2,128]{1,0:T(2,128)S(1)} %pad_maximum_fusion.4.routing, bf16[80,1664]{1,0:T(8,128)(2,1)S(1)} %get-tuple-element.89.kept, bf16[80,1664]{1,0:T(8,128)(2,1)S(1)} %collective-permute-done.18.got, bf16[80,1664]{1,0:T(8,128)(2,1)S(1)} %collective-permute-done.26.back), custom_call_target="tpu_custom_call" | custom-call | tf_op jit(solution)/shard_map/slots_to_tokens/pallas_call | solution.py:137
  (53 shorter events, 1.0 us)
Async XLA Ops:
  0.6 38.6 %copy-start = (bf16[1536,768]{1,0:T(8,128)(2,1)S(1)}, bf16[1536,768]{1,0:T(8,128)(2,1)}, u32[]{:S(2)}) copy-start(bf16[1536,768]{1,0:T(8,128)(2,1)} %param.16) | copy-start | bytes 7077892
  2.2 1.0 copy-start.3
  3.5 11.3 %collective-permute-start = (bf16[80,1536]{1,0:T(8,128)(2,1)S(1)}, bf16[80,1536]{1,0:T(8,128)(2,1)S(1)}, u32[]{:S(2)}, u32[]{:S(2)}) collective-permute-start(bf16[80,1536]{1,0:T(8,128)(2,1)S(1)} %get-tuple-element.42), channel_id=1, source_target_pairs={{0,4},{1,3},{2,6},{3,1},{4,0},{5,7},{6,2},{7,5},{8,12},{9,11},{10,... | collective-permute-start | bytes 737288 | tf_op jit(solution)/shard_map/ppermute | solution.py:31
  6.6 8.2 %collective-permute-start.1 = (bf16[40,1536]{1,0:T(8,128)(2,1)S(1)}, bf16[40,1536]{1,0:T(8,128)(2,1)S(1)}, u32[]{:S(2)}, u32[]{:S(2)}) collective-permute-start(bf16[40,1536]{1,0:T(8,128)(2,1)S(1)} %get-tuple-element.97), channel_id=1, source_target_pairs={{0,8},{1,9},{2,10},{3,11},{4,12},{5,13},{6,14},{7,15},{8,0},{9,1},... | collective-permute-start | bytes 368648 | tf_op jit(solution)/shard_map/ppermute | solution.py:37
  9.3 1.0 copy-start.4
  10.6 1.5 %copy-start.1 = (bf16[1280,768]{1,0:T(8,128)(2,1)S(1)}, bf16[1280,768]{1,0:T(8,128)(2,1)}, u32[]{:S(2)}) copy-start(bf16[1280,768]{1,0:T(8,128)(2,1)} %param.15) | copy-start | bytes 5898244
  12.1 7.9 %copy-start.2 = (bf16[1280,768]{1,0:T(8,128)(2,1)S(1)}, bf16[1280,768]{1,0:T(8,128)(2,1)}, u32[]{:S(2)}) copy-start(bf16[1280,768]{1,0:T(8,128)(2,1)} %param.15) | copy-start | bytes 5898244
  15.6 12.5 %collective-permute-start.2 = (bf16[160,1536]{1,0:T(8,128)(2,1)S(1)}, bf16[160,1536]{1,0:T(8,128)(2,1)S(1)}, u32[]{:S(2)}, u32[]{:S(2)}) collective-permute-start(bf16[160,1536]{1,0:T(8,128)(2,1)S(1)} %get-tuple-element.98), channel_id=1, source_target_pairs={{0,2},{1,5},{2,0},{3,7},{4,6},{5,1},{6,4},{7,3},{8,10},{9,13},{10,... | collective-permute-start | bytes 1474568 | tf_op jit(solution)/shard_map/ppermute | solution.py:31
  17.1 7.3 %collective-permute-start.3 = (bf16[40,1536]{1,0:T(8,128)(2,1)S(1)}, bf16[40,1536]{1,0:T(8,128)(2,1)S(1)}, u32[]{:S(2)}, u32[]{:S(2)}) collective-permute-start(bf16[40,1536]{1,0:T(8,128)(2,1)S(1)} %get-tuple-element.48), channel_id=1, source_target_pairs={{0,8},{1,9},{2,10},{3,11},{4,12},{5,13},{6,14},{7,15},{8,0},{9,1},... | collective-permute-start | bytes 368648 | tf_op jit(solution)/shard_map/ppermute | solution.py:37
  19.5 14.4 %collective-permute-start.4 = (bf16[160,1536]{1,0:T(8,128)(2,1)S(1)}, bf16[160,1536]{1,0:T(8,128)(2,1)S(1)}, u32[]{:S(2)}, u32[]{:S(2)}) collective-permute-start(bf16[160,1536]{1,0:T(8,128)(2,1)S(1)} %get-tuple-element.98), channel_id=1, source_target_pairs={{0,1},{1,0},{2,3},{3,2},{4,5},{5,4},{6,7},{7,6},{8,9},{9,8},{10,11... | collective-permute-start | bytes 1474568 | tf_op jit(solution)/shard_map/ppermute | solution.py:31
  24.4 8.8 %collective-permute-start.6 = (bf16[80,1536]{1,0:T(8,128)(2,1)S(1)}, bf16[80,1536]{1,0:T(8,128)(2,1)S(1)}, u32[]{:S(2)}, u32[]{:S(2)}) collective-permute-start(bf16[80,1536]{1,0:T(8,128)(2,1)S(1)} %get-tuple-element.53), channel_id=1, source_target_pairs={{0,4},{1,3},{2,6},{3,1},{4,0},{5,7},{6,2},{7,5},{8,12},{9,11},{10,... | collective-permute-start | bytes 737288 | tf_op jit(solution)/shard_map/ppermute | solution.py:31
  25.0 10.5 %copy-start.6 = (bf16[768,1536]{1,0:T(8,128)(2,1)S(1)}, bf16[768,1536]{1,0:T(8,128)(2,1)}, u32[]{:S(2)}) copy-start(bf16[768,1536]{1,0:T(8,128)(2,1)} %param.17) | copy-start | bytes 7077892
  25.1 13.9 %collective-permute-start.7 = (bf16[80,1536]{1,0:T(8,128)(2,1)S(1)}, bf16[80,1536]{1,0:T(8,128)(2,1)S(1)}, u32[]{:S(2)}, u32[]{:S(2)}) collective-permute-start(bf16[80,1536]{1,0:T(8,128)(2,1)S(1)} %maximum_bitcast_fusion), channel_id=1, source_target_pairs={{0,4},{1,3},{2,6},{3,1},{4,0},{5,7},{6,2},{7,5},{8,12},{9,11},{10,... | collective-permute-start | bytes 737288 | tf_op jit(solution)/shard_map/ppermute | solution.py:31
  26.5 17.2 %collective-permute-start.9 = (bf16[40,1536]{1,0:T(8,128)(2,1)S(1)}, bf16[40,1536]{1,0:T(8,128)(2,1)S(1)}, u32[]{:S(2)}, u32[]{:S(2)}) collective-permute-start(bf16[40,1536]{1,0:T(8,128)(2,1)S(1)} %get-tuple-element.60), channel_id=1, source_target_pairs={{0,8},{1,9},{2,10},{3,11},{4,12},{5,13},{6,14},{7,15},{8,0},{9,1},... | collective-permute-start | bytes 368648 | tf_op jit(solution)/shard_map/ppermute | solution.py:37
  28.1 6.7 %collective-permute-start.5 = (bf16[160,1536]{1,0:T(8,128)(2,1)S(1)}, bf16[160,1536]{1,0:T(8,128)(2,1)S(1)}, u32[]{:S(2)}, u32[]{:S(2)}) collective-permute-start(bf16[160,1536]{1,0:T(8,128)(2,1)S(1)} %collective-permute-done.2), channel_id=1, source_target_pairs={{0,1},{1,0},{2,3},{3,2},{4,5},{5,4},{6,7},{7,6},{8,9},{9,8},{10,11... | collective-permute-start | bytes 1474568 | tf_op jit(solution)/shard_map/ppermute | solution.py:31
  39.0 8.9 %collective-permute-start.11 = (bf16[160,1536]{1,0:T(8,128)(2,1)S(1)}, bf16[160,1536]{1,0:T(8,128)(2,1)S(1)}, u32[]{:S(2)}, u32[]{:S(2)}) collective-permute-start(bf16[160,1536]{1,0:T(8,128)(2,1)S(1)} %pad_maximum_fusion.2), channel_id=1, source_target_pairs={{0,2},{1,5},{2,0},{3,7},{4,6},{5,1},{6,4},{7,3},{8,10},{9,13},{10,... | collective-permute-start | bytes 1474568 | tf_op jit(solution)/shard_map/ppermute | solution.py:31
  39.1 8.9 %collective-permute-start.12 = (bf16[160,1536]{1,0:T(8,128)(2,1)S(1)}, bf16[160,1536]{1,0:T(8,128)(2,1)S(1)}, u32[]{:S(2)}, u32[]{:S(2)}) collective-permute-start(bf16[160,1536]{1,0:T(8,128)(2,1)S(1)} %pad_maximum_fusion.2), channel_id=1, source_target_pairs={{0,1},{1,0},{2,3},{3,2},{4,5},{5,4},{6,7},{7,6},{8,9},{9,8},{10,11... | collective-permute-start | bytes 1474568 | tf_op jit(solution)/shard_map/ppermute | solution.py:31
  41.2 8.5 %collective-permute-start.8 = (bf16[320,1664]{1,0:T(8,128)(2,1)S(1)}, bf16[320,1664]{1,0:T(8,128)(2,1)S(1)}, u32[]{:S(2)}, u32[]{:S(2)}) collective-permute-start(bf16[320,1664]{1,0:T(8,128)(2,1)S(1)} %fusion.16), channel_id=1, source_target_pairs={{0,1},{1,0},{2,3},{3,2},{4,5},{5,4},{6,7},{7,6},{8,9},{9,8},{10,11... | collective-permute-start | bytes 3194888 | tf_op jit(solution)/shard_map/ppermute | solution.py:31
  41.7 12.8 %collective-permute-start.19 = (bf16[160,1536]{1,0:T(8,128)(2,1)S(1)}, bf16[160,1536]{1,0:T(8,128)(2,1)S(1)}, u32[]{:S(2)}, u32[]{:S(2)}) collective-permute-start(bf16[160,1536]{1,0:T(8,128)(2,1)S(1)} %get-tuple-element.91), channel_id=1, source_target_pairs={{0,2},{1,5},{2,0},{3,7},{4,6},{5,1},{6,4},{7,3},{8,10},{9,13},{10,... | collective-permute-start | bytes 1474568 | tf_op jit(solution)/shard_map/ppermute | solution.py:31
  47.9 1.9 %collective-permute-start.13 = (bf16[160,1536]{1,0:T(8,128)(2,1)S(1)}, bf16[160,1536]{1,0:T(8,128)(2,1)S(1)}, u32[]{:S(2)}, u32[]{:S(2)}) collective-permute-start(bf16[160,1536]{1,0:T(8,128)(2,1)S(1)} %collective-permute-done.11), channel_id=1, source_target_pairs={{0,1},{1,0},{2,3},{3,2},{4,5},{5,4},{6,7},{7,6},{8,9},{9,8},{10,11... | collective-permute-start | bytes 1474568 | tf_op jit(solution)/shard_map/ppermute | solution.py:31
  52.0 2.7 %copy-start.5 = (bf16[1280,1536]{1,0:T(8,128)(2,1)S(1)}, bf16[1280,1536]{1,0:T(8,128)(2,1)}, u32[]{:S(2)}) copy-start(bf16[1280,1536]{1,0:T(8,128)(2,1)} %get-tuple-element.90) | copy-start | bytes 11796484
  53.9 4.3 %collective-permute-start.14 = (bf16[320,1664]{1,0:T(8,128)(2,1)S(1)}, bf16[320,1664]{1,0:T(8,128)(2,1)S(1)}, u32[]{:S(2)}, u32[]{:S(2)}) collective-permute-start(bf16[320,1664]{1,0:T(8,128)(2,1)S(1)} %fusion.15), channel_id=1, source_target_pairs={{0,1},{1,0},{2,3},{3,2},{4,5},{5,4},{6,7},{7,6},{8,9},{9,8},{10,11... | collective-permute-start | bytes 3194888 | tf_op jit(solution)/shard_map/ppermute | solution.py:31
  54.1 3.2 %collective-permute-start.20 = (bf16[160,1536]{1,0:T(8,128)(2,1)S(1)}, bf16[160,1536]{1,0:T(8,128)(2,1)S(1)}, u32[]{:S(2)}, u32[]{:S(2)}) collective-permute-start(bf16[160,1536]{1,0:T(8,128)(2,1)S(1)} %get-tuple-element.91), channel_id=1, source_target_pairs={{0,1},{1,0},{2,3},{3,2},{4,5},{5,4},{6,7},{7,6},{8,9},{9,8},{10,11... | collective-permute-start | bytes 1474568 | tf_op jit(solution)/shard_map/ppermute | solution.py:31
  54.5 3.6 %collective-permute-start.21 = (bf16[160,1536]{1,0:T(8,128)(2,1)S(1)}, bf16[160,1536]{1,0:T(8,128)(2,1)S(1)}, u32[]{:S(2)}, u32[]{:S(2)}) collective-permute-start(bf16[160,1536]{1,0:T(8,128)(2,1)S(1)} %collective-permute-done.19), channel_id=1, source_target_pairs={{0,1},{1,0},{2,3},{3,2},{4,5},{5,4},{6,7},{7,6},{8,9},{9,8},{10,11... | collective-permute-start | bytes 1474568 | tf_op jit(solution)/shard_map/ppermute | solution.py:31
  54.7 8.2 %collective-permute-start.16 = (bf16[40,1536]{1,0:T(8,128)(2,1)S(1)}, bf16[40,1536]{1,0:T(8,128)(2,1)S(1)}, u32[]{:S(2)}, u32[]{:S(2)}) collective-permute-start(bf16[40,1536]{1,0:T(8,128)(2,1)S(1)} %get-tuple-element.66), channel_id=1, source_target_pairs={{0,8},{1,9},{2,10},{3,11},{4,12},{5,13},{6,14},{7,15},{8,0},{9,1},... | collective-permute-start | bytes 368648 | tf_op jit(solution)/shard_map/ppermute | solution.py:37
  58.1 17.8 %collective-permute-start.10 = (bf16[160,1664]{1,0:T(8,128)(2,1)S(1)}, bf16[160,1664]{1,0:T(8,128)(2,1)S(1)}, u32[]{:S(2)}, u32[]{:S(2)}) collective-permute-start(bf16[160,1664]{1,0:T(8,128)(2,1)S(1)} %get-tuple-element.82), channel_id=1, source_target_pairs={{0,2},{1,5},{2,0},{3,7},{4,6},{5,1},{6,4},{7,3},{8,10},{9,13},{10,... | collective-permute-start | bytes 1597448 | tf_op jit(solution)/shard_map/ppermute | solution.py:31
  58.5 17.3 %collective-permute-start.15 = (bf16[160,1664]{1,0:T(8,128)(2,1)S(1)}, bf16[160,1664]{1,0:T(8,128)(2,1)S(1)}, u32[]{:S(2)}, u32[]{:S(2)}) collective-permute-start(bf16[160,1664]{1,0:T(8,128)(2,1)S(1)} %get-tuple-element.80), channel_id=1, source_target_pairs={{0,2},{1,5},{2,0},{3,7},{4,6},{5,1},{6,4},{7,3},{8,10},{9,13},{10,... | collective-permute-start | bytes 1597448 | tf_op jit(solution)/shard_map/ppermute | solution.py:31
  62.9 9.0 %collective-permute-start.17 = (bf16[80,1536]{1,0:T(8,128)(2,1)S(1)}, bf16[80,1536]{1,0:T(8,128)(2,1)S(1)}, u32[]{:S(2)}, u32[]{:S(2)}) collective-permute-start(bf16[80,1536]{1,0:T(8,128)(2,1)S(1)} %maximum_bitcast_fusion.1), channel_id=1, source_target_pairs={{0,4},{1,3},{2,6},{3,1},{4,0},{5,7},{6,2},{7,5},{8,12},{9,11},{10,... | collective-permute-start | bytes 737288 | tf_op jit(solution)/shard_map/ppermute | solution.py:31
  71.9 13.2 %collective-permute-start.22 = (bf16[160,1536]{1,0:T(8,128)(2,1)S(1)}, bf16[160,1536]{1,0:T(8,128)(2,1)S(1)}, u32[]{:S(2)}, u32[]{:S(2)}) collective-permute-start(bf16[160,1536]{1,0:T(8,128)(2,1)S(1)} %pad_maximum_fusion.3), channel_id=1, source_target_pairs={{0,2},{1,5},{2,0},{3,7},{4,6},{5,1},{6,4},{7,3},{8,10},{9,13},{10,... | collective-permute-start | bytes 1474568 | tf_op jit(solution)/shard_map/ppermute | solution.py:31
  72.8 13.5 %collective-permute-start.24 = (bf16[160,1536]{1,0:T(8,128)(2,1)S(1)}, bf16[160,1536]{1,0:T(8,128)(2,1)S(1)}, u32[]{:S(2)}, u32[]{:S(2)}) collective-permute-start(bf16[160,1536]{1,0:T(8,128)(2,1)S(1)} %pad_maximum_fusion.3), channel_id=1, source_target_pairs={{0,1},{1,0},{2,3},{3,2},{4,5},{5,4},{6,7},{7,6},{8,9},{9,8},{10,11... | collective-permute-start | bytes 1474568 | tf_op jit(solution)/shard_map/ppermute | solution.py:31
  75.9 9.1 %collective-permute-start.23 = (bf16[80,1664]{1,0:T(8,128)(2,1)S(1)}, bf16[80,1664]{1,0:T(8,128)(2,1)S(1)}, u32[]{:S(2)}, u32[]{:S(2)}) collective-permute-start(bf16[80,1664]{1,0:T(8,128)(2,1)S(1)} %add_convert_fusion.8), channel_id=1, source_target_pairs={{0,4},{1,3},{2,6},{3,1},{4,0},{5,7},{6,2},{7,5},{8,12},{9,11},{10,... | collective-permute-start | bytes 798728 | tf_op jit(solution)/shard_map/ppermute | solution.py:31
  85.1 1.9 %collective-permute-start.25 = (bf16[160,1536]{1,0:T(8,128)(2,1)S(1)}, bf16[160,1536]{1,0:T(8,128)(2,1)S(1)}, u32[]{:S(2)}, u32[]{:S(2)}) collective-permute-start(bf16[160,1536]{1,0:T(8,128)(2,1)S(1)} %collective-permute-done.22), channel_id=1, source_target_pairs={{0,1},{1,0},{2,3},{3,2},{4,5},{5,4},{6,7},{7,6},{8,9},{9,8},{10,11... | collective-permute-start | bytes 1474568 | tf_op jit(solution)/shard_map/ppermute | solution.py:31
  85.2 7.6 %collective-permute-start.18 = (bf16[80,1664]{1,0:T(8,128)(2,1)S(1)}, bf16[80,1664]{1,0:T(8,128)(2,1)S(1)}, u32[]{:S(2)}, u32[]{:S(2)}) collective-permute-start(bf16[80,1664]{1,0:T(8,128)(2,1)S(1)} %get-tuple-element.88), channel_id=1, source_target_pairs={{0,4},{1,3},{2,6},{3,1},{4,0},{5,7},{6,2},{7,5},{8,12},{9,11},{10,... | collective-permute-start | bytes 798728 | tf_op jit(solution)/shard_map/ppermute | solution.py:31
  85.3 15.1 %collective-permute-start.26 = (bf16[80,1664]{1,0:T(8,128)(2,1)S(1)}, bf16[80,1664]{1,0:T(8,128)(2,1)S(1)}, u32[]{:S(2)}, u32[]{:S(2)}) collective-permute-start(bf16[80,1664]{1,0:T(8,128)(2,1)S(1)} %add_convert_fusion.4), channel_id=1, source_target_pairs={{0,8},{1,9},{2,10},{3,11},{4,12},{5,13},{6,14},{7,15},{8,0},{9,1},... | collective-permute-start | bytes 798728 | tf_op jit(solution)/shard_map/ppermute | solution.py:37

commit v6 on v5

--- a/solution.py
+++ b/solution.py
@@ -14,8 +14,8 @@
 F32, BF16 = jnp.float32, jnp.bfloat16
 
 
-def params():
-    return pltpu.CompilerParams(vmem_limit_bytes=48 * 1024 * 1024)
+def params(mib):
+    return pltpu.CompilerParams(vmem_limit_bytes=mib * 1024 * 1024)
 
 
 def cost(flops, moved, exps=0):
@@ -72,7 +72,7 @@
     ahead = expert_id - (lax.axis_index("expert") >> 3)
     ahead = jnp.where(ahead < 0, ahead + devices // SPLIT, ahead)
     place = jnp.where(dropped == 1, -1, ahead * slots + slot)
-    return jnp.stack([place.astype(F32), gate])
+    return place.reshape(1, -1), gate.reshape(1, -1)
 
 
 def chosen(place, first, count):
@@ -80,22 +80,21 @@
     return rows == place
 
 
-def place_kernel(slots, scale, routing, values, near, far):
-    place = routing[0:1, :].astype(jnp.int32)
+def place_kernel(slots, scale, place, gate, values, near, far):
     rows = values[...]
     if scale:
         count = rows.shape[0]
         across = lax.broadcasted_iota(jnp.int32, (count, count), 1)
         down = lax.broadcasted_iota(jnp.int32, (count, count), 0)
-        gates = jnp.where(across == down, routing[1:2, :], 0.0)
+        gates = jnp.where(across == down, gate[...], 0.0)
         column = jnp.sum(gates, axis=1, keepdims=True)
         rows = (column * rows.astype(F32)).astype(BF16)
     for first, out in ((0, near), (slots, far)):
-        onehot = chosen(place, first, out.shape[0]).astype(F32).astype(BF16)
+        onehot = chosen(place[...], first, out.shape[0]).astype(F32).astype(BF16)
         out[...] = jnp.dot(onehot, rows, preferred_element_type=F32).astype(BF16)
 
 
-def to_slots(slots, scale, routing, values):
+def to_slots(slots, scale, place, gate, values):
     experts = lax.axis_size("expert") // SPLIT
     width = values.shape[1]
     return pl.pallas_call(
@@ -104,22 +103,21 @@
             jax.ShapeDtypeStruct((slots, width), BF16),
             jax.ShapeDtypeStruct(((experts - 1) * slots, width), BF16),
         ),
-        in_specs=[VMEM] * 2,
+        in_specs=[VMEM] * 3,
         out_specs=(VMEM, VMEM),
-        compiler_params=params(),
+        compiler_params=params(6),
         cost_estimate=cost(values.size, values.size),
         name="rows_to_slots",
-    )(routing, values)
-
-
-def home_kernel(slots, routing, kept, got, back, token_grad, gate_grad):
-    place = routing[0:1, :].astype(jnp.int32)
+    )(place, gate, values)
+
+
+def home_kernel(slots, place, gate, kept, got, back, token_grad, gate_grad):
     width = token_grad.shape[1]
     near = kept[...].astype(F32) + got[...].astype(F32)
     total = jnp.zeros(token_grad.shape, F32)
     gates = jnp.zeros(gate_grad.shape, F32)
     for first, rows in ((0, near), (slots, back[...].astype(F32))):
-        picks = chosen(place, first, rows.shape[0])
+        picks = chosen(place[...], first, rows.shape[0])
         total += lax.dot_general(
             picks.astype(F32).astype(BF16),
             rows[:, :width].astype(BF16),
@@ -129,22 +127,22 @@
         column = rows[:, width : width + 1]
         gates += jnp.sum(jnp.where(picks, column, 0.0), axis=0, keepdims=True)
     token_grad[...] = total.astype(BF16)
-    gate_grad[...] = jnp.where(place < 0, 0.0, gates / routing[1:2, :])
-
-
-def to_tokens(slots, routing, kept, got, back):
-    count, width = routing.shape[1], kept.shape[1] - LANES
+    gate_grad[...] = jnp.where(place[...] < 0, 0.0, gates / gate[...])
+
+
+def to_tokens(slots, place, gate, kept, got, back):
+    count, width = place.shape[1], kept.shape[1] - LANES
     return pl.pallas_call(
         functools.partial(home_kernel, slots),
         out_shape=(
             jax.ShapeDtypeStruct((count, width), BF16),
             jax.ShapeDtypeStruct((1, count), F32),
         ),
-        in_specs=[VMEM] * 4,
+        in_specs=[VMEM] * 5,
         out_specs=(VMEM, VMEM),
-        compiler_params=params(),
+        compiler_params=params(12),
         name="slots_to_tokens",
-    )(routing, kept, got, back)
+    )(place, gate, kept, got, back)
 
 
 def activation_kernel(order, hidden, activated, slope):
@@ -177,11 +175,34 @@
             out_specs=[pl.BlockSpec(block, lambda i, order: (i, 0, 0))] * 2,
         ),
         out_shape=(jax.ShapeDtypeStruct(shape, BF16), jax.ShapeDtypeStruct(shape, F32)),
-        compiler_params=params(),
+        compiler_params=params(6),
         cost_estimate=cost(size, size),
         name="activation",
     )(order, by_source)
     return act.reshape(-1, units), slope.reshape(-1, units)
+
+
+def stack_kernel(*refs):
+    out, first = refs[-1], 0
+    for ref in refs[:-1]:
+        count = ref.shape[0]
+        out[first : first + count, :] = ref[...]
+        first += count
+
+
+def join(*pieces):
+    if any(x.shape[0] % 16 for x in pieces):
+        return jnp.concatenate(pieces)
+    rows, width = sum(x.shape[0] for x in pieces), pieces[0].shape[1]
+    return pl.pallas_call(
+        stack_kernel,
+        out_shape=jax.ShapeDtypeStruct((rows, width), BF16),
+        in_specs=[VMEM] * len(pieces),
+        out_specs=VMEM,
+        compiler_params=params(2 + rows * width * 4 // 1000000),
+        cost_estimate=cost(0, rows * width),
+        name="stack_rows",
+    )(*pieces)
 
 
 def add(a, b):
@@ -230,79 +251,68 @@
     slots = saved_hidden.shape[0] // devices
     units = saved_hidden.shape[1]
     me = lax.axis_index("expert")
-    routing = pack_routing(expert_id, dropped, slot, gate, slots)
+    place, gate = pack_routing(expert_id, dropped, slot, gate, slots)
     near_order, far_order = sources_met(me, experts)
     by_source = saved_hidden.reshape(devices, slots, units)
-    join = jnp.concatenate
-
-    near_grad, far_grad = to_slots(slots, True, routing, out_grad)
-    near_row, far_row = to_slots(slots, False, routing, tokens)
-
-    far_grad_a, far_grad_b = split_slots(far_grad, experts)
-    far_grad_a = cross(far_grad_a, 1)
+
+    near_grad, far_grad = to_slots(slots, True, place, gate, out_grad)
+    near_row, far_row = to_slots(slots, False, place, gate, tokens)
+
+    far_grad = cross(far_grad, 1)
     got = meet(near_grad, 0)
     near_act, near_slope = activation(by_source, near_order)
-    far_grad_a = after(far_grad_a, near_act, near_row)
-    far_grad_b = cross(after(far_grad_b, far_grad_a), 1)
-    got = after(got, far_grad_a)
-    near_two = join([near_grad, got])
-    near_more = meet(near_two, 1)
-    near_last = meet(near_two, 2)
-    near_row_got = meet(after(near_row, near_two), 0)
-    far_act, far_slope = activation(by_source, after(far_order, near_two))
-    far_grad = join_slots(far_grad_a, after(far_grad_b, far_act), experts)
+    far_act, far_slope = activation(by_source, far_order)
+    near_two = join(near_grad, after(got, near_act, far_act, near_row))
+    got = meet(near_two, 1)
+    row_got = meet(after(near_row, near_two), 0)
+    far_grad = after(far_grad, near_two)
     far_got = meet(far_grad, 0)
-    far_row_a, far_row_b = split_slots(far_row, experts)
-    far_row_a = cross(after(far_row_a, far_grad), 1)
-    near_more = after(near_more, far_grad)
-    near_last = near_last, meet(near_more, 2)
-    near_row2 = join([near_row, after(near_row_got, near_more)])
-    near_row4 = meet(near_row2, 1)
-
-    near_grads = join([near_two, near_more, *near_last])
-    near_grads = after(near_grads, near_row2)
+    near_row2 = join(near_row, after(row_got, far_grad))
+    far_two = join(far_grad, after(far_got, near_row2))
+    far_got = meet(far_two, 1)
+    near_four = join(near_two, after(got, far_two))
+    got = meet(near_four, 2)
+
+    near_grads = join(near_four, got)
     near_hg, near_gates = hidden_part(near_grads, w_out, near_act, near_slope)
-    far_two = join([far_grad, after(far_got, near_hg)])
-    far_more = meet(far_two, 1)
-    far_last = meet(far_two, 2)
-    near_kept, near_sent = slot_part(after(near_hg, far_two), near_gates, w_in)
+    near_kept, near_sent = slot_part(near_hg, near_gates, w_in)
     near_got = meet(near_sent, 2)
-    far_row_a = after(far_row_a, near_sent)
-    far_more = after(far_more, far_row_a)
-    far_last = far_last, meet(far_more, 2)
-    far_row_b = cross(after(far_row_b, far_row_a), 1)
-    near_row4 = after(near_row4, far_more)
-    near_rows = join([near_row2, near_row4, meet(near_row2, 2), meet(near_row4, 2)])
-    near_kept, near_sent = add_halves(near_kept, after(near_got, far_row_a))
+    far_four = join(far_two, after(far_got, near_sent))
+    far_got = meet(far_four, 2)
+    far_row_a, far_row_b = split_slots(after(far_row, far_four), experts)
+    far_row_a = cross(far_row_a, 1)
+    row_got = meet(after(near_row2, far_four), 1)
+    far_grads = join(far_four, far_got)
+    near_kept, near_sent = add_halves(near_kept, after(near_got, far_grads))
     near_got = meet(near_sent, 1)
-
-    far_grads = join([far_two, far_more, *far_last])
     far_grads = after(far_grads, near_sent)
+
     far_hg, far_gates = hidden_part(far_grads, w_out, far_act, far_slope)
     far_kept, far_sent = slot_part(far_hg, far_gates, w_in)
-    far_kept, far_sent = add_halves(far_kept, meet(far_sent, 2))
+    far_got = meet(far_sent, 2)
+    near_row4 = join(near_row2, after(row_got, far_sent))
+    row_got = meet(near_row4, 2)
+    far_row_a = after(far_row_a, near_row4)
+    far_row_b = cross(after(far_row_b, far_row_a), 1)
+    far_kept, far_sent = add_halves(far_kept, after(far_got, far_row_a))
     far_got = meet(far_sent, 1)
-    far_row = join_slots(far_row_a, after(far_row_b, far_sent), experts)
-    far_row_got = meet(far_row, 0)
-    near_act, near_grads = after(near_act, far_row), after(near_grads, far_row)
-    w_out_grad = product(
-        join([near_act, far_act]), join([near_grads, far_grads]), ((0,), (0,))
-    ).astype(BF16)
-    far_row2 = join([far_row, after(far_row_got, w_out_grad)])
-    far_row4 = meet(far_row2, 1)
-    far_kept, far_sent = add_halves(far_kept, after(far_got, far_row2))
-    far_got = meet(far_sent, 0)
     near_kept, near_sent = add_halves(near_kept, after(near_got, far_sent))
     near_got = meet(near_sent, 0)
-    far_sum = add(far_kept, after(far_got, near_sent))
+    acts = join(after(near_act, near_sent), far_act)
+    w_out_grad = product(acts, join(near_grads, far_grads), ((0,), (0,))).astype(BF16)
+    far_row = join_slots(far_row_a, after(far_row_b, w_out_grad), experts)
+    far_row_got = meet(far_row, 0)
+    far_kept, far_sent = add_halves(far_kept, after(far_got, far_row))
+    far_got = meet(far_sent, 0)
+    far_row2 = join(far_row, after(far_row_got, far_sent))
+    far_row_got = meet(far_row2, 1)
+    far_sum = add(far_kept, after(far_got, far_row2))
     back = cross(far_sum, -1)
-    far_row4 = after(far_row4, far_sum)
-    far_rows = join([far_row2, far_row4, meet(far_row2, 2), meet(far_row4, 2)])
-    w_in_grad = product(
-        join([near_rows, far_rows]), join([near_hg, far_hg]), ((0,), (0,))
-    ).astype(BF16)
+    far_row4 = join(far_row2, after(far_row_got, far_sum))
+    rows = join(near_row4, row_got, far_row4, meet(far_row4, 2))
+    w_in_grad = product(rows, join(near_hg, far_hg), ((0,), (0,))).astype(BF16)
     near_got, back = after(near_got, w_in_grad), after(back, w_in_grad)
-    token_grad, gate_grad = to_tokens(slots, routing, near_kept, near_got, back)
+    token_grad, gate_grad = to_tokens(slots, place, gate, near_kept, near_got, back)
     return (token_grad, gate_grad.reshape(-1), w_in_grad, w_out_grad)
 
 

time: 102 us -> 112 us (1.098)
  waiting for transfers between devices: 41.4 us -> 49.2 us
  Pallas kernels: 5.69 us -> 9.82 us
  matrix products: 19.6 us -> 16.5 us
  starting transfers between devices: 21.7 us -> 24.3 us
    ppermute x22 -> x18, waiting for transfers between devices: 29.1 us -> 40.9 us  [meet(): lax.ppermute(rows, 'expert', [(i, i ^ bits(i % 2)[step]) for i in range(d...]
    ppermute x22 -> x18, starting transfers between devices: 14.8 us -> 20.3 us  [meet(): lax.ppermute(rows, 'expert', [(i, i ^ bits(i % 2)[step]) for i in range(d...]
    ppermute x5 -> x4, waiting for transfers between devices: 12.3 us -> 8.37 us  [shift(): return lax.ppermute(rows, 'expert', pairs)]
    pallas_call x0 -> x14, Pallas kernels: none -> 3.42 us  [join(): pl.pallas_call(stack_kernel, out_shape=jax.ShapeDtypeStruct((rows, width)...]
    dot_general x6, matrix products: 19.6 us -> 16.5 us  [product(): return lax.dot_general(a, b, (dims, ((), ())), preferred_element_type=F32)]
    ppermute x5 -> x4, starting transfers between devices: 6.89 us -> 3.93 us  [shift(): return lax.ppermute(rows, 'expert', pairs)]
    concatenate x4 -> x0, local copies, waits for them, and re-layouts: 1.6 us -> none  [the longest x1 0.81 us: body(): near_grads = join([near_two, near_more, *near_last])]
    another operation x2 -> x0, other arithmetic: 1.51 us -> none  [pack_routing(): return jnp.stack([place.astype(F32), gate])]
  transfers between devices with their start and end apart: 27 -> 22, of which waited for: 13 -> 13; matrix products, arithmetic and copies ran while one was open for 26% -> 12% of each run, Pallas kernels for 4% -> 7%
where the time goes in v6:
time: 112 us; the launch traced here: 111 us
  waiting for transfers between devices  49.2 us (44%)
  starting transfers between devices  24.3 us (22%)
  matrix products  16.5 us (15%)
  Pallas kernels  9.82 us (9%)
  local copies, waits for them, and re-layouts  8.59 us (8%)
  other arithmetic  1.89 us (2%)
    ppermute x18, waiting for transfers between devices, meet(): lax.ppermute(rows, 'expert', [(i, i ^ bits(i % 2)[step]) for i in range(d...  40.9 us
    ppermute x18, starting transfers between devices, meet(): lax.ppermute(rows, 'expert', [(i, i ^ bits(i % 2)[step]) for i in range(d...  20.3 us
    dot_general x6, matrix products, product(): return lax.dot_general(a, b, (dims, ((), ())), preferred_element_type=F32)  16.5 us
    ppermute x4, waiting for transfers between devices, shift(): return lax.ppermute(rows, 'expert', pairs)  8.37 us
    unnamed x20, local copies, waits for them, and re-layouts  8.28 us
    ppermute x4, starting transfers between devices, shift(): return lax.ppermute(rows, 'expert', pairs)  3.93 us
    pallas_call x2, Pallas kernels, activation(): pl.pallas_call(activation_kernel, grid_spec=pltpu.PrefetchScalarGridSpec(...  3.89 us
    pallas_call x14, Pallas kernels, join(): pl.pallas_call(stack_kernel, out_shape=jax.ShapeDtypeStruct((rows, width)...  3.42 us
  transfers between devices with their start and end apart: 22, of which 13 were waited for; matrix products, arithmetic and copies ran while one was open for 12% of the time, Pallas kernels for 7%

profile of v6, /device:TPU:0, one launch (start us, length us, event | category | flops | bytes accessed | tf_op | source)
XLA Modules:
  0.0 111.2 jit_solution(8512755464006252463)
XLA Ops:
  0.7 0.8 fusion.4.place
  1.5 1.0 copy-done.3
  2.5 0.7 copy-done.5
  3.2 1.1 rows_to_slots.2
  4.2 3.0 %collective-permute-start = (bf16[80,1536]{1,0:T(8,128)(2,1)}, bf16[80,1536]{1,0:T(8,128)(2,1)}, u32[]{:S(2)}, u32[]{:S(2)}) collective-permute-start(bf16[80,1536]{1,0:T(8,128)(2,1)} %get-tuple-element.38.refs_0_), channel_id=1, source_target_pairs={{0,4},{1,3},{2,6},{3,1},{4,0},{5,7},{6,2},{7,5},{8,12},{9,11},{10,... | collective-permute-start | bytes 737288 | tf_op jit(solution)/shard_map/ppermute | solution.py:31
  7.3 2.6 %collective-permute-start.2 = (bf16[80,1536]{1,0:T(8,128)(2,1)}, bf16[80,1536]{1,0:T(8,128)(2,1)}, u32[]{:S(2)}, u32[]{:S(2)}) collective-permute-start(bf16[80,1536]{1,0:T(8,128)(2,1)} %get-tuple-element.43), channel_id=1, source_target_pairs={{0,8},{1,9},{2,10},{3,11},{4,12},{5,13},{6,14},{7,15},{8,0},{9,1},... | collective-permute-start | bytes 737288 | tf_op jit(solution)/shard_map/ppermute | solution.py:37
  9.9 1.5 %copy-done.1 = bf16[1280,768]{1,0:T(8,128)(2,1)S(1)} copy-done((bf16[1280,768]{1,0:T(8,128)(2,1)S(1)}, bf16[1280,768]{1,0:T(8,128)(2,1)}, u32[]{:S(2)}) %copy-start.1) | copy-done | bytes 1966104
  11.4 1.9 %activation.3 = (bf16[8,80,768]{2,1,0:T(8,128)(2,1)S(1)}, f32[8,80,768]{2,1,0:T(8,128)S(1)}) custom-call(s32[8]{0:T(128)S(1)} %broadcast_add_fusion.order, bf16[16,80,768]{2,1,0:T(8,128)(2,1)S(1)} %bitcast.38), custom_call_target="tpu_custom_call" | custom-call | flops 491520 | bytes 491520 | tf_op jit(solution)/shard_map/activation/pallas_call | solution.py:169
  13.4 1.3 %copy-done.7 = f32[8,80,768]{2,1,0:T(8,128)} copy-done((f32[8,80,768]{2,1,0:T(8,128)}, f32[8,80,768]{2,1,0:T(8,128)S(1)}, u32[]{:S(2)}) %copy-start.7) | copy-done | bytes 1966104
  14.7 1.0 copy-done.4
  15.7 0.3 rows_to_slots.3
  16.0 1.5 %copy-done.2 = bf16[1280,768]{1,0:T(8,128)(2,1)S(1)} copy-done((bf16[1280,768]{1,0:T(8,128)(2,1)S(1)}, bf16[1280,768]{1,0:T(8,128)(2,1)}, u32[]{:S(2)}) %copy-start.2) | copy-done | bytes 1966104
  17.5 1.9 %activation.2 = (bf16[8,80,768]{2,1,0:T(8,128)(2,1)S(1)}, f32[8,80,768]{2,1,0:T(8,128)S(1)}) custom-call(s32[8]{0:T(128)S(1)} %broadcast_add_fusion.1.order, bf16[16,80,768]{2,1,0:T(8,128)(2,1)S(1)} %bitcast.39), custom_call_target="tpu_custom_call" | custom-call | flops 491520 | bytes 491520 | tf_op jit(solution)/shard_map/activation/pallas_call | solution.py:169
  19.5 1.1 stack_rows.14.refs_0_
  20.6 1.6 %collective-permute-start.1 = (bf16[160,1536]{1,0:T(8,128)(2,1)S(1)}, bf16[160,1536]{1,0:T(8,128)(2,1)S(1)}, u32[]{:S(2)}, u32[]{:S(2)}) collective-permute-start(bf16[160,1536]{1,0:T(8,128)(2,1)S(1)} %stack_rows.14.refs_0_), channel_id=1, source_target_pairs={{0,2},{1,5},{2,0},{3,7},{4,6},{5,1},{6,4},{7,3},{8,10},{9,13},{10,... | collective-permute-start | bytes 1474568 | tf_op jit(solution)/shard_map/ppermute | solution.py:31
  22.2 0.4 collective-permute-start.4
  22.6 1.6 %collective-permute-start.3 = (bf16[80,1536]{1,0:T(8,128)(2,1)}, bf16[80,1536]{1,0:T(8,128)(2,1)S(1)}, u32[]{:S(2)}, u32[]{:S(2)}) collective-permute-start(bf16[80,1536]{1,0:T(8,128)(2,1)} %collective-permute-done.2.refs_0_), channel_id=1, source_target_pairs={{0,4},{1,3},{2,6},{3,1},{4,0},{5,7},{6,2},{7,5},{8,12},{9,11},{10,... | collective-permute-start | bytes 737288 | tf_op jit(solution)/shard_map/ppermute | solution.py:31
  24.2 6.2 %collective-permute-done.4.refs_1_ = bf16[80,1536]{1,0:T(8,128)(2,1)S(1)} collective-permute-done((bf16[80,1536]{1,0:T(8,128)(2,1)S(1)}, bf16[80,1536]{1,0:T(8,128)(2,1)S(1)}, u32[]{:S(2)}, u32[]{:S(2)}) %collective-permute-start.4) | collective-permute-done | bytes 245792 | tf_op jit(solution)/shard_map/ppermute | solution.py:31
  30.4 2.6 %collective-permute-done.3.refs_1_ = bf16[80,1536]{1,0:T(8,128)(2,1)S(1)} collective-permute-done((bf16[80,1536]{1,0:T(8,128)(2,1)}, bf16[80,1536]{1,0:T(8,128)(2,1)S(1)}, u32[]{:S(2)}, u32[]{:S(2)}) %collective-permute-start.3) | collective-permute-done | bytes 245792 | tf_op jit(solution)/shard_map/ppermute | solution.py:31
  33.0 1.0 stack_rows.16.refs_0_
  34.0 0.3 collective-permute-done.1.refs_1_
  34.4 0.8 collective-permute-start.5
  35.2 2.2 %collective-permute-done.5.refs_1_ = bf16[320,1536]{1,0:T(8,128)(2,1)S(1)} collective-permute-done((bf16[320,1536]{1,0:T(8,128)(2,1)S(1)}, bf16[320,1536]{1,0:T(8,128)(2,1)S(1)}, u32[]{:S(2)}, u32[]{:S(2)}) %collective-permute-start.5) | collective-permute-done | bytes 983072 | tf_op jit(solution)/shard_map/ppermute | solution.py:31
  37.4 0.1 stack_rows.18.refs_0_
  37.5 1.9 %fusion.1 = (bf16[640,768]{1,0:T(8,128)(2,1)S(1)}, bf16[640]{0:T(1024)(128)(2,1)S(1)}) fusion(f32[8,80,768]{2,1,0:T(8,128)S(1)} %get-tuple-element.49, bf16[8,80,768]{2,1,0:T(8,128)(2,1)S(1)} %get-tuple-element.39, bf16[640,1536]{1,0:T(8,128)(2,1)S(1)} %stack_rows.18.refs_0_, bf16[768,1536]{1,0:T(8,128)(2,1)S(1)} %copy-done.9), kind=kOutput, calls=%fused_computation.11 | convolution fusion | flops 1512406400 | bytes 8258816 | tf_op jit(solution)/shard_map/dot_general | solution.py:233
  39.4 1.7 %convolution_convert_fusion.3 = bf16[640,1536]{1,0:T(8,128)(2,1)S(1)} fusion(bf16[640,768]{1,0:T(8,128)(2,1)S(1)} %get-tuple-element.78.refs_0_, bf16[1536,768]{1,0:T(8,128)(2,1)S(1)} %copy-done), kind=kOutput, calls=%fused_computation.3 | convolution fusion | flops 1510932480 | bytes 5308416 | tf_op jit(solution)/shard_map/dot_general | solution.py:233
  41.2 0.1 broadcast_in_dim.26
  41.4 0.4 collective-permute-start.6
  41.8 2.2 %collective-permute-done.7.refs_1_ = bf16[160,1536]{1,0:T(8,128)(2,1)S(1)} collective-permute-done((bf16[160,1536]{1,0:T(8,128)(2,1)S(1)}, bf16[160,1536]{1,0:T(8,128)(2,1)S(1)}, u32[]{:S(2)}, u32[]{:S(2)}) %collective-permute-start.7) | collective-permute-done | bytes 491552 | tf_op jit(solution)/shard_map/ppermute | solution.py:31
  44.1 2.6 %collective-permute-done.8.refs_1_ = bf16[320,1536]{1,0:T(8,128)(2,1)S(1)} collective-permute-done((bf16[320,1536]{1,0:T(8,128)(2,1)S(1)}, bf16[320,1536]{1,0:T(8,128)(2,1)S(1)}, u32[]{:S(2)}, u32[]{:S(2)}) %collective-permute-start.8) | collective-permute-done | bytes 983072 | tf_op jit(solution)/shard_map/ppermute | solution.py:31
  46.7 0.1 stack_rows.20.refs_1_
  46.9 0.3 add_convert_fusion.2
  47.1 1.3 %copy-done.8 = f32[8,80,768]{2,1,0:T(8,128)S(1)} copy-done((f32[8,80,768]{2,1,0:T(8,128)S(1)}, f32[8,80,768]{2,1,0:T(8,128)}, u32[]{:S(2)}) %copy-start.8) | copy-done | bytes 1966104
  48.4 1.9 %fusion = (bf16[640,768]{1,0:T(8,128)(2,1)S(1)}, bf16[640]{0:T(1024)(128)(2,1)S(1)}) fusion(f32[8,80,768]{2,1,0:T(8,128)S(1)} %copy-done.8, bf16[8,80,768]{2,1,0:T(8,128)(2,1)S(1)} %get-tuple-element.40, bf16[640,1536]{1,0:T(8,128)(2,1)S(1)} %stack_rows.20.refs_1_, bf16[768,1536]{1,0:T(8,128)(2,1)S(1)} %copy-done.9), kind=kOutput, calls=%fused_computation.9 | convolution fusion | flops 1512406400 | bytes 8258816 | tf_op jit(solution)/shard_map/dot_general | solution.py:233
  50.3 1.7 %convolution_convert_fusion.2 = bf16[640,1536]{1,0:T(8,128)(2,1)S(1)} fusion(bf16[640,768]{1,0:T(8,128)(2,1)S(1)} %get-tuple-element.76.refs_1_, bf16[1536,768]{1,0:T(8,128)(2,1)S(1)} %copy-done), kind=kOutput, calls=%fused_computation.2 | convolution fusion | flops 1510932480 | bytes 5308416 | tf_op jit(solution)/shard_map/dot_general | solution.py:233
  52.0 0.1 broadcast_in_dim.27
  52.3 0.2 collective-permute-start.10
  52.5 0.4 collective-permute-start.11
  52.9 2.0 %collective-permute-start.9 = (bf16[160,1664]{1,0:T(8,128)(2,1)S(1)}, bf16[160,1664]{1,0:T(8,128)(2,1)S(1)}, u32[]{:S(2)}, u32[]{:S(2)}) collective-permute-start(bf16[160,1664]{1,0:T(8,128)(2,1)S(1)} %get-tuple-element.74), channel_id=1, source_target_pairs={{0,2},{1,5},{2,0},{3,7},{4,6},{5,1},{6,4},{7,3},{8,10},{9,13},{10,... | collective-permute-start | bytes 1597448 | tf_op jit(solution)/shard_map/ppermute | solution.py:31
  54.9 0.3 stack_rows.23
  55.2 6.1 %collective-permute-done.12.refs_1_ = bf16[160,1536]{1,0:T(8,128)(2,1)S(1)} collective-permute-done((bf16[160,1536]{1,0:T(8,128)(2,1)S(1)}, bf16[160,1536]{1,0:T(8,128)(2,1)S(1)}, u32[]{:S(2)}, u32[]{:S(2)}) %collective-permute-start.12) | collective-permute-done | bytes 491552 | tf_op jit(solution)/shard_map/ppermute | solution.py:31
  61.4 0.4 collective-permute-start.15
  61.8 0.3 add_convert_fusion
  62.0 0.4 collective-permute-start.17
  62.4 4.6 %collective-permute-done.9 = bf16[160,1664]{1,0:T(8,128)(2,1)S(1)} collective-permute-done((bf16[160,1664]{1,0:T(8,128)(2,1)S(1)}, bf16[160,1664]{1,0:T(8,128)(2,1)S(1)}, u32[]{:S(2)}, u32[]{:S(2)}) %collective-permute-start.9) | collective-permute-done | bytes 532512 | tf_op jit(solution)/shard_map/ppermute | solution.py:31
  67.0 0.1 add_convert_fusion.7
  67.1 0.1 stack_rows.22
  67.3 4.6 %convolution_convert_fusion.1 = bf16[768,1536]{1,0:T(8,128)(2,1)} fusion(bf16[1280,768]{1,0:T(8,128)(2,1)S(1)} %stack_rows.22, bf16[1280,1536]{1,0:T(8,128)(2,1)S(1)} %stack_rows.23), kind=kOutput, calls=%fused_computation.1 | convolution fusion | flops 3021078528 | bytes 8257536 | tf_op jit(solution)/shard_map/dot_general | solution.py:233
  71.9 0.8 collective-permute-done.17
  72.8 0.7 collective-permute-start.19
  73.5 1.4 %collective-permute-start.16 = (bf16[80,1536]{1,0:T(8,128)(2,1)S(1)}, bf16[80,1536]{1,0:T(8,128)(2,1)S(1)}, u32[]{:S(2)}, u32[]{:S(2)}) collective-permute-start(bf16[80,1536]{1,0:T(8,128)(2,1)S(1)} %maximum_bitcast_fusion.refs_0_), channel_id=1, source_target_pairs={{0,4},{1,3},{2,6},{3,1},{4,0},{5,7},{6,2},{7,5},{8,12},{9,11},{10,... | collective-permute-start | bytes 737288 | tf_op jit(solution)/shard_map/ppermute | solution.py:31
  74.9 8.0 %collective-permute-done.16.refs_1_ = bf16[80,1536]{1,0:T(8,128)(2,1)S(1)} collective-permute-done((bf16[80,1536]{1,0:T(8,128)(2,1)S(1)}, bf16[80,1536]{1,0:T(8,128)(2,1)S(1)}, u32[]{:S(2)}, u32[]{:S(2)}) %collective-permute-start.16) | collective-permute-done | bytes 245792 | tf_op jit(solution)/shard_map/ppermute | solution.py:31
  83.0 4.2 %collective-permute-start.14 = (bf16[320,1536]{1,0:T(8,128)(2,1)S(1)}, bf16[320,1536]{1,0:T(8,128)(2,1)S(1)}, u32[]{:S(2)}, u32[]{:S(2)}) collective-permute-start(bf16[320,1536]{1,0:T(8,128)(2,1)S(1)} %stack_rows.21.refs_0_), channel_id=1, source_target_pairs={{0,1},{1,0},{2,3},{3,2},{4,5},{5,4},{6,7},{7,6},{8,9},{9,8},{10,11... | collective-permute-start | bytes 2949128 | tf_op jit(solution)/shard_map/ppermute | solution.py:31
  87.2 0.1 add_convert_fusion.4
  87.3 4.6 %collective-permute-done.18.refs_1_ = bf16[160,1536]{1,0:T(8,128)(2,1)S(1)} collective-permute-done((bf16[160,1536]{1,0:T(8,128)(2,1)S(1)}, bf16[160,1536]{1,0:T(8,128)(2,1)S(1)}, u32[]{:S(2)}, u32[]{:S(2)}) %collective-permute-start.18) | collective-permute-done | bytes 491552 | tf_op jit(solution)/shard_map/ppermute | solution.py:31
  91.9 2.7 %collective-permute-start.20 = (bf16[320,1536]{1,0:T(8,128)(2,1)S(1)}, bf16[320,1536]{1,0:T(8,128)(2,1)S(1)}, u32[]{:S(2)}, u32[]{:S(2)}) collective-permute-start(bf16[320,1536]{1,0:T(8,128)(2,1)S(1)} %stack_rows.25.refs_2_), channel_id=1, source_target_pairs={{0,1},{1,0},{2,3},{3,2},{4,5},{5,4},{6,7},{7,6},{8,9},{9,8},{10,11... | collective-permute-start | bytes 2949128 | tf_op jit(solution)/shard_map/ppermute | solution.py:31
  94.6 0.1 stack_rows.27
  94.8 0.7 collective-permute-start.13
  95.5 0.6 collective-permute-start.21
  96.1 0.8 collective-permute-done.20.refs_3_
  96.8 0.3 stack_rows.26
  97.1 4.6 %convolution_convert_fusion = bf16[1536,768]{1,0:T(8,128)(2,1)} fusion(bf16[1280,1536]{1,0:T(8,128)(2,1)S(1)} %stack_rows.26, bf16[1280,768]{1,0:T(8,128)(2,1)S(1)} %stack_rows.27), kind=kOutput, calls=%fused_computation | convolution fusion | flops 3021078528 | bytes 8257536 | tf_op jit(solution)/shard_map/dot_general | solution.py:233
  101.7 8.4 %collective-permute-done.21.back = bf16[80,1664]{1,0:T(8,128)(2,1)S(1)} collective-permute-done((bf16[80,1664]{1,0:T(8,128)(2,1)S(1)}, bf16[80,1664]{1,0:T(8,128)(2,1)S(1)}, u32[]{:S(2)}, u32[]{:S(2)}) %collective-permute-start.21) | collective-permute-done | bytes 266272 | tf_op jit(solution)/shard_map/ppermute | solution.py:37
  110.0 1.1 %slots_to_tokens.1 = (bf16[128,1536]{1,0:T(8,128)(2,1)}, f32[1,128]{1,0:T(1,128)}) custom-call(s32[1,128]{1,0:T(1,128)S(1)} %fusion.4.place, f32[1,128]{1,0:T(1,128)S(1)} %bitcast.45, bf16[80,1664]{1,0:T(8,128)(2,1)S(1)} %get-tuple-element.81.kept, bf16[80,1664]{1,0:T(8,128)(2,1)S(1)} %collective-permute-done.13.got, ...), custom_call_target="tpu_custom_call" | custom-call | tf_op jit(solution)/shard_map/slots_to_tokens/pallas_call | solution.py:135
  (39 shorter events, 0.8 us)
Async XLA Ops:
  0.6 38.8 %copy-start = (bf16[1536,768]{1,0:T(8,128)(2,1)S(1)}, bf16[1536,768]{1,0:T(8,128)(2,1)}, u32[]{:S(2)}) copy-start(bf16[1536,768]{1,0:T(8,128)(2,1)} %param.16) | copy-start | bytes 7077892
  0.6 14.0 %copy-start.6 = (f32[128]{0:T(128)S(1)}, f32[128]{0:T(128)}, u32[]{:S(2)}) copy-start(f32[128]{0:T(128)} %param.11) | copy-start | bytes 1540
  1.5 1.0 copy-start.3
  2.5 0.7 copy-start.5
  4.2 15.2 %collective-permute-start = (bf16[80,1536]{1,0:T(8,128)(2,1)}, bf16[80,1536]{1,0:T(8,128)(2,1)}, u32[]{:S(2)}, u32[]{:S(2)}) collective-permute-start(bf16[80,1536]{1,0:T(8,128)(2,1)} %get-tuple-element.38.refs_0_), channel_id=1, source_target_pairs={{0,4},{1,3},{2,6},{3,1},{4,0},{5,7},{6,2},{7,5},{8,12},{9,11},{10,... | collective-permute-start | bytes 737288 | tf_op jit(solution)/shard_map/ppermute | solution.py:31
  7.3 15.3 %collective-permute-start.2 = (bf16[80,1536]{1,0:T(8,128)(2,1)}, bf16[80,1536]{1,0:T(8,128)(2,1)}, u32[]{:S(2)}, u32[]{:S(2)}) collective-permute-start(bf16[80,1536]{1,0:T(8,128)(2,1)} %get-tuple-element.43), channel_id=1, source_target_pairs={{0,8},{1,9},{2,10},{3,11},{4,12},{5,13},{6,14},{7,15},{8,0},{9,1},... | collective-permute-start | bytes 737288 | tf_op jit(solution)/shard_map/ppermute | solution.py:37
  9.9 1.5 %copy-start.1 = (bf16[1280,768]{1,0:T(8,128)(2,1)S(1)}, bf16[1280,768]{1,0:T(8,128)(2,1)}, u32[]{:S(2)}) copy-start(bf16[1280,768]{1,0:T(8,128)(2,1)} %param.15) | copy-start | bytes 5898244
  13.4 1.3 %copy-start.7 = (f32[8,80,768]{2,1,0:T(8,128)}, f32[8,80,768]{2,1,0:T(8,128)S(1)}, u32[]{:S(2)}) copy-start(f32[8,80,768]{2,1,0:T(8,128)S(1)} %get-tuple-element.53) | copy-start | bytes 5898244
  14.7 1.0 copy-start.4
  16.0 1.5 %copy-start.2 = (bf16[1280,768]{1,0:T(8,128)(2,1)S(1)}, bf16[1280,768]{1,0:T(8,128)(2,1)}, u32[]{:S(2)}) copy-start(bf16[1280,768]{1,0:T(8,128)(2,1)} %param.15) | copy-start | bytes 5898244
  20.6 13.7 %collective-permute-start.1 = (bf16[160,1536]{1,0:T(8,128)(2,1)S(1)}, bf16[160,1536]{1,0:T(8,128)(2,1)S(1)}, u32[]{:S(2)}, u32[]{:S(2)}) collective-permute-start(bf16[160,1536]{1,0:T(8,128)(2,1)S(1)} %stack_rows.14.refs_0_), channel_id=1, source_target_pairs={{0,2},{1,5},{2,0},{3,7},{4,6},{5,1},{6,4},{7,3},{8,10},{9,13},{10,... | collective-permute-start | bytes 1474568 | tf_op jit(solution)/shard_map/ppermute | solution.py:31
  22.2 8.2 %collective-permute-start.4 = (bf16[80,1536]{1,0:T(8,128)(2,1)S(1)}, bf16[80,1536]{1,0:T(8,128)(2,1)S(1)}, u32[]{:S(2)}, u32[]{:S(2)}) collective-permute-start(bf16[80,1536]{1,0:T(8,128)(2,1)S(1)} %get-tuple-element.45.refs_0_), channel_id=1, source_target_pairs={{0,4},{1,3},{2,6},{3,1},{4,0},{5,7},{6,2},{7,5},{8,12},{9,11},{10,... | collective-permute-start | bytes 737288 | tf_op jit(solution)/shard_map/ppermute | solution.py:31
  22.6 10.4 %collective-permute-start.3 = (bf16[80,1536]{1,0:T(8,128)(2,1)}, bf16[80,1536]{1,0:T(8,128)(2,1)S(1)}, u32[]{:S(2)}, u32[]{:S(2)}) collective-permute-start(bf16[80,1536]{1,0:T(8,128)(2,1)} %collective-permute-done.2.refs_0_), channel_id=1, source_target_pairs={{0,4},{1,3},{2,6},{3,1},{4,0},{5,7},{6,2},{7,5},{8,12},{9,11},{10,... | collective-permute-start | bytes 737288 | tf_op jit(solution)/shard_map/ppermute | solution.py:31
  34.3 3.1 %copy-start.9 = (bf16[768,1536]{1,0:T(8,128)(2,1)S(1)}, bf16[768,1536]{1,0:T(8,128)(2,1)}, u32[]{:S(2)}) copy-start(bf16[768,1536]{1,0:T(8,128)(2,1)} %param.17) | copy-start | bytes 7077892
  34.4 3.0 %collective-permute-start.5 = (bf16[320,1536]{1,0:T(8,128)(2,1)S(1)}, bf16[320,1536]{1,0:T(8,128)(2,1)S(1)}, u32[]{:S(2)}, u32[]{:S(2)}) collective-permute-start(bf16[320,1536]{1,0:T(8,128)(2,1)S(1)} %stack_rows.17.refs_0_), channel_id=1, source_target_pairs={{0,1},{1,0},{2,3},{3,2},{4,5},{5,4},{6,7},{7,6},{8,9},{9,8},{10,11... | collective-permute-start | bytes 2949128 | tf_op jit(solution)/shard_map/ppermute | solution.py:31
  35.2 8.8 %collective-permute-start.7 = (bf16[160,1536]{1,0:T(8,128)(2,1)S(1)}, bf16[160,1536]{1,0:T(8,128)(2,1)S(1)}, u32[]{:S(2)}, u32[]{:S(2)}) collective-permute-start(bf16[160,1536]{1,0:T(8,128)(2,1)S(1)} %stack_rows.16.refs_0_), channel_id=1, source_target_pairs={{0,2},{1,5},{2,0},{3,7},{4,6},{5,1},{6,4},{7,3},{8,10},{9,13},{10,... | collective-permute-start | bytes 1474568 | tf_op jit(solution)/shard_map/ppermute | solution.py:31
  41.4 5.4 %collective-permute-start.6 = (bf16[320,1664]{1,0:T(8,128)(2,1)S(1)}, bf16[320,1664]{1,0:T(8,128)(2,1)S(1)}, u32[]{:S(2)}, u32[]{:S(2)}) collective-permute-start(bf16[320,1664]{1,0:T(8,128)(2,1)S(1)} %fusion.3), channel_id=1, source_target_pairs={{0,1},{1,0},{2,3},{3,2},{4,5},{5,4},{6,7},{7,6},{8,9},{9,8},{10,11... | collective-permute-start | bytes 3194888 | tf_op jit(solution)/shard_map/ppermute | solution.py:31
  44.1 2.6 %collective-permute-start.8 = (bf16[320,1536]{1,0:T(8,128)(2,1)S(1)}, bf16[320,1536]{1,0:T(8,128)(2,1)S(1)}, u32[]{:S(2)}, u32[]{:S(2)}) collective-permute-start(bf16[320,1536]{1,0:T(8,128)(2,1)S(1)} %stack_rows.19.refs_0_), channel_id=1, source_target_pairs={{0,1},{1,0},{2,3},{3,2},{4,5},{5,4},{6,7},{7,6},{8,9},{9,8},{10,11... | collective-permute-start | bytes 2949128 | tf_op jit(solution)/shard_map/ppermute | solution.py:31
  46.8 1.5 %copy-start.8 = (f32[8,80,768]{2,1,0:T(8,128)S(1)}, f32[8,80,768]{2,1,0:T(8,128)}, u32[]{:S(2)}) copy-start(f32[8,80,768]{2,1,0:T(8,128)} %copy-done.7) | copy-start | bytes 5898244
  52.3 9.5 %collective-permute-start.10 = (bf16[320,1664]{1,0:T(8,128)(2,1)S(1)}, bf16[320,1664]{1,0:T(8,128)(2,1)S(1)}, u32[]{:S(2)}, u32[]{:S(2)}) collective-permute-start(bf16[320,1664]{1,0:T(8,128)(2,1)S(1)} %fusion.2), channel_id=1, source_target_pairs={{0,1},{1,0},{2,3},{3,2},{4,5},{5,4},{6,7},{7,6},{8,9},{9,8},{10,11... | collective-permute-start | bytes 3194888 | tf_op jit(solution)/shard_map/ppermute | solution.py:31
  52.5 8.8 %collective-permute-start.12 = (bf16[160,1536]{1,0:T(8,128)(2,1)S(1)}, bf16[160,1536]{1,0:T(8,128)(2,1)S(1)}, u32[]{:S(2)}, u32[]{:S(2)}) collective-permute-start(bf16[160,1536]{1,0:T(8,128)(2,1)S(1)} %stack_rows.15.refs_0_), channel_id=1, source_target_pairs={{0,2},{1,5},{2,0},{3,7},{4,6},{5,1},{6,4},{7,3},{8,10},{9,13},{10,... | collective-permute-start | bytes 1474568 | tf_op jit(solution)/shard_map/ppermute | solution.py:31
  52.5 8.9 %collective-permute-start.11 = (bf16[40,1536]{1,0:T(8,128)(2,1)S(1)}, bf16[40,1536]{1,0:T(8,128)(2,1)S(1)}, u32[]{:S(2)}, u32[]{:S(2)}) collective-permute-start(bf16[40,1536]{1,0:T(8,128)(2,1)S(1)} %get-tuple-element.83), channel_id=1, source_target_pairs={{0,8},{1,9},{2,10},{3,11},{4,12},{5,13},{6,14},{7,15},{8,0},{9,1},... | collective-permute-start | bytes 368648 | tf_op jit(solution)/shard_map/ppermute | solution.py:37
  52.9 14.1 %collective-permute-start.9 = (bf16[160,1664]{1,0:T(8,128)(2,1)S(1)}, bf16[160,1664]{1,0:T(8,128)(2,1)S(1)}, u32[]{:S(2)}, u32[]{:S(2)}) collective-permute-start(bf16[160,1664]{1,0:T(8,128)(2,1)S(1)} %get-tuple-element.74), channel_id=1, source_target_pairs={{0,2},{1,5},{2,0},{3,7},{4,6},{5,1},{6,4},{7,3},{8,10},{9,13},{10,... | collective-permute-start | bytes 1597448 | tf_op jit(solution)/shard_map/ppermute | solution.py:31
  61.4 10.5 %collective-permute-start.15 = (bf16[40,1536]{1,0:T(8,128)(2,1)S(1)}, bf16[40,1536]{1,0:T(8,128)(2,1)S(1)}, u32[]{:S(2)}, u32[]{:S(2)}) collective-permute-start(bf16[40,1536]{1,0:T(8,128)(2,1)S(1)} %get-tuple-element.61), channel_id=1, source_target_pairs={{0,8},{1,9},{2,10},{3,11},{4,12},{5,13},{6,14},{7,15},{8,0},{9,1},... | collective-permute-start | bytes 368648 | tf_op jit(solution)/shard_map/ppermute | solution.py:37
  62.0 10.7 %collective-permute-start.17 = (bf16[160,1664]{1,0:T(8,128)(2,1)S(1)}, bf16[160,1664]{1,0:T(8,128)(2,1)S(1)}, u32[]{:S(2)}, u32[]{:S(2)}) collective-permute-start(bf16[160,1664]{1,0:T(8,128)(2,1)S(1)} %get-tuple-element.73), channel_id=1, source_target_pairs={{0,2},{1,5},{2,0},{3,7},{4,6},{5,1},{6,4},{7,3},{8,10},{9,13},{10,... | collective-permute-start | bytes 1597448 | tf_op jit(solution)/shard_map/ppermute | solution.py:31
  72.8 14.4 %collective-permute-start.19 = (bf16[80,1664]{1,0:T(8,128)(2,1)S(1)}, bf16[80,1664]{1,0:T(8,128)(2,1)S(1)}, u32[]{:S(2)}, u32[]{:S(2)}) collective-permute-start(bf16[80,1664]{1,0:T(8,128)(2,1)S(1)} %add_convert_fusion.6), channel_id=1, source_target_pairs={{0,4},{1,3},{2,6},{3,1},{4,0},{5,7},{6,2},{7,5},{8,12},{9,11},{10,... | collective-permute-start | bytes 798728 | tf_op jit(solution)/shard_map/ppermute | solution.py:31
  73.5 9.4 %collective-permute-start.16 = (bf16[80,1536]{1,0:T(8,128)(2,1)S(1)}, bf16[80,1536]{1,0:T(8,128)(2,1)S(1)}, u32[]{:S(2)}, u32[]{:S(2)}) collective-permute-start(bf16[80,1536]{1,0:T(8,128)(2,1)S(1)} %maximum_bitcast_fusion.refs_0_), channel_id=1, source_target_pairs={{0,4},{1,3},{2,6},{3,1},{4,0},{5,7},{6,2},{7,5},{8,12},{9,11},{10,... | collective-permute-start | bytes 737288 | tf_op jit(solution)/shard_map/ppermute | solution.py:31
  82.9 9.0 %collective-permute-start.18 = (bf16[160,1536]{1,0:T(8,128)(2,1)S(1)}, bf16[160,1536]{1,0:T(8,128)(2,1)S(1)}, u32[]{:S(2)}, u32[]{:S(2)}) collective-permute-start(bf16[160,1536]{1,0:T(8,128)(2,1)S(1)} %stack_rows.24.refs_0_), channel_id=1, source_target_pairs={{0,2},{1,5},{2,0},{3,7},{4,6},{5,1},{6,4},{7,3},{8,10},{9,13},{10,... | collective-permute-start | bytes 1474568 | tf_op jit(solution)/shard_map/ppermute | solution.py:31
  83.0 13.1 %collective-permute-start.14 = (bf16[320,1536]{1,0:T(8,128)(2,1)S(1)}, bf16[320,1536]{1,0:T(8,128)(2,1)S(1)}, u32[]{:S(2)}, u32[]{:S(2)}) collective-permute-start(bf16[320,1536]{1,0:T(8,128)(2,1)S(1)} %stack_rows.21.refs_0_), channel_id=1, source_target_pairs={{0,1},{1,0},{2,3},{3,2},{4,5},{5,4},{6,7},{7,6},{8,9},{9,8},{10,11... | collective-permute-start | bytes 2949128 | tf_op jit(solution)/shard_map/ppermute | solution.py:31
  91.9 4.9 %collective-permute-start.20 = (bf16[320,1536]{1,0:T(8,128)(2,1)S(1)}, bf16[320,1536]{1,0:T(8,128)(2,1)S(1)}, u32[]{:S(2)}, u32[]{:S(2)}) collective-permute-start(bf16[320,1536]{1,0:T(8,128)(2,1)S(1)} %stack_rows.25.refs_2_), channel_id=1, source_target_pairs={{0,1},{1,0},{2,3},{3,2},{4,5},{5,4},{6,7},{7,6},{8,9},{9,8},{10,11... | collective-permute-start | bytes 2949128 | tf_op jit(solution)/shard_map/ppermute | solution.py:31
  94.8 15.3 %collective-permute-start.13 = (bf16[80,1664]{1,0:T(8,128)(2,1)S(1)}, bf16[80,1664]{1,0:T(8,128)(2,1)S(1)}, u32[]{:S(2)}, u32[]{:S(2)}) collective-permute-start(bf16[80,1664]{1,0:T(8,128)(2,1)S(1)} %get-tuple-element.80), channel_id=1, source_target_pairs={{0,4},{1,3},{2,6},{3,1},{4,0},{5,7},{6,2},{7,5},{8,12},{9,11},{10,... | collective-permute-start | bytes 798728 | tf_op jit(solution)/shard_map/ppermute | solution.py:31
  95.5 14.6 %collective-permute-start.21 = (bf16[80,1664]{1,0:T(8,128)(2,1)S(1)}, bf16[80,1664]{1,0:T(8,128)(2,1)S(1)}, u32[]{:S(2)}, u32[]{:S(2)}) collective-permute-start(bf16[80,1664]{1,0:T(8,128)(2,1)S(1)} %add_convert_fusion.4), channel_id=1, source_target_pairs={{0,8},{1,9},{2,10},{3,11},{4,12},{5,13},{6,14},{7,15},{8,0},{9,1},... | collective-permute-start | bytes 798728 | tf_op jit(solution)/shard_map/ppermute | solution.py:37

commit v7 on v6

--- a/solution.py
+++ b/solution.py
@@ -9,7 +9,7 @@
 
 SPLIT = 8
 CORE, LOW, HIGH = 1, 2, 4
-LANES = 128
+LANES, TILE = 128, 256
 VMEM = pl.BlockSpec(memory_space=pltpu.VMEM)
 F32, BF16 = jnp.float32, jnp.bfloat16
 
@@ -64,7 +64,7 @@
     from_expert = my_expert - 1 - block % (experts - 1)
     from_expert = jnp.where(from_expert < 0, from_expert + experts, from_expert)
     near = my_expert * SPLIT + place(block[:SPLIT])
-    return near, from_expert * SPLIT + place(block // (experts - 1))
+    return jnp.concatenate([near, from_expert * SPLIT + place(block // (experts - 1))])
 
 
 def pack_routing(expert_id, dropped, slot, gate, slots):
@@ -155,7 +155,7 @@
         cdf = 0.5 * (1.0 + lax.erf(h * 0.7071067811865476))
         density = jnp.exp(-0.5 * h * h) * 0.3989422804014327
         activated[0, at, :] = (h * cdf).astype(BF16)
-        slope[0, at, :] = cdf + h * density
+        slope[0, at, :] = (cdf + h * density).astype(BF16)
         return carry
 
     lax.fori_loop(0, rows // step, chunk, 0)
@@ -165,7 +165,6 @@
     _, slots, units = by_source.shape
     block = (1, slots, units)
     shape = (order.shape[0], slots, units)
-    size = order.shape[0] * slots * units
     act, slope = pl.pallas_call(
         activation_kernel,
         grid_spec=pltpu.PrefetchScalarGridSpec(
@@ -174,9 +173,9 @@
             in_specs=[pl.BlockSpec(block, lambda i, order: (order[i], 0, 0))],
             out_specs=[pl.BlockSpec(block, lambda i, order: (i, 0, 0))] * 2,
         ),
-        out_shape=(jax.ShapeDtypeStruct(shape, BF16), jax.ShapeDtypeStruct(shape, F32)),
+        out_shape=(jax.ShapeDtypeStruct(shape, BF16),) * 2,
         compiler_params=params(6),
-        cost_estimate=cost(size, size),
+        cost_estimate=cost(0, 0),
         name="activation",
     )(order, by_source)
     return act.reshape(-1, units), slope.reshape(-1, units)
@@ -233,16 +232,41 @@
     return lax.dot_general(a, b, (dims, ((), ())), preferred_element_type=F32)
 
 
-def hidden_part(grads, w_out, act, slope):
-    grad_act = product(grads, w_out, ((1,), (1,)))
-    gates = jnp.sum(grad_act * act.astype(F32), axis=1, keepdims=True)
-    return (grad_act * slope).astype(BF16), gates
-
-
-def slot_part(hidden_grad, gates, w_in):
-    part = product(hidden_grad, w_in, ((1,), (1,))).astype(BF16)
-    gates = jnp.broadcast_to(gates, (gates.shape[0], LANES)).astype(BF16)
-    return halves(jnp.concatenate([part, gates], axis=1))
+def slot_grad_kernel(grads, w_out, w_in, act, slope, hidden_grad, kept, sent):
+    rows, units = act.shape
+    width, half = grads.shape[1], rows // 2
+    gates = jnp.zeros((rows, 1), F32)
+    for j in range(units // TILE):
+        at = slice(j * TILE, (j + 1) * TILE)
+        grad_act = product(grads[...], w_out[at, :], ((1,), (1,)))
+        hidden_grad[:, at] = (grad_act * slope[:, at].astype(F32)).astype(BF16)
+        gates += jnp.sum(grad_act * act[:, at].astype(F32), axis=1, keepdims=True)
+    gates = jnp.broadcast_to(gates, (rows, LANES)).astype(BF16)
+    kept[:, width:] = gates[:half]
+    sent[:, width:] = gates[half:]
+    for j in range(width // TILE):
+        at = slice(j * TILE, (j + 1) * TILE)
+        part = product(hidden_grad[...], w_in[at, :], ((1,), (1,))).astype(BF16)
+        kept[:, at] = part[:half]
+        sent[:, at] = part[half:]
+
+
+def slot_grads(grads, w_out, w_in, act, slope):
+    rows, units = act.shape
+    wide = w_in.shape[0] + LANES
+    return pl.pallas_call(
+        slot_grad_kernel,
+        out_shape=(
+            jax.ShapeDtypeStruct((rows, units), BF16),
+            jax.ShapeDtypeStruct((rows // 2, wide), BF16),
+            jax.ShapeDtypeStruct((rows // 2, wide), BF16),
+        ),
+        in_specs=[VMEM] * 5,
+        out_specs=(VMEM, VMEM, VMEM),
+        compiler_params=params(16 + rows // 64),
+        cost_estimate=cost(0, 0),
+        name="slot_grads",
+    )(grads, w_out, w_in, act, slope)
 
 
 def body(tokens, out_grad, gate, expert_id, dropped, slot, saved_hidden, w_in, w_out):
@@ -252,20 +276,20 @@
     units = saved_hidden.shape[1]
     me = lax.axis_index("expert")
     place, gate = pack_routing(expert_id, dropped, slot, gate, slots)
-    near_order, far_order = sources_met(me, experts)
+    order = sources_met(me, experts)
     by_source = saved_hidden.reshape(devices, slots, units)
+    near_count = SPLIT * slots
 
     near_grad, far_grad = to_slots(slots, True, place, gate, out_grad)
     near_row, far_row = to_slots(slots, False, place, gate, tokens)
 
     far_grad = cross(far_grad, 1)
     got = meet(near_grad, 0)
-    near_act, near_slope = activation(by_source, near_order)
-    far_act, far_slope = activation(by_source, far_order)
-    near_two = join(near_grad, after(got, near_act, far_act, near_row))
+    near_two = join(near_grad, after(got, near_row))
     got = meet(near_two, 1)
     row_got = meet(after(near_row, near_two), 0)
-    far_grad = after(far_grad, near_two)
+    act, slope = activation(by_source, after(order, near_two))
+    far_grad = after(far_grad, act)
     far_got = meet(far_grad, 0)
     near_row2 = join(near_row, after(row_got, far_grad))
     far_two = join(far_grad, after(far_got, near_row2))
@@ -273,40 +297,42 @@
     near_four = join(near_two, after(got, far_two))
     got = meet(near_four, 2)
 
+    far_row_a, far_row_b = split_slots(after(far_row, far_two), experts)
+    far_row_a = cross(far_row_a, 1)
     near_grads = join(near_four, got)
-    near_hg, near_gates = hidden_part(near_grads, w_out, near_act, near_slope)
-    near_kept, near_sent = slot_part(near_hg, near_gates, w_in)
+    near_hg, near_kept, near_sent = slot_grads(
+        near_grads, w_out, w_in, act[:near_count], slope[:near_count]
+    )
     near_got = meet(near_sent, 2)
-    far_four = join(far_two, after(far_got, near_sent))
+    far_row_a = after(far_row_a, near_sent)
+    far_four = join(far_two, after(far_got, far_row_a))
     far_got = meet(far_four, 2)
-    far_row_a, far_row_b = split_slots(after(far_row, far_four), experts)
-    far_row_a = cross(far_row_a, 1)
+    far_row_b = cross(after(far_row_b, far_four), 1)
     row_got = meet(after(near_row2, far_four), 1)
     far_grads = join(far_four, far_got)
-    near_kept, near_sent = add_halves(near_kept, after(near_got, far_grads))
+
+    far_hg, far_kept, far_sent = slot_grads(
+        far_grads, w_out, w_in, act[near_count:], slope[near_count:]
+    )
+    far_row = join_slots(far_row_a, after(far_row_b, far_sent), experts)
+    near_row4 = join(near_row2, after(row_got, far_row))
+    near_kept, near_sent = add_halves(near_kept, after(near_got, near_row4))
+    far_got = meet(after(far_sent, near_sent), 2)
+    far_row_got = meet(far_row, 0)
+    row_got = meet(near_row4, 2)
     near_got = meet(near_sent, 1)
-    far_grads = after(far_grads, near_sent)
-
-    far_hg, far_gates = hidden_part(far_grads, w_out, far_act, far_slope)
-    far_kept, far_sent = slot_part(far_hg, far_gates, w_in)
-    far_got = meet(far_sent, 2)
-    near_row4 = join(near_row2, after(row_got, far_sent))
-    row_got = meet(near_row4, 2)
-    far_row_a = after(far_row_a, near_row4)
-    far_row_b = cross(after(far_row_b, far_row_a), 1)
-    far_kept, far_sent = add_halves(far_kept, after(far_got, far_row_a))
+    far_kept, far_sent = add_halves(far_kept, far_got)
     far_got = meet(far_sent, 1)
+    w_out_grad = product(
+        after(act, far_sent), join(near_grads, far_grads), ((0,), (0,))
+    ).astype(BF16)
+    far_row2 = join(far_row, after(far_row_got, w_out_grad))
+    far_row_got = meet(far_row2, 1)
+    far_kept, far_sent = add_halves(far_kept, after(far_got, far_row2))
+    far_got = meet(far_sent, 0)
     near_kept, near_sent = add_halves(near_kept, after(near_got, far_sent))
     near_got = meet(near_sent, 0)
-    acts = join(after(near_act, near_sent), far_act)
-    w_out_grad = product(acts, join(near_grads, far_grads), ((0,), (0,))).astype(BF16)
-    far_row = join_slots(far_row_a, after(far_row_b, w_out_grad), experts)
-    far_row_got = meet(far_row, 0)
-    far_kept, far_sent = add_halves(far_kept, after(far_got, far_row))
-    far_got = meet(far_sent, 0)
-    far_row2 = join(far_row, after(far_row_got, far_sent))
-    far_row_got = meet(far_row2, 1)
-    far_sum = add(far_kept, after(far_got, far_row2))
+    far_sum = add(far_kept, after(far_got, near_sent))
     back = cross(far_sum, -1)
     far_row4 = join(far_row2, after(far_row_got, far_sum))
     rows = join(near_row4, row_got, far_row4, meet(far_row4, 2))

time: 112 us -> 95.2 us (0.85)
  waiting for transfers between devices: 49.2 us -> 31.5 us
  matrix products: 16.5 us -> 9.13 us
  starting transfers between devices: 24.3 us -> 31 us
  Pallas kernels: 9.82 us -> 14.3 us
  local copies, waits for them, and re-layouts: 8.59 us -> 6.5 us
    ppermute x18, waiting for transfers between devices: 40.9 us -> 24.7 us  [meet(): lax.ppermute(rows, 'expert', [(i, i ^ bits(i % 2)[step]) for i in range(d...]
    pallas_call x0 -> x2, Pallas kernels: none -> 7.82 us  [slot_grads(): pl.pallas_call(slot_grad_kernel, out_shape=(jax.ShapeDtypeStruct((rows, u...]
    dot_general x6 -> x2, matrix products: 16.5 us -> 9.13 us  [product(): return lax.dot_general(a, b, (dims, ((), ())), preferred_element_type=F32)]
    ppermute x4, starting transfers between devices: 3.93 us -> 8.31 us  [shift(): return lax.ppermute(rows, 'expert', pairs)]
    ppermute x18, starting transfers between devices: 20.3 us -> 22.7 us  [meet(): lax.ppermute(rows, 'expert', [(i, i ^ bits(i % 2)[step]) for i in range(d...]
    pallas_call x14 -> x13, Pallas kernels: 3.42 us -> 1.29 us  [join(): pl.pallas_call(stack_kernel, out_shape=jax.ShapeDtypeStruct((rows, width)...]
    unnamed x20 -> x14, local copies, waits for them, and re-layouts: 8.28 us -> 6.17 us
    ppermute x4, waiting for transfers between devices: 8.37 us -> 6.79 us  [shift(): return lax.ppermute(rows, 'expert', pairs)]
  transfers between devices with their start and end apart: 22 -> 22, of which waited for: 13 -> 9; matrix products, arithmetic and copies ran while one was open for 12% -> 11% of each run, Pallas kernels for 7% -> 13%
where the time goes in v7:
time: 95.2 us; the launch traced here: 95 us
  waiting for transfers between devices  31.5 us (33%)
  starting transfers between devices  31 us (33%)
  Pallas kernels  14.3 us (15%)
  matrix products  9.13 us (10%)
  local copies, waits for them, and re-layouts  6.5 us (7%)
  other arithmetic  1.65 us (2%)
    ppermute x18, waiting for transfers between devices, meet(): lax.ppermute(rows, 'expert', [(i, i ^ bits(i % 2)[step]) for i in range(d...  24.7 us
    ppermute x18, starting transfers between devices, meet(): lax.ppermute(rows, 'expert', [(i, i ^ bits(i % 2)[step]) for i in range(d...  22.7 us
    dot_general x2, matrix products, product(): return lax.dot_general(a, b, (dims, ((), ())), preferred_element_type=F32)  9.13 us
    ppermute x4, starting transfers between devices, shift(): return lax.ppermute(rows, 'expert', pairs)  8.31 us
    pallas_call x2, Pallas kernels, slot_grads(): pl.pallas_call(slot_grad_kernel, out_shape=(jax.ShapeDtypeStruct((rows, u...  7.82 us
    ppermute x4, waiting for transfers between devices, shift(): return lax.ppermute(rows, 'expert', pairs)  6.79 us
    unnamed x14, local copies, waits for them, and re-layouts  6.17 us
    pallas_call x1, Pallas kernels, activation(): pl.pallas_call(activation_kernel, grid_spec=pltpu.PrefetchScalarGridSpec(...  3.36 us
  transfers between devices with their start and end apart: 22, of which 9 were waited for; matrix products, arithmetic and copies ran while one was open for 11% of the time, Pallas kernels for 13%

profile of v7, /device:TPU:0, one launch (start us, length us, event | category | flops | bytes accessed | tf_op | source)
XLA Modules:
  0.0 95.0 jit_solution(8630270845605025534)
XLA Ops:
  0.6 0.7 fusion.place
  1.3 1.0 %copy-done.3 = bf16[128,1536]{1,0:T(8,128)(2,1)S(1)} copy-done((bf16[128,1536]{1,0:T(8,128)(2,1)S(1)}, bf16[128,1536]{1,0:T(8,128)(2,1)}, u32[]{:S(2)}) %copy-start.3) | copy-done | bytes 393240
  2.3 0.7 copy-done.5
  3.0 0.4 rows_to_slots.2
  3.4 3.1 %collective-permute-start = (bf16[80,1536]{1,0:T(8,128)(2,1)S(1)}, bf16[80,1536]{1,0:T(8,128)(2,1)S(1)}, u32[]{:S(2)}, u32[]{:S(2)}) collective-permute-start(bf16[80,1536]{1,0:T(8,128)(2,1)S(1)} %get-tuple-element.42.refs_0_), channel_id=1, source_target_pairs={{0,4},{1,3},{2,6},{3,1},{4,0},{5,7},{6,2},{7,5},{8,12},{9,11},{10,... | collective-permute-start | bytes 737288 | tf_op jit(solution)/shard_map/ppermute | solution.py:31
  6.5 2.6 %collective-permute-start.2 = (bf16[80,1536]{1,0:T(8,128)(2,1)S(1)}, bf16[80,1536]{1,0:T(8,128)(2,1)S(1)}, u32[]{:S(2)}, u32[]{:S(2)}) collective-permute-start(bf16[80,1536]{1,0:T(8,128)(2,1)S(1)} %get-tuple-element.45), channel_id=1, source_target_pairs={{0,8},{1,9},{2,10},{3,11},{4,12},{5,13},{6,14},{7,15},{8,0},{9,1},... | collective-permute-start | bytes 737288 | tf_op jit(solution)/shard_map/ppermute | solution.py:37
  9.0 1.0 %copy-done.4 = bf16[128,1536]{1,0:T(8,128)(2,1)S(1)} copy-done((bf16[128,1536]{1,0:T(8,128)(2,1)S(1)}, bf16[128,1536]{1,0:T(8,128)(2,1)}, u32[]{:S(2)}) %copy-start.4) | copy-done | bytes 393240
  10.0 0.3 rows_to_slots.3
  10.3 2.4 %collective-permute-done.refs_1_ = bf16[80,1536]{1,0:T(8,128)(2,1)S(1)} collective-permute-done((bf16[80,1536]{1,0:T(8,128)(2,1)S(1)}, bf16[80,1536]{1,0:T(8,128)(2,1)S(1)}, u32[]{:S(2)}, u32[]{:S(2)}) %collective-permute-start) | collective-permute-done | bytes 245792 | tf_op jit(solution)/shard_map/ppermute | solution.py:31
  12.8 4.4 %collective-permute-start.1 = (bf16[160,1536]{1,0:T(8,128)(2,1)S(1)}, bf16[160,1536]{1,0:T(8,128)(2,1)S(1)}, u32[]{:S(2)}, u32[]{:S(2)}) collective-permute-start(bf16[160,1536]{1,0:T(8,128)(2,1)S(1)} %stack_rows.13.refs_0_), channel_id=1, source_target_pairs={{0,2},{1,5},{2,0},{3,7},{4,6},{5,1},{6,4},{7,3},{8,10},{9,13},{10,... | collective-permute-start | bytes 1474568 | tf_op jit(solution)/shard_map/ppermute | solution.py:31
  17.2 0.1 pad_add_fusion.order
  17.3 0.0 collective-permute-start.4
  17.3 0.0 copy-start.2
  17.3 1.5 %copy-done.2 = bf16[1280,768]{1,0:T(8,128)(2,1)S(1)} copy-done((bf16[1280,768]{1,0:T(8,128)(2,1)S(1)}, bf16[1280,768]{1,0:T(8,128)(2,1)}, u32[]{:S(2)}) %copy-start.2) | copy-done | bytes 1966104
  18.8 3.4 %activation.1 = (bf16[16,80,768]{2,1,0:T(8,128)(2,1)S(1)}, bf16[16,80,768]{2,1,0:T(8,128)(2,1)S(1)}) custom-call(s32[16]{0:T(128)S(1)} %pad_add_fusion.order, bf16[16,80,768]{2,1,0:T(8,128)(2,1)S(1)} %bitcast.27), custom_call_target="tpu_custom_call" | custom-call | tf_op jit(solution)/shard_map/activation/pallas_call | solution.py:168
  22.2 2.1 %collective-permute-start.3 = (bf16[80,1536]{1,0:T(8,128)(2,1)S(1)}, bf16[80,1536]{1,0:T(8,128)(2,1)S(1)}, u32[]{:S(2)}, u32[]{:S(2)}) collective-permute-start(bf16[80,1536]{1,0:T(8,128)(2,1)S(1)} %collective-permute-done.2.refs_0_), channel_id=1, source_target_pairs={{0,4},{1,3},{2,6},{3,1},{4,0},{5,7},{6,2},{7,5},{8,12},{9,11},{10,... | collective-permute-start | bytes 737288 | tf_op jit(solution)/shard_map/ppermute | solution.py:31
  24.3 4.1 %collective-permute-done.3.refs_1_ = bf16[80,1536]{1,0:T(8,128)(2,1)S(1)} collective-permute-done((bf16[80,1536]{1,0:T(8,128)(2,1)S(1)}, bf16[80,1536]{1,0:T(8,128)(2,1)S(1)}, u32[]{:S(2)}, u32[]{:S(2)}) %collective-permute-start.3) | collective-permute-done | bytes 245792 | tf_op jit(solution)/shard_map/ppermute | solution.py:31
  28.5 0.1 stack_rows.16.refs_0_
  28.6 0.1 collective-permute-start.5
  28.7 0.2 collective-permute-start.7
  28.9 2.9 %collective-permute-start.8 = (bf16[40,1536]{1,0:T(8,128)(2,1)S(1)}, bf16[40,1536]{1,0:T(8,128)(2,1)S(1)}, u32[]{:S(2)}, u32[]{:S(2)}) collective-permute-start(bf16[40,1536]{1,0:T(8,128)(2,1)S(1)} %get-tuple-element.91), channel_id=1, source_target_pairs={{0,8},{1,9},{2,10},{3,11},{4,12},{5,13},{6,14},{7,15},{8,0},{9,1},... | collective-permute-start | bytes 368648 | tf_op jit(solution)/shard_map/ppermute | solution.py:37
  31.8 0.3 fusion.3
  32.1 0.0 copy-start
  32.1 0.1 stack_rows.17.grads.refs_0_
  32.3 1.2 %copy-done.1 = bf16[1536,768]{1,0:T(8,128)(2,1)S(1)} copy-done((bf16[1536,768]{1,0:T(8,128)(2,1)S(1)}, bf16[1536,768]{1,0:T(8,128)(2,1)}, u32[]{:S(2)}) %copy-start.1) | copy-done | bytes 2359320
  33.4 0.8 copy-done
  34.2 3.9 %slot_grads.2 = (bf16[640,768]{1,0:T(8,128)(2,1)S(1)}, bf16[320,1664]{1,0:T(8,128)(2,1)S(1)}, bf16[320,1664]{1,0:T(8,128)(2,1)S(1)}) custom-call(bf16[640,1536]{1,0:T(8,128)(2,1)S(1)} %stack_rows.17.grads.refs_0_, bf16[768,1536]{1,0:T(8,128)(2,1)S(1)} %copy-done, bf16[1536,768]{1,0:T(8,128)(2,1)S(1)} %copy-done.1, bf16[640,768]{1,0:T(8,128)(2,1)S(1)} %bitcast.26, ...), custom_call_target="tpu_custom_call" | custom-call | tf_op jit(solution)/shard_map/slot_grads/pallas_call | solution.py:257
  38.2 0.1 stack_rows.18.refs_0_
  38.2 1.6 %collective-permute-start.11 = (bf16[320,1536]{1,0:T(8,128)(2,1)S(1)}, bf16[320,1536]{1,0:T(8,128)(2,1)S(1)}, u32[]{:S(2)}, u32[]{:S(2)}) collective-permute-start(bf16[320,1536]{1,0:T(8,128)(2,1)S(1)} %stack_rows.18.refs_0_), channel_id=1, source_target_pairs={{0,1},{1,0},{2,3},{3,2},{4,5},{5,4},{6,7},{7,6},{8,9},{9,8},{10,11... | collective-permute-start | bytes 2949128 | tf_op jit(solution)/shard_map/ppermute | solution.py:31
  39.9 0.1 collective-permute-start.6
  40.0 0.9 collective-permute-start.9
  40.8 1.8 %collective-permute-start.10 = (bf16[40,1536]{1,0:T(8,128)(2,1)S(1)}, bf16[40,1536]{1,0:T(8,128)(2,1)S(1)}, u32[]{:S(2)}, u32[]{:S(2)}) collective-permute-start(bf16[40,1536]{1,0:T(8,128)(2,1)S(1)} %get-tuple-element.61), channel_id=1, source_target_pairs={{0,8},{1,9},{2,10},{3,11},{4,12},{5,13},{6,14},{7,15},{8,0},{9,1},... | collective-permute-start | bytes 368648 | tf_op jit(solution)/shard_map/ppermute | solution.py:37
  42.6 0.1 stack_rows.19.grads.refs_1_
  42.8 3.9 %slot_grads.3 = (bf16[640,768]{1,0:T(8,128)(2,1)S(1)}, bf16[320,1664]{1,0:T(8,128)(2,1)S(1)}, bf16[320,1664]{1,0:T(8,128)(2,1)S(1)}) custom-call(bf16[640,1536]{1,0:T(8,128)(2,1)S(1)} %stack_rows.19.grads.refs_1_, bf16[768,1536]{1,0:T(8,128)(2,1)S(1)} %copy-done, bf16[1536,768]{1,0:T(8,128)(2,1)S(1)} %copy-done.1, bf16[640,768]{1,0:T(8,128)(2,1)S(1)} %bitcast.24, ...), custom_call_target="tpu_custom_call" | custom-call | tf_op jit(solution)/shard_map/slot_grads/pallas_call | solution.py:257
  46.7 0.7 collective-permute-done.10
  47.4 1.4 %collective-permute-done.9.refs_1_ = bf16[160,1536]{1,0:T(8,128)(2,1)S(1)} collective-permute-done((bf16[160,1536]{1,0:T(8,128)(2,1)S(1)}, bf16[160,1536]{1,0:T(8,128)(2,1)S(1)}, u32[]{:S(2)}, u32[]{:S(2)}) %collective-permute-start.9) | collective-permute-done | bytes 491552 | tf_op jit(solution)/shard_map/ppermute | solution.py:31
  48.8 0.1 stack_rows.20.refs_0_
  48.9 0.2 add_convert_fusion.2
  49.1 2.9 %collective-permute-start.13 = (bf16[320,1664]{1,0:T(8,128)(2,1)S(1)}, bf16[320,1664]{1,0:T(8,128)(2,1)S(1)}, u32[]{:S(2)}, u32[]{:S(2)}) collective-permute-start(bf16[320,1664]{1,0:T(8,128)(2,1)S(1)} %get-tuple-element.67), channel_id=1, source_target_pairs={{0,1},{1,0},{2,3},{3,2},{4,5},{5,4},{6,7},{7,6},{8,9},{9,8},{10,11... | collective-permute-start | bytes 3194888 | tf_op jit(solution)/shard_map/ppermute | solution.py:31
  52.0 1.8 %collective-permute-start.15 = (bf16[80,1536]{1,0:T(8,128)(2,1)S(1)}, bf16[80,1536]{1,0:T(8,128)(2,1)S(1)}, u32[]{:S(2)}, u32[]{:S(2)}) collective-permute-start(bf16[80,1536]{1,0:T(8,128)(2,1)S(1)} %maximum_bitcast_fusion.refs_0_), channel_id=1, source_target_pairs={{0,4},{1,3},{2,6},{3,1},{4,0},{5,7},{6,2},{7,5},{8,12},{9,11},{10,... | collective-permute-start | bytes 737288 | tf_op jit(solution)/shard_map/ppermute | solution.py:31
  53.8 0.3 stack_rows.21
  54.1 0.1 collective-permute-start.17
  54.1 0.1 collective-permute-start.12
  54.2 0.1 collective-permute-done.13
  54.3 0.3 add_convert_fusion
  54.6 2.0 %collective-permute-start.14 = (bf16[160,1664]{1,0:T(8,128)(2,1)S(1)}, bf16[160,1664]{1,0:T(8,128)(2,1)S(1)}, u32[]{:S(2)}, u32[]{:S(2)}) collective-permute-start(bf16[160,1664]{1,0:T(8,128)(2,1)S(1)} %get-tuple-element.80), channel_id=1, source_target_pairs={{0,2},{1,5},{2,0},{3,7},{4,6},{5,1},{6,4},{7,3},{8,10},{9,13},{10,... | collective-permute-start | bytes 1597448 | tf_op jit(solution)/shard_map/ppermute | solution.py:31
  56.6 4.5 %convolution_convert_fusion.1 = bf16[768,1536]{1,0:T(8,128)(2,1)} fusion(bf16[1280,768]{1,0:T(8,128)(2,1)S(1)} %bitcast.28, bf16[1280,1536]{1,0:T(8,128)(2,1)S(1)} %stack_rows.21), kind=kOutput, calls=%fused_computation.1 | convolution fusion | flops 3021078528 | bytes 8257536 | tf_op jit(solution)/shard_map/dot_general | solution.py:232
  61.2 0.2 collective-permute-start.18
  61.4 7.8 %collective-permute-done.14 = bf16[160,1664]{1,0:T(8,128)(2,1)S(1)} collective-permute-done((bf16[160,1664]{1,0:T(8,128)(2,1)S(1)}, bf16[160,1664]{1,0:T(8,128)(2,1)S(1)}, u32[]{:S(2)}, u32[]{:S(2)}) %collective-permute-start.14) | collective-permute-done | bytes 532512 | tf_op jit(solution)/shard_map/ppermute | solution.py:31
  69.2 0.1 add_convert_fusion.8
  69.3 1.4 %collective-permute-start.19 = (bf16[80,1664]{1,0:T(8,128)(2,1)S(1)}, bf16[80,1664]{1,0:T(8,128)(2,1)S(1)}, u32[]{:S(2)}, u32[]{:S(2)}) collective-permute-start(bf16[80,1664]{1,0:T(8,128)(2,1)S(1)} %add_convert_fusion.8), channel_id=1, source_target_pairs={{0,4},{1,3},{2,6},{3,1},{4,0},{5,7},{6,2},{7,5},{8,12},{9,11},{10,... | collective-permute-start | bytes 798728 | tf_op jit(solution)/shard_map/ppermute | solution.py:31
  70.7 0.1 add_convert_fusion.6
  70.8 7.0 %collective-permute-done.19 = bf16[80,1664]{1,0:T(8,128)(2,1)S(1)} collective-permute-done((bf16[80,1664]{1,0:T(8,128)(2,1)S(1)}, bf16[80,1664]{1,0:T(8,128)(2,1)S(1)}, u32[]{:S(2)}, u32[]{:S(2)}) %collective-permute-start.19) | collective-permute-done | bytes 266272 | tf_op jit(solution)/shard_map/ppermute | solution.py:31
  77.8 0.1 add_convert_fusion.4
  77.9 0.1 stack_rows.23.refs_2_
  78.0 0.1 collective-permute-start.20
  78.1 0.1 stack_rows.25
  78.2 1.8 %collective-permute-start.16 = (bf16[80,1664]{1,0:T(8,128)(2,1)S(1)}, bf16[80,1664]{1,0:T(8,128)(2,1)S(1)}, u32[]{:S(2)}, u32[]{:S(2)}) collective-permute-start(bf16[80,1664]{1,0:T(8,128)(2,1)S(1)} %get-tuple-element.88), channel_id=1, source_target_pairs={{0,4},{1,3},{2,6},{3,1},{4,0},{5,7},{6,2},{7,5},{8,12},{9,11},{10,... | collective-permute-start | bytes 798728 | tf_op jit(solution)/shard_map/ppermute | solution.py:31
  80.0 1.0 %collective-permute-start.21 = (bf16[80,1664]{1,0:T(8,128)(2,1)S(1)}, bf16[80,1664]{1,0:T(8,128)(2,1)S(1)}, u32[]{:S(2)}, u32[]{:S(2)}) collective-permute-start(bf16[80,1664]{1,0:T(8,128)(2,1)S(1)} %add_convert_fusion.4), channel_id=1, source_target_pairs={{0,8},{1,9},{2,10},{3,11},{4,12},{5,13},{6,14},{7,15},{8,0},{9,1},... | collective-permute-start | bytes 798728 | tf_op jit(solution)/shard_map/ppermute | solution.py:37
  81.0 0.3 stack_rows.24
  81.3 4.6 %convolution_convert_fusion = bf16[1536,768]{1,0:T(8,128)(2,1)} fusion(bf16[1280,1536]{1,0:T(8,128)(2,1)S(1)} %stack_rows.24, bf16[1280,768]{1,0:T(8,128)(2,1)S(1)} %stack_rows.25), kind=kOutput, calls=%fused_computation | convolution fusion | flops 3021078528 | bytes 8257536 | tf_op jit(solution)/shard_map/dot_general | solution.py:232
  85.9 1.8 %collective-permute-done.16.got = bf16[80,1664]{1,0:T(8,128)(2,1)S(1)} collective-permute-done((bf16[80,1664]{1,0:T(8,128)(2,1)S(1)}, bf16[80,1664]{1,0:T(8,128)(2,1)S(1)}, u32[]{:S(2)}, u32[]{:S(2)}) %collective-permute-start.16) | collective-permute-done | bytes 266272 | tf_op jit(solution)/shard_map/ppermute | solution.py:31
  87.7 6.1 %collective-permute-done.21.back = bf16[80,1664]{1,0:T(8,128)(2,1)S(1)} collective-permute-done((bf16[80,1664]{1,0:T(8,128)(2,1)S(1)}, bf16[80,1664]{1,0:T(8,128)(2,1)S(1)}, u32[]{:S(2)}, u32[]{:S(2)}) %collective-permute-start.21) | collective-permute-done | bytes 266272 | tf_op jit(solution)/shard_map/ppermute | solution.py:37
  93.8 1.1 %slots_to_tokens.1 = (bf16[128,1536]{1,0:T(8,128)(2,1)}, f32[1,128]{1,0:T(1,128)}) custom-call(s32[1,128]{1,0:T(1,128)S(1)} %fusion.place, f32[1,128]{1,0:T(1,128)S(1)} %bitcast.32, bf16[80,1664]{1,0:T(8,128)(2,1)S(1)} %get-tuple-element.89.kept, bf16[80,1664]{1,0:T(8,128)(2,1)S(1)} %collective-permute-done.16.got, ...), custom_call_target="tpu_custom_call" | custom-call | tf_op jit(solution)/shard_map/slots_to_tokens/pallas_call | solution.py:135
  (27 shorter events, 0.2 us)
Async XLA Ops:
  1.3 1.0 %copy-start.3 = (bf16[128,1536]{1,0:T(8,128)(2,1)S(1)}, bf16[128,1536]{1,0:T(8,128)(2,1)}, u32[]{:S(2)}) copy-start(bf16[128,1536]{1,0:T(8,128)(2,1)} %values.2) | copy-start | bytes 1179652
  2.3 0.7 copy-start.5
  3.4 9.4 %collective-permute-start = (bf16[80,1536]{1,0:T(8,128)(2,1)S(1)}, bf16[80,1536]{1,0:T(8,128)(2,1)S(1)}, u32[]{:S(2)}, u32[]{:S(2)}) collective-permute-start(bf16[80,1536]{1,0:T(8,128)(2,1)S(1)} %get-tuple-element.42.refs_0_), channel_id=1, source_target_pairs={{0,4},{1,3},{2,6},{3,1},{4,0},{5,7},{6,2},{7,5},{8,12},{9,11},{10,... | collective-permute-start | bytes 737288 | tf_op jit(solution)/shard_map/ppermute | solution.py:31
  6.5 15.8 %collective-permute-start.2 = (bf16[80,1536]{1,0:T(8,128)(2,1)S(1)}, bf16[80,1536]{1,0:T(8,128)(2,1)S(1)}, u32[]{:S(2)}, u32[]{:S(2)}) collective-permute-start(bf16[80,1536]{1,0:T(8,128)(2,1)S(1)} %get-tuple-element.45), channel_id=1, source_target_pairs={{0,8},{1,9},{2,10},{3,11},{4,12},{5,13},{6,14},{7,15},{8,0},{9,1},... | collective-permute-start | bytes 737288 | tf_op jit(solution)/shard_map/ppermute | solution.py:37
  9.0 1.0 %copy-start.4 = (bf16[128,1536]{1,0:T(8,128)(2,1)S(1)}, bf16[128,1536]{1,0:T(8,128)(2,1)}, u32[]{:S(2)}) copy-start(bf16[128,1536]{1,0:T(8,128)(2,1)} %values.3) | copy-start | bytes 1179652
  12.8 15.7 %collective-permute-start.1 = (bf16[160,1536]{1,0:T(8,128)(2,1)S(1)}, bf16[160,1536]{1,0:T(8,128)(2,1)S(1)}, u32[]{:S(2)}, u32[]{:S(2)}) collective-permute-start(bf16[160,1536]{1,0:T(8,128)(2,1)S(1)} %stack_rows.13.refs_0_), channel_id=1, source_target_pairs={{0,2},{1,5},{2,0},{3,7},{4,6},{5,1},{6,4},{7,3},{8,10},{9,13},{10,... | collective-permute-start | bytes 1474568 | tf_op jit(solution)/shard_map/ppermute | solution.py:31
  17.3 7.0 %collective-permute-start.4 = (bf16[80,1536]{1,0:T(8,128)(2,1)S(1)}, bf16[80,1536]{1,0:T(8,128)(2,1)S(1)}, u32[]{:S(2)}, u32[]{:S(2)}) collective-permute-start(bf16[80,1536]{1,0:T(8,128)(2,1)S(1)} %get-tuple-element.49.refs_0_), channel_id=1, source_target_pairs={{0,4},{1,3},{2,6},{3,1},{4,0},{5,7},{6,2},{7,5},{8,12},{9,11},{10,... | collective-permute-start | bytes 737288 | tf_op jit(solution)/shard_map/ppermute | solution.py:31
  17.3 1.5 %copy-start.2 = (bf16[1280,768]{1,0:T(8,128)(2,1)S(1)}, bf16[1280,768]{1,0:T(8,128)(2,1)}, u32[]{:S(2)}) copy-start(bf16[1280,768]{1,0:T(8,128)(2,1)} %param.15) | copy-start | bytes 5898244
  22.2 6.3 %collective-permute-start.3 = (bf16[80,1536]{1,0:T(8,128)(2,1)S(1)}, bf16[80,1536]{1,0:T(8,128)(2,1)S(1)}, u32[]{:S(2)}, u32[]{:S(2)}) collective-permute-start(bf16[80,1536]{1,0:T(8,128)(2,1)S(1)} %collective-permute-done.2.refs_0_), channel_id=1, source_target_pairs={{0,4},{1,3},{2,6},{3,1},{4,0},{5,7},{6,2},{7,5},{8,12},{9,11},{10,... | collective-permute-start | bytes 737288 | tf_op jit(solution)/shard_map/ppermute | solution.py:31
  28.6 3.5 %collective-permute-start.5 = (bf16[320,1536]{1,0:T(8,128)(2,1)S(1)}, bf16[320,1536]{1,0:T(8,128)(2,1)S(1)}, u32[]{:S(2)}, u32[]{:S(2)}) collective-permute-start(bf16[320,1536]{1,0:T(8,128)(2,1)S(1)} %stack_rows.16.refs_0_), channel_id=1, source_target_pairs={{0,1},{1,0},{2,3},{3,2},{4,5},{5,4},{6,7},{7,6},{8,9},{9,8},{10,11... | collective-permute-start | bytes 2949128 | tf_op jit(solution)/shard_map/ppermute | solution.py:31
  28.7 9.5 %collective-permute-start.7 = (bf16[160,1536]{1,0:T(8,128)(2,1)S(1)}, bf16[160,1536]{1,0:T(8,128)(2,1)S(1)}, u32[]{:S(2)}, u32[]{:S(2)}) collective-permute-start(bf16[160,1536]{1,0:T(8,128)(2,1)S(1)} %stack_rows.15.refs_0_), channel_id=1, source_target_pairs={{0,2},{1,5},{2,0},{3,7},{4,6},{5,1},{6,4},{7,3},{8,10},{9,13},{10,... | collective-permute-start | bytes 1474568 | tf_op jit(solution)/shard_map/ppermute | solution.py:31
  28.9 9.3 %collective-permute-start.8 = (bf16[40,1536]{1,0:T(8,128)(2,1)S(1)}, bf16[40,1536]{1,0:T(8,128)(2,1)S(1)}, u32[]{:S(2)}, u32[]{:S(2)}) collective-permute-start(bf16[40,1536]{1,0:T(8,128)(2,1)S(1)} %get-tuple-element.91), channel_id=1, source_target_pairs={{0,8},{1,9},{2,10},{3,11},{4,12},{5,13},{6,14},{7,15},{8,0},{9,1},... | collective-permute-start | bytes 368648 | tf_op jit(solution)/shard_map/ppermute | solution.py:37
  31.8 1.7 %copy-start.1 = (bf16[1536,768]{1,0:T(8,128)(2,1)S(1)}, bf16[1536,768]{1,0:T(8,128)(2,1)}, u32[]{:S(2)}) copy-start(bf16[1536,768]{1,0:T(8,128)(2,1)} %w_in.3) | copy-start | bytes 7077892
  32.1 2.1 %copy-start = (bf16[768,1536]{1,0:T(8,128)(2,1)S(1)}, bf16[768,1536]{1,0:T(8,128)(2,1)}, u32[]{:S(2)}) copy-start(bf16[768,1536]{1,0:T(8,128)(2,1)} %w_out.3) | copy-start | bytes 7077892
  38.2 4.4 %collective-permute-start.11 = (bf16[320,1536]{1,0:T(8,128)(2,1)S(1)}, bf16[320,1536]{1,0:T(8,128)(2,1)S(1)}, u32[]{:S(2)}, u32[]{:S(2)}) collective-permute-start(bf16[320,1536]{1,0:T(8,128)(2,1)S(1)} %stack_rows.18.refs_0_), channel_id=1, source_target_pairs={{0,1},{1,0},{2,3},{3,2},{4,5},{5,4},{6,7},{7,6},{8,9},{9,8},{10,11... | collective-permute-start | bytes 2949128 | tf_op jit(solution)/shard_map/ppermute | solution.py:31
  39.9 9.0 %collective-permute-start.6 = (bf16[320,1664]{1,0:T(8,128)(2,1)S(1)}, bf16[320,1664]{1,0:T(8,128)(2,1)S(1)}, u32[]{:S(2)}, u32[]{:S(2)}) collective-permute-start(bf16[320,1664]{1,0:T(8,128)(2,1)S(1)} %get-tuple-element.55), channel_id=1, source_target_pairs={{0,1},{1,0},{2,3},{3,2},{4,5},{5,4},{6,7},{7,6},{8,9},{9,8},{10,11... | collective-permute-start | bytes 3194888 | tf_op jit(solution)/shard_map/ppermute | solution.py:31
  40.0 8.8 %collective-permute-start.9 = (bf16[160,1536]{1,0:T(8,128)(2,1)S(1)}, bf16[160,1536]{1,0:T(8,128)(2,1)S(1)}, u32[]{:S(2)}, u32[]{:S(2)}) collective-permute-start(bf16[160,1536]{1,0:T(8,128)(2,1)S(1)} %stack_rows.14.refs_0_), channel_id=1, source_target_pairs={{0,2},{1,5},{2,0},{3,7},{4,6},{5,1},{6,4},{7,3},{8,10},{9,13},{10,... | collective-permute-start | bytes 1474568 | tf_op jit(solution)/shard_map/ppermute | solution.py:31
  40.8 6.6 %collective-permute-start.10 = (bf16[40,1536]{1,0:T(8,128)(2,1)S(1)}, bf16[40,1536]{1,0:T(8,128)(2,1)S(1)}, u32[]{:S(2)}, u32[]{:S(2)}) collective-permute-start(bf16[40,1536]{1,0:T(8,128)(2,1)S(1)} %get-tuple-element.61), channel_id=1, source_target_pairs={{0,8},{1,9},{2,10},{3,11},{4,12},{5,13},{6,14},{7,15},{8,0},{9,1},... | collective-permute-start | bytes 368648 | tf_op jit(solution)/shard_map/ppermute | solution.py:37
  49.1 5.2 %collective-permute-start.13 = (bf16[320,1664]{1,0:T(8,128)(2,1)S(1)}, bf16[320,1664]{1,0:T(8,128)(2,1)S(1)}, u32[]{:S(2)}, u32[]{:S(2)}) collective-permute-start(bf16[320,1664]{1,0:T(8,128)(2,1)S(1)} %get-tuple-element.67), channel_id=1, source_target_pairs={{0,1},{1,0},{2,3},{3,2},{4,5},{5,4},{6,7},{7,6},{8,9},{9,8},{10,11... | collective-permute-start | bytes 3194888 | tf_op jit(solution)/shard_map/ppermute | solution.py:31
  52.0 9.1 %collective-permute-start.15 = (bf16[80,1536]{1,0:T(8,128)(2,1)S(1)}, bf16[80,1536]{1,0:T(8,128)(2,1)S(1)}, u32[]{:S(2)}, u32[]{:S(2)}) collective-permute-start(bf16[80,1536]{1,0:T(8,128)(2,1)S(1)} %maximum_bitcast_fusion.refs_0_), channel_id=1, source_target_pairs={{0,4},{1,3},{2,6},{3,1},{4,0},{5,7},{6,2},{7,5},{8,12},{9,11},{10,... | collective-permute-start | bytes 737288 | tf_op jit(solution)/shard_map/ppermute | solution.py:31
  54.1 27.0 %collective-permute-start.17 = (bf16[320,1536]{1,0:T(8,128)(2,1)S(1)}, bf16[320,1536]{1,0:T(8,128)(2,1)S(1)}, u32[]{:S(2)}, u32[]{:S(2)}) collective-permute-start(bf16[320,1536]{1,0:T(8,128)(2,1)S(1)} %stack_rows.20.refs_0_), channel_id=1, source_target_pairs={{0,1},{1,0},{2,3},{3,2},{4,5},{5,4},{6,7},{7,6},{8,9},{9,8},{10,11... | collective-permute-start | bytes 2949128 | tf_op jit(solution)/shard_map/ppermute | solution.py:31
  54.1 16.5 %collective-permute-start.12 = (bf16[160,1664]{1,0:T(8,128)(2,1)S(1)}, bf16[160,1664]{1,0:T(8,128)(2,1)S(1)}, u32[]{:S(2)}, u32[]{:S(2)}) collective-permute-start(bf16[160,1664]{1,0:T(8,128)(2,1)S(1)} %get-tuple-element.82), channel_id=1, source_target_pairs={{0,2},{1,5},{2,0},{3,7},{4,6},{5,1},{6,4},{7,3},{8,10},{9,13},{10,... | collective-permute-start | bytes 1597448 | tf_op jit(solution)/shard_map/ppermute | solution.py:31
  54.6 14.6 %collective-permute-start.14 = (bf16[160,1664]{1,0:T(8,128)(2,1)S(1)}, bf16[160,1664]{1,0:T(8,128)(2,1)S(1)}, u32[]{:S(2)}, u32[]{:S(2)}) collective-permute-start(bf16[160,1664]{1,0:T(8,128)(2,1)S(1)} %get-tuple-element.80), channel_id=1, source_target_pairs={{0,2},{1,5},{2,0},{3,7},{4,6},{5,1},{6,4},{7,3},{8,10},{9,13},{10,... | collective-permute-start | bytes 1597448 | tf_op jit(solution)/shard_map/ppermute | solution.py:31
  61.2 16.7 %collective-permute-start.18 = (bf16[160,1536]{1,0:T(8,128)(2,1)S(1)}, bf16[160,1536]{1,0:T(8,128)(2,1)S(1)}, u32[]{:S(2)}, u32[]{:S(2)}) collective-permute-start(bf16[160,1536]{1,0:T(8,128)(2,1)S(1)} %stack_rows.22.refs_0_), channel_id=1, source_target_pairs={{0,2},{1,5},{2,0},{3,7},{4,6},{5,1},{6,4},{7,3},{8,10},{9,13},{10,... | collective-permute-start | bytes 1474568 | tf_op jit(solution)/shard_map/ppermute | solution.py:31
  69.3 8.5 %collective-permute-start.19 = (bf16[80,1664]{1,0:T(8,128)(2,1)S(1)}, bf16[80,1664]{1,0:T(8,128)(2,1)S(1)}, u32[]{:S(2)}, u32[]{:S(2)}) collective-permute-start(bf16[80,1664]{1,0:T(8,128)(2,1)S(1)} %add_convert_fusion.8), channel_id=1, source_target_pairs={{0,4},{1,3},{2,6},{3,1},{4,0},{5,7},{6,2},{7,5},{8,12},{9,11},{10,... | collective-permute-start | bytes 798728 | tf_op jit(solution)/shard_map/ppermute | solution.py:31
  78.0 3.0 %collective-permute-start.20 = (bf16[320,1536]{1,0:T(8,128)(2,1)S(1)}, bf16[320,1536]{1,0:T(8,128)(2,1)S(1)}, u32[]{:S(2)}, u32[]{:S(2)}) collective-permute-start(bf16[320,1536]{1,0:T(8,128)(2,1)S(1)} %stack_rows.23.refs_2_), channel_id=1, source_target_pairs={{0,1},{1,0},{2,3},{3,2},{4,5},{5,4},{6,7},{7,6},{8,9},{9,8},{10,11... | collective-permute-start | bytes 2949128 | tf_op jit(solution)/shard_map/ppermute | solution.py:31
  78.2 9.5 %collective-permute-start.16 = (bf16[80,1664]{1,0:T(8,128)(2,1)S(1)}, bf16[80,1664]{1,0:T(8,128)(2,1)S(1)}, u32[]{:S(2)}, u32[]{:S(2)}) collective-permute-start(bf16[80,1664]{1,0:T(8,128)(2,1)S(1)} %get-tuple-element.88), channel_id=1, source_target_pairs={{0,4},{1,3},{2,6},{3,1},{4,0},{5,7},{6,2},{7,5},{8,12},{9,11},{10,... | collective-permute-start | bytes 798728 | tf_op jit(solution)/shard_map/ppermute | solution.py:31
  80.0 13.8 %collective-permute-start.21 = (bf16[80,1664]{1,0:T(8,128)(2,1)S(1)}, bf16[80,1664]{1,0:T(8,128)(2,1)S(1)}, u32[]{:S(2)}, u32[]{:S(2)}) collective-permute-start(bf16[80,1664]{1,0:T(8,128)(2,1)S(1)} %add_convert_fusion.4), channel_id=1, source_target_pairs={{0,8},{1,9},{2,10},{3,11},{4,12},{5,13},{6,14},{7,15},{8,0},{9,1},... | collective-permute-start | bytes 798728 | tf_op jit(solution)/shard_map/ppermute | solution.py:37
  81.3 12.5 %copy-start.6 = (f32[128]{0:T(128)S(1)}, f32[128]{0:T(128)}, u32[]{:S(2)}) copy-start(f32[128]{0:T(128)} %param.11) | copy-start | bytes 1540

commit v8 on v7

--- a/solution.py
+++ b/solution.py
@@ -10,6 +10,7 @@
 SPLIT = 8
 CORE, LOW, HIGH = 1, 2, 4
 LANES, TILE = 128, 256
+LONG = 20_000_000_000
 VMEM = pl.BlockSpec(memory_space=pltpu.VMEM)
 F32, BF16 = jnp.float32, jnp.bfloat16
 
@@ -189,7 +190,7 @@
         first += count
 
 
-def join(*pieces):
+def join(*pieces, long=False):
     if any(x.shape[0] % 16 for x in pieces):
         return jnp.concatenate(pieces)
     rows, width = sum(x.shape[0] for x in pieces), pieces[0].shape[1]
@@ -199,7 +200,7 @@
         in_specs=[VMEM] * len(pieces),
         out_specs=VMEM,
         compiler_params=params(2 + rows * width * 4 // 1000000),
-        cost_estimate=cost(0, rows * width),
+        cost_estimate=cost(LONG if long else 0, rows * width),
         name="stack_rows",
     )(*pieces)
 
@@ -219,8 +220,25 @@
 
 
 def split_slots(rows, experts):
-    rows = rows.reshape(experts - 1, 2, -1, rows.shape[1])
-    return [rows[:, i].reshape(-1, rows.shape[3]) for i in range(2)]
+    rows = rows.reshape(experts - 1, -1, rows.shape[1])
+    cut = rows.shape[1] - rows.shape[1] // 5
+    return [x.reshape(-1, rows.shape[2]) for x in (rows[:, :cut], rows[:, cut:])]
+
+
+def pause_kernel(rows, out):
+    out[...] = rows[...]
+
+
+def pause(rows):
+    return pl.pallas_call(
+        pause_kernel,
+        out_shape=jax.ShapeDtypeStruct(rows.shape, rows.dtype),
+        in_specs=[VMEM],
+        out_specs=VMEM,
+        compiler_params=params(4),
+        cost_estimate=cost(LONG, 0),
+        name="pause",
+    )(rows)
 
 
 def join_slots(a, b, experts):
@@ -287,57 +305,62 @@
     got = meet(near_grad, 0)
     near_two = join(near_grad, after(got, near_row))
     got = meet(near_two, 1)
-    row_got = meet(after(near_row, near_two), 0)
     act, slope = activation(by_source, after(order, near_two))
-    far_grad = after(far_grad, act)
+    far_grad = pause(after(far_grad, act))
     far_got = meet(far_grad, 0)
-    near_row2 = join(near_row, after(row_got, far_grad))
-    far_two = join(far_grad, after(far_got, near_row2))
+    near_four = join(near_two, after(got, far_grad))
+    got = meet(near_four, 2)
+    far_two = join(far_grad, after(far_got, near_four), long=True)
     far_got = meet(far_two, 1)
-    near_four = join(near_two, after(got, far_two))
-    got = meet(near_four, 2)
 
     far_row_a, far_row_b = split_slots(after(far_row, far_two), experts)
     far_row_a = cross(far_row_a, 1)
-    near_grads = join(near_four, got)
+    near_grads = join(near_four, after(got, far_two))
     near_hg, near_kept, near_sent = slot_grads(
         near_grads, w_out, w_in, act[:near_count], slope[:near_count]
     )
     near_got = meet(near_sent, 2)
     far_row_a = after(far_row_a, near_sent)
-    far_four = join(far_two, after(far_got, far_row_a))
+    far_four = join(far_two, after(far_got, far_row_a), long=True)
     far_got = meet(far_four, 2)
     far_row_b = cross(after(far_row_b, far_four), 1)
-    row_got = meet(after(near_row2, far_four), 1)
-    far_grads = join(far_four, far_got)
+    row_got = meet(after(near_row, far_four), 0)
+    near_kept, near_sent = add_halves(near_kept, after(near_got, far_four))
+    near_got = meet(near_sent, 1)
+    far_grads = join(far_four, after(far_got, near_sent))
 
     far_hg, far_kept, far_sent = slot_grads(
         far_grads, w_out, w_in, act[near_count:], slope[near_count:]
     )
     far_row = join_slots(far_row_a, after(far_row_b, far_sent), experts)
-    near_row4 = join(near_row2, after(row_got, far_row))
-    near_kept, near_sent = add_halves(near_kept, after(near_got, near_row4))
-    far_got = meet(after(far_sent, near_sent), 2)
+    near_row2 = join(near_row, after(row_got, far_sent))
+    far_kept, far_on = halves(far_kept)
+    far_sent = halves(after(far_sent, far_row, near_row2))
+    far_got, on_got = [meet(x, 2) for x in far_sent]
+    row_got = meet(near_row2, 1)
     far_row_got = meet(far_row, 0)
-    row_got = meet(near_row4, 2)
-    near_got = meet(near_sent, 1)
-    far_kept, far_sent = add_halves(far_kept, far_got)
-    far_got = meet(far_sent, 1)
+    near_kept, near_sent = add_halves(near_kept, after(near_got, far_sent[1]))
+    near_got = meet(near_sent, 0)
+    far_sent = add(far_on, after(on_got, near_sent))
+    on_got = meet(far_sent, 1)
+    far_kept = add(far_kept, after(far_got, far_sent))
     w_out_grad = product(
-        after(act, far_sent), join(near_grads, far_grads), ((0,), (0,))
+        after(act, far_kept), join(near_grads, far_grads), ((0,), (0,))
     ).astype(BF16)
     far_row2 = join(far_row, after(far_row_got, w_out_grad))
     far_row_got = meet(far_row2, 1)
-    far_kept, far_sent = add_halves(far_kept, after(far_got, far_row2))
+    near_row4 = join(near_row2, after(row_got, far_row2))
+    row_got = meet(near_row4, 2)
+    far_kept, far_sent = add_halves(far_kept, after(on_got, near_row4))
     far_got = meet(far_sent, 0)
-    near_kept, near_sent = add_halves(near_kept, after(near_got, far_sent))
-    near_got = meet(near_sent, 0)
-    far_sum = add(far_kept, after(far_got, near_sent))
+    far_row4 = join(far_row2, after(far_row_got, far_sent))
+    near_sent = far_row4
+    far_sum = pause(add(far_kept, after(far_got, near_sent)))
     back = cross(far_sum, -1)
-    far_row4 = join(far_row2, after(far_row_got, far_sum))
     rows = join(near_row4, row_got, far_row4, meet(far_row4, 2))
     w_in_grad = product(rows, join(near_hg, far_hg), ((0,), (0,))).astype(BF16)
-    near_got, back = after(near_got, w_in_grad), after(back, w_in_grad)
+    back = after(back, w_in_grad)
+    near_got = after(near_got, back)
     token_grad, gate_grad = to_tokens(slots, place, gate, near_kept, near_got, back)
     return (token_grad, gate_grad.reshape(-1), w_in_grad, w_out_grad)
 

time: 95.2 us -> 92.5 us (0.972)
  starting transfers between devices: 31 us -> 26.1 us
  waiting for transfers between devices: 31.5 us -> 32.8 us
    ppermute x4, waiting for transfers between devices: 6.79 us -> 9.31 us  [shift(): return lax.ppermute(rows, 'expert', pairs)]
    ppermute x18 -> x19, starting transfers between devices: 22.7 us -> 20.2 us  [meet(): lax.ppermute(rows, 'expert', [(i, i ^ bits(i % 2)[step]) for i in range(d...]
    ppermute x4, starting transfers between devices: 8.31 us -> 5.96 us  [shift(): return lax.ppermute(rows, 'expert', pairs)]
    ppermute x18 -> x19, waiting for transfers between devices: 24.7 us -> 23.5 us  [meet(): lax.ppermute(rows, 'expert', [(i, i ^ bits(i % 2)[step]) for i in range(d...]
    unnamed x14 -> x16, local copies, waits for them, and re-layouts: 6.17 us -> 6.82 us
  transfers between devices with their start and end apart: 22 -> 23, of which waited for: 9 -> 12; matrix products, arithmetic and copies ran while one was open for 11% -> 11% of each run, Pallas kernels for 13% -> 14%
where the time goes in v8:
time: 92.5 us; the launch traced here: 92.2 us
  waiting for transfers between devices  32.8 us (35%)
  starting transfers between devices  26.1 us (28%)
  Pallas kernels  14.3 us (15%)
  matrix products  9.15 us (10%)
  local copies, waits for them, and re-layouts  7.23 us (8%)
  other arithmetic  1.62 us (2%)
  between operations  0.96 us (1%)
    ppermute x19, waiting for transfers between devices, meet(): lax.ppermute(rows, 'expert', [(i, i ^ bits(i % 2)[step]) for i in range(d...  23.5 us
    ppermute x19, starting transfers between devices, meet(): lax.ppermute(rows, 'expert', [(i, i ^ bits(i % 2)[step]) for i in range(d...  20.2 us
    ppermute x4, waiting for transfers between devices, shift(): return lax.ppermute(rows, 'expert', pairs)  9.31 us
    dot_general x2, matrix products, product(): return lax.dot_general(a, b, (dims, ((), ())), preferred_element_type=F32)  9.15 us
    pallas_call x2, Pallas kernels, slot_grads(): pl.pallas_call(slot_grad_kernel, out_shape=(jax.ShapeDtypeStruct((rows, u...  7.81 us
    unnamed x16, local copies, waits for them, and re-layouts  6.82 us
    ppermute x4, starting transfers between devices, shift(): return lax.ppermute(rows, 'expert', pairs)  5.96 us
    pallas_call x1, Pallas kernels, activation(): pl.pallas_call(activation_kernel, grid_spec=pltpu.PrefetchScalarGridSpec(...  3.36 us
  transfers between devices with their start and end apart: 23, of which 12 were waited for; matrix products, arithmetic and copies ran while one was open for 11% of the time, Pallas kernels for 14%

profile of v8, /device:TPU:0, one launch (start us, length us, event | category | flops | bytes accessed | tf_op | source)
XLA Modules:
  0.0 92.2 jit_solution(14205135978691480569)
XLA Ops:
  0.6 0.7 fusion.place
  1.3 1.0 %copy-done.3 = bf16[128,1536]{1,0:T(8,128)(2,1)S(1)} copy-done((bf16[128,1536]{1,0:T(8,128)(2,1)S(1)}, bf16[128,1536]{1,0:T(8,128)(2,1)}, u32[]{:S(2)}) %copy-start.3) | copy-done | bytes 393240
  2.3 0.7 copy-done.5
  3.0 0.4 rows_to_slots.2
  3.4 3.1 %collective-permute-start = (bf16[80,1536]{1,0:T(8,128)(2,1)S(1)}, bf16[80,1536]{1,0:T(8,128)(2,1)S(1)}, u32[]{:S(2)}, u32[]{:S(2)}) collective-permute-start(bf16[80,1536]{1,0:T(8,128)(2,1)S(1)} %get-tuple-element.45.refs_0_), channel_id=1, source_target_pairs={{0,4},{1,3},{2,6},{3,1},{4,0},{5,7},{6,2},{7,5},{8,12},{9,11},{10,... | collective-permute-start | bytes 737288 | tf_op jit(solution)/shard_map/ppermute | solution.py:32
  6.5 2.6 %collective-permute-start.2 = (bf16[80,1536]{1,0:T(8,128)(2,1)S(1)}, bf16[80,1536]{1,0:T(8,128)(2,1)S(1)}, u32[]{:S(2)}, u32[]{:S(2)}) collective-permute-start(bf16[80,1536]{1,0:T(8,128)(2,1)S(1)} %get-tuple-element.48), channel_id=1, source_target_pairs={{0,8},{1,9},{2,10},{3,11},{4,12},{5,13},{6,14},{7,15},{8,0},{9,1},... | collective-permute-start | bytes 737288 | tf_op jit(solution)/shard_map/ppermute | solution.py:38
  9.1 1.0 %copy-done.4 = bf16[128,1536]{1,0:T(8,128)(2,1)S(1)} copy-done((bf16[128,1536]{1,0:T(8,128)(2,1)S(1)}, bf16[128,1536]{1,0:T(8,128)(2,1)}, u32[]{:S(2)}) %copy-start.4) | copy-done | bytes 393240
  10.1 0.7 copy-done.6
  10.7 0.3 rows_to_slots.3
  11.0 0.1 pad_add_fusion.order
  11.1 1.6 %collective-permute-done.refs_1_ = bf16[80,1536]{1,0:T(8,128)(2,1)S(1)} collective-permute-done((bf16[80,1536]{1,0:T(8,128)(2,1)S(1)}, bf16[80,1536]{1,0:T(8,128)(2,1)S(1)}, u32[]{:S(2)}, u32[]{:S(2)}) %collective-permute-start) | collective-permute-done | bytes 245792 | tf_op jit(solution)/shard_map/ppermute | solution.py:32
  12.8 4.4 %collective-permute-start.1 = (bf16[160,1536]{1,0:T(8,128)(2,1)S(1)}, bf16[160,1536]{1,0:T(8,128)(2,1)S(1)}, u32[]{:S(2)}, u32[]{:S(2)}) collective-permute-start(bf16[160,1536]{1,0:T(8,128)(2,1)S(1)} %stack_rows.13.refs_0_), channel_id=1, source_target_pairs={{0,2},{1,5},{2,0},{3,7},{4,6},{5,1},{6,4},{7,3},{8,10},{9,13},{10,... | collective-permute-start | bytes 1474568 | tf_op jit(solution)/shard_map/ppermute | solution.py:32
  17.2 1.5 %copy-done.2 = bf16[1280,768]{1,0:T(8,128)(2,1)S(1)} copy-done((bf16[1280,768]{1,0:T(8,128)(2,1)S(1)}, bf16[1280,768]{1,0:T(8,128)(2,1)}, u32[]{:S(2)}) %copy-start.2) | copy-done | bytes 1966104
  18.7 3.4 %activation.1 = (bf16[16,80,768]{2,1,0:T(8,128)(2,1)S(1)}, bf16[16,80,768]{2,1,0:T(8,128)(2,1)S(1)}) custom-call(s32[16]{0:T(128)S(1)} %pad_add_fusion.order, bf16[16,80,768]{2,1,0:T(8,128)(2,1)S(1)} %bitcast.27), custom_call_target="tpu_custom_call" | custom-call | tf_op jit(solution)/shard_map/activation/pallas_call | solution.py:169
  22.1 0.1 collective-permute-start.4
  22.2 4.4 %collective-permute-done.1.refs_1_ = bf16[160,1536]{1,0:T(8,128)(2,1)S(1)} collective-permute-done((bf16[160,1536]{1,0:T(8,128)(2,1)S(1)}, bf16[160,1536]{1,0:T(8,128)(2,1)S(1)}, u32[]{:S(2)}, u32[]{:S(2)}) %collective-permute-start.1) | collective-permute-done | bytes 491552 | tf_op jit(solution)/shard_map/ppermute | solution.py:32
  26.7 0.1 collective-permute-start.3
  26.8 1.6 %collective-permute-done.4.refs_1_ = bf16[80,1536]{1,0:T(8,128)(2,1)S(1)} collective-permute-done((bf16[80,1536]{1,0:T(8,128)(2,1)S(1)}, bf16[80,1536]{1,0:T(8,128)(2,1)S(1)}, u32[]{:S(2)}, u32[]{:S(2)}) %collective-permute-start.4) | collective-permute-done | bytes 245792 | tf_op jit(solution)/shard_map/ppermute | solution.py:32
  28.4 0.3 collective-permute-start.6
  28.8 1.1 %collective-permute-start.7 = (bf16[64,1536]{1,0:T(8,128)(2,1)S(1)}, bf16[64,1536]{1,0:T(8,128)(2,1)S(1)}, u32[]{:S(2)}, u32[]{:S(2)}) collective-permute-start(bf16[64,1536]{1,0:T(8,128)(2,1)S(1)} %slice_bitcast_fusion), channel_id=1, source_target_pairs={{0,8},{1,9},{2,10},{3,11},{4,12},{5,13},{6,14},{7,15},{8,0},{9,1},... | collective-permute-start | bytes 589832 | tf_op jit(solution)/shard_map/ppermute | solution.py:38
  29.8 0.3 fusion.3
  30.2 0.1 stack_rows.16.grads.refs_0_
  30.3 1.2 %copy-done.1 = bf16[1536,768]{1,0:T(8,128)(2,1)S(1)} copy-done((bf16[1536,768]{1,0:T(8,128)(2,1)S(1)}, bf16[1536,768]{1,0:T(8,128)(2,1)}, u32[]{:S(2)}) %copy-start.1) | copy-done | bytes 2359320
  31.5 0.8 copy-done
  32.3 3.9 %slot_grads.2 = (bf16[640,768]{1,0:T(8,128)(2,1)S(1)}, bf16[320,1664]{1,0:T(8,128)(2,1)S(1)}, bf16[320,1664]{1,0:T(8,128)(2,1)S(1)}) custom-call(bf16[640,1536]{1,0:T(8,128)(2,1)S(1)} %stack_rows.16.grads.refs_0_, bf16[768,1536]{1,0:T(8,128)(2,1)S(1)} %copy-done, bf16[1536,768]{1,0:T(8,128)(2,1)S(1)} %copy-done.1, bf16[640,768]{1,0:T(8,128)(2,1)S(1)} %bitcast.26, ...), custom_call_target="tpu_custom_call" | custom-call | tf_op jit(solution)/shard_map/slot_grads/pallas_call | solution.py:275
  36.2 0.1 collective-permute-start.5
  36.3 1.1 %collective-permute-done.7 = bf16[64,1536]{1,0:T(8,128)(2,1)S(1)} collective-permute-done((bf16[64,1536]{1,0:T(8,128)(2,1)S(1)}, bf16[64,1536]{1,0:T(8,128)(2,1)S(1)}, u32[]{:S(2)}, u32[]{:S(2)}) %collective-permute-start.7) | collective-permute-done | bytes 196640 | tf_op jit(solution)/shard_map/ppermute | solution.py:38
  37.5 1.9 %collective-permute-start.9 = (bf16[320,1536]{1,0:T(8,128)(2,1)S(1)}, bf16[320,1536]{1,0:T(8,128)(2,1)S(1)}, u32[]{:S(2)}, u32[]{:S(2)}) collective-permute-start(bf16[320,1536]{1,0:T(8,128)(2,1)S(1)} %stack_rows.17.refs_0_), channel_id=1, source_target_pairs={{0,1},{1,0},{2,3},{3,2},{4,5},{5,4},{6,7},{7,6},{8,9},{9,8},{10,11... | collective-permute-start | bytes 2949128 | tf_op jit(solution)/shard_map/ppermute | solution.py:32
  39.4 1.3 %collective-permute-start.10 = (bf16[16,1536]{1,0:T(8,128)(2,1)S(1)}, bf16[16,1536]{1,0:T(8,128)(2,1)S(1)}, u32[]{:S(2)}, u32[]{:S(2)}) collective-permute-start(bf16[16,1536]{1,0:T(8,128)(2,1)S(1)} %slice_bitcast_fusion.1), channel_id=1, source_target_pairs={{0,8},{1,9},{2,10},{3,11},{4,12},{5,13},{6,14},{7,15},{8,0},{9,1},... | collective-permute-start | bytes 147464 | tf_op jit(solution)/shard_map/ppermute | solution.py:38
  40.7 1.9 %collective-permute-start.11 = (bf16[80,1536]{1,0:T(8,128)(2,1)S(1)}, bf16[80,1536]{1,0:T(8,128)(2,1)S(1)}, u32[]{:S(2)}, u32[]{:S(2)}) collective-permute-start(bf16[80,1536]{1,0:T(8,128)(2,1)S(1)} %get-tuple-element.67.refs_0_), channel_id=1, source_target_pairs={{0,4},{1,3},{2,6},{3,1},{4,0},{5,7},{6,2},{7,5},{8,12},{9,11},{10,... | collective-permute-start | bytes 737288 | tf_op jit(solution)/shard_map/ppermute | solution.py:32
  42.6 0.2 add_convert_fusion.2
  42.9 1.7 %collective-permute-start.8 = (bf16[160,1664]{1,0:T(8,128)(2,1)S(1)}, bf16[160,1664]{1,0:T(8,128)(2,1)S(1)}, u32[]{:S(2)}, u32[]{:S(2)}) collective-permute-start(bf16[160,1664]{1,0:T(8,128)(2,1)S(1)} %get-tuple-element.86), channel_id=1, source_target_pairs={{0,2},{1,5},{2,0},{3,7},{4,6},{5,1},{6,4},{7,3},{8,10},{9,13},{10,... | collective-permute-start | bytes 1597448 | tf_op jit(solution)/shard_map/ppermute | solution.py:32
  44.6 0.1 stack_rows.18.grads.refs_1_
  44.7 3.9 %slot_grads.3 = (bf16[640,768]{1,0:T(8,128)(2,1)S(1)}, bf16[320,1664]{1,0:T(8,128)(2,1)S(1)}, bf16[320,1664]{1,0:T(8,128)(2,1)S(1)}) custom-call(bf16[640,1536]{1,0:T(8,128)(2,1)S(1)} %stack_rows.18.grads.refs_1_, bf16[768,1536]{1,0:T(8,128)(2,1)S(1)} %copy-done, bf16[1536,768]{1,0:T(8,128)(2,1)S(1)} %copy-done.1, bf16[640,768]{1,0:T(8,128)(2,1)S(1)} %bitcast.24, ...), custom_call_target="tpu_custom_call" | custom-call | tf_op jit(solution)/shard_map/slot_grads/pallas_call | solution.py:275
  48.7 0.7 collective-permute-done.11.refs_1_
  49.4 0.1 fusion.5
  49.5 0.1 collective-permute-start.14
  49.6 2.7 %collective-permute-start.16 = (bf16[160,1536]{1,0:T(8,128)(2,1)S(1)}, bf16[160,1536]{1,0:T(8,128)(2,1)S(1)}, u32[]{:S(2)}, u32[]{:S(2)}) collective-permute-start(bf16[160,1536]{1,0:T(8,128)(2,1)S(1)} %stack_rows.19.refs_0_), channel_id=1, source_target_pairs={{0,2},{1,5},{2,0},{3,7},{4,6},{5,1},{6,4},{7,3},{8,10},{9,13},{10,... | collective-permute-start | bytes 1474568 | tf_op jit(solution)/shard_map/ppermute | solution.py:32
  52.3 1.1 %collective-permute-start.17 = (bf16[80,1536]{1,0:T(8,128)(2,1)S(1)}, bf16[80,1536]{1,0:T(8,128)(2,1)S(1)}, u32[]{:S(2)}, u32[]{:S(2)}) collective-permute-start(bf16[80,1536]{1,0:T(8,128)(2,1)S(1)} %maximum_bitcast_fusion.refs_0_), channel_id=1, source_target_pairs={{0,4},{1,3},{2,6},{3,1},{4,0},{5,7},{6,2},{7,5},{8,12},{9,11},{10,... | collective-permute-start | bytes 737288 | tf_op jit(solution)/shard_map/ppermute | solution.py:32
  53.3 0.3 stack_rows.20
  53.6 0.1 collective-permute-start.13
  53.7 0.1 add_convert_fusion.7
  53.8 0.1 add_convert_fusion.1
  54.0 0.3 collective-permute-start.15
  54.3 1.3 %collective-permute-done.13 = bf16[160,1664]{1,0:T(8,128)(2,1)S(1)} collective-permute-done((bf16[160,1664]{1,0:T(8,128)(2,1)S(1)}, bf16[160,1664]{1,0:T(8,128)(2,1)S(1)}, u32[]{:S(2)}, u32[]{:S(2)}) %collective-permute-start.13) | collective-permute-done | bytes 532512 | tf_op jit(solution)/shard_map/ppermute | solution.py:32
  55.6 0.1 add_convert_fusion
  55.7 4.6 %convolution_convert_fusion.1 = bf16[768,1536]{1,0:T(8,128)(2,1)} fusion(bf16[1280,768]{1,0:T(8,128)(2,1)S(1)} %bitcast.28, bf16[1280,1536]{1,0:T(8,128)(2,1)S(1)} %stack_rows.20), kind=kOutput, calls=%fused_computation.1 | convolution fusion | flops 3021078528 | bytes 8257536 | tf_op jit(solution)/shard_map/dot_general | solution.py:250
  60.3 0.9 collective-permute-done.17.refs_1_
  61.2 0.1 collective-permute-start.19
  61.3 0.4 collective-permute-done.16.refs_1_
  61.8 5.6 %collective-permute-done.15 = bf16[160,1664]{1,0:T(8,128)(2,1)S(1)} collective-permute-done((bf16[160,1664]{1,0:T(8,128)(2,1)S(1)}, bf16[160,1664]{1,0:T(8,128)(2,1)S(1)}, u32[]{:S(2)}, u32[]{:S(2)}) %collective-permute-start.15) | collective-permute-done | bytes 532512 | tf_op jit(solution)/shard_map/ppermute | solution.py:32
  67.4 0.1 add_convert_fusion.5
  67.5 1.2 %collective-permute-start.18 = (bf16[80,1664]{1,0:T(8,128)(2,1)S(1)}, bf16[80,1664]{1,0:T(8,128)(2,1)S(1)}, u32[]{:S(2)}, u32[]{:S(2)}) collective-permute-start(bf16[80,1664]{1,0:T(8,128)(2,1)S(1)} %add_convert_fusion.5), channel_id=1, source_target_pairs={{0,4},{1,3},{2,6},{3,1},{4,0},{5,7},{6,2},{7,5},{8,12},{9,11},{10,... | collective-permute-start | bytes 798728 | tf_op jit(solution)/shard_map/ppermute | solution.py:32
  68.6 0.1 stack_rows.25
  68.8 1.0 %collective-permute-start.12 = (bf16[80,1664]{1,0:T(8,128)(2,1)S(1)}, bf16[80,1664]{1,0:T(8,128)(2,1)S(1)}, u32[]{:S(2)}, u32[]{:S(2)}) collective-permute-start(bf16[80,1664]{1,0:T(8,128)(2,1)S(1)} %get-tuple-element.94), channel_id=1, source_target_pairs={{0,4},{1,3},{2,6},{3,1},{4,0},{5,7},{6,2},{7,5},{8,12},{9,11},{10,... | collective-permute-start | bytes 798728 | tf_op jit(solution)/shard_map/ppermute | solution.py:32
  69.8 5.5 %collective-permute-done.19.refs_1_ = bf16[160,1536]{1,0:T(8,128)(2,1)S(1)} collective-permute-done((bf16[160,1536]{1,0:T(8,128)(2,1)S(1)}, bf16[160,1536]{1,0:T(8,128)(2,1)S(1)}, u32[]{:S(2)}, u32[]{:S(2)}) %collective-permute-start.19) | collective-permute-done | bytes 491552 | tf_op jit(solution)/shard_map/ppermute | solution.py:32
  75.3 0.1 collective-permute-start.22
  75.4 0.1 add_convert_fusion.4.rows
  75.6 1.0 %collective-permute-start.20 = (bf16[80,1664]{1,0:T(8,128)(2,1)S(1)}, bf16[80,1664]{1,0:T(8,128)(2,1)S(1)}, u32[]{:S(2)}, u32[]{:S(2)}) collective-permute-start(bf16[80,1664]{1,0:T(8,128)(2,1)S(1)} %pause.3), channel_id=1, source_target_pairs={{0,8},{1,9},{2,10},{3,11},{4,12},{5,13},{6,14},{7,15},{8,0},{9,1},... | collective-permute-start | bytes 798728 | tf_op jit(solution)/shard_map/ppermute | solution.py:38
  76.6 1.4 %collective-permute-done.22.refs_3_ = bf16[320,1536]{1,0:T(8,128)(2,1)S(1)} collective-permute-done((bf16[320,1536]{1,0:T(8,128)(2,1)S(1)}, bf16[320,1536]{1,0:T(8,128)(2,1)S(1)}, u32[]{:S(2)}, u32[]{:S(2)}) %collective-permute-start.22) | collective-permute-done | bytes 983072 | tf_op jit(solution)/shard_map/ppermute | solution.py:32
  78.0 0.3 stack_rows.24
  78.2 4.6 %convolution_convert_fusion = bf16[1536,768]{1,0:T(8,128)(2,1)} fusion(bf16[1280,1536]{1,0:T(8,128)(2,1)S(1)} %stack_rows.24, bf16[1280,768]{1,0:T(8,128)(2,1)S(1)} %stack_rows.25), kind=kOutput, calls=%fused_computation | convolution fusion | flops 3021078528 | bytes 8257536 | tf_op jit(solution)/shard_map/dot_general | solution.py:250
  82.8 8.2 %collective-permute-done.20.back = bf16[80,1664]{1,0:T(8,128)(2,1)S(1)} collective-permute-done((bf16[80,1664]{1,0:T(8,128)(2,1)S(1)}, bf16[80,1664]{1,0:T(8,128)(2,1)S(1)}, u32[]{:S(2)}, u32[]{:S(2)}) %collective-permute-start.20) | collective-permute-done | bytes 266272 | tf_op jit(solution)/shard_map/ppermute | solution.py:38
  91.0 1.2 %slots_to_tokens.1 = (bf16[128,1536]{1,0:T(8,128)(2,1)}, f32[1,128]{1,0:T(1,128)}) custom-call(s32[1,128]{1,0:T(1,128)S(1)} %fusion.place, f32[1,128]{1,0:T(1,128)S(1)} %bitcast.33, bf16[80,1664]{1,0:T(8,128)(2,1)S(1)} %get-tuple-element.95.kept, bf16[80,1664]{1,0:T(8,128)(2,1)S(1)} %collective-permute-done.12.got, ...), custom_call_target="tpu_custom_call" | custom-call | tf_op jit(solution)/shard_map/slots_to_tokens/pallas_call | solution.py:136
  (36 shorter events, 0.5 us)
Async XLA Ops:
  1.3 1.0 %copy-start.3 = (bf16[128,1536]{1,0:T(8,128)(2,1)S(1)}, bf16[128,1536]{1,0:T(8,128)(2,1)}, u32[]{:S(2)}) copy-start(bf16[128,1536]{1,0:T(8,128)(2,1)} %values.2) | copy-start | bytes 1179652
  2.3 0.7 copy-start.5
  3.4 9.4 %collective-permute-start = (bf16[80,1536]{1,0:T(8,128)(2,1)S(1)}, bf16[80,1536]{1,0:T(8,128)(2,1)S(1)}, u32[]{:S(2)}, u32[]{:S(2)}) collective-permute-start(bf16[80,1536]{1,0:T(8,128)(2,1)S(1)} %get-tuple-element.45.refs_0_), channel_id=1, source_target_pairs={{0,4},{1,3},{2,6},{3,1},{4,0},{5,7},{6,2},{7,5},{8,12},{9,11},{10,... | collective-permute-start | bytes 737288 | tf_op jit(solution)/shard_map/ppermute | solution.py:32
  6.5 15.6 %collective-permute-start.2 = (bf16[80,1536]{1,0:T(8,128)(2,1)S(1)}, bf16[80,1536]{1,0:T(8,128)(2,1)S(1)}, u32[]{:S(2)}, u32[]{:S(2)}) collective-permute-start(bf16[80,1536]{1,0:T(8,128)(2,1)S(1)} %get-tuple-element.48), channel_id=1, source_target_pairs={{0,8},{1,9},{2,10},{3,11},{4,12},{5,13},{6,14},{7,15},{8,0},{9,1},... | collective-permute-start | bytes 737288 | tf_op jit(solution)/shard_map/ppermute | solution.py:38
  9.1 1.0 %copy-start.4 = (bf16[128,1536]{1,0:T(8,128)(2,1)S(1)}, bf16[128,1536]{1,0:T(8,128)(2,1)}, u32[]{:S(2)}) copy-start(bf16[128,1536]{1,0:T(8,128)(2,1)} %values.3) | copy-start | bytes 1179652
  10.1 0.7 copy-start.6
  12.8 13.8 %collective-permute-start.1 = (bf16[160,1536]{1,0:T(8,128)(2,1)S(1)}, bf16[160,1536]{1,0:T(8,128)(2,1)S(1)}, u32[]{:S(2)}, u32[]{:S(2)}) collective-permute-start(bf16[160,1536]{1,0:T(8,128)(2,1)S(1)} %stack_rows.13.refs_0_), channel_id=1, source_target_pairs={{0,2},{1,5},{2,0},{3,7},{4,6},{5,1},{6,4},{7,3},{8,10},{9,13},{10,... | collective-permute-start | bytes 1474568 | tf_op jit(solution)/shard_map/ppermute | solution.py:32
  17.2 1.5 %copy-start.2 = (bf16[1280,768]{1,0:T(8,128)(2,1)S(1)}, bf16[1280,768]{1,0:T(8,128)(2,1)}, u32[]{:S(2)}) copy-start(bf16[1280,768]{1,0:T(8,128)(2,1)} %param.15) | copy-start | bytes 5898244
  22.1 6.3 %collective-permute-start.4 = (bf16[80,1536]{1,0:T(8,128)(2,1)S(1)}, bf16[80,1536]{1,0:T(8,128)(2,1)S(1)}, u32[]{:S(2)}, u32[]{:S(2)}) collective-permute-start(bf16[80,1536]{1,0:T(8,128)(2,1)S(1)} %pause.2.refs_0_), channel_id=1, source_target_pairs={{0,4},{1,3},{2,6},{3,1},{4,0},{5,7},{6,2},{7,5},{8,12},{9,11},{10,... | collective-permute-start | bytes 737288 | tf_op jit(solution)/shard_map/ppermute | solution.py:32
  26.7 3.5 %collective-permute-start.3 = (bf16[320,1536]{1,0:T(8,128)(2,1)S(1)}, bf16[320,1536]{1,0:T(8,128)(2,1)S(1)}, u32[]{:S(2)}, u32[]{:S(2)}) collective-permute-start(bf16[320,1536]{1,0:T(8,128)(2,1)S(1)} %stack_rows.14.refs_0_), channel_id=1, source_target_pairs={{0,1},{1,0},{2,3},{3,2},{4,5},{5,4},{6,7},{7,6},{8,9},{9,8},{10,11... | collective-permute-start | bytes 2949128 | tf_op jit(solution)/shard_map/ppermute | solution.py:32
  28.4 9.0 %collective-permute-start.6 = (bf16[160,1536]{1,0:T(8,128)(2,1)S(1)}, bf16[160,1536]{1,0:T(8,128)(2,1)S(1)}, u32[]{:S(2)}, u32[]{:S(2)}) collective-permute-start(bf16[160,1536]{1,0:T(8,128)(2,1)S(1)} %stack_rows.15.refs_0_), channel_id=1, source_target_pairs={{0,2},{1,5},{2,0},{3,7},{4,6},{5,1},{6,4},{7,3},{8,10},{9,13},{10,... | collective-permute-start | bytes 1474568 | tf_op jit(solution)/shard_map/ppermute | solution.py:32
  28.8 8.6 %collective-permute-start.7 = (bf16[64,1536]{1,0:T(8,128)(2,1)S(1)}, bf16[64,1536]{1,0:T(8,128)(2,1)S(1)}, u32[]{:S(2)}, u32[]{:S(2)}) collective-permute-start(bf16[64,1536]{1,0:T(8,128)(2,1)S(1)} %slice_bitcast_fusion), channel_id=1, source_target_pairs={{0,8},{1,9},{2,10},{3,11},{4,12},{5,13},{6,14},{7,15},{8,0},{9,1},... | collective-permute-start | bytes 589832 | tf_op jit(solution)/shard_map/ppermute | solution.py:38
  29.8 1.7 %copy-start.1 = (bf16[1536,768]{1,0:T(8,128)(2,1)S(1)}, bf16[1536,768]{1,0:T(8,128)(2,1)}, u32[]{:S(2)}) copy-start(bf16[1536,768]{1,0:T(8,128)(2,1)} %w_in.3) | copy-start | bytes 7077892
  30.1 2.1 %copy-start = (bf16[768,1536]{1,0:T(8,128)(2,1)S(1)}, bf16[768,1536]{1,0:T(8,128)(2,1)}, u32[]{:S(2)}) copy-start(bf16[768,1536]{1,0:T(8,128)(2,1)} %w_out.3) | copy-start | bytes 7077892
  36.2 6.4 %collective-permute-start.5 = (bf16[320,1664]{1,0:T(8,128)(2,1)S(1)}, bf16[320,1664]{1,0:T(8,128)(2,1)S(1)}, u32[]{:S(2)}, u32[]{:S(2)}) collective-permute-start(bf16[320,1664]{1,0:T(8,128)(2,1)S(1)} %get-tuple-element.57), channel_id=1, source_target_pairs={{0,1},{1,0},{2,3},{3,2},{4,5},{5,4},{6,7},{7,6},{8,9},{9,8},{10,11... | collective-permute-start | bytes 3194888 | tf_op jit(solution)/shard_map/ppermute | solution.py:32
  37.5 7.2 %collective-permute-start.9 = (bf16[320,1536]{1,0:T(8,128)(2,1)S(1)}, bf16[320,1536]{1,0:T(8,128)(2,1)S(1)}, u32[]{:S(2)}, u32[]{:S(2)}) collective-permute-start(bf16[320,1536]{1,0:T(8,128)(2,1)S(1)} %stack_rows.17.refs_0_), channel_id=1, source_target_pairs={{0,1},{1,0},{2,3},{3,2},{4,5},{5,4},{6,7},{7,6},{8,9},{9,8},{10,11... | collective-permute-start | bytes 2949128 | tf_op jit(solution)/shard_map/ppermute | solution.py:32
  39.4 9.3 %collective-permute-start.10 = (bf16[16,1536]{1,0:T(8,128)(2,1)S(1)}, bf16[16,1536]{1,0:T(8,128)(2,1)S(1)}, u32[]{:S(2)}, u32[]{:S(2)}) collective-permute-start(bf16[16,1536]{1,0:T(8,128)(2,1)S(1)} %slice_bitcast_fusion.1), channel_id=1, source_target_pairs={{0,8},{1,9},{2,10},{3,11},{4,12},{5,13},{6,14},{7,15},{8,0},{9,1},... | collective-permute-start | bytes 147464 | tf_op jit(solution)/shard_map/ppermute | solution.py:38
  40.7 8.6 %collective-permute-start.11 = (bf16[80,1536]{1,0:T(8,128)(2,1)S(1)}, bf16[80,1536]{1,0:T(8,128)(2,1)S(1)}, u32[]{:S(2)}, u32[]{:S(2)}) collective-permute-start(bf16[80,1536]{1,0:T(8,128)(2,1)S(1)} %get-tuple-element.67.refs_0_), channel_id=1, source_target_pairs={{0,4},{1,3},{2,6},{3,1},{4,0},{5,7},{6,2},{7,5},{8,12},{9,11},{10,... | collective-permute-start | bytes 737288 | tf_op jit(solution)/shard_map/ppermute | solution.py:32
  42.9 10.8 %collective-permute-start.8 = (bf16[160,1664]{1,0:T(8,128)(2,1)S(1)}, bf16[160,1664]{1,0:T(8,128)(2,1)S(1)}, u32[]{:S(2)}, u32[]{:S(2)}) collective-permute-start(bf16[160,1664]{1,0:T(8,128)(2,1)S(1)} %get-tuple-element.86), channel_id=1, source_target_pairs={{0,2},{1,5},{2,0},{3,7},{4,6},{5,1},{6,4},{7,3},{8,10},{9,13},{10,... | collective-permute-start | bytes 1597448 | tf_op jit(solution)/shard_map/ppermute | solution.py:32
  49.5 4.3 %collective-permute-start.14 = (bf16[160,1664]{1,0:T(8,128)(2,1)S(1)}, bf16[160,1664]{1,0:T(8,128)(2,1)S(1)}, u32[]{:S(2)}, u32[]{:S(2)}) collective-permute-start(bf16[160,1664]{1,0:T(8,128)(2,1)S(1)} %get-tuple-element.93), channel_id=1, source_target_pairs={{0,1},{1,0},{2,3},{3,2},{4,5},{5,4},{6,7},{7,6},{8,9},{9,8},{10,11... | collective-permute-start | bytes 1597448 | tf_op jit(solution)/shard_map/ppermute | solution.py:32
  49.6 12.1 %collective-permute-start.16 = (bf16[160,1536]{1,0:T(8,128)(2,1)S(1)}, bf16[160,1536]{1,0:T(8,128)(2,1)S(1)}, u32[]{:S(2)}, u32[]{:S(2)}) collective-permute-start(bf16[160,1536]{1,0:T(8,128)(2,1)S(1)} %stack_rows.19.refs_0_), channel_id=1, source_target_pairs={{0,2},{1,5},{2,0},{3,7},{4,6},{5,1},{6,4},{7,3},{8,10},{9,13},{10,... | collective-permute-start | bytes 1474568 | tf_op jit(solution)/shard_map/ppermute | solution.py:32
  52.3 8.9 %collective-permute-start.17 = (bf16[80,1536]{1,0:T(8,128)(2,1)S(1)}, bf16[80,1536]{1,0:T(8,128)(2,1)S(1)}, u32[]{:S(2)}, u32[]{:S(2)}) collective-permute-start(bf16[80,1536]{1,0:T(8,128)(2,1)S(1)} %maximum_bitcast_fusion.refs_0_), channel_id=1, source_target_pairs={{0,4},{1,3},{2,6},{3,1},{4,0},{5,7},{6,2},{7,5},{8,12},{9,11},{10,... | collective-permute-start | bytes 737288 | tf_op jit(solution)/shard_map/ppermute | solution.py:32
  53.6 2.0 %collective-permute-start.13 = (bf16[160,1664]{1,0:T(8,128)(2,1)S(1)}, bf16[160,1664]{1,0:T(8,128)(2,1)S(1)}, u32[]{:S(2)}, u32[]{:S(2)}) collective-permute-start(bf16[160,1664]{1,0:T(8,128)(2,1)S(1)} %get-tuple-element.92), channel_id=1, source_target_pairs={{0,1},{1,0},{2,3},{3,2},{4,5},{5,4},{6,7},{7,6},{8,9},{9,8},{10,11... | collective-permute-start | bytes 1597448 | tf_op jit(solution)/shard_map/ppermute | solution.py:32
  54.0 13.4 %collective-permute-start.15 = (bf16[160,1664]{1,0:T(8,128)(2,1)S(1)}, bf16[160,1664]{1,0:T(8,128)(2,1)S(1)}, u32[]{:S(2)}, u32[]{:S(2)}) collective-permute-start(bf16[160,1664]{1,0:T(8,128)(2,1)S(1)} %add_convert_fusion.1), channel_id=1, source_target_pairs={{0,2},{1,5},{2,0},{3,7},{4,6},{5,1},{6,4},{7,3},{8,10},{9,13},{10,... | collective-permute-start | bytes 1597448 | tf_op jit(solution)/shard_map/ppermute | solution.py:32
  61.2 14.1 %collective-permute-start.19 = (bf16[160,1536]{1,0:T(8,128)(2,1)S(1)}, bf16[160,1536]{1,0:T(8,128)(2,1)S(1)}, u32[]{:S(2)}, u32[]{:S(2)}) collective-permute-start(bf16[160,1536]{1,0:T(8,128)(2,1)S(1)} %stack_rows.21.refs_0_), channel_id=1, source_target_pairs={{0,2},{1,5},{2,0},{3,7},{4,6},{5,1},{6,4},{7,3},{8,10},{9,13},{10,... | collective-permute-start | bytes 1474568 | tf_op jit(solution)/shard_map/ppermute | solution.py:32
  67.5 8.0 %collective-permute-start.18 = (bf16[80,1664]{1,0:T(8,128)(2,1)S(1)}, bf16[80,1664]{1,0:T(8,128)(2,1)S(1)}, u32[]{:S(2)}, u32[]{:S(2)}) collective-permute-start(bf16[80,1664]{1,0:T(8,128)(2,1)S(1)} %add_convert_fusion.5), channel_id=1, source_target_pairs={{0,4},{1,3},{2,6},{3,1},{4,0},{5,7},{6,2},{7,5},{8,12},{9,11},{10,... | collective-permute-start | bytes 798728 | tf_op jit(solution)/shard_map/ppermute | solution.py:32
  68.8 22.3 %collective-permute-start.12 = (bf16[80,1664]{1,0:T(8,128)(2,1)S(1)}, bf16[80,1664]{1,0:T(8,128)(2,1)S(1)}, u32[]{:S(2)}, u32[]{:S(2)}) collective-permute-start(bf16[80,1664]{1,0:T(8,128)(2,1)S(1)} %get-tuple-element.94), channel_id=1, source_target_pairs={{0,4},{1,3},{2,6},{3,1},{4,0},{5,7},{6,2},{7,5},{8,12},{9,11},{10,... | collective-permute-start | bytes 798728 | tf_op jit(solution)/shard_map/ppermute | solution.py:32
  69.8 6.8 %collective-permute-start.21 = (bf16[320,1536]{1,0:T(8,128)(2,1)S(1)}, bf16[320,1536]{1,0:T(8,128)(2,1)S(1)}, u32[]{:S(2)}, u32[]{:S(2)}) collective-permute-start(bf16[320,1536]{1,0:T(8,128)(2,1)S(1)} %stack_rows.22.refs_0_), channel_id=1, source_target_pairs={{0,1},{1,0},{2,3},{3,2},{4,5},{5,4},{6,7},{7,6},{8,9},{9,8},{10,11... | collective-permute-start | bytes 2949128 | tf_op jit(solution)/shard_map/ppermute | solution.py:32
  75.3 2.6 %collective-permute-start.22 = (bf16[320,1536]{1,0:T(8,128)(2,1)S(1)}, bf16[320,1536]{1,0:T(8,128)(2,1)S(1)}, u32[]{:S(2)}, u32[]{:S(2)}) collective-permute-start(bf16[320,1536]{1,0:T(8,128)(2,1)S(1)} %stack_rows.23.refs_2_), channel_id=1, source_target_pairs={{0,1},{1,0},{2,3},{3,2},{4,5},{5,4},{6,7},{7,6},{8,9},{9,8},{10,11... | collective-permute-start | bytes 2949128 | tf_op jit(solution)/shard_map/ppermute | solution.py:32
  75.6 15.5 %collective-permute-start.20 = (bf16[80,1664]{1,0:T(8,128)(2,1)S(1)}, bf16[80,1664]{1,0:T(8,128)(2,1)S(1)}, u32[]{:S(2)}, u32[]{:S(2)}) collective-permute-start(bf16[80,1664]{1,0:T(8,128)(2,1)S(1)} %pause.3), channel_id=1, source_target_pairs={{0,8},{1,9},{2,10},{3,11},{4,12},{5,13},{6,14},{7,15},{8,0},{9,1},... | collective-permute-start | bytes 798728 | tf_op jit(solution)/shard_map/ppermute | solution.py:38
  78.2 12.8 %copy-start.7 = (f32[128]{0:T(128)S(1)}, f32[128]{0:T(128)}, u32[]{:S(2)}) copy-start(f32[128]{0:T(128)} %param.11) | copy-start | bytes 1540

commit v9 on v8

--- a/solution.py
+++ b/solution.py
@@ -303,10 +303,12 @@
 
     far_grad = cross(far_grad, 1)
     got = meet(near_grad, 0)
-    near_two = join(near_grad, after(got, near_row))
+    row_got = meet(near_row, 0)
+    act, slope = activation(by_source, order)
+    near_two = join(near_grad, after(got, act))
     got = meet(near_two, 1)
-    act, slope = activation(by_source, after(order, near_two))
-    far_grad = pause(after(far_grad, act))
+    near_row2 = join(near_row, after(row_got, near_two))
+    far_grad = pause(after(far_grad, near_row2))
     far_got = meet(far_grad, 0)
     near_four = join(near_two, after(got, far_grad))
     got = meet(near_four, 2)
@@ -324,7 +326,7 @@
     far_four = join(far_two, after(far_got, far_row_a), long=True)
     far_got = meet(far_four, 2)
     far_row_b = cross(after(far_row_b, far_four), 1)
-    row_got = meet(after(near_row, far_four), 0)
+    row_got = meet(after(near_row2, far_four), 1)
     near_kept, near_sent = add_halves(near_kept, after(near_got, far_four))
     near_got = meet(near_sent, 1)
     far_grads = join(far_four, after(far_got, near_sent))
@@ -333,25 +335,24 @@
         far_grads, w_out, w_in, act[near_count:], slope[near_count:]
     )
     far_row = join_slots(far_row_a, after(far_row_b, far_sent), experts)
-    near_row2 = join(near_row, after(row_got, far_sent))
     far_kept, far_on = halves(far_kept)
-    far_sent = halves(after(far_sent, far_row, near_row2))
-    far_got, on_got = [meet(x, 2) for x in far_sent]
-    row_got = meet(near_row2, 1)
-    far_row_got = meet(far_row, 0)
+    far_sent = halves(after(far_sent, far_row))
+    on_got = meet(far_sent[1], 2)
     near_kept, near_sent = add_halves(near_kept, after(near_got, far_sent[1]))
-    near_got = meet(near_sent, 0)
-    far_sent = add(far_on, after(on_got, near_sent))
-    on_got = meet(far_sent, 1)
-    far_kept = add(far_kept, after(far_got, far_sent))
+    near_row4 = join(near_row2, after(row_got, near_sent), long=True)
+    far_on = add(far_on, after(on_got, near_row4))
+    on_got = meet(far_on, 1)
+    far_row_got = meet(after(far_row, far_on), 0)
+    far_got = meet(after(far_sent[0], far_on), 2)
     w_out_grad = product(
-        after(act, far_kept), join(near_grads, far_grads), ((0,), (0,))
+        after(act, far_on), join(near_grads, far_grads), ((0,), (0,))
     ).astype(BF16)
+    far_kept = add(far_kept, after(far_got, w_out_grad))
     far_row2 = join(far_row, after(far_row_got, w_out_grad))
     far_row_got = meet(far_row2, 1)
-    near_row4 = join(near_row2, after(row_got, far_row2))
     row_got = meet(near_row4, 2)
-    far_kept, far_sent = add_halves(far_kept, after(on_got, near_row4))
+    near_got = meet(near_sent, 0)
+    far_kept, far_sent = add_halves(far_kept, after(on_got, far_row2))
     far_got = meet(far_sent, 0)
     far_row4 = join(far_row2, after(far_row_got, far_sent))
     near_sent = far_row4

time: 92.5 us -> 98.8 us (1.068)
  waiting for transfers between devices: 32.8 us -> 42.5 us
  starting transfers between devices: 26.1 us -> 23.4 us
    ppermute x19, waiting for transfers between devices: 23.5 us -> 31.3 us  [meet(): lax.ppermute(rows, 'expert', [(i, i ^ bits(i % 2)[step]) for i in range(d...]
    ppermute x19, starting transfers between devices: 20.2 us -> 15.7 us  [meet(): lax.ppermute(rows, 'expert', [(i, i ^ bits(i % 2)[step]) for i in range(d...]
    ppermute x4, waiting for transfers between devices: 9.31 us -> 11.3 us  [shift(): return lax.ppermute(rows, 'expert', pairs)]
    ppermute x4, starting transfers between devices: 5.96 us -> 7.68 us  [shift(): return lax.ppermute(rows, 'expert', pairs)]
    unnamed x16 -> x14, local copies, waits for them, and re-layouts: 6.82 us -> 6.18 us
  transfers between devices with their start and end apart: 23 -> 23, of which waited for: 12 -> 10; matrix products, arithmetic and copies ran while one was open for 11% -> 10% of each run, Pallas kernels for 14% -> 13%
where the time goes in v9:
time: 98.8 us; the launch traced here: 98.5 us
  waiting for transfers between devices  42.5 us (43%)
  starting transfers between devices  23.4 us (24%)
  Pallas kernels  14.3 us (14%)
  matrix products  9.13 us (9%)
  local copies, waits for them, and re-layouts  6.59 us (7%)
  other arithmetic  1.61 us (2%)
    ppermute x19, waiting for transfers between devices, meet(): lax.ppermute(rows, 'expert', [(i, i ^ bits(i % 2)[step]) for i in range(d...  31.3 us
    ppermute x19, starting transfers between devices, meet(): lax.ppermute(rows, 'expert', [(i, i ^ bits(i % 2)[step]) for i in range(d...  15.7 us
    ppermute x4, waiting for transfers between devices, shift(): return lax.ppermute(rows, 'expert', pairs)  11.3 us
    dot_general x2, matrix products, product(): return lax.dot_general(a, b, (dims, ((), ())), preferred_element_type=F32)  9.13 us
    pallas_call x2, Pallas kernels, slot_grads(): pl.pallas_call(slot_grad_kernel, out_shape=(jax.ShapeDtypeStruct((rows, u...  7.81 us
    ppermute x4, starting transfers between devices, shift(): return lax.ppermute(rows, 'expert', pairs)  7.68 us
    unnamed x14, local copies, waits for them, and re-layouts  6.18 us
    pallas_call x1, Pallas kernels, activation(): pl.pallas_call(activation_kernel, grid_spec=pltpu.PrefetchScalarGridSpec(...  3.36 us
  transfers between devices with their start and end apart: 23, of which 10 were waited for; matrix products, arithmetic and copies ran while one was open for 10% of the time, Pallas kernels for 13%

profile of v9, /device:TPU:0, one launch (start us, length us, event | category | flops | bytes accessed | tf_op | source)
XLA Modules:
  0.0 98.5 jit_solution(358623623704905443)
XLA Ops:
  0.6 0.7 fusion.place
  1.3 1.0 %copy-done.3 = bf16[128,1536]{1,0:T(8,128)(2,1)S(1)} copy-done((bf16[128,1536]{1,0:T(8,128)(2,1)S(1)}, bf16[128,1536]{1,0:T(8,128)(2,1)}, u32[]{:S(2)}) %copy-start.3) | copy-done | bytes 393240
  2.3 0.7 copy-done.5
  3.0 0.4 rows_to_slots.2
  3.4 3.1 %collective-permute-start = (bf16[80,1536]{1,0:T(8,128)(2,1)S(1)}, bf16[80,1536]{1,0:T(8,128)(2,1)S(1)}, u32[]{:S(2)}, u32[]{:S(2)}) collective-permute-start(bf16[80,1536]{1,0:T(8,128)(2,1)S(1)} %get-tuple-element.46.refs_0_), channel_id=1, source_target_pairs={{0,4},{1,3},{2,6},{3,1},{4,0},{5,7},{6,2},{7,5},{8,12},{9,11},{10,... | collective-permute-start | bytes 737288 | tf_op jit(solution)/shard_map/ppermute | solution.py:32
  6.5 2.6 %collective-permute-start.2 = (bf16[80,1536]{1,0:T(8,128)(2,1)S(1)}, bf16[80,1536]{1,0:T(8,128)(2,1)S(1)}, u32[]{:S(2)}, u32[]{:S(2)}) collective-permute-start(bf16[80,1536]{1,0:T(8,128)(2,1)S(1)} %get-tuple-element.49), channel_id=1, source_target_pairs={{0,8},{1,9},{2,10},{3,11},{4,12},{5,13},{6,14},{7,15},{8,0},{9,1},... | collective-permute-start | bytes 737288 | tf_op jit(solution)/shard_map/ppermute | solution.py:38
  9.0 1.0 %copy-done.4 = bf16[128,1536]{1,0:T(8,128)(2,1)S(1)} copy-done((bf16[128,1536]{1,0:T(8,128)(2,1)S(1)}, bf16[128,1536]{1,0:T(8,128)(2,1)}, u32[]{:S(2)}) %copy-start.4) | copy-done | bytes 393240
  10.0 0.3 rows_to_slots.3
  10.3 0.5 collective-permute-start.3
  10.9 0.1 pad_add_fusion.order
  11.0 1.5 %copy-done.2 = bf16[1280,768]{1,0:T(8,128)(2,1)S(1)} copy-done((bf16[1280,768]{1,0:T(8,128)(2,1)S(1)}, bf16[1280,768]{1,0:T(8,128)(2,1)}, u32[]{:S(2)}) %copy-start.2) | copy-done | bytes 1966104
  12.5 3.4 %activation.1 = (bf16[16,80,768]{2,1,0:T(8,128)(2,1)S(1)}, bf16[16,80,768]{2,1,0:T(8,128)(2,1)S(1)}) custom-call(s32[16]{0:T(128)S(1)} %pad_add_fusion.order, bf16[16,80,768]{2,1,0:T(8,128)(2,1)S(1)} %bitcast.27), custom_call_target="tpu_custom_call" | custom-call | tf_op jit(solution)/shard_map/activation/pallas_call | solution.py:169
  15.9 1.6 %collective-permute-start.1 = (bf16[160,1536]{1,0:T(8,128)(2,1)S(1)}, bf16[160,1536]{1,0:T(8,128)(2,1)S(1)}, u32[]{:S(2)}, u32[]{:S(2)}) collective-permute-start(bf16[160,1536]{1,0:T(8,128)(2,1)S(1)} %stack_rows.13.refs_0_), channel_id=1, source_target_pairs={{0,2},{1,5},{2,0},{3,7},{4,6},{5,1},{6,4},{7,3},{8,10},{9,13},{10,... | collective-permute-start | bytes 1474568 | tf_op jit(solution)/shard_map/ppermute | solution.py:32
  17.5 2.0 %collective-permute-done.3.refs_1_ = bf16[80,1536]{1,0:T(8,128)(2,1)S(1)} collective-permute-done((bf16[80,1536]{1,0:T(8,128)(2,1)S(1)}, bf16[80,1536]{1,0:T(8,128)(2,1)S(1)}, u32[]{:S(2)}, u32[]{:S(2)}) %collective-permute-start.3) | collective-permute-done | bytes 245792 | tf_op jit(solution)/shard_map/ppermute | solution.py:32
  19.5 0.6 collective-permute-done.2.rows
  20.1 2.0 %collective-permute-start.5 = (bf16[80,1536]{1,0:T(8,128)(2,1)S(1)}, bf16[80,1536]{1,0:T(8,128)(2,1)S(1)}, u32[]{:S(2)}, u32[]{:S(2)}) collective-permute-start(bf16[80,1536]{1,0:T(8,128)(2,1)S(1)} %pause.2.refs_0_), channel_id=1, source_target_pairs={{0,4},{1,3},{2,6},{3,1},{4,0},{5,7},{6,2},{7,5},{8,12},{9,11},{10,... | collective-permute-start | bytes 737288 | tf_op jit(solution)/shard_map/ppermute | solution.py:32
  22.1 5.3 %collective-permute-done.1.refs_1_ = bf16[160,1536]{1,0:T(8,128)(2,1)S(1)} collective-permute-done((bf16[160,1536]{1,0:T(8,128)(2,1)S(1)}, bf16[160,1536]{1,0:T(8,128)(2,1)S(1)}, u32[]{:S(2)}, u32[]{:S(2)}) %collective-permute-start.1) | collective-permute-done | bytes 491552 | tf_op jit(solution)/shard_map/ppermute | solution.py:32
  27.5 0.1 stack_rows.15.refs_0_
  27.5 0.1 collective-permute-start.4
  27.7 1.6 %collective-permute-start.7 = (bf16[160,1536]{1,0:T(8,128)(2,1)S(1)}, bf16[160,1536]{1,0:T(8,128)(2,1)S(1)}, u32[]{:S(2)}, u32[]{:S(2)}) collective-permute-start(bf16[160,1536]{1,0:T(8,128)(2,1)S(1)} %stack_rows.16.refs_0_), channel_id=1, source_target_pairs={{0,2},{1,5},{2,0},{3,7},{4,6},{5,1},{6,4},{7,3},{8,10},{9,13},{10,... | collective-permute-start | bytes 1474568 | tf_op jit(solution)/shard_map/ppermute | solution.py:32
  29.2 2.7 %collective-permute-start.8 = (bf16[64,1536]{1,0:T(8,128)(2,1)S(1)}, bf16[64,1536]{1,0:T(8,128)(2,1)S(1)}, u32[]{:S(2)}, u32[]{:S(2)}) collective-permute-start(bf16[64,1536]{1,0:T(8,128)(2,1)S(1)} %slice_bitcast_fusion), channel_id=1, source_target_pairs={{0,8},{1,9},{2,10},{3,11},{4,12},{5,13},{6,14},{7,15},{8,0},{9,1},... | collective-permute-start | bytes 589832 | tf_op jit(solution)/shard_map/ppermute | solution.py:38
  32.0 0.3 fusion.3
  32.3 0.1 stack_rows.17.grads.refs_0_
  32.5 1.2 %copy-done.1 = bf16[1536,768]{1,0:T(8,128)(2,1)S(1)} copy-done((bf16[1536,768]{1,0:T(8,128)(2,1)S(1)}, bf16[1536,768]{1,0:T(8,128)(2,1)}, u32[]{:S(2)}) %copy-start.1) | copy-done | bytes 2359320
  33.6 0.8 copy-done
  34.4 3.9 %slot_grads.2 = (bf16[640,768]{1,0:T(8,128)(2,1)S(1)}, bf16[320,1664]{1,0:T(8,128)(2,1)S(1)}, bf16[320,1664]{1,0:T(8,128)(2,1)S(1)}) custom-call(bf16[640,1536]{1,0:T(8,128)(2,1)S(1)} %stack_rows.17.grads.refs_0_, bf16[768,1536]{1,0:T(8,128)(2,1)S(1)} %copy-done, bf16[1536,768]{1,0:T(8,128)(2,1)S(1)} %copy-done.1, bf16[640,768]{1,0:T(8,128)(2,1)S(1)} %bitcast.26, ...), custom_call_target="tpu_custom_call" | custom-call | tf_op jit(solution)/shard_map/slot_grads/pallas_call | solution.py:275
  38.3 0.1 collective-permute-start.6
  38.4 3.1 %collective-permute-done.8 = bf16[64,1536]{1,0:T(8,128)(2,1)S(1)} collective-permute-done((bf16[64,1536]{1,0:T(8,128)(2,1)S(1)}, bf16[64,1536]{1,0:T(8,128)(2,1)S(1)}, u32[]{:S(2)}, u32[]{:S(2)}) %collective-permute-start.8) | collective-permute-done | bytes 196640 | tf_op jit(solution)/shard_map/ppermute | solution.py:38
  41.6 0.1 stack_rows.18.refs_0_
  41.6 0.1 collective-permute-start.10
  41.7 1.0 %collective-permute-start.11 = (bf16[16,1536]{1,0:T(8,128)(2,1)S(1)}, bf16[16,1536]{1,0:T(8,128)(2,1)S(1)}, u32[]{:S(2)}, u32[]{:S(2)}) collective-permute-start(bf16[16,1536]{1,0:T(8,128)(2,1)S(1)} %slice_bitcast_fusion.1), channel_id=1, source_target_pairs={{0,8},{1,9},{2,10},{3,11},{4,12},{5,13},{6,14},{7,15},{8,0},{9,1},... | collective-permute-start | bytes 147464 | tf_op jit(solution)/shard_map/ppermute | solution.py:38
  42.7 1.5 %collective-permute-start.14 = (bf16[160,1536]{1,0:T(8,128)(2,1)S(1)}, bf16[160,1536]{1,0:T(8,128)(2,1)S(1)}, u32[]{:S(2)}, u32[]{:S(2)}) collective-permute-start(bf16[160,1536]{1,0:T(8,128)(2,1)S(1)} %stack_rows.14.refs_0_), channel_id=1, source_target_pairs={{0,2},{1,5},{2,0},{3,7},{4,6},{5,1},{6,4},{7,3},{8,10},{9,13},{10,... | collective-permute-start | bytes 1474568 | tf_op jit(solution)/shard_map/ppermute | solution.py:32
  44.2 0.2 add_convert_fusion.2
  44.5 0.6 collective-permute-start.9
  45.1 0.1 stack_rows.19.grads.refs_1_
  45.2 3.9 %slot_grads.3 = (bf16[640,768]{1,0:T(8,128)(2,1)S(1)}, bf16[320,1664]{1,0:T(8,128)(2,1)S(1)}, bf16[320,1664]{1,0:T(8,128)(2,1)S(1)}) custom-call(bf16[640,1536]{1,0:T(8,128)(2,1)S(1)} %stack_rows.19.grads.refs_1_, bf16[768,1536]{1,0:T(8,128)(2,1)S(1)} %copy-done, bf16[1536,768]{1,0:T(8,128)(2,1)S(1)} %copy-done.1, bf16[640,768]{1,0:T(8,128)(2,1)S(1)} %bitcast.24, ...), custom_call_target="tpu_custom_call" | custom-call | tf_op jit(solution)/shard_map/slot_grads/pallas_call | solution.py:275
  49.1 0.1 fusion.5
  49.2 0.3 stack_rows.21
  49.5 0.1 collective-permute-start.13
  49.6 7.7 %collective-permute-done.9 = bf16[160,1664]{1,0:T(8,128)(2,1)S(1)} collective-permute-done((bf16[160,1664]{1,0:T(8,128)(2,1)S(1)}, bf16[160,1664]{1,0:T(8,128)(2,1)S(1)}, u32[]{:S(2)}, u32[]{:S(2)}) %collective-permute-start.9) | collective-permute-done | bytes 532512 | tf_op jit(solution)/shard_map/ppermute | solution.py:32
  57.3 0.1 add_convert_fusion.7
  57.4 0.1 stack_rows.20.refs_0_
  57.5 0.1 add_convert_fusion.1
  57.6 1.6 %collective-permute-start.16 = (bf16[160,1664]{1,0:T(8,128)(2,1)S(1)}, bf16[160,1664]{1,0:T(8,128)(2,1)S(1)}, u32[]{:S(2)}, u32[]{:S(2)}) collective-permute-start(bf16[160,1664]{1,0:T(8,128)(2,1)S(1)} %add_convert_fusion.1), channel_id=1, source_target_pairs={{0,2},{1,5},{2,0},{3,7},{4,6},{5,1},{6,4},{7,3},{8,10},{9,13},{10,... | collective-permute-start | bytes 1597448 | tf_op jit(solution)/shard_map/ppermute | solution.py:32
  59.2 0.2 collective-permute-start.17
  59.4 4.5 %convolution_convert_fusion.1 = bf16[768,1536]{1,0:T(8,128)(2,1)} fusion(bf16[1280,768]{1,0:T(8,128)(2,1)S(1)} %bitcast.28, bf16[1280,1536]{1,0:T(8,128)(2,1)S(1)} %stack_rows.21), kind=kOutput, calls=%fused_computation.1 | convolution fusion | flops 3021078528 | bytes 8257536 | tf_op jit(solution)/shard_map/dot_general | solution.py:250
  64.0 4.1 %collective-permute-done.17.refs_1_ = bf16[80,1536]{1,0:T(8,128)(2,1)S(1)} collective-permute-done((bf16[80,1536]{1,0:T(8,128)(2,1)S(1)}, bf16[80,1536]{1,0:T(8,128)(2,1)S(1)}, u32[]{:S(2)}, u32[]{:S(2)}) %collective-permute-start.17) | collective-permute-done | bytes 245792 | tf_op jit(solution)/shard_map/ppermute | solution.py:32
  68.1 0.6 collective-permute-start.19
  68.7 0.1 add_convert_fusion
  68.8 0.7 collective-permute-done.16
  69.6 0.1 add_convert_fusion.5
  69.6 0.6 collective-permute-start.18
  70.2 0.1 stack_rows.25
  70.4 1.6 %collective-permute-start.12 = (bf16[80,1664]{1,0:T(8,128)(2,1)S(1)}, bf16[80,1664]{1,0:T(8,128)(2,1)S(1)}, u32[]{:S(2)}, u32[]{:S(2)}) collective-permute-start(bf16[80,1664]{1,0:T(8,128)(2,1)S(1)} %get-tuple-element.96), channel_id=1, source_target_pairs={{0,4},{1,3},{2,6},{3,1},{4,0},{5,7},{6,2},{7,5},{8,12},{9,11},{10,... | collective-permute-start | bytes 798728 | tf_op jit(solution)/shard_map/ppermute | solution.py:32
  71.9 10.3 %collective-permute-done.19.refs_1_ = bf16[160,1536]{1,0:T(8,128)(2,1)S(1)} collective-permute-done((bf16[160,1536]{1,0:T(8,128)(2,1)S(1)}, bf16[160,1536]{1,0:T(8,128)(2,1)S(1)}, u32[]{:S(2)}, u32[]{:S(2)}) %collective-permute-start.19) | collective-permute-done | bytes 491552 | tf_op jit(solution)/shard_map/ppermute | solution.py:32
  82.3 0.1 stack_rows.23.refs_2_
  82.3 0.1 collective-permute-start.22
  82.4 0.1 add_convert_fusion.4.rows
  82.6 1.4 %collective-permute-start.20 = (bf16[80,1664]{1,0:T(8,128)(2,1)S(1)}, bf16[80,1664]{1,0:T(8,128)(2,1)S(1)}, u32[]{:S(2)}, u32[]{:S(2)}) collective-permute-start(bf16[80,1664]{1,0:T(8,128)(2,1)S(1)} %pause.3), channel_id=1, source_target_pairs={{0,8},{1,9},{2,10},{3,11},{4,12},{5,13},{6,14},{7,15},{8,0},{9,1},... | collective-permute-start | bytes 798728 | tf_op jit(solution)/shard_map/ppermute | solution.py:38
  83.9 1.0 %collective-permute-done.22.refs_3_ = bf16[320,1536]{1,0:T(8,128)(2,1)S(1)} collective-permute-done((bf16[320,1536]{1,0:T(8,128)(2,1)S(1)}, bf16[320,1536]{1,0:T(8,128)(2,1)S(1)}, u32[]{:S(2)}, u32[]{:S(2)}) %collective-permute-start.22) | collective-permute-done | bytes 983072 | tf_op jit(solution)/shard_map/ppermute | solution.py:32
  85.0 0.3 stack_rows.24
  85.2 4.6 %convolution_convert_fusion = bf16[1536,768]{1,0:T(8,128)(2,1)} fusion(bf16[1280,1536]{1,0:T(8,128)(2,1)S(1)} %stack_rows.24, bf16[1280,768]{1,0:T(8,128)(2,1)S(1)} %stack_rows.25), kind=kOutput, calls=%fused_computation | convolution fusion | flops 3021078528 | bytes 8257536 | tf_op jit(solution)/shard_map/dot_general | solution.py:250
  89.8 7.5 %collective-permute-done.20.back = bf16[80,1664]{1,0:T(8,128)(2,1)S(1)} collective-permute-done((bf16[80,1664]{1,0:T(8,128)(2,1)S(1)}, bf16[80,1664]{1,0:T(8,128)(2,1)S(1)}, u32[]{:S(2)}, u32[]{:S(2)}) %collective-permute-start.20) | collective-permute-done | bytes 266272 | tf_op jit(solution)/shard_map/ppermute | solution.py:38
  97.4 1.1 %slots_to_tokens.1 = (bf16[128,1536]{1,0:T(8,128)(2,1)}, f32[1,128]{1,0:T(1,128)}) custom-call(s32[1,128]{1,0:T(1,128)S(1)} %fusion.place, f32[1,128]{1,0:T(1,128)S(1)} %bitcast.33, bf16[80,1664]{1,0:T(8,128)(2,1)S(1)} %get-tuple-element.97.kept, bf16[80,1664]{1,0:T(8,128)(2,1)S(1)} %collective-permute-done.12.got, ...), custom_call_target="tpu_custom_call" | custom-call | tf_op jit(solution)/shard_map/slots_to_tokens/pallas_call | solution.py:136
  (34 shorter events, 0.3 us)
Async XLA Ops:
  1.3 1.0 %copy-start.3 = (bf16[128,1536]{1,0:T(8,128)(2,1)S(1)}, bf16[128,1536]{1,0:T(8,128)(2,1)}, u32[]{:S(2)}) copy-start(bf16[128,1536]{1,0:T(8,128)(2,1)} %values.2) | copy-start | bytes 1179652
  2.3 0.7 copy-start.5
  3.4 12.5 %collective-permute-start = (bf16[80,1536]{1,0:T(8,128)(2,1)S(1)}, bf16[80,1536]{1,0:T(8,128)(2,1)S(1)}, u32[]{:S(2)}, u32[]{:S(2)}) collective-permute-start(bf16[80,1536]{1,0:T(8,128)(2,1)S(1)} %get-tuple-element.46.refs_0_), channel_id=1, source_target_pairs={{0,4},{1,3},{2,6},{3,1},{4,0},{5,7},{6,2},{7,5},{8,12},{9,11},{10,... | collective-permute-start | bytes 737288 | tf_op jit(solution)/shard_map/ppermute | solution.py:32
  6.5 13.7 %collective-permute-start.2 = (bf16[80,1536]{1,0:T(8,128)(2,1)S(1)}, bf16[80,1536]{1,0:T(8,128)(2,1)S(1)}, u32[]{:S(2)}, u32[]{:S(2)}) collective-permute-start(bf16[80,1536]{1,0:T(8,128)(2,1)S(1)} %get-tuple-element.49), channel_id=1, source_target_pairs={{0,8},{1,9},{2,10},{3,11},{4,12},{5,13},{6,14},{7,15},{8,0},{9,1},... | collective-permute-start | bytes 737288 | tf_op jit(solution)/shard_map/ppermute | solution.py:38
  9.0 1.0 %copy-start.4 = (bf16[128,1536]{1,0:T(8,128)(2,1)S(1)}, bf16[128,1536]{1,0:T(8,128)(2,1)}, u32[]{:S(2)}) copy-start(bf16[128,1536]{1,0:T(8,128)(2,1)} %values.3) | copy-start | bytes 1179652
  10.3 9.2 %collective-permute-start.3 = (bf16[80,1536]{1,0:T(8,128)(2,1)S(1)}, bf16[80,1536]{1,0:T(8,128)(2,1)S(1)}, u32[]{:S(2)}, u32[]{:S(2)}) collective-permute-start(bf16[80,1536]{1,0:T(8,128)(2,1)S(1)} %get-tuple-element.50.refs_0_), channel_id=1, source_target_pairs={{0,4},{1,3},{2,6},{3,1},{4,0},{5,7},{6,2},{7,5},{8,12},{9,11},{10,... | collective-permute-start | bytes 737288 | tf_op jit(solution)/shard_map/ppermute | solution.py:32
  11.0 1.5 %copy-start.2 = (bf16[1280,768]{1,0:T(8,128)(2,1)S(1)}, bf16[1280,768]{1,0:T(8,128)(2,1)}, u32[]{:S(2)}) copy-start(bf16[1280,768]{1,0:T(8,128)(2,1)} %param.15) | copy-start | bytes 5898244
  15.9 11.5 %collective-permute-start.1 = (bf16[160,1536]{1,0:T(8,128)(2,1)S(1)}, bf16[160,1536]{1,0:T(8,128)(2,1)S(1)}, u32[]{:S(2)}, u32[]{:S(2)}) collective-permute-start(bf16[160,1536]{1,0:T(8,128)(2,1)S(1)} %stack_rows.13.refs_0_), channel_id=1, source_target_pairs={{0,2},{1,5},{2,0},{3,7},{4,6},{5,1},{6,4},{7,3},{8,10},{9,13},{10,... | collective-permute-start | bytes 1474568 | tf_op jit(solution)/shard_map/ppermute | solution.py:32
  20.1 7.5 %collective-permute-start.5 = (bf16[80,1536]{1,0:T(8,128)(2,1)S(1)}, bf16[80,1536]{1,0:T(8,128)(2,1)S(1)}, u32[]{:S(2)}, u32[]{:S(2)}) collective-permute-start(bf16[80,1536]{1,0:T(8,128)(2,1)S(1)} %pause.2.refs_0_), channel_id=1, source_target_pairs={{0,4},{1,3},{2,6},{3,1},{4,0},{5,7},{6,2},{7,5},{8,12},{9,11},{10,... | collective-permute-start | bytes 737288 | tf_op jit(solution)/shard_map/ppermute | solution.py:32
  27.5 4.8 %collective-permute-start.4 = (bf16[320,1536]{1,0:T(8,128)(2,1)S(1)}, bf16[320,1536]{1,0:T(8,128)(2,1)S(1)}, u32[]{:S(2)}, u32[]{:S(2)}) collective-permute-start(bf16[320,1536]{1,0:T(8,128)(2,1)S(1)} %stack_rows.15.refs_0_), channel_id=1, source_target_pairs={{0,1},{1,0},{2,3},{3,2},{4,5},{5,4},{6,7},{7,6},{8,9},{9,8},{10,11... | collective-permute-start | bytes 2949128 | tf_op jit(solution)/shard_map/ppermute | solution.py:32
  27.7 13.9 %collective-permute-start.7 = (bf16[160,1536]{1,0:T(8,128)(2,1)S(1)}, bf16[160,1536]{1,0:T(8,128)(2,1)S(1)}, u32[]{:S(2)}, u32[]{:S(2)}) collective-permute-start(bf16[160,1536]{1,0:T(8,128)(2,1)S(1)} %stack_rows.16.refs_0_), channel_id=1, source_target_pairs={{0,2},{1,5},{2,0},{3,7},{4,6},{5,1},{6,4},{7,3},{8,10},{9,13},{10,... | collective-permute-start | bytes 1474568 | tf_op jit(solution)/shard_map/ppermute | solution.py:32
  29.2 12.3 %collective-permute-start.8 = (bf16[64,1536]{1,0:T(8,128)(2,1)S(1)}, bf16[64,1536]{1,0:T(8,128)(2,1)S(1)}, u32[]{:S(2)}, u32[]{:S(2)}) collective-permute-start(bf16[64,1536]{1,0:T(8,128)(2,1)S(1)} %slice_bitcast_fusion), channel_id=1, source_target_pairs={{0,8},{1,9},{2,10},{3,11},{4,12},{5,13},{6,14},{7,15},{8,0},{9,1},... | collective-permute-start | bytes 589832 | tf_op jit(solution)/shard_map/ppermute | solution.py:38
  32.0 1.7 %copy-start.1 = (bf16[1536,768]{1,0:T(8,128)(2,1)S(1)}, bf16[1536,768]{1,0:T(8,128)(2,1)}, u32[]{:S(2)}) copy-start(bf16[1536,768]{1,0:T(8,128)(2,1)} %w_in.3) | copy-start | bytes 7077892
  32.3 2.1 %copy-start = (bf16[768,1536]{1,0:T(8,128)(2,1)S(1)}, bf16[768,1536]{1,0:T(8,128)(2,1)}, u32[]{:S(2)}) copy-start(bf16[768,1536]{1,0:T(8,128)(2,1)} %w_out.3) | copy-start | bytes 7077892
  38.3 5.9 %collective-permute-start.6 = (bf16[320,1664]{1,0:T(8,128)(2,1)S(1)}, bf16[320,1664]{1,0:T(8,128)(2,1)S(1)}, u32[]{:S(2)}, u32[]{:S(2)}) collective-permute-start(bf16[320,1664]{1,0:T(8,128)(2,1)S(1)} %get-tuple-element.58), channel_id=1, source_target_pairs={{0,1},{1,0},{2,3},{3,2},{4,5},{5,4},{6,7},{7,6},{8,9},{9,8},{10,11... | collective-permute-start | bytes 3194888 | tf_op jit(solution)/shard_map/ppermute | solution.py:32
  41.6 3.4 %collective-permute-start.10 = (bf16[320,1536]{1,0:T(8,128)(2,1)S(1)}, bf16[320,1536]{1,0:T(8,128)(2,1)S(1)}, u32[]{:S(2)}, u32[]{:S(2)}) collective-permute-start(bf16[320,1536]{1,0:T(8,128)(2,1)S(1)} %stack_rows.18.refs_0_), channel_id=1, source_target_pairs={{0,1},{1,0},{2,3},{3,2},{4,5},{5,4},{6,7},{7,6},{8,9},{9,8},{10,11... | collective-permute-start | bytes 2949128 | tf_op jit(solution)/shard_map/ppermute | solution.py:32
  41.7 7.4 %collective-permute-start.11 = (bf16[16,1536]{1,0:T(8,128)(2,1)S(1)}, bf16[16,1536]{1,0:T(8,128)(2,1)S(1)}, u32[]{:S(2)}, u32[]{:S(2)}) collective-permute-start(bf16[16,1536]{1,0:T(8,128)(2,1)S(1)} %slice_bitcast_fusion.1), channel_id=1, source_target_pairs={{0,8},{1,9},{2,10},{3,11},{4,12},{5,13},{6,14},{7,15},{8,0},{9,1},... | collective-permute-start | bytes 147464 | tf_op jit(solution)/shard_map/ppermute | solution.py:38
  42.7 14.7 %collective-permute-start.14 = (bf16[160,1536]{1,0:T(8,128)(2,1)S(1)}, bf16[160,1536]{1,0:T(8,128)(2,1)S(1)}, u32[]{:S(2)}, u32[]{:S(2)}) collective-permute-start(bf16[160,1536]{1,0:T(8,128)(2,1)S(1)} %stack_rows.14.refs_0_), channel_id=1, source_target_pairs={{0,2},{1,5},{2,0},{3,7},{4,6},{5,1},{6,4},{7,3},{8,10},{9,13},{10,... | collective-permute-start | bytes 1474568 | tf_op jit(solution)/shard_map/ppermute | solution.py:32
  44.5 12.8 %collective-permute-start.9 = (bf16[160,1664]{1,0:T(8,128)(2,1)S(1)}, bf16[160,1664]{1,0:T(8,128)(2,1)S(1)}, u32[]{:S(2)}, u32[]{:S(2)}) collective-permute-start(bf16[160,1664]{1,0:T(8,128)(2,1)S(1)} %get-tuple-element.88), channel_id=1, source_target_pairs={{0,2},{1,5},{2,0},{3,7},{4,6},{5,1},{6,4},{7,3},{8,10},{9,13},{10,... | collective-permute-start | bytes 1597448 | tf_op jit(solution)/shard_map/ppermute | solution.py:32
  49.5 8.0 %collective-permute-start.13 = (bf16[160,1664]{1,0:T(8,128)(2,1)S(1)}, bf16[160,1664]{1,0:T(8,128)(2,1)S(1)}, u32[]{:S(2)}, u32[]{:S(2)}) collective-permute-start(bf16[160,1664]{1,0:T(8,128)(2,1)S(1)} %get-tuple-element.95), channel_id=1, source_target_pairs={{0,1},{1,0},{2,3},{3,2},{4,5},{5,4},{6,7},{7,6},{8,9},{9,8},{10,11... | collective-permute-start | bytes 1597448 | tf_op jit(solution)/shard_map/ppermute | solution.py:32
  57.6 12.0 %collective-permute-start.16 = (bf16[160,1664]{1,0:T(8,128)(2,1)S(1)}, bf16[160,1664]{1,0:T(8,128)(2,1)S(1)}, u32[]{:S(2)}, u32[]{:S(2)}) collective-permute-start(bf16[160,1664]{1,0:T(8,128)(2,1)S(1)} %add_convert_fusion.1), channel_id=1, source_target_pairs={{0,2},{1,5},{2,0},{3,7},{4,6},{5,1},{6,4},{7,3},{8,10},{9,13},{10,... | collective-permute-start | bytes 1597448 | tf_op jit(solution)/shard_map/ppermute | solution.py:32
  59.2 9.5 %collective-permute-start.15 = (bf16[160,1664]{1,0:T(8,128)(2,1)S(1)}, bf16[160,1664]{1,0:T(8,128)(2,1)S(1)}, u32[]{:S(2)}, u32[]{:S(2)}) collective-permute-start(bf16[160,1664]{1,0:T(8,128)(2,1)S(1)} %get-tuple-element.74), channel_id=1, source_target_pairs={{0,1},{1,0},{2,3},{3,2},{4,5},{5,4},{6,7},{7,6},{8,9},{9,8},{10,11... | collective-permute-start | bytes 1597448 | tf_op jit(solution)/shard_map/ppermute | solution.py:32
  59.2 8.9 %collective-permute-start.17 = (bf16[80,1536]{1,0:T(8,128)(2,1)S(1)}, bf16[80,1536]{1,0:T(8,128)(2,1)S(1)}, u32[]{:S(2)}, u32[]{:S(2)}) collective-permute-start(bf16[80,1536]{1,0:T(8,128)(2,1)S(1)} %maximum_bitcast_fusion.refs_0_), channel_id=1, source_target_pairs={{0,4},{1,3},{2,6},{3,1},{4,0},{5,7},{6,2},{7,5},{8,12},{9,11},{10,... | collective-permute-start | bytes 737288 | tf_op jit(solution)/shard_map/ppermute | solution.py:32
  68.1 14.2 %collective-permute-start.19 = (bf16[160,1536]{1,0:T(8,128)(2,1)S(1)}, bf16[160,1536]{1,0:T(8,128)(2,1)S(1)}, u32[]{:S(2)}, u32[]{:S(2)}) collective-permute-start(bf16[160,1536]{1,0:T(8,128)(2,1)S(1)} %stack_rows.22.refs_0_), channel_id=1, source_target_pairs={{0,2},{1,5},{2,0},{3,7},{4,6},{5,1},{6,4},{7,3},{8,10},{9,13},{10,... | collective-permute-start | bytes 1474568 | tf_op jit(solution)/shard_map/ppermute | solution.py:32
  69.6 12.8 %collective-permute-start.18 = (bf16[80,1664]{1,0:T(8,128)(2,1)S(1)}, bf16[80,1664]{1,0:T(8,128)(2,1)S(1)}, u32[]{:S(2)}, u32[]{:S(2)}) collective-permute-start(bf16[80,1664]{1,0:T(8,128)(2,1)S(1)} %add_convert_fusion.5), channel_id=1, source_target_pairs={{0,4},{1,3},{2,6},{3,1},{4,0},{5,7},{6,2},{7,5},{8,12},{9,11},{10,... | collective-permute-start | bytes 798728 | tf_op jit(solution)/shard_map/ppermute | solution.py:32
  70.4 27.0 %collective-permute-start.12 = (bf16[80,1664]{1,0:T(8,128)(2,1)S(1)}, bf16[80,1664]{1,0:T(8,128)(2,1)S(1)}, u32[]{:S(2)}, u32[]{:S(2)}) collective-permute-start(bf16[80,1664]{1,0:T(8,128)(2,1)S(1)} %get-tuple-element.96), channel_id=1, source_target_pairs={{0,4},{1,3},{2,6},{3,1},{4,0},{5,7},{6,2},{7,5},{8,12},{9,11},{10,... | collective-permute-start | bytes 798728 | tf_op jit(solution)/shard_map/ppermute | solution.py:32
  71.9 12.0 %collective-permute-start.21 = (bf16[320,1536]{1,0:T(8,128)(2,1)S(1)}, bf16[320,1536]{1,0:T(8,128)(2,1)S(1)}, u32[]{:S(2)}, u32[]{:S(2)}) collective-permute-start(bf16[320,1536]{1,0:T(8,128)(2,1)S(1)} %stack_rows.20.refs_0_), channel_id=1, source_target_pairs={{0,1},{1,0},{2,3},{3,2},{4,5},{5,4},{6,7},{7,6},{8,9},{9,8},{10,11... | collective-permute-start | bytes 2949128 | tf_op jit(solution)/shard_map/ppermute | solution.py:32
  82.3 2.6 %collective-permute-start.22 = (bf16[320,1536]{1,0:T(8,128)(2,1)S(1)}, bf16[320,1536]{1,0:T(8,128)(2,1)S(1)}, u32[]{:S(2)}, u32[]{:S(2)}) collective-permute-start(bf16[320,1536]{1,0:T(8,128)(2,1)S(1)} %stack_rows.23.refs_2_), channel_id=1, source_target_pairs={{0,1},{1,0},{2,3},{3,2},{4,5},{5,4},{6,7},{7,6},{8,9},{9,8},{10,11... | collective-permute-start | bytes 2949128 | tf_op jit(solution)/shard_map/ppermute | solution.py:32
  82.6 14.8 %collective-permute-start.20 = (bf16[80,1664]{1,0:T(8,128)(2,1)S(1)}, bf16[80,1664]{1,0:T(8,128)(2,1)S(1)}, u32[]{:S(2)}, u32[]{:S(2)}) collective-permute-start(bf16[80,1664]{1,0:T(8,128)(2,1)S(1)} %pause.3), channel_id=1, source_target_pairs={{0,8},{1,9},{2,10},{3,11},{4,12},{5,13},{6,14},{7,15},{8,0},{9,1},... | collective-permute-start | bytes 798728 | tf_op jit(solution)/shard_map/ppermute | solution.py:38
  85.2 12.1 %copy-start.6 = (f32[128]{0:T(128)S(1)}, f32[128]{0:T(128)}, u32[]{:S(2)}) copy-start(f32[128]{0:T(128)} %param.11) | copy-start | bytes 1540

commit v10 on v8

--- a/solution.py
+++ b/solution.py
@@ -142,6 +142,7 @@
         in_specs=[VMEM] * 5,
         out_specs=(VMEM, VMEM),
         compiler_params=params(12),
+        cost_estimate=cost(LONG, 0),
         name="slots_to_tokens",
     )(place, gate, kept, got, back)
 
@@ -303,10 +304,10 @@
 
     far_grad = cross(far_grad, 1)
     got = meet(near_grad, 0)
-    near_two = join(near_grad, after(got, near_row))
+    act, slope = activation(by_source, order)
+    near_two = join(near_grad, after(got, near_row, act))
     got = meet(near_two, 1)
-    act, slope = activation(by_source, after(order, near_two))
-    far_grad = pause(after(far_grad, act))
+    far_grad = pause(after(far_grad, near_two))
     far_got = meet(far_grad, 0)
     near_four = join(near_two, after(got, far_grad))
     got = meet(near_four, 2)
@@ -340,28 +341,29 @@
     row_got = meet(near_row2, 1)
     far_row_got = meet(far_row, 0)
     near_kept, near_sent = add_halves(near_kept, after(near_got, far_sent[1]))
-    near_got = meet(near_sent, 0)
     far_sent = add(far_on, after(on_got, near_sent))
     on_got = meet(far_sent, 1)
+    near_got = meet(after(near_sent, far_sent), 0)
     far_kept = add(far_kept, after(far_got, far_sent))
     w_out_grad = product(
         after(act, far_kept), join(near_grads, far_grads), ((0,), (0,))
     ).astype(BF16)
     far_row2 = join(far_row, after(far_row_got, w_out_grad))
-    far_row_got = meet(far_row2, 1)
     near_row4 = join(near_row2, after(row_got, far_row2))
     row_got = meet(near_row4, 2)
-    far_kept, far_sent = add_halves(far_kept, after(on_got, near_row4))
+    near_got = after(near_got, near_row4)
+    far_kept, far_sent = add_halves(far_kept, after(on_got, near_got))
     far_got = meet(far_sent, 0)
-    far_row4 = join(far_row2, after(far_row_got, far_sent))
-    near_sent = far_row4
-    far_sum = pause(add(far_kept, after(far_got, near_sent)))
+    far_sum = pause(add(far_kept, far_got))
     back = cross(far_sum, -1)
-    rows = join(near_row4, row_got, far_row4, meet(far_row4, 2))
+
+    far_row_got = meet(after(far_row2, far_sum), 1)
+    far_row4 = join(far_row2, far_row_got)
+    far_row_got = meet(far_row4, 2)
+    back = after(back, far_row4)
+    token_grad, gate_grad = to_tokens(slots, place, gate, near_kept, near_got, back)
+    rows = join(near_row4, row_got, far_row4, after(far_row_got, token_grad))
     w_in_grad = product(rows, join(near_hg, far_hg), ((0,), (0,))).astype(BF16)
-    back = after(back, w_in_grad)
-    near_got = after(near_got, back)
-    token_grad, gate_grad = to_tokens(slots, place, gate, near_kept, near_got, back)
     return (token_grad, gate_grad.reshape(-1), w_in_grad, w_out_grad)
 
 

time: 92.5 us -> 98.7 us (1.067)
  waiting for transfers between devices: 32.8 us -> 42.2 us
  starting transfers between devices: 26.1 us -> 23.4 us
    ppermute x19, waiting for transfers between devices: 23.5 us -> 32.3 us  [meet(): lax.ppermute(rows, 'expert', [(i, i ^ bits(i % 2)[step]) for i in range(d...]
    ppermute x19, starting transfers between devices: 20.2 us -> 18.6 us  [meet(): lax.ppermute(rows, 'expert', [(i, i ^ bits(i % 2)[step]) for i in range(d...]
    ppermute x4, starting transfers between devices: 5.96 us -> 4.77 us  [shift(): return lax.ppermute(rows, 'expert', pairs)]
  transfers between devices with their start and end apart: 23 -> 23, of which waited for: 12 -> 12; matrix products, arithmetic and copies ran while one was open for 11% -> 6% of each run, Pallas kernels for 14% -> 14%
where the time goes in v10:
time: 98.7 us; the launch traced here: 98.4 us
  waiting for transfers between devices  42.2 us (43%)
  starting transfers between devices  23.4 us (24%)
  Pallas kernels  14.3 us (14%)
  matrix products  9.15 us (9%)
  local copies, waits for them, and re-layouts  6.77 us (7%)
  other arithmetic  1.64 us (2%)
    ppermute x19, waiting for transfers between devices, meet(): lax.ppermute(rows, 'expert', [(i, i ^ bits(i % 2)[step]) for i in range(d...  32.3 us
    ppermute x19, starting transfers between devices, meet(): lax.ppermute(rows, 'expert', [(i, i ^ bits(i % 2)[step]) for i in range(d...  18.6 us
    ppermute x4, waiting for transfers between devices, shift(): return lax.ppermute(rows, 'expert', pairs)  9.91 us
    dot_general x2, matrix products, product(): return lax.dot_general(a, b, (dims, ((), ())), preferred_element_type=F32)  9.15 us
    pallas_call x2, Pallas kernels, slot_grads(): pl.pallas_call(slot_grad_kernel, out_shape=(jax.ShapeDtypeStruct((rows, u...  7.81 us
    unnamed x16, local copies, waits for them, and re-layouts  6.36 us
    ppermute x4, starting transfers between devices, shift(): return lax.ppermute(rows, 'expert', pairs)  4.77 us
    pallas_call x1, Pallas kernels, activation(): pl.pallas_call(activation_kernel, grid_spec=pltpu.PrefetchScalarGridSpec(...  3.36 us
  transfers between devices with their start and end apart: 23, of which 12 were waited for; matrix products, arithmetic and copies ran while one was open for 6% of the time, Pallas kernels for 14%

profile of v10, /device:TPU:0, one launch (start us, length us, event | category | flops | bytes accessed | tf_op | source)
XLA Modules:
  0.0 98.4 jit_solution(9028236488183964563)
XLA Ops:
  0.6 0.7 fusion.place
  1.3 1.0 %copy-done.3 = bf16[128,1536]{1,0:T(8,128)(2,1)S(1)} copy-done((bf16[128,1536]{1,0:T(8,128)(2,1)S(1)}, bf16[128,1536]{1,0:T(8,128)(2,1)}, u32[]{:S(2)}) %copy-start.3) | copy-done | bytes 393240
  2.3 0.7 copy-done.5
  3.0 0.4 rows_to_slots.2
  3.4 3.1 %collective-permute-start = (bf16[80,1536]{1,0:T(8,128)(2,1)S(1)}, bf16[80,1536]{1,0:T(8,128)(2,1)S(1)}, u32[]{:S(2)}, u32[]{:S(2)}) collective-permute-start(bf16[80,1536]{1,0:T(8,128)(2,1)S(1)} %get-tuple-element.45.refs_0_), channel_id=1, source_target_pairs={{0,4},{1,3},{2,6},{3,1},{4,0},{5,7},{6,2},{7,5},{8,12},{9,11},{10,... | collective-permute-start | bytes 737288 | tf_op jit(solution)/shard_map/ppermute | solution.py:32
  6.5 2.6 %collective-permute-start.2 = (bf16[80,1536]{1,0:T(8,128)(2,1)S(1)}, bf16[80,1536]{1,0:T(8,128)(2,1)S(1)}, u32[]{:S(2)}, u32[]{:S(2)}) collective-permute-start(bf16[80,1536]{1,0:T(8,128)(2,1)S(1)} %get-tuple-element.49), channel_id=1, source_target_pairs={{0,8},{1,9},{2,10},{3,11},{4,12},{5,13},{6,14},{7,15},{8,0},{9,1},... | collective-permute-start | bytes 737288 | tf_op jit(solution)/shard_map/ppermute | solution.py:38
  9.1 1.0 %copy-done.4 = bf16[128,1536]{1,0:T(8,128)(2,1)S(1)} copy-done((bf16[128,1536]{1,0:T(8,128)(2,1)S(1)}, bf16[128,1536]{1,0:T(8,128)(2,1)}, u32[]{:S(2)}) %copy-start.4) | copy-done | bytes 393240
  10.1 0.7 copy-done.6
  10.7 0.3 rows_to_slots.3
  11.0 0.1 pad_add_fusion.order
  11.1 1.5 %copy-done.2 = bf16[1280,768]{1,0:T(8,128)(2,1)S(1)} copy-done((bf16[1280,768]{1,0:T(8,128)(2,1)S(1)}, bf16[1280,768]{1,0:T(8,128)(2,1)}, u32[]{:S(2)}) %copy-start.2) | copy-done | bytes 1966104
  12.6 3.4 %activation.1 = (bf16[16,80,768]{2,1,0:T(8,128)(2,1)S(1)}, bf16[16,80,768]{2,1,0:T(8,128)(2,1)S(1)}) custom-call(s32[16]{0:T(128)S(1)} %pad_add_fusion.order, bf16[16,80,768]{2,1,0:T(8,128)(2,1)S(1)} %bitcast.27), custom_call_target="tpu_custom_call" | custom-call | tf_op jit(solution)/shard_map/activation/pallas_call | solution.py:170
  16.1 1.6 %collective-permute-start.1 = (bf16[160,1536]{1,0:T(8,128)(2,1)S(1)}, bf16[160,1536]{1,0:T(8,128)(2,1)S(1)}, u32[]{:S(2)}, u32[]{:S(2)}) collective-permute-start(bf16[160,1536]{1,0:T(8,128)(2,1)S(1)} %stack_rows.13.refs_0_), channel_id=1, source_target_pairs={{0,2},{1,5},{2,0},{3,7},{4,6},{5,1},{6,4},{7,3},{8,10},{9,13},{10,... | collective-permute-start | bytes 1474568 | tf_op jit(solution)/shard_map/ppermute | solution.py:32
  17.6 2.5 %collective-permute-done.2.rows = bf16[80,1536]{1,0:T(8,128)(2,1)S(1)} collective-permute-done((bf16[80,1536]{1,0:T(8,128)(2,1)S(1)}, bf16[80,1536]{1,0:T(8,128)(2,1)S(1)}, u32[]{:S(2)}, u32[]{:S(2)}) %collective-permute-start.2) | collective-permute-done | bytes 245792 | tf_op jit(solution)/shard_map/ppermute | solution.py:38
  20.1 0.7 collective-permute-start.4
  20.8 6.8 %collective-permute-done.1.refs_1_ = bf16[160,1536]{1,0:T(8,128)(2,1)S(1)} collective-permute-done((bf16[160,1536]{1,0:T(8,128)(2,1)S(1)}, bf16[160,1536]{1,0:T(8,128)(2,1)S(1)}, u32[]{:S(2)}, u32[]{:S(2)}) %collective-permute-start.1) | collective-permute-done | bytes 491552 | tf_op jit(solution)/shard_map/ppermute | solution.py:32
  27.7 0.1 collective-permute-start.3
  27.8 1.6 %collective-permute-start.6 = (bf16[160,1536]{1,0:T(8,128)(2,1)S(1)}, bf16[160,1536]{1,0:T(8,128)(2,1)S(1)}, u32[]{:S(2)}, u32[]{:S(2)}) collective-permute-start(bf16[160,1536]{1,0:T(8,128)(2,1)S(1)} %stack_rows.15.refs_0_), channel_id=1, source_target_pairs={{0,2},{1,5},{2,0},{3,7},{4,6},{5,1},{6,4},{7,3},{8,10},{9,13},{10,... | collective-permute-start | bytes 1474568 | tf_op jit(solution)/shard_map/ppermute | solution.py:32
  29.4 0.1 collective-permute-start.7
  29.5 0.3 fusion.3
  29.8 0.5 collective-permute-done.3.refs_1_
  30.3 0.1 stack_rows.16.grads.refs_0_
  30.4 0.7 copy-done.1
  31.1 0.8 copy-done
  31.9 3.9 %slot_grads.2 = (bf16[640,768]{1,0:T(8,128)(2,1)S(1)}, bf16[320,1664]{1,0:T(8,128)(2,1)S(1)}, bf16[320,1664]{1,0:T(8,128)(2,1)S(1)}) custom-call(bf16[640,1536]{1,0:T(8,128)(2,1)S(1)} %stack_rows.16.grads.refs_0_, bf16[768,1536]{1,0:T(8,128)(2,1)S(1)} %copy-done, bf16[1536,768]{1,0:T(8,128)(2,1)S(1)} %copy-done.1, bf16[640,768]{1,0:T(8,128)(2,1)S(1)} %bitcast.26, ...), custom_call_target="tpu_custom_call" | custom-call | tf_op jit(solution)/shard_map/slot_grads/pallas_call | solution.py:276
  35.8 0.2 collective-permute-start.5
  36.1 4.3 %collective-permute-done.7 = bf16[64,1536]{1,0:T(8,128)(2,1)S(1)} collective-permute-done((bf16[64,1536]{1,0:T(8,128)(2,1)S(1)}, bf16[64,1536]{1,0:T(8,128)(2,1)S(1)}, u32[]{:S(2)}, u32[]{:S(2)}) %collective-permute-start.7) | collective-permute-done | bytes 196640 | tf_op jit(solution)/shard_map/ppermute | solution.py:38
  40.5 0.1 collective-permute-start.9
  40.6 1.0 collective-permute-start.10
  41.6 0.6 collective-permute-start.11
  42.2 0.2 add_convert_fusion.2
  42.4 1.2 %collective-permute-start.8 = (bf16[160,1664]{1,0:T(8,128)(2,1)S(1)}, bf16[160,1664]{1,0:T(8,128)(2,1)S(1)}, u32[]{:S(2)}, u32[]{:S(2)}) collective-permute-start(bf16[160,1664]{1,0:T(8,128)(2,1)S(1)} %get-tuple-element.86), channel_id=1, source_target_pairs={{0,2},{1,5},{2,0},{3,7},{4,6},{5,1},{6,4},{7,3},{8,10},{9,13},{10,... | collective-permute-start | bytes 1597448 | tf_op jit(solution)/shard_map/ppermute | solution.py:32
  43.6 0.1 stack_rows.18.grads.refs_1_
  43.7 3.9 %slot_grads.3 = (bf16[640,768]{1,0:T(8,128)(2,1)S(1)}, bf16[320,1664]{1,0:T(8,128)(2,1)S(1)}, bf16[320,1664]{1,0:T(8,128)(2,1)S(1)}) custom-call(bf16[640,1536]{1,0:T(8,128)(2,1)S(1)} %stack_rows.18.grads.refs_1_, bf16[768,1536]{1,0:T(8,128)(2,1)S(1)} %copy-done, bf16[1536,768]{1,0:T(8,128)(2,1)S(1)} %copy-done.1, bf16[640,768]{1,0:T(8,128)(2,1)S(1)} %bitcast.24, ...), custom_call_target="tpu_custom_call" | custom-call | tf_op jit(solution)/shard_map/slot_grads/pallas_call | solution.py:276
  47.6 3.3 %collective-permute-done.11.refs_1_ = bf16[80,1536]{1,0:T(8,128)(2,1)S(1)} collective-permute-done((bf16[80,1536]{1,0:T(8,128)(2,1)S(1)}, bf16[80,1536]{1,0:T(8,128)(2,1)S(1)}, u32[]{:S(2)}, u32[]{:S(2)}) %collective-permute-start.11) | collective-permute-done | bytes 245792 | tf_op jit(solution)/shard_map/ppermute | solution.py:32
  51.0 0.1 fusion.5
  51.1 0.1 collective-permute-start.12
  51.1 1.8 %collective-permute-start.14 = (bf16[160,1536]{1,0:T(8,128)(2,1)S(1)}, bf16[160,1536]{1,0:T(8,128)(2,1)S(1)}, u32[]{:S(2)}, u32[]{:S(2)}) collective-permute-start(bf16[160,1536]{1,0:T(8,128)(2,1)S(1)} %stack_rows.19.refs_0_), channel_id=1, source_target_pairs={{0,2},{1,5},{2,0},{3,7},{4,6},{5,1},{6,4},{7,3},{8,10},{9,13},{10,... | collective-permute-start | bytes 1474568 | tf_op jit(solution)/shard_map/ppermute | solution.py:32
  53.0 0.5 collective-permute-start.15
  53.4 0.3 stack_rows.20
  53.7 0.1 collective-permute-start.16
  53.8 0.1 add_convert_fusion.7
  53.9 0.1 add_convert_fusion.1
  54.0 0.9 collective-permute-start.17
  55.0 1.0 collective-permute-start.13
  55.9 0.1 add_convert_fusion
  56.1 4.6 %convolution_convert_fusion.1 = bf16[768,1536]{1,0:T(8,128)(2,1)} fusion(bf16[1280,768]{1,0:T(8,128)(2,1)S(1)} %bitcast.28, bf16[1280,1536]{1,0:T(8,128)(2,1)S(1)} %stack_rows.20), kind=kOutput, calls=%fused_computation.1 | convolution fusion | flops 3021078528 | bytes 8257536 | tf_op jit(solution)/shard_map/dot_general | solution.py:251
  60.6 1.2 %collective-permute-done.15.refs_1_ = bf16[80,1536]{1,0:T(8,128)(2,1)S(1)} collective-permute-done((bf16[80,1536]{1,0:T(8,128)(2,1)S(1)}, bf16[80,1536]{1,0:T(8,128)(2,1)S(1)}, u32[]{:S(2)}, u32[]{:S(2)}) %collective-permute-start.15) | collective-permute-done | bytes 245792 | tf_op jit(solution)/shard_map/ppermute | solution.py:32
  61.9 3.3 %collective-permute-done.14.refs_1_ = bf16[160,1536]{1,0:T(8,128)(2,1)S(1)} collective-permute-done((bf16[160,1536]{1,0:T(8,128)(2,1)S(1)}, bf16[160,1536]{1,0:T(8,128)(2,1)S(1)}, u32[]{:S(2)}, u32[]{:S(2)}) %collective-permute-start.14) | collective-permute-done | bytes 491552 | tf_op jit(solution)/shard_map/ppermute | solution.py:32
  65.2 2.3 %collective-permute-done.13.got = bf16[80,1664]{1,0:T(8,128)(2,1)S(1)} collective-permute-done((bf16[80,1664]{1,0:T(8,128)(2,1)S(1)}, bf16[80,1664]{1,0:T(8,128)(2,1)S(1)}, u32[]{:S(2)}, u32[]{:S(2)}) %collective-permute-start.13) | collective-permute-done | bytes 266272 | tf_op jit(solution)/shard_map/ppermute | solution.py:32
  67.5 3.3 %collective-permute-done.17 = bf16[160,1664]{1,0:T(8,128)(2,1)S(1)} collective-permute-done((bf16[160,1664]{1,0:T(8,128)(2,1)S(1)}, bf16[160,1664]{1,0:T(8,128)(2,1)S(1)}, u32[]{:S(2)}, u32[]{:S(2)}) %collective-permute-start.17) | collective-permute-done | bytes 532512 | tf_op jit(solution)/shard_map/ppermute | solution.py:32
  71.0 0.6 collective-permute-start.18
  71.6 5.9 %collective-permute-done.18 = bf16[80,1664]{1,0:T(8,128)(2,1)S(1)} collective-permute-done((bf16[80,1664]{1,0:T(8,128)(2,1)S(1)}, bf16[80,1664]{1,0:T(8,128)(2,1)S(1)}, u32[]{:S(2)}, u32[]{:S(2)}) %collective-permute-start.18) | collective-permute-done | bytes 266272 | tf_op jit(solution)/shard_map/ppermute | solution.py:32
  77.4 0.1 add_convert_fusion.4.rows
  77.6 1.8 %collective-permute-start.20 = (bf16[160,1536]{1,0:T(8,128)(2,1)S(1)}, bf16[160,1536]{1,0:T(8,128)(2,1)S(1)}, u32[]{:S(2)}, u32[]{:S(2)}) collective-permute-start(bf16[160,1536]{1,0:T(8,128)(2,1)S(1)} %stack_rows.21.refs_0_), channel_id=1, source_target_pairs={{0,2},{1,5},{2,0},{3,7},{4,6},{5,1},{6,4},{7,3},{8,10},{9,13},{10,... | collective-permute-start | bytes 1474568 | tf_op jit(solution)/shard_map/ppermute | solution.py:32
  79.4 1.1 %collective-permute-start.19 = (bf16[80,1664]{1,0:T(8,128)(2,1)S(1)}, bf16[80,1664]{1,0:T(8,128)(2,1)S(1)}, u32[]{:S(2)}, u32[]{:S(2)}) collective-permute-start(bf16[80,1664]{1,0:T(8,128)(2,1)S(1)} %pause.3), channel_id=1, source_target_pairs={{0,8},{1,9},{2,10},{3,11},{4,12},{5,13},{6,14},{7,15},{8,0},{9,1},... | collective-permute-start | bytes 798728 | tf_op jit(solution)/shard_map/ppermute | solution.py:38
  80.5 0.1 stack_rows.25
  80.7 0.1 collective-permute-start.21
  80.7 5.7 %collective-permute-done.20.refs_1_ = bf16[160,1536]{1,0:T(8,128)(2,1)S(1)} collective-permute-done((bf16[160,1536]{1,0:T(8,128)(2,1)S(1)}, bf16[160,1536]{1,0:T(8,128)(2,1)S(1)}, u32[]{:S(2)}, u32[]{:S(2)}) %collective-permute-start.20) | collective-permute-done | bytes 491552 | tf_op jit(solution)/shard_map/ppermute | solution.py:32
  86.6 2.8 %collective-permute-start.22 = (bf16[320,1536]{1,0:T(8,128)(2,1)S(1)}, bf16[320,1536]{1,0:T(8,128)(2,1)S(1)}, u32[]{:S(2)}, u32[]{:S(2)}) collective-permute-start(bf16[320,1536]{1,0:T(8,128)(2,1)S(1)} %stack_rows.23.refs_2_), channel_id=1, source_target_pairs={{0,1},{1,0},{2,3},{3,2},{4,5},{5,4},{6,7},{7,6},{8,9},{9,8},{10,11... | collective-permute-start | bytes 2949128 | tf_op jit(solution)/shard_map/ppermute | solution.py:32
  89.3 3.1 %collective-permute-done.19.back = bf16[80,1664]{1,0:T(8,128)(2,1)S(1)} collective-permute-done((bf16[80,1664]{1,0:T(8,128)(2,1)S(1)}, bf16[80,1664]{1,0:T(8,128)(2,1)S(1)}, u32[]{:S(2)}, u32[]{:S(2)}) %collective-permute-start.19) | collective-permute-done | bytes 266272 | tf_op jit(solution)/shard_map/ppermute | solution.py:38
  92.4 1.1 %slots_to_tokens.1 = (bf16[128,1536]{1,0:T(8,128)(2,1)}, f32[1,128]{1,0:T(1,128)}) custom-call(s32[1,128]{1,0:T(1,128)S(1)} %fusion.place, f32[1,128]{1,0:T(1,128)S(1)} %bitcast.33, bf16[80,1664]{1,0:T(8,128)(2,1)S(1)} %get-tuple-element.95.kept, bf16[80,1664]{1,0:T(8,128)(2,1)S(1)} %collective-permute-done.13.got, ...), custom_call_target="tpu_custom_call" | custom-call | flops 20000000000 | tf_op jit(solution)/shard_map/slots_to_tokens/pallas_call | solution.py:136
  93.6 0.3 stack_rows.24
  93.8 4.6 %convolution_convert_fusion = bf16[1536,768]{1,0:T(8,128)(2,1)} fusion(bf16[1280,1536]{1,0:T(8,128)(2,1)S(1)} %stack_rows.24, bf16[1280,768]{1,0:T(8,128)(2,1)S(1)} %stack_rows.25), kind=kOutput, calls=%fused_computation | convolution fusion | flops 3021078528 | bytes 8257536 | tf_op jit(solution)/shard_map/dot_general | solution.py:251
  (36 shorter events, 0.6 us)
Async XLA Ops:
  1.3 1.0 %copy-start.3 = (bf16[128,1536]{1,0:T(8,128)(2,1)S(1)}, bf16[128,1536]{1,0:T(8,128)(2,1)}, u32[]{:S(2)}) copy-start(bf16[128,1536]{1,0:T(8,128)(2,1)} %values.2) | copy-start | bytes 1179652
  2.3 0.7 copy-start.5
  3.4 12.7 %collective-permute-start = (bf16[80,1536]{1,0:T(8,128)(2,1)S(1)}, bf16[80,1536]{1,0:T(8,128)(2,1)S(1)}, u32[]{:S(2)}, u32[]{:S(2)}) collective-permute-start(bf16[80,1536]{1,0:T(8,128)(2,1)S(1)} %get-tuple-element.45.refs_0_), channel_id=1, source_target_pairs={{0,4},{1,3},{2,6},{3,1},{4,0},{5,7},{6,2},{7,5},{8,12},{9,11},{10,... | collective-permute-start | bytes 737288 | tf_op jit(solution)/shard_map/ppermute | solution.py:32
  6.5 13.7 %collective-permute-start.2 = (bf16[80,1536]{1,0:T(8,128)(2,1)S(1)}, bf16[80,1536]{1,0:T(8,128)(2,1)S(1)}, u32[]{:S(2)}, u32[]{:S(2)}) collective-permute-start(bf16[80,1536]{1,0:T(8,128)(2,1)S(1)} %get-tuple-element.49), channel_id=1, source_target_pairs={{0,8},{1,9},{2,10},{3,11},{4,12},{5,13},{6,14},{7,15},{8,0},{9,1},... | collective-permute-start | bytes 737288 | tf_op jit(solution)/shard_map/ppermute | solution.py:38
  9.1 1.0 %copy-start.4 = (bf16[128,1536]{1,0:T(8,128)(2,1)S(1)}, bf16[128,1536]{1,0:T(8,128)(2,1)}, u32[]{:S(2)}) copy-start(bf16[128,1536]{1,0:T(8,128)(2,1)} %values.3) | copy-start | bytes 1179652
  10.1 0.7 copy-start.6
  11.1 1.5 %copy-start.2 = (bf16[1280,768]{1,0:T(8,128)(2,1)S(1)}, bf16[1280,768]{1,0:T(8,128)(2,1)}, u32[]{:S(2)}) copy-start(bf16[1280,768]{1,0:T(8,128)(2,1)} %param.15) | copy-start | bytes 5898244
  16.1 11.5 %collective-permute-start.1 = (bf16[160,1536]{1,0:T(8,128)(2,1)S(1)}, bf16[160,1536]{1,0:T(8,128)(2,1)S(1)}, u32[]{:S(2)}, u32[]{:S(2)}) collective-permute-start(bf16[160,1536]{1,0:T(8,128)(2,1)S(1)} %stack_rows.13.refs_0_), channel_id=1, source_target_pairs={{0,2},{1,5},{2,0},{3,7},{4,6},{5,1},{6,4},{7,3},{8,10},{9,13},{10,... | collective-permute-start | bytes 1474568 | tf_op jit(solution)/shard_map/ppermute | solution.py:32
  20.1 7.6 %collective-permute-start.4 = (bf16[80,1536]{1,0:T(8,128)(2,1)S(1)}, bf16[80,1536]{1,0:T(8,128)(2,1)S(1)}, u32[]{:S(2)}, u32[]{:S(2)}) collective-permute-start(bf16[80,1536]{1,0:T(8,128)(2,1)S(1)} %pause.2.refs_0_), channel_id=1, source_target_pairs={{0,4},{1,3},{2,6},{3,1},{4,0},{5,7},{6,2},{7,5},{8,12},{9,11},{10,... | collective-permute-start | bytes 737288 | tf_op jit(solution)/shard_map/ppermute | solution.py:32
  27.7 2.6 %collective-permute-start.3 = (bf16[320,1536]{1,0:T(8,128)(2,1)S(1)}, bf16[320,1536]{1,0:T(8,128)(2,1)S(1)}, u32[]{:S(2)}, u32[]{:S(2)}) collective-permute-start(bf16[320,1536]{1,0:T(8,128)(2,1)S(1)} %stack_rows.14.refs_0_), channel_id=1, source_target_pairs={{0,1},{1,0},{2,3},{3,2},{4,5},{5,4},{6,7},{7,6},{8,9},{9,8},{10,11... | collective-permute-start | bytes 2949128 | tf_op jit(solution)/shard_map/ppermute | solution.py:32
  27.8 12.6 %collective-permute-start.6 = (bf16[160,1536]{1,0:T(8,128)(2,1)S(1)}, bf16[160,1536]{1,0:T(8,128)(2,1)S(1)}, u32[]{:S(2)}, u32[]{:S(2)}) collective-permute-start(bf16[160,1536]{1,0:T(8,128)(2,1)S(1)} %stack_rows.15.refs_0_), channel_id=1, source_target_pairs={{0,2},{1,5},{2,0},{3,7},{4,6},{5,1},{6,4},{7,3},{8,10},{9,13},{10,... | collective-permute-start | bytes 1474568 | tf_op jit(solution)/shard_map/ppermute | solution.py:32
  29.4 11.0 %collective-permute-start.7 = (bf16[64,1536]{1,0:T(8,128)(2,1)S(1)}, bf16[64,1536]{1,0:T(8,128)(2,1)S(1)}, u32[]{:S(2)}, u32[]{:S(2)}) collective-permute-start(bf16[64,1536]{1,0:T(8,128)(2,1)S(1)} %slice_bitcast_fusion), channel_id=1, source_target_pairs={{0,8},{1,9},{2,10},{3,11},{4,12},{5,13},{6,14},{7,15},{8,0},{9,1},... | collective-permute-start | bytes 589832 | tf_op jit(solution)/shard_map/ppermute | solution.py:38
  29.5 1.7 %copy-start.1 = (bf16[1536,768]{1,0:T(8,128)(2,1)S(1)}, bf16[1536,768]{1,0:T(8,128)(2,1)}, u32[]{:S(2)}) copy-start(bf16[1536,768]{1,0:T(8,128)(2,1)} %w_in.3) | copy-start | bytes 7077892
  29.8 2.1 %copy-start = (bf16[768,1536]{1,0:T(8,128)(2,1)S(1)}, bf16[768,1536]{1,0:T(8,128)(2,1)}, u32[]{:S(2)}) copy-start(bf16[768,1536]{1,0:T(8,128)(2,1)} %w_out.3) | copy-start | bytes 7077892
  35.8 6.3 %collective-permute-start.5 = (bf16[320,1664]{1,0:T(8,128)(2,1)S(1)}, bf16[320,1664]{1,0:T(8,128)(2,1)S(1)}, u32[]{:S(2)}, u32[]{:S(2)}) collective-permute-start(bf16[320,1664]{1,0:T(8,128)(2,1)S(1)} %get-tuple-element.56), channel_id=1, source_target_pairs={{0,1},{1,0},{2,3},{3,2},{4,5},{5,4},{6,7},{7,6},{8,9},{9,8},{10,11... | collective-permute-start | bytes 3194888 | tf_op jit(solution)/shard_map/ppermute | solution.py:32
  40.5 3.1 %collective-permute-start.9 = (bf16[320,1536]{1,0:T(8,128)(2,1)S(1)}, bf16[320,1536]{1,0:T(8,128)(2,1)S(1)}, u32[]{:S(2)}, u32[]{:S(2)}) collective-permute-start(bf16[320,1536]{1,0:T(8,128)(2,1)S(1)} %stack_rows.17.refs_0_), channel_id=1, source_target_pairs={{0,1},{1,0},{2,3},{3,2},{4,5},{5,4},{6,7},{7,6},{8,9},{9,8},{10,11... | collective-permute-start | bytes 2949128 | tf_op jit(solution)/shard_map/ppermute | solution.py:32
  40.6 7.0 %collective-permute-start.10 = (bf16[16,1536]{1,0:T(8,128)(2,1)S(1)}, bf16[16,1536]{1,0:T(8,128)(2,1)S(1)}, u32[]{:S(2)}, u32[]{:S(2)}) collective-permute-start(bf16[16,1536]{1,0:T(8,128)(2,1)S(1)} %slice_bitcast_fusion.1), channel_id=1, source_target_pairs={{0,8},{1,9},{2,10},{3,11},{4,12},{5,13},{6,14},{7,15},{8,0},{9,1},... | collective-permute-start | bytes 147464 | tf_op jit(solution)/shard_map/ppermute | solution.py:38
  41.6 9.3 %collective-permute-start.11 = (bf16[80,1536]{1,0:T(8,128)(2,1)S(1)}, bf16[80,1536]{1,0:T(8,128)(2,1)S(1)}, u32[]{:S(2)}, u32[]{:S(2)}) collective-permute-start(bf16[80,1536]{1,0:T(8,128)(2,1)S(1)} %get-tuple-element.66.refs_0_), channel_id=1, source_target_pairs={{0,4},{1,3},{2,6},{3,1},{4,0},{5,7},{6,2},{7,5},{8,12},{9,11},{10,... | collective-permute-start | bytes 737288 | tf_op jit(solution)/shard_map/ppermute | solution.py:32
  42.4 11.3 %collective-permute-start.8 = (bf16[160,1664]{1,0:T(8,128)(2,1)S(1)}, bf16[160,1664]{1,0:T(8,128)(2,1)S(1)}, u32[]{:S(2)}, u32[]{:S(2)}) collective-permute-start(bf16[160,1664]{1,0:T(8,128)(2,1)S(1)} %get-tuple-element.86), channel_id=1, source_target_pairs={{0,2},{1,5},{2,0},{3,7},{4,6},{5,1},{6,4},{7,3},{8,10},{9,13},{10,... | collective-permute-start | bytes 1597448 | tf_op jit(solution)/shard_map/ppermute | solution.py:32
  51.1 2.9 %collective-permute-start.12 = (bf16[160,1664]{1,0:T(8,128)(2,1)S(1)}, bf16[160,1664]{1,0:T(8,128)(2,1)S(1)}, u32[]{:S(2)}, u32[]{:S(2)}) collective-permute-start(bf16[160,1664]{1,0:T(8,128)(2,1)S(1)} %get-tuple-element.93), channel_id=1, source_target_pairs={{0,1},{1,0},{2,3},{3,2},{4,5},{5,4},{6,7},{7,6},{8,9},{9,8},{10,11... | collective-permute-start | bytes 1597448 | tf_op jit(solution)/shard_map/ppermute | solution.py:32
  51.1 14.0 %collective-permute-start.14 = (bf16[160,1536]{1,0:T(8,128)(2,1)S(1)}, bf16[160,1536]{1,0:T(8,128)(2,1)S(1)}, u32[]{:S(2)}, u32[]{:S(2)}) collective-permute-start(bf16[160,1536]{1,0:T(8,128)(2,1)S(1)} %stack_rows.19.refs_0_), channel_id=1, source_target_pairs={{0,2},{1,5},{2,0},{3,7},{4,6},{5,1},{6,4},{7,3},{8,10},{9,13},{10,... | collective-permute-start | bytes 1474568 | tf_op jit(solution)/shard_map/ppermute | solution.py:32
  53.0 8.9 %collective-permute-start.15 = (bf16[80,1536]{1,0:T(8,128)(2,1)S(1)}, bf16[80,1536]{1,0:T(8,128)(2,1)S(1)}, u32[]{:S(2)}, u32[]{:S(2)}) collective-permute-start(bf16[80,1536]{1,0:T(8,128)(2,1)S(1)} %maximum_bitcast_fusion.refs_0_), channel_id=1, source_target_pairs={{0,4},{1,3},{2,6},{3,1},{4,0},{5,7},{6,2},{7,5},{8,12},{9,11},{10,... | collective-permute-start | bytes 737288 | tf_op jit(solution)/shard_map/ppermute | solution.py:32
  53.7 2.3 %collective-permute-start.16 = (bf16[160,1664]{1,0:T(8,128)(2,1)S(1)}, bf16[160,1664]{1,0:T(8,128)(2,1)S(1)}, u32[]{:S(2)}, u32[]{:S(2)}) collective-permute-start(bf16[160,1664]{1,0:T(8,128)(2,1)S(1)} %get-tuple-element.92), channel_id=1, source_target_pairs={{0,1},{1,0},{2,3},{3,2},{4,5},{5,4},{6,7},{7,6},{8,9},{9,8},{10,11... | collective-permute-start | bytes 1597448 | tf_op jit(solution)/shard_map/ppermute | solution.py:32
  54.0 16.8 %collective-permute-start.17 = (bf16[160,1664]{1,0:T(8,128)(2,1)S(1)}, bf16[160,1664]{1,0:T(8,128)(2,1)S(1)}, u32[]{:S(2)}, u32[]{:S(2)}) collective-permute-start(bf16[160,1664]{1,0:T(8,128)(2,1)S(1)} %add_convert_fusion.1), channel_id=1, source_target_pairs={{0,2},{1,5},{2,0},{3,7},{4,6},{5,1},{6,4},{7,3},{8,10},{9,13},{10,... | collective-permute-start | bytes 1597448 | tf_op jit(solution)/shard_map/ppermute | solution.py:32
  55.0 12.6 %collective-permute-start.13 = (bf16[80,1664]{1,0:T(8,128)(2,1)S(1)}, bf16[80,1664]{1,0:T(8,128)(2,1)S(1)}, u32[]{:S(2)}, u32[]{:S(2)}) collective-permute-start(bf16[80,1664]{1,0:T(8,128)(2,1)S(1)} %get-tuple-element.72), channel_id=1, source_target_pairs={{0,4},{1,3},{2,6},{3,1},{4,0},{5,7},{6,2},{7,5},{8,12},{9,11},{10,... | collective-permute-start | bytes 798728 | tf_op jit(solution)/shard_map/ppermute | solution.py:32
  71.0 6.5 %collective-permute-start.18 = (bf16[80,1664]{1,0:T(8,128)(2,1)S(1)}, bf16[80,1664]{1,0:T(8,128)(2,1)S(1)}, u32[]{:S(2)}, u32[]{:S(2)}) collective-permute-start(bf16[80,1664]{1,0:T(8,128)(2,1)S(1)} %add_convert_fusion.5), channel_id=1, source_target_pairs={{0,4},{1,3},{2,6},{3,1},{4,0},{5,7},{6,2},{7,5},{8,12},{9,11},{10,... | collective-permute-start | bytes 798728 | tf_op jit(solution)/shard_map/ppermute | solution.py:32
  77.6 8.9 %collective-permute-start.20 = (bf16[160,1536]{1,0:T(8,128)(2,1)S(1)}, bf16[160,1536]{1,0:T(8,128)(2,1)S(1)}, u32[]{:S(2)}, u32[]{:S(2)}) collective-permute-start(bf16[160,1536]{1,0:T(8,128)(2,1)S(1)} %stack_rows.21.refs_0_), channel_id=1, source_target_pairs={{0,2},{1,5},{2,0},{3,7},{4,6},{5,1},{6,4},{7,3},{8,10},{9,13},{10,... | collective-permute-start | bytes 1474568 | tf_op jit(solution)/shard_map/ppermute | solution.py:32
  79.4 13.0 %collective-permute-start.19 = (bf16[80,1664]{1,0:T(8,128)(2,1)S(1)}, bf16[80,1664]{1,0:T(8,128)(2,1)S(1)}, u32[]{:S(2)}, u32[]{:S(2)}) collective-permute-start(bf16[80,1664]{1,0:T(8,128)(2,1)S(1)} %pause.3), channel_id=1, source_target_pairs={{0,8},{1,9},{2,10},{3,11},{4,12},{5,13},{6,14},{7,15},{8,0},{9,1},... | collective-permute-start | bytes 798728 | tf_op jit(solution)/shard_map/ppermute | solution.py:38
  80.7 11.8 %copy-start.7 = (f32[128]{0:T(128)S(1)}, f32[128]{0:T(128)}, u32[]{:S(2)}) copy-start(f32[128]{0:T(128)} %param.11) | copy-start | bytes 1540
  80.7 12.9 %collective-permute-start.21 = (bf16[320,1536]{1,0:T(8,128)(2,1)S(1)}, bf16[320,1536]{1,0:T(8,128)(2,1)S(1)}, u32[]{:S(2)}, u32[]{:S(2)}) collective-permute-start(bf16[320,1536]{1,0:T(8,128)(2,1)S(1)} %stack_rows.22.refs_0_), channel_id=1, source_target_pairs={{0,1},{1,0},{2,3},{3,2},{4,5},{5,4},{6,7},{7,6},{8,9},{9,8},{10,11... | collective-permute-start | bytes 2949128 | tf_op jit(solution)/shard_map/ppermute | solution.py:32
  86.6 7.0 %collective-permute-start.22 = (bf16[320,1536]{1,0:T(8,128)(2,1)S(1)}, bf16[320,1536]{1,0:T(8,128)(2,1)S(1)}, u32[]{:S(2)}, u32[]{:S(2)}) collective-permute-start(bf16[320,1536]{1,0:T(8,128)(2,1)S(1)} %stack_rows.23.refs_2_), channel_id=1, source_target_pairs={{0,1},{1,0},{2,3},{3,2},{4,5},{5,4},{6,7},{7,6},{8,9},{9,8},{10,11... | collective-permute-start | bytes 2949128 | tf_op jit(solution)/shard_map/ppermute | solution.py:32

commit v11 on v8

--- a/solution.py
+++ b/solution.py
@@ -221,7 +221,7 @@
 
 def split_slots(rows, experts):
     rows = rows.reshape(experts - 1, -1, rows.shape[1])
-    cut = rows.shape[1] - rows.shape[1] // 5
+    cut = rows.shape[1] // 2
     return [x.reshape(-1, rows.shape[2]) for x in (rows[:, :cut], rows[:, cut:])]
 
 
@@ -315,16 +315,17 @@
 
     far_row_a, far_row_b = split_slots(after(far_row, far_two), experts)
     far_row_a = cross(far_row_a, 1)
+    row_got = meet(after(near_row, far_two), 0)
     near_grads = join(near_four, after(got, far_two))
     near_hg, near_kept, near_sent = slot_grads(
         near_grads, w_out, w_in, act[:near_count], slope[:near_count]
     )
     near_got = meet(near_sent, 2)
     far_row_a = after(far_row_a, near_sent)
-    far_four = join(far_two, after(far_got, far_row_a), long=True)
+    near_row2 = join(near_row, after(row_got, far_row_a))
+    far_four = join(far_two, after(far_got, near_row2), long=True)
     far_got = meet(far_four, 2)
     far_row_b = cross(after(far_row_b, far_four), 1)
-    row_got = meet(after(near_row, far_four), 0)
     near_kept, near_sent = add_halves(near_kept, after(near_got, far_four))
     near_got = meet(near_sent, 1)
     far_grads = join(far_four, after(far_got, near_sent))
@@ -333,14 +334,12 @@
         far_grads, w_out, w_in, act[near_count:], slope[near_count:]
     )
     far_row = join_slots(far_row_a, after(far_row_b, far_sent), experts)
-    near_row2 = join(near_row, after(row_got, far_sent))
     far_kept, far_on = halves(far_kept)
-    far_sent = halves(after(far_sent, far_row, near_row2))
+    far_sent = halves(after(far_sent, far_row))
     far_got, on_got = [meet(x, 2) for x in far_sent]
     row_got = meet(near_row2, 1)
     far_row_got = meet(far_row, 0)
     near_kept, near_sent = add_halves(near_kept, after(near_got, far_sent[1]))
-    near_got = meet(near_sent, 0)
     far_sent = add(far_on, after(on_got, near_sent))
     on_got = meet(far_sent, 1)
     far_kept = add(far_kept, after(far_got, far_sent))
@@ -354,9 +353,9 @@
     far_kept, far_sent = add_halves(far_kept, after(on_got, near_row4))
     far_got = meet(far_sent, 0)
     far_row4 = join(far_row2, after(far_row_got, far_sent))
-    near_sent = far_row4
-    far_sum = pause(add(far_kept, after(far_got, near_sent)))
+    far_sum = pause(add(far_kept, after(far_got, far_row4)))
     back = cross(far_sum, -1)
+    near_got = meet(after(near_sent, far_sum), 0)
     rows = join(near_row4, row_got, far_row4, meet(far_row4, 2))
     w_in_grad = product(rows, join(near_hg, far_hg), ((0,), (0,))).astype(BF16)
     back = after(back, w_in_grad)

time: 92.5 us -> 90.7 us (0.981)
  starting transfers between devices: 26.1 us -> 24.5 us
    ppermute x19, starting transfers between devices: 20.2 us -> 17.2 us  [meet(): lax.ppermute(rows, 'expert', [(i, i ^ bits(i % 2)[step]) for i in range(d...]
    ppermute x4, starting transfers between devices: 5.96 us -> 7.36 us  [shift(): return lax.ppermute(rows, 'expert', pairs)]
  transfers between devices with their start and end apart: 23 -> 23, of which waited for: 12 -> 11; matrix products, arithmetic and copies ran while one was open for 11% -> 12% of each run, Pallas kernels for 14% -> 14%
where the time goes in v11:
time: 90.7 us; the launch traced here: 90.4 us
  waiting for transfers between devices  32.6 us (36%)
  starting transfers between devices  24.5 us (27%)
  Pallas kernels  14.3 us (16%)
  matrix products  9.15 us (10%)
  local copies, waits for them, and re-layouts  7.23 us (8%)
  other arithmetic  1.66 us (2%)
  between operations  0.95 us (1%)
    ppermute x19, waiting for transfers between devices, meet(): lax.ppermute(rows, 'expert', [(i, i ^ bits(i % 2)[step]) for i in range(d...  24 us
    ppermute x19, starting transfers between devices, meet(): lax.ppermute(rows, 'expert', [(i, i ^ bits(i % 2)[step]) for i in range(d...  17.2 us
    dot_general x2, matrix products, product(): return lax.dot_general(a, b, (dims, ((), ())), preferred_element_type=F32)  9.15 us
    ppermute x4, waiting for transfers between devices, shift(): return lax.ppermute(rows, 'expert', pairs)  8.53 us
    pallas_call x2, Pallas kernels, slot_grads(): pl.pallas_call(slot_grad_kernel, out_shape=(jax.ShapeDtypeStruct((rows, u...  7.82 us
    ppermute x4, starting transfers between devices, shift(): return lax.ppermute(rows, 'expert', pairs)  7.36 us
    unnamed x16, local copies, waits for them, and re-layouts  6.82 us
    pallas_call x1, Pallas kernels, activation(): pl.pallas_call(activation_kernel, grid_spec=pltpu.PrefetchScalarGridSpec(...  3.36 us
  transfers between devices with their start and end apart: 23, of which 11 were waited for; matrix products, arithmetic and copies ran while one was open for 12% of the time, Pallas kernels for 14%

profile of v11, /device:TPU:0, one launch (start us, length us, event | category | flops | bytes accessed | tf_op | source)
XLA Modules:
  0.0 90.4 jit_solution(9169403430323295548)
XLA Ops:
  0.6 0.7 fusion.place
  1.3 1.0 %copy-done.3 = bf16[128,1536]{1,0:T(8,128)(2,1)S(1)} copy-done((bf16[128,1536]{1,0:T(8,128)(2,1)S(1)}, bf16[128,1536]{1,0:T(8,128)(2,1)}, u32[]{:S(2)}) %copy-start.3) | copy-done | bytes 393240
  2.3 0.7 copy-done.5
  3.0 0.4 rows_to_slots.2
  3.4 3.1 %collective-permute-start = (bf16[80,1536]{1,0:T(8,128)(2,1)S(1)}, bf16[80,1536]{1,0:T(8,128)(2,1)S(1)}, u32[]{:S(2)}, u32[]{:S(2)}) collective-permute-start(bf16[80,1536]{1,0:T(8,128)(2,1)S(1)} %get-tuple-element.46.refs_0_), channel_id=1, source_target_pairs={{0,4},{1,3},{2,6},{3,1},{4,0},{5,7},{6,2},{7,5},{8,12},{9,11},{10,... | collective-permute-start | bytes 737288 | tf_op jit(solution)/shard_map/ppermute | solution.py:32
  6.5 2.6 %collective-permute-start.2 = (bf16[80,1536]{1,0:T(8,128)(2,1)S(1)}, bf16[80,1536]{1,0:T(8,128)(2,1)S(1)}, u32[]{:S(2)}, u32[]{:S(2)}) collective-permute-start(bf16[80,1536]{1,0:T(8,128)(2,1)S(1)} %get-tuple-element.49), channel_id=1, source_target_pairs={{0,8},{1,9},{2,10},{3,11},{4,12},{5,13},{6,14},{7,15},{8,0},{9,1},... | collective-permute-start | bytes 737288 | tf_op jit(solution)/shard_map/ppermute | solution.py:38
  9.1 1.0 %copy-done.4 = bf16[128,1536]{1,0:T(8,128)(2,1)S(1)} copy-done((bf16[128,1536]{1,0:T(8,128)(2,1)S(1)}, bf16[128,1536]{1,0:T(8,128)(2,1)}, u32[]{:S(2)}) %copy-start.4) | copy-done | bytes 393240
  10.1 0.7 copy-done.6
  10.7 0.3 rows_to_slots.3
  11.0 0.1 pad_add_fusion.order
  11.1 1.6 %collective-permute-done.refs_1_ = bf16[80,1536]{1,0:T(8,128)(2,1)S(1)} collective-permute-done((bf16[80,1536]{1,0:T(8,128)(2,1)S(1)}, bf16[80,1536]{1,0:T(8,128)(2,1)S(1)}, u32[]{:S(2)}, u32[]{:S(2)}) %collective-permute-start) | collective-permute-done | bytes 245792 | tf_op jit(solution)/shard_map/ppermute | solution.py:32
  12.8 4.4 %collective-permute-start.1 = (bf16[160,1536]{1,0:T(8,128)(2,1)S(1)}, bf16[160,1536]{1,0:T(8,128)(2,1)S(1)}, u32[]{:S(2)}, u32[]{:S(2)}) collective-permute-start(bf16[160,1536]{1,0:T(8,128)(2,1)S(1)} %stack_rows.13.refs_0_), channel_id=1, source_target_pairs={{0,2},{1,5},{2,0},{3,7},{4,6},{5,1},{6,4},{7,3},{8,10},{9,13},{10,... | collective-permute-start | bytes 1474568 | tf_op jit(solution)/shard_map/ppermute | solution.py:32
  17.2 1.5 %copy-done.2 = bf16[1280,768]{1,0:T(8,128)(2,1)S(1)} copy-done((bf16[1280,768]{1,0:T(8,128)(2,1)S(1)}, bf16[1280,768]{1,0:T(8,128)(2,1)}, u32[]{:S(2)}) %copy-start.2) | copy-done | bytes 1966104
  18.7 3.4 %activation.1 = (bf16[16,80,768]{2,1,0:T(8,128)(2,1)S(1)}, bf16[16,80,768]{2,1,0:T(8,128)(2,1)S(1)}) custom-call(s32[16]{0:T(128)S(1)} %pad_add_fusion.order, bf16[16,80,768]{2,1,0:T(8,128)(2,1)S(1)} %bitcast.27), custom_call_target="tpu_custom_call" | custom-call | tf_op jit(solution)/shard_map/activation/pallas_call | solution.py:169
  22.1 0.1 collective-permute-start.4
  22.2 4.4 %collective-permute-done.1.refs_1_ = bf16[160,1536]{1,0:T(8,128)(2,1)S(1)} collective-permute-done((bf16[160,1536]{1,0:T(8,128)(2,1)S(1)}, bf16[160,1536]{1,0:T(8,128)(2,1)S(1)}, u32[]{:S(2)}, u32[]{:S(2)}) %collective-permute-start.1) | collective-permute-done | bytes 491552 | tf_op jit(solution)/shard_map/ppermute | solution.py:32
  26.6 0.1 stack_rows.14.refs_0_
  26.7 0.1 collective-permute-start.3
  26.8 1.6 %collective-permute-done.4.refs_1_ = bf16[80,1536]{1,0:T(8,128)(2,1)S(1)} collective-permute-done((bf16[80,1536]{1,0:T(8,128)(2,1)S(1)}, bf16[80,1536]{1,0:T(8,128)(2,1)S(1)}, u32[]{:S(2)}, u32[]{:S(2)}) %collective-permute-start.4) | collective-permute-done | bytes 245792 | tf_op jit(solution)/shard_map/ppermute | solution.py:32
  28.4 0.3 collective-permute-start.6
  28.8 2.8 %collective-permute-start.8 = (bf16[40,1536]{1,0:T(8,128)(2,1)S(1)}, bf16[40,1536]{1,0:T(8,128)(2,1)S(1)}, u32[]{:S(2)}, u32[]{:S(2)}) collective-permute-start(bf16[40,1536]{1,0:T(8,128)(2,1)S(1)} %get-tuple-element.99), channel_id=1, source_target_pairs={{0,8},{1,9},{2,10},{3,11},{4,12},{5,13},{6,14},{7,15},{8,0},{9,1},... | collective-permute-start | bytes 368648 | tf_op jit(solution)/shard_map/ppermute | solution.py:38
  31.6 0.3 fusion.3
  31.9 0.1 stack_rows.16.grads.refs_0_
  32.1 1.2 %copy-done.1 = bf16[1536,768]{1,0:T(8,128)(2,1)S(1)} copy-done((bf16[1536,768]{1,0:T(8,128)(2,1)S(1)}, bf16[1536,768]{1,0:T(8,128)(2,1)}, u32[]{:S(2)}) %copy-start.1) | copy-done | bytes 2359320
  33.3 0.8 copy-done
  34.0 3.9 %slot_grads.2 = (bf16[640,768]{1,0:T(8,128)(2,1)S(1)}, bf16[320,1664]{1,0:T(8,128)(2,1)S(1)}, bf16[320,1664]{1,0:T(8,128)(2,1)S(1)}) custom-call(bf16[640,1536]{1,0:T(8,128)(2,1)S(1)} %stack_rows.16.grads.refs_0_, bf16[768,1536]{1,0:T(8,128)(2,1)S(1)} %copy-done, bf16[1536,768]{1,0:T(8,128)(2,1)S(1)} %copy-done.1, bf16[640,768]{1,0:T(8,128)(2,1)S(1)} %bitcast.26, ...), custom_call_target="tpu_custom_call" | custom-call | tf_op jit(solution)/shard_map/slot_grads/pallas_call | solution.py:275
  38.0 0.1 collective-permute-start.5
  38.0 2.2 %collective-permute-done.7.refs_1_ = bf16[80,1536]{1,0:T(8,128)(2,1)S(1)} collective-permute-done((bf16[80,1536]{1,0:T(8,128)(2,1)S(1)}, bf16[80,1536]{1,0:T(8,128)(2,1)S(1)}, u32[]{:S(2)}, u32[]{:S(2)}) %collective-permute-start.7) | collective-permute-done | bytes 245792 | tf_op jit(solution)/shard_map/ppermute | solution.py:32
  40.3 0.1 stack_rows.18.refs_0_
  40.4 0.1 collective-permute-start.10
  40.5 1.2 %collective-permute-start.11 = (bf16[40,1536]{1,0:T(8,128)(2,1)S(1)}, bf16[40,1536]{1,0:T(8,128)(2,1)S(1)}, u32[]{:S(2)}, u32[]{:S(2)}) collective-permute-start(bf16[40,1536]{1,0:T(8,128)(2,1)S(1)} %get-tuple-element.68), channel_id=1, source_target_pairs={{0,8},{1,9},{2,10},{3,11},{4,12},{5,13},{6,14},{7,15},{8,0},{9,1},... | collective-permute-start | bytes 368648 | tf_op jit(solution)/shard_map/ppermute | solution.py:38
  41.7 0.2 add_convert_fusion.2
  41.9 1.9 %collective-permute-start.9 = (bf16[160,1664]{1,0:T(8,128)(2,1)S(1)}, bf16[160,1664]{1,0:T(8,128)(2,1)S(1)}, u32[]{:S(2)}, u32[]{:S(2)}) collective-permute-start(bf16[160,1664]{1,0:T(8,128)(2,1)S(1)} %get-tuple-element.88), channel_id=1, source_target_pairs={{0,2},{1,5},{2,0},{3,7},{4,6},{5,1},{6,4},{7,3},{8,10},{9,13},{10,... | collective-permute-start | bytes 1597448 | tf_op jit(solution)/shard_map/ppermute | solution.py:32
  43.9 0.1 stack_rows.19.grads.refs_1_
  44.0 3.9 %slot_grads.3 = (bf16[640,768]{1,0:T(8,128)(2,1)S(1)}, bf16[320,1664]{1,0:T(8,128)(2,1)S(1)}, bf16[320,1664]{1,0:T(8,128)(2,1)S(1)}) custom-call(bf16[640,1536]{1,0:T(8,128)(2,1)S(1)} %stack_rows.19.grads.refs_1_, bf16[768,1536]{1,0:T(8,128)(2,1)S(1)} %copy-done, bf16[1536,768]{1,0:T(8,128)(2,1)S(1)} %copy-done.1, bf16[640,768]{1,0:T(8,128)(2,1)S(1)} %bitcast.24, ...), custom_call_target="tpu_custom_call" | custom-call | tf_op jit(solution)/shard_map/slot_grads/pallas_call | solution.py:275
  47.9 1.9 %collective-permute-done.11 = bf16[40,1536]{1,0:T(8,128)(2,1)S(1)} collective-permute-done((bf16[40,1536]{1,0:T(8,128)(2,1)S(1)}, bf16[40,1536]{1,0:T(8,128)(2,1)S(1)}, u32[]{:S(2)}, u32[]{:S(2)}) %collective-permute-start.11) | collective-permute-done | bytes 122912 | tf_op jit(solution)/shard_map/ppermute | solution.py:38
  49.9 0.1 fusion.5
  50.0 0.1 collective-permute-start.13
  50.0 1.5 %collective-permute-start.15 = (bf16[160,1536]{1,0:T(8,128)(2,1)S(1)}, bf16[160,1536]{1,0:T(8,128)(2,1)S(1)}, u32[]{:S(2)}, u32[]{:S(2)}) collective-permute-start(bf16[160,1536]{1,0:T(8,128)(2,1)S(1)} %stack_rows.17.refs_0_), channel_id=1, source_target_pairs={{0,2},{1,5},{2,0},{3,7},{4,6},{5,1},{6,4},{7,3},{8,10},{9,13},{10,... | collective-permute-start | bytes 1474568 | tf_op jit(solution)/shard_map/ppermute | solution.py:32
  51.5 0.3 stack_rows.20
  51.8 0.2 collective-permute-start.12
  52.0 0.1 add_convert_fusion.7
  52.1 0.1 add_convert_fusion.1
  52.3 1.3 %collective-permute-start.14 = (bf16[160,1664]{1,0:T(8,128)(2,1)S(1)}, bf16[160,1664]{1,0:T(8,128)(2,1)S(1)}, u32[]{:S(2)}, u32[]{:S(2)}) collective-permute-start(bf16[160,1664]{1,0:T(8,128)(2,1)S(1)} %add_convert_fusion.1), channel_id=1, source_target_pairs={{0,2},{1,5},{2,0},{3,7},{4,6},{5,1},{6,4},{7,3},{8,10},{9,13},{10,... | collective-permute-start | bytes 1597448 | tf_op jit(solution)/shard_map/ppermute | solution.py:32
  53.5 0.2 collective-permute-done.12
  53.8 0.2 add_convert_fusion
  53.9 4.6 %convolution_convert_fusion.1 = bf16[768,1536]{1,0:T(8,128)(2,1)} fusion(bf16[1280,768]{1,0:T(8,128)(2,1)S(1)} %bitcast.28, bf16[1280,1536]{1,0:T(8,128)(2,1)S(1)} %stack_rows.20), kind=kOutput, calls=%fused_computation.1 | convolution fusion | flops 3021078528 | bytes 8257536 | tf_op jit(solution)/shard_map/dot_general | solution.py:250
  58.5 1.9 %collective-permute-done.16.refs_1_ = bf16[80,1536]{1,0:T(8,128)(2,1)S(1)} collective-permute-done((bf16[80,1536]{1,0:T(8,128)(2,1)S(1)}, bf16[80,1536]{1,0:T(8,128)(2,1)S(1)}, u32[]{:S(2)}, u32[]{:S(2)}) %collective-permute-start.16) | collective-permute-done | bytes 245792 | tf_op jit(solution)/shard_map/ppermute | solution.py:32
  60.4 0.6 collective-permute-start.18
  61.1 5.6 %collective-permute-done.14 = bf16[160,1664]{1,0:T(8,128)(2,1)S(1)} collective-permute-done((bf16[160,1664]{1,0:T(8,128)(2,1)S(1)}, bf16[160,1664]{1,0:T(8,128)(2,1)S(1)}, u32[]{:S(2)}, u32[]{:S(2)}) %collective-permute-start.14) | collective-permute-done | bytes 532512 | tf_op jit(solution)/shard_map/ppermute | solution.py:32
  66.7 0.1 add_convert_fusion.5
  66.8 0.1 collective-permute-start.17
  66.9 0.1 stack_rows.25
  67.0 1.3 %collective-permute-start.21 = (bf16[320,1536]{1,0:T(8,128)(2,1)S(1)}, bf16[320,1536]{1,0:T(8,128)(2,1)S(1)}, u32[]{:S(2)}, u32[]{:S(2)}) collective-permute-start(bf16[320,1536]{1,0:T(8,128)(2,1)S(1)} %stack_rows.22.refs_0_), channel_id=1, source_target_pairs={{0,1},{1,0},{2,3},{3,2},{4,5},{5,4},{6,7},{7,6},{8,9},{9,8},{10,11... | collective-permute-start | bytes 2949128 | tf_op jit(solution)/shard_map/ppermute | solution.py:32
  68.3 6.0 %collective-permute-done.18.refs_1_ = bf16[160,1536]{1,0:T(8,128)(2,1)S(1)} collective-permute-done((bf16[160,1536]{1,0:T(8,128)(2,1)S(1)}, bf16[160,1536]{1,0:T(8,128)(2,1)S(1)}, u32[]{:S(2)}, u32[]{:S(2)}) %collective-permute-start.18) | collective-permute-done | bytes 491552 | tf_op jit(solution)/shard_map/ppermute | solution.py:32
  74.4 0.1 collective-permute-start.22
  74.5 0.3 collective-permute-done.17
  74.8 0.1 add_convert_fusion.4.rows
  75.0 0.8 collective-permute-start.20
  75.8 2.0 %collective-permute-start.19 = (bf16[80,1664]{1,0:T(8,128)(2,1)S(1)}, bf16[80,1664]{1,0:T(8,128)(2,1)S(1)}, u32[]{:S(2)}, u32[]{:S(2)}) collective-permute-start(bf16[80,1664]{1,0:T(8,128)(2,1)S(1)} %get-tuple-element.81), channel_id=1, source_target_pairs={{0,4},{1,3},{2,6},{3,1},{4,0},{5,7},{6,2},{7,5},{8,12},{9,11},{10,... | collective-permute-start | bytes 798728 | tf_op jit(solution)/shard_map/ppermute | solution.py:32
  77.8 0.3 stack_rows.24
  78.0 4.6 %convolution_convert_fusion = bf16[1536,768]{1,0:T(8,128)(2,1)} fusion(bf16[1280,1536]{1,0:T(8,128)(2,1)S(1)} %stack_rows.24, bf16[1280,768]{1,0:T(8,128)(2,1)S(1)} %stack_rows.25), kind=kOutput, calls=%fused_computation | convolution fusion | flops 3021078528 | bytes 8257536 | tf_op jit(solution)/shard_map/dot_general | solution.py:250
  82.6 6.6 %collective-permute-done.20.back = bf16[80,1664]{1,0:T(8,128)(2,1)S(1)} collective-permute-done((bf16[80,1664]{1,0:T(8,128)(2,1)S(1)}, bf16[80,1664]{1,0:T(8,128)(2,1)S(1)}, u32[]{:S(2)}, u32[]{:S(2)}) %collective-permute-start.20) | collective-permute-done | bytes 266272 | tf_op jit(solution)/shard_map/ppermute | solution.py:38
  89.2 1.2 %slots_to_tokens.1 = (bf16[128,1536]{1,0:T(8,128)(2,1)}, f32[1,128]{1,0:T(1,128)}) custom-call(s32[1,128]{1,0:T(1,128)S(1)} %fusion.place, f32[1,128]{1,0:T(1,128)S(1)} %bitcast.32, bf16[80,1664]{1,0:T(8,128)(2,1)S(1)} %get-tuple-element.97.kept, bf16[80,1664]{1,0:T(8,128)(2,1)S(1)} %collective-permute-done.19.got, ...), custom_call_target="tpu_custom_call" | custom-call | tf_op jit(solution)/shard_map/slots_to_tokens/pallas_call | solution.py:136
  (35 shorter events, 0.4 us)
Async XLA Ops:
  1.3 1.0 %copy-start.3 = (bf16[128,1536]{1,0:T(8,128)(2,1)S(1)}, bf16[128,1536]{1,0:T(8,128)(2,1)}, u32[]{:S(2)}) copy-start(bf16[128,1536]{1,0:T(8,128)(2,1)} %values.2) | copy-start | bytes 1179652
  2.3 0.7 copy-start.5
  3.4 9.4 %collective-permute-start = (bf16[80,1536]{1,0:T(8,128)(2,1)S(1)}, bf16[80,1536]{1,0:T(8,128)(2,1)S(1)}, u32[]{:S(2)}, u32[]{:S(2)}) collective-permute-start(bf16[80,1536]{1,0:T(8,128)(2,1)S(1)} %get-tuple-element.46.refs_0_), channel_id=1, source_target_pairs={{0,4},{1,3},{2,6},{3,1},{4,0},{5,7},{6,2},{7,5},{8,12},{9,11},{10,... | collective-permute-start | bytes 737288 | tf_op jit(solution)/shard_map/ppermute | solution.py:32
  6.5 15.6 %collective-permute-start.2 = (bf16[80,1536]{1,0:T(8,128)(2,1)S(1)}, bf16[80,1536]{1,0:T(8,128)(2,1)S(1)}, u32[]{:S(2)}, u32[]{:S(2)}) collective-permute-start(bf16[80,1536]{1,0:T(8,128)(2,1)S(1)} %get-tuple-element.49), channel_id=1, source_target_pairs={{0,8},{1,9},{2,10},{3,11},{4,12},{5,13},{6,14},{7,15},{8,0},{9,1},... | collective-permute-start | bytes 737288 | tf_op jit(solution)/shard_map/ppermute | solution.py:38
  9.1 1.0 %copy-start.4 = (bf16[128,1536]{1,0:T(8,128)(2,1)S(1)}, bf16[128,1536]{1,0:T(8,128)(2,1)}, u32[]{:S(2)}) copy-start(bf16[128,1536]{1,0:T(8,128)(2,1)} %values.3) | copy-start | bytes 1179652
  10.1 0.7 copy-start.6
  12.8 13.8 %collective-permute-start.1 = (bf16[160,1536]{1,0:T(8,128)(2,1)S(1)}, bf16[160,1536]{1,0:T(8,128)(2,1)S(1)}, u32[]{:S(2)}, u32[]{:S(2)}) collective-permute-start(bf16[160,1536]{1,0:T(8,128)(2,1)S(1)} %stack_rows.13.refs_0_), channel_id=1, source_target_pairs={{0,2},{1,5},{2,0},{3,7},{4,6},{5,1},{6,4},{7,3},{8,10},{9,13},{10,... | collective-permute-start | bytes 1474568 | tf_op jit(solution)/shard_map/ppermute | solution.py:32
  17.2 1.5 %copy-start.2 = (bf16[1280,768]{1,0:T(8,128)(2,1)S(1)}, bf16[1280,768]{1,0:T(8,128)(2,1)}, u32[]{:S(2)}) copy-start(bf16[1280,768]{1,0:T(8,128)(2,1)} %param.15) | copy-start | bytes 5898244
  22.1 6.3 %collective-permute-start.4 = (bf16[80,1536]{1,0:T(8,128)(2,1)S(1)}, bf16[80,1536]{1,0:T(8,128)(2,1)S(1)}, u32[]{:S(2)}, u32[]{:S(2)}) collective-permute-start(bf16[80,1536]{1,0:T(8,128)(2,1)S(1)} %pause.2.refs_0_), channel_id=1, source_target_pairs={{0,4},{1,3},{2,6},{3,1},{4,0},{5,7},{6,2},{7,5},{8,12},{9,11},{10,... | collective-permute-start | bytes 737288 | tf_op jit(solution)/shard_map/ppermute | solution.py:32
  26.7 5.2 %collective-permute-start.3 = (bf16[320,1536]{1,0:T(8,128)(2,1)S(1)}, bf16[320,1536]{1,0:T(8,128)(2,1)S(1)}, u32[]{:S(2)}, u32[]{:S(2)}) collective-permute-start(bf16[320,1536]{1,0:T(8,128)(2,1)S(1)} %stack_rows.14.refs_0_), channel_id=1, source_target_pairs={{0,1},{1,0},{2,3},{3,2},{4,5},{5,4},{6,7},{7,6},{8,9},{9,8},{10,11... | collective-permute-start | bytes 2949128 | tf_op jit(solution)/shard_map/ppermute | solution.py:32
  28.4 11.9 %collective-permute-start.6 = (bf16[160,1536]{1,0:T(8,128)(2,1)S(1)}, bf16[160,1536]{1,0:T(8,128)(2,1)S(1)}, u32[]{:S(2)}, u32[]{:S(2)}) collective-permute-start(bf16[160,1536]{1,0:T(8,128)(2,1)S(1)} %stack_rows.15.refs_0_), channel_id=1, source_target_pairs={{0,2},{1,5},{2,0},{3,7},{4,6},{5,1},{6,4},{7,3},{8,10},{9,13},{10,... | collective-permute-start | bytes 1474568 | tf_op jit(solution)/shard_map/ppermute | solution.py:32
  28.7 11.5 %collective-permute-start.7 = (bf16[80,1536]{1,0:T(8,128)(2,1)S(1)}, bf16[80,1536]{1,0:T(8,128)(2,1)S(1)}, u32[]{:S(2)}, u32[]{:S(2)}) collective-permute-start(bf16[80,1536]{1,0:T(8,128)(2,1)S(1)} %get-tuple-element.59.refs_0_), channel_id=1, source_target_pairs={{0,4},{1,3},{2,6},{3,1},{4,0},{5,7},{6,2},{7,5},{8,12},{9,11},{10,... | collective-permute-start | bytes 737288 | tf_op jit(solution)/shard_map/ppermute | solution.py:32
  28.8 9.3 %collective-permute-start.8 = (bf16[40,1536]{1,0:T(8,128)(2,1)S(1)}, bf16[40,1536]{1,0:T(8,128)(2,1)S(1)}, u32[]{:S(2)}, u32[]{:S(2)}) collective-permute-start(bf16[40,1536]{1,0:T(8,128)(2,1)S(1)} %get-tuple-element.99), channel_id=1, source_target_pairs={{0,8},{1,9},{2,10},{3,11},{4,12},{5,13},{6,14},{7,15},{8,0},{9,1},... | collective-permute-start | bytes 368648 | tf_op jit(solution)/shard_map/ppermute | solution.py:38
  31.6 1.7 %copy-start.1 = (bf16[1536,768]{1,0:T(8,128)(2,1)S(1)}, bf16[1536,768]{1,0:T(8,128)(2,1)}, u32[]{:S(2)}) copy-start(bf16[1536,768]{1,0:T(8,128)(2,1)} %w_in.3) | copy-start | bytes 7077892
  31.9 2.1 %copy-start = (bf16[768,1536]{1,0:T(8,128)(2,1)S(1)}, bf16[768,1536]{1,0:T(8,128)(2,1)}, u32[]{:S(2)}) copy-start(bf16[768,1536]{1,0:T(8,128)(2,1)} %w_out.3) | copy-start | bytes 7077892
  38.0 3.7 %collective-permute-start.5 = (bf16[320,1664]{1,0:T(8,128)(2,1)S(1)}, bf16[320,1664]{1,0:T(8,128)(2,1)S(1)}, u32[]{:S(2)}, u32[]{:S(2)}) collective-permute-start(bf16[320,1664]{1,0:T(8,128)(2,1)S(1)} %get-tuple-element.58), channel_id=1, source_target_pairs={{0,1},{1,0},{2,3},{3,2},{4,5},{5,4},{6,7},{7,6},{8,9},{9,8},{10,11... | collective-permute-start | bytes 3194888 | tf_op jit(solution)/shard_map/ppermute | solution.py:32
  40.4 3.5 %collective-permute-start.10 = (bf16[320,1536]{1,0:T(8,128)(2,1)S(1)}, bf16[320,1536]{1,0:T(8,128)(2,1)S(1)}, u32[]{:S(2)}, u32[]{:S(2)}) collective-permute-start(bf16[320,1536]{1,0:T(8,128)(2,1)S(1)} %stack_rows.18.refs_0_), channel_id=1, source_target_pairs={{0,1},{1,0},{2,3},{3,2},{4,5},{5,4},{6,7},{7,6},{8,9},{9,8},{10,11... | collective-permute-start | bytes 2949128 | tf_op jit(solution)/shard_map/ppermute | solution.py:32
  40.5 9.3 %collective-permute-start.11 = (bf16[40,1536]{1,0:T(8,128)(2,1)S(1)}, bf16[40,1536]{1,0:T(8,128)(2,1)S(1)}, u32[]{:S(2)}, u32[]{:S(2)}) collective-permute-start(bf16[40,1536]{1,0:T(8,128)(2,1)S(1)} %get-tuple-element.68), channel_id=1, source_target_pairs={{0,8},{1,9},{2,10},{3,11},{4,12},{5,13},{6,14},{7,15},{8,0},{9,1},... | collective-permute-start | bytes 368648 | tf_op jit(solution)/shard_map/ppermute | solution.py:38
  41.9 10.0 %collective-permute-start.9 = (bf16[160,1664]{1,0:T(8,128)(2,1)S(1)}, bf16[160,1664]{1,0:T(8,128)(2,1)S(1)}, u32[]{:S(2)}, u32[]{:S(2)}) collective-permute-start(bf16[160,1664]{1,0:T(8,128)(2,1)S(1)} %get-tuple-element.88), channel_id=1, source_target_pairs={{0,2},{1,5},{2,0},{3,7},{4,6},{5,1},{6,4},{7,3},{8,10},{9,13},{10,... | collective-permute-start | bytes 1597448 | tf_op jit(solution)/shard_map/ppermute | solution.py:32
  50.0 2.2 %collective-permute-start.13 = (bf16[160,1664]{1,0:T(8,128)(2,1)S(1)}, bf16[160,1664]{1,0:T(8,128)(2,1)S(1)}, u32[]{:S(2)}, u32[]{:S(2)}) collective-permute-start(bf16[160,1664]{1,0:T(8,128)(2,1)S(1)} %get-tuple-element.95), channel_id=1, source_target_pairs={{0,1},{1,0},{2,3},{3,2},{4,5},{5,4},{6,7},{7,6},{8,9},{9,8},{10,11... | collective-permute-start | bytes 1597448 | tf_op jit(solution)/shard_map/ppermute | solution.py:32
  50.0 11.0 %collective-permute-start.15 = (bf16[160,1536]{1,0:T(8,128)(2,1)S(1)}, bf16[160,1536]{1,0:T(8,128)(2,1)S(1)}, u32[]{:S(2)}, u32[]{:S(2)}) collective-permute-start(bf16[160,1536]{1,0:T(8,128)(2,1)S(1)} %stack_rows.17.refs_0_), channel_id=1, source_target_pairs={{0,2},{1,5},{2,0},{3,7},{4,6},{5,1},{6,4},{7,3},{8,10},{9,13},{10,... | collective-permute-start | bytes 1474568 | tf_op jit(solution)/shard_map/ppermute | solution.py:32
  51.5 8.9 %collective-permute-start.16 = (bf16[80,1536]{1,0:T(8,128)(2,1)S(1)}, bf16[80,1536]{1,0:T(8,128)(2,1)S(1)}, u32[]{:S(2)}, u32[]{:S(2)}) collective-permute-start(bf16[80,1536]{1,0:T(8,128)(2,1)S(1)} %maximum_bitcast_fusion.refs_0_), channel_id=1, source_target_pairs={{0,4},{1,3},{2,6},{3,1},{4,0},{5,7},{6,2},{7,5},{8,12},{9,11},{10,... | collective-permute-start | bytes 737288 | tf_op jit(solution)/shard_map/ppermute | solution.py:32
  51.8 2.0 %collective-permute-start.12 = (bf16[160,1664]{1,0:T(8,128)(2,1)S(1)}, bf16[160,1664]{1,0:T(8,128)(2,1)S(1)}, u32[]{:S(2)}, u32[]{:S(2)}) collective-permute-start(bf16[160,1664]{1,0:T(8,128)(2,1)S(1)} %get-tuple-element.94), channel_id=1, source_target_pairs={{0,1},{1,0},{2,3},{3,2},{4,5},{5,4},{6,7},{7,6},{8,9},{9,8},{10,11... | collective-permute-start | bytes 1597448 | tf_op jit(solution)/shard_map/ppermute | solution.py:32
  52.3 14.5 %collective-permute-start.14 = (bf16[160,1664]{1,0:T(8,128)(2,1)S(1)}, bf16[160,1664]{1,0:T(8,128)(2,1)S(1)}, u32[]{:S(2)}, u32[]{:S(2)}) collective-permute-start(bf16[160,1664]{1,0:T(8,128)(2,1)S(1)} %add_convert_fusion.1), channel_id=1, source_target_pairs={{0,2},{1,5},{2,0},{3,7},{4,6},{5,1},{6,4},{7,3},{8,10},{9,13},{10,... | collective-permute-start | bytes 1597448 | tf_op jit(solution)/shard_map/ppermute | solution.py:32
  60.4 13.9 %collective-permute-start.18 = (bf16[160,1536]{1,0:T(8,128)(2,1)S(1)}, bf16[160,1536]{1,0:T(8,128)(2,1)S(1)}, u32[]{:S(2)}, u32[]{:S(2)}) collective-permute-start(bf16[160,1536]{1,0:T(8,128)(2,1)S(1)} %stack_rows.21.refs_0_), channel_id=1, source_target_pairs={{0,2},{1,5},{2,0},{3,7},{4,6},{5,1},{6,4},{7,3},{8,10},{9,13},{10,... | collective-permute-start | bytes 1474568 | tf_op jit(solution)/shard_map/ppermute | solution.py:32
  66.8 8.0 %collective-permute-start.17 = (bf16[80,1664]{1,0:T(8,128)(2,1)S(1)}, bf16[80,1664]{1,0:T(8,128)(2,1)S(1)}, u32[]{:S(2)}, u32[]{:S(2)}) collective-permute-start(bf16[80,1664]{1,0:T(8,128)(2,1)S(1)} %add_convert_fusion.5), channel_id=1, source_target_pairs={{0,4},{1,3},{2,6},{3,1},{4,0},{5,7},{6,2},{7,5},{8,12},{9,11},{10,... | collective-permute-start | bytes 798728 | tf_op jit(solution)/shard_map/ppermute | solution.py:32
  67.0 10.7 %collective-permute-start.21 = (bf16[320,1536]{1,0:T(8,128)(2,1)S(1)}, bf16[320,1536]{1,0:T(8,128)(2,1)S(1)}, u32[]{:S(2)}, u32[]{:S(2)}) collective-permute-start(bf16[320,1536]{1,0:T(8,128)(2,1)S(1)} %stack_rows.22.refs_0_), channel_id=1, source_target_pairs={{0,1},{1,0},{2,3},{3,2},{4,5},{5,4},{6,7},{7,6},{8,9},{9,8},{10,11... | collective-permute-start | bytes 2949128 | tf_op jit(solution)/shard_map/ppermute | solution.py:32
  74.4 3.3 %collective-permute-start.22 = (bf16[320,1536]{1,0:T(8,128)(2,1)S(1)}, bf16[320,1536]{1,0:T(8,128)(2,1)S(1)}, u32[]{:S(2)}, u32[]{:S(2)}) collective-permute-start(bf16[320,1536]{1,0:T(8,128)(2,1)S(1)} %stack_rows.23.refs_2_), channel_id=1, source_target_pairs={{0,1},{1,0},{2,3},{3,2},{4,5},{5,4},{6,7},{7,6},{8,9},{9,8},{10,11... | collective-permute-start | bytes 2949128 | tf_op jit(solution)/shard_map/ppermute | solution.py:32
  75.0 14.2 %collective-permute-start.20 = (bf16[80,1664]{1,0:T(8,128)(2,1)S(1)}, bf16[80,1664]{1,0:T(8,128)(2,1)S(1)}, u32[]{:S(2)}, u32[]{:S(2)}) collective-permute-start(bf16[80,1664]{1,0:T(8,128)(2,1)S(1)} %pause.3), channel_id=1, source_target_pairs={{0,8},{1,9},{2,10},{3,11},{4,12},{5,13},{6,14},{7,15},{8,0},{9,1},... | collective-permute-start | bytes 798728 | tf_op jit(solution)/shard_map/ppermute | solution.py:38
  75.8 13.5 %collective-permute-start.19 = (bf16[80,1664]{1,0:T(8,128)(2,1)S(1)}, bf16[80,1664]{1,0:T(8,128)(2,1)S(1)}, u32[]{:S(2)}, u32[]{:S(2)}) collective-permute-start(bf16[80,1664]{1,0:T(8,128)(2,1)S(1)} %get-tuple-element.81), channel_id=1, source_target_pairs={{0,4},{1,3},{2,6},{3,1},{4,0},{5,7},{6,2},{7,5},{8,12},{9,11},{10,... | collective-permute-start | bytes 798728 | tf_op jit(solution)/shard_map/ppermute | solution.py:32
  78.0 11.2 %copy-start.7 = (f32[128]{0:T(128)S(1)}, f32[128]{0:T(128)}, u32[]{:S(2)}) copy-start(f32[128]{0:T(128)} %param.11) | copy-start | bytes 1540

commit v12 on v11

--- a/solution.py
+++ b/solution.py
@@ -81,35 +81,27 @@
     return rows == place
 
 
-def place_kernel(slots, scale, place, gate, values, near, far):
-    rows = values[...]
-    if scale:
-        count = rows.shape[0]
-        across = lax.broadcasted_iota(jnp.int32, (count, count), 1)
-        down = lax.broadcasted_iota(jnp.int32, (count, count), 0)
-        gates = jnp.where(across == down, gate[...], 0.0)
-        column = jnp.sum(gates, axis=1, keepdims=True)
-        rows = (column * rows.astype(F32)).astype(BF16)
+def place_kernel(slots, place, values, near, far):
     for first, out in ((0, near), (slots, far)):
         onehot = chosen(place[...], first, out.shape[0]).astype(F32).astype(BF16)
-        out[...] = jnp.dot(onehot, rows, preferred_element_type=F32).astype(BF16)
-
-
-def to_slots(slots, scale, place, gate, values):
+        out[...] = jnp.dot(onehot, values[...], preferred_element_type=F32).astype(BF16)
+
+
+def to_slots(slots, place, values):
     experts = lax.axis_size("expert") // SPLIT
     width = values.shape[1]
     return pl.pallas_call(
-        functools.partial(place_kernel, slots, scale),
+        functools.partial(place_kernel, slots),
         out_shape=(
             jax.ShapeDtypeStruct((slots, width), BF16),
             jax.ShapeDtypeStruct(((experts - 1) * slots, width), BF16),
         ),
-        in_specs=[VMEM] * 3,
+        in_specs=[VMEM] * 2,
         out_specs=(VMEM, VMEM),
         compiler_params=params(6),
         cost_estimate=cost(values.size, values.size),
         name="rows_to_slots",
-    )(place, gate, values)
+    )(place, values)
 
 
 def home_kernel(slots, place, gate, kept, got, back, token_grad, gate_grad):
@@ -293,22 +285,23 @@
     slots = saved_hidden.shape[0] // devices
     units = saved_hidden.shape[1]
     me = lax.axis_index("expert")
+    scaled = (gate[:, None] * out_grad.astype(F32)).astype(BF16)
     place, gate = pack_routing(expert_id, dropped, slot, gate, slots)
     order = sources_met(me, experts)
     by_source = saved_hidden.reshape(devices, slots, units)
     near_count = SPLIT * slots
 
-    near_grad, far_grad = to_slots(slots, True, place, gate, out_grad)
-    near_row, far_row = to_slots(slots, False, place, gate, tokens)
+    near_grad, far_grad = to_slots(slots, place, scaled)
+    near_row, far_row = to_slots(slots, place, tokens)
 
     far_grad = cross(far_grad, 1)
     got = meet(near_grad, 0)
     near_two = join(near_grad, after(got, near_row))
     got = meet(near_two, 1)
-    act, slope = activation(by_source, after(order, near_two))
-    far_grad = pause(after(far_grad, act))
+    far_grad = pause(after(far_grad, near_two))
+    act, slope = activation(by_source, after(order, far_grad))
     far_got = meet(far_grad, 0)
-    near_four = join(near_two, after(got, far_grad))
+    near_four = join(near_two, after(got, act))
     got = meet(near_four, 2)
     far_two = join(far_grad, after(far_got, near_four), long=True)
     far_got = meet(far_two, 1)

time: 90.7 us -> 93.3 us (1.029)
  starting transfers between devices: 24.5 us -> 30.2 us
  local copies, waits for them, and re-layouts: 7.23 us -> 3.4 us
  waiting for transfers between devices: 32.6 us -> 28.9 us
  Pallas kernels: 14.3 us -> 17.6 us
  other arithmetic: 1.66 us -> 2.8 us
    ppermute x19, waiting for transfers between devices: 24 us -> 18.7 us  [meet(): lax.ppermute(rows, 'expert', [(i, i ^ bits(i % 2)[step]) for i in range(d...]
    unnamed x16 -> x10, local copies, waits for them, and re-layouts: 6.82 us -> 2.99 us
    ppermute x19, starting transfers between devices: 17.2 us -> 20.6 us  [meet(): lax.ppermute(rows, 'expert', [(i, i ^ bits(i % 2)[step]) for i in range(d...]
    ppermute x4, starting transfers between devices: 7.36 us -> 9.53 us  [shift(): return lax.ppermute(rows, 'expert', pairs)]
    ppermute x4, waiting for transfers between devices: 8.53 us -> 10.2 us  [shift(): return lax.ppermute(rows, 'expert', pairs)]
    pallas_call x2, Pallas kernels: 0.04 us -> 1.67 us  [pause(): pl.pallas_call(pause_kernel, out_shape=jax.ShapeDtypeStruct(rows.shape, r...]
    convert_element_type x0 -> x1, other arithmetic: none -> 1.13 us  [body(): scaled = (gate[:, None] * out_grad.astype(F32)).astype(BF16)]
    pallas_call x13, Pallas kernels: 1.28 us -> 2.34 us  [join(): pl.pallas_call(stack_kernel, out_shape=jax.ShapeDtypeStruct((rows, width)...]
  transfers between devices with their start and end apart: 23 -> 23, of which waited for: 11 -> 11; matrix products, arithmetic and copies ran while one was open for 12% -> 11% of each run, Pallas kernels for 14% -> 17%
where the time goes in v12:
time: 93.3 us; the launch traced here: 93 us
  starting transfers between devices  30.2 us (32%)
  waiting for transfers between devices  28.9 us (31%)
  Pallas kernels  17.6 us (19%)
  matrix products  9.16 us (10%)
  local copies, waits for them, and re-layouts  3.4 us (4%)
  other arithmetic  2.8 us (3%)
  between operations  0.94 us (1%)
    ppermute x19, starting transfers between devices, meet(): lax.ppermute(rows, 'expert', [(i, i ^ bits(i % 2)[step]) for i in range(d...  20.6 us
    ppermute x19, waiting for transfers between devices, meet(): lax.ppermute(rows, 'expert', [(i, i ^ bits(i % 2)[step]) for i in range(d...  18.7 us
    ppermute x4, waiting for transfers between devices, shift(): return lax.ppermute(rows, 'expert', pairs)  10.2 us
    ppermute x4, starting transfers between devices, shift(): return lax.ppermute(rows, 'expert', pairs)  9.53 us
    dot_general x2, matrix products, product(): return lax.dot_general(a, b, (dims, ((), ())), preferred_element_type=F32)  9.16 us
    pallas_call x2, Pallas kernels, slot_grads(): pl.pallas_call(slot_grad_kernel, out_shape=(jax.ShapeDtypeStruct((rows, u...  7.81 us
    pallas_call x1, Pallas kernels, activation(): pl.pallas_call(activation_kernel, grid_spec=pltpu.PrefetchScalarGridSpec(...  3.36 us
    unnamed x10, local copies, waits for them, and re-layouts  2.99 us
  transfers between devices with their start and end apart: 23, of which 11 were waited for; matrix products, arithmetic and copies ran while one was open for 11% of the time, Pallas kernels for 17%

profile of v12, /device:TPU:0, one launch (start us, length us, event | category | flops | bytes accessed | tf_op | source)
XLA Modules:
  0.0 93.0 jit_solution(10697061205577461025)
XLA Ops:
  0.6 1.1 %multiply_convert_fusion.values = bf16[128,1536]{1,0:T(8,128)(2,1)S(1)} fusion(bf16[128,1536]{1,0:T(8,128)(2,1)} %param.10, f32[128]{0:T(128)} %param.11), kind=kLoop, calls=%fused_computation.6 | loop fusion | flops 589824 | bytes 786944 | tf_op jit(solution)/shard_map/convert_element_type | solution.py:288
  1.8 0.7 fusion.place
  2.5 1.0 %rows_to_slots.2 = (bf16[80,1536]{1,0:T(8,128)(2,1)S(1)}, bf16[80,1536]{1,0:T(8,128)(2,1)}) custom-call(s32[1,128]{1,0:T(1,128)S(1)} %fusion.place, bf16[128,1536]{1,0:T(8,128)(2,1)S(1)} %multiply_convert_fusion.values), custom_call_target="tpu_custom_call" | custom-call | flops 196608 | bytes 196608 | tf_op jit(solution)/shard_map/rows_to_slots/pallas_call | solution.py:93
  3.5 3.0 %collective-permute-start = (bf16[80,1536]{1,0:T(8,128)(2,1)S(1)}, bf16[80,1536]{1,0:T(8,128)(2,1)S(1)}, u32[]{:S(2)}, u32[]{:S(2)}) collective-permute-start(bf16[80,1536]{1,0:T(8,128)(2,1)S(1)} %get-tuple-element.46.refs_0_), channel_id=1, source_target_pairs={{0,4},{1,3},{2,6},{3,1},{4,0},{5,7},{6,2},{7,5},{8,12},{9,11},{10,... | collective-permute-start | bytes 737288 | tf_op jit(solution)/shard_map/ppermute | solution.py:32
  6.5 2.6 %collective-permute-start.2 = (bf16[80,1536]{1,0:T(8,128)(2,1)}, bf16[80,1536]{1,0:T(8,128)(2,1)}, u32[]{:S(2)}, u32[]{:S(2)}) collective-permute-start(bf16[80,1536]{1,0:T(8,128)(2,1)} %get-tuple-element.49), channel_id=1, source_target_pairs={{0,8},{1,9},{2,10},{3,11},{4,12},{5,13},{6,14},{7,15},{8,0},{9,1},... | collective-permute-start | bytes 737288 | tf_op jit(solution)/shard_map/ppermute | solution.py:38
  9.1 1.0 %copy-done.3 = bf16[128,1536]{1,0:T(8,128)(2,1)S(1)} copy-done((bf16[128,1536]{1,0:T(8,128)(2,1)S(1)}, bf16[128,1536]{1,0:T(8,128)(2,1)}, u32[]{:S(2)}) %copy-start.3) | copy-done | bytes 393240
  10.1 0.3 rows_to_slots.3
  10.4 2.2 %collective-permute-done.refs_1_ = bf16[80,1536]{1,0:T(8,128)(2,1)S(1)} collective-permute-done((bf16[80,1536]{1,0:T(8,128)(2,1)S(1)}, bf16[80,1536]{1,0:T(8,128)(2,1)S(1)}, u32[]{:S(2)}, u32[]{:S(2)}) %collective-permute-start) | collective-permute-done | bytes 245792 | tf_op jit(solution)/shard_map/ppermute | solution.py:32
  12.6 4.5 %collective-permute-start.1 = (bf16[160,1536]{1,0:T(8,128)(2,1)S(1)}, bf16[160,1536]{1,0:T(8,128)(2,1)S(1)}, u32[]{:S(2)}, u32[]{:S(2)}) collective-permute-start(bf16[160,1536]{1,0:T(8,128)(2,1)S(1)} %stack_rows.13.refs_0_), channel_id=1, source_target_pairs={{0,2},{1,5},{2,0},{3,7},{4,6},{5,1},{6,4},{7,3},{8,10},{9,13},{10,... | collective-permute-start | bytes 1474568 | tf_op jit(solution)/shard_map/ppermute | solution.py:32
  17.1 2.7 %collective-permute-done.2.rows = bf16[80,1536]{1,0:T(8,128)(2,1)} collective-permute-done((bf16[80,1536]{1,0:T(8,128)(2,1)}, bf16[80,1536]{1,0:T(8,128)(2,1)}, u32[]{:S(2)}, u32[]{:S(2)}) %collective-permute-start.2) | collective-permute-done | bytes 245792 | tf_op jit(solution)/shard_map/ppermute | solution.py:38
  19.8 1.7 %pause.2.refs_0_ = bf16[80,1536]{1,0:T(8,128)(2,1)} custom-call(bf16[80,1536]{1,0:T(8,128)(2,1)} %collective-permute-done.2.rows), custom_call_target="tpu_custom_call" | custom-call | flops 20000000000 | tf_op jit(solution)/shard_map/pause/pallas_call | solution.py:225
  21.4 1.7 %collective-permute-start.4 = (bf16[80,1536]{1,0:T(8,128)(2,1)}, bf16[80,1536]{1,0:T(8,128)(2,1)}, u32[]{:S(2)}, u32[]{:S(2)}) collective-permute-start(bf16[80,1536]{1,0:T(8,128)(2,1)} %pause.2.refs_0_), channel_id=1, source_target_pairs={{0,4},{1,3},{2,6},{3,1},{4,0},{5,7},{6,2},{7,5},{8,12},{9,11},{10,... | collective-permute-start | bytes 737288 | tf_op jit(solution)/shard_map/ppermute | solution.py:32
  23.2 0.1 pad_add_fusion.order
  23.3 3.4 %activation.1 = (bf16[16,80,768]{2,1,0:T(8,128)(2,1)S(1)}, bf16[16,80,768]{2,1,0:T(8,128)(2,1)S(1)}) custom-call(s32[16]{0:T(128)S(1)} %pad_add_fusion.order, bf16[16,80,768]{2,1,0:T(8,128)(2,1)S(1)} %bitcast.27), custom_call_target="tpu_custom_call" | custom-call | tf_op jit(solution)/shard_map/activation/pallas_call | solution.py:161
  26.6 0.1 stack_rows.14.refs_0_
  26.7 0.1 collective-permute-start.3
  26.8 1.2 %collective-permute-done.4.refs_1_ = bf16[80,1536]{1,0:T(8,128)(2,1)} collective-permute-done((bf16[80,1536]{1,0:T(8,128)(2,1)}, bf16[80,1536]{1,0:T(8,128)(2,1)}, u32[]{:S(2)}, u32[]{:S(2)}) %collective-permute-start.4) | collective-permute-done | bytes 245792 | tf_op jit(solution)/shard_map/ppermute | solution.py:32
  28.0 1.1 %stack_rows.15.refs_0_ = bf16[160,1536]{1,0:T(8,128)(2,1)S(1)} custom-call(bf16[80,1536]{1,0:T(8,128)(2,1)} %pause.2.refs_0_, bf16[80,1536]{1,0:T(8,128)(2,1)} %collective-permute-done.4.refs_1_), custom_call_target="tpu_custom_call" | custom-call | flops 20000000000 | bytes 245760 | tf_op jit(solution)/shard_map/stack_rows/pallas_call | solution.py:189
  29.1 0.9 collective-permute-start.6
  29.9 1.9 %collective-permute-start.7 = (bf16[80,1536]{1,0:T(8,128)(2,1)S(1)}, bf16[80,1536]{1,0:T(8,128)(2,1)S(1)}, u32[]{:S(2)}, u32[]{:S(2)}) collective-permute-start(bf16[80,1536]{1,0:T(8,128)(2,1)S(1)} %get-tuple-element.59.refs_0_), channel_id=1, source_target_pairs={{0,4},{1,3},{2,6},{3,1},{4,0},{5,7},{6,2},{7,5},{8,12},{9,11},{10,... | collective-permute-start | bytes 737288 | tf_op jit(solution)/shard_map/ppermute | solution.py:32
  31.8 2.6 %collective-permute-start.8 = (bf16[40,1536]{1,0:T(8,128)(2,1)S(1)}, bf16[40,1536]{1,0:T(8,128)(2,1)S(1)}, u32[]{:S(2)}, u32[]{:S(2)}) collective-permute-start(bf16[40,1536]{1,0:T(8,128)(2,1)S(1)} %get-tuple-element.99), channel_id=1, source_target_pairs={{0,8},{1,9},{2,10},{3,11},{4,12},{5,13},{6,14},{7,15},{8,0},{9,1},... | collective-permute-start | bytes 368648 | tf_op jit(solution)/shard_map/ppermute | solution.py:38
  34.5 0.3 fusion.3
  34.8 0.1 stack_rows.16.grads.refs_0_
  34.9 1.2 %copy-done.1 = bf16[1536,768]{1,0:T(8,128)(2,1)S(1)} copy-done((bf16[1536,768]{1,0:T(8,128)(2,1)S(1)}, bf16[1536,768]{1,0:T(8,128)(2,1)}, u32[]{:S(2)}) %copy-start.1) | copy-done | bytes 2359320
  36.1 0.8 copy-done
  36.9 3.9 %slot_grads.2 = (bf16[640,768]{1,0:T(8,128)(2,1)S(1)}, bf16[320,1664]{1,0:T(8,128)(2,1)S(1)}, bf16[320,1664]{1,0:T(8,128)(2,1)S(1)}) custom-call(bf16[640,1536]{1,0:T(8,128)(2,1)S(1)} %stack_rows.16.grads.refs_0_, bf16[768,1536]{1,0:T(8,128)(2,1)S(1)} %copy-done, bf16[1536,768]{1,0:T(8,128)(2,1)S(1)} %copy-done.1, bf16[640,768]{1,0:T(8,128)(2,1)S(1)} %bitcast.26, ...), custom_call_target="tpu_custom_call" | custom-call | tf_op jit(solution)/shard_map/slot_grads/pallas_call | solution.py:267
  40.8 0.1 collective-permute-start.5
  40.9 0.5 collective-permute-done.7.refs_1_
  41.5 0.1 stack_rows.18.refs_0_
  41.6 0.1 collective-permute-start.10
  41.7 2.1 %collective-permute-start.11 = (bf16[40,1536]{1,0:T(8,128)(2,1)S(1)}, bf16[40,1536]{1,0:T(8,128)(2,1)S(1)}, u32[]{:S(2)}, u32[]{:S(2)}) collective-permute-start(bf16[40,1536]{1,0:T(8,128)(2,1)S(1)} %get-tuple-element.68), channel_id=1, source_target_pairs={{0,8},{1,9},{2,10},{3,11},{4,12},{5,13},{6,14},{7,15},{8,0},{9,1},... | collective-permute-start | bytes 368648 | tf_op jit(solution)/shard_map/ppermute | solution.py:38
  43.8 0.2 add_convert_fusion.2
  44.1 1.4 %collective-permute-start.9 = (bf16[160,1664]{1,0:T(8,128)(2,1)S(1)}, bf16[160,1664]{1,0:T(8,128)(2,1)S(1)}, u32[]{:S(2)}, u32[]{:S(2)}) collective-permute-start(bf16[160,1664]{1,0:T(8,128)(2,1)S(1)} %get-tuple-element.88), channel_id=1, source_target_pairs={{0,2},{1,5},{2,0},{3,7},{4,6},{5,1},{6,4},{7,3},{8,10},{9,13},{10,... | collective-permute-start | bytes 1597448 | tf_op jit(solution)/shard_map/ppermute | solution.py:32
  45.4 0.1 stack_rows.19.grads.refs_1_
  45.6 3.9 %slot_grads.3 = (bf16[640,768]{1,0:T(8,128)(2,1)S(1)}, bf16[320,1664]{1,0:T(8,128)(2,1)S(1)}, bf16[320,1664]{1,0:T(8,128)(2,1)S(1)}) custom-call(bf16[640,1536]{1,0:T(8,128)(2,1)S(1)} %stack_rows.19.grads.refs_1_, bf16[768,1536]{1,0:T(8,128)(2,1)S(1)} %copy-done, bf16[1536,768]{1,0:T(8,128)(2,1)S(1)} %copy-done.1, bf16[640,768]{1,0:T(8,128)(2,1)S(1)} %bitcast.24, ...), custom_call_target="tpu_custom_call" | custom-call | tf_op jit(solution)/shard_map/slot_grads/pallas_call | solution.py:267
  49.5 1.1 %collective-permute-done.11 = bf16[40,1536]{1,0:T(8,128)(2,1)S(1)} collective-permute-done((bf16[40,1536]{1,0:T(8,128)(2,1)S(1)}, bf16[40,1536]{1,0:T(8,128)(2,1)S(1)}, u32[]{:S(2)}, u32[]{:S(2)}) %collective-permute-start.11) | collective-permute-done | bytes 122912 | tf_op jit(solution)/shard_map/ppermute | solution.py:38
  50.6 0.1 fusion.5
  50.7 0.1 collective-permute-start.13
  50.8 1.9 %collective-permute-start.15 = (bf16[160,1536]{1,0:T(8,128)(2,1)S(1)}, bf16[160,1536]{1,0:T(8,128)(2,1)S(1)}, u32[]{:S(2)}, u32[]{:S(2)}) collective-permute-start(bf16[160,1536]{1,0:T(8,128)(2,1)S(1)} %stack_rows.17.refs_0_), channel_id=1, source_target_pairs={{0,2},{1,5},{2,0},{3,7},{4,6},{5,1},{6,4},{7,3},{8,10},{9,13},{10,... | collective-permute-start | bytes 1474568 | tf_op jit(solution)/shard_map/ppermute | solution.py:32
  52.7 0.3 stack_rows.20
  53.0 0.2 collective-permute-start.12
  53.2 0.3 collective-permute-done.9
  53.4 0.1 add_convert_fusion.7
  53.6 0.1 add_convert_fusion.1
  53.7 1.4 %collective-permute-start.14 = (bf16[160,1664]{1,0:T(8,128)(2,1)S(1)}, bf16[160,1664]{1,0:T(8,128)(2,1)S(1)}, u32[]{:S(2)}, u32[]{:S(2)}) collective-permute-start(bf16[160,1664]{1,0:T(8,128)(2,1)S(1)} %add_convert_fusion.1), channel_id=1, source_target_pairs={{0,2},{1,5},{2,0},{3,7},{4,6},{5,1},{6,4},{7,3},{8,10},{9,13},{10,... | collective-permute-start | bytes 1597448 | tf_op jit(solution)/shard_map/ppermute | solution.py:32
  55.0 0.2 add_convert_fusion
  55.2 4.6 %convolution_convert_fusion.1 = bf16[768,1536]{1,0:T(8,128)(2,1)} fusion(bf16[1280,768]{1,0:T(8,128)(2,1)S(1)} %bitcast.28, bf16[1280,1536]{1,0:T(8,128)(2,1)S(1)} %stack_rows.20), kind=kOutput, calls=%fused_computation.1 | convolution fusion | flops 3021078528 | bytes 8257536 | tf_op jit(solution)/shard_map/dot_general | solution.py:242
  59.8 1.8 %collective-permute-done.16.refs_1_ = bf16[80,1536]{1,0:T(8,128)(2,1)S(1)} collective-permute-done((bf16[80,1536]{1,0:T(8,128)(2,1)S(1)}, bf16[80,1536]{1,0:T(8,128)(2,1)S(1)}, u32[]{:S(2)}, u32[]{:S(2)}) %collective-permute-start.16) | collective-permute-done | bytes 245792 | tf_op jit(solution)/shard_map/ppermute | solution.py:32
  61.6 0.2 collective-permute-start.18
  61.8 0.5 collective-permute-done.15.refs_1_
  62.4 5.6 %collective-permute-done.14 = bf16[160,1664]{1,0:T(8,128)(2,1)S(1)} collective-permute-done((bf16[160,1664]{1,0:T(8,128)(2,1)S(1)}, bf16[160,1664]{1,0:T(8,128)(2,1)S(1)}, u32[]{:S(2)}, u32[]{:S(2)}) %collective-permute-start.14) | collective-permute-done | bytes 532512 | tf_op jit(solution)/shard_map/ppermute | solution.py:32
  68.0 0.1 add_convert_fusion.5
  68.1 1.2 %collective-permute-start.17 = (bf16[80,1664]{1,0:T(8,128)(2,1)S(1)}, bf16[80,1664]{1,0:T(8,128)(2,1)S(1)}, u32[]{:S(2)}, u32[]{:S(2)}) collective-permute-start(bf16[80,1664]{1,0:T(8,128)(2,1)S(1)} %add_convert_fusion.5), channel_id=1, source_target_pairs={{0,4},{1,3},{2,6},{3,1},{4,0},{5,7},{6,2},{7,5},{8,12},{9,11},{10,... | collective-permute-start | bytes 798728 | tf_op jit(solution)/shard_map/ppermute | solution.py:32
  69.3 0.1 stack_rows.25
  69.5 0.1 collective-permute-start.21
  69.5 6.5 %collective-permute-done.18.refs_1_ = bf16[160,1536]{1,0:T(8,128)(2,1)S(1)} collective-permute-done((bf16[160,1536]{1,0:T(8,128)(2,1)S(1)}, bf16[160,1536]{1,0:T(8,128)(2,1)S(1)}, u32[]{:S(2)}, u32[]{:S(2)}) %collective-permute-start.18) | collective-permute-done | bytes 491552 | tf_op jit(solution)/shard_map/ppermute | solution.py:32
  76.1 0.1 collective-permute-start.22
  76.2 0.1 add_convert_fusion.4.rows
  76.4 2.2 %collective-permute-start.20 = (bf16[80,1664]{1,0:T(8,128)(2,1)S(1)}, bf16[80,1664]{1,0:T(8,128)(2,1)S(1)}, u32[]{:S(2)}, u32[]{:S(2)}) collective-permute-start(bf16[80,1664]{1,0:T(8,128)(2,1)S(1)} %pause.3), channel_id=1, source_target_pairs={{0,8},{1,9},{2,10},{3,11},{4,12},{5,13},{6,14},{7,15},{8,0},{9,1},... | collective-permute-start | bytes 798728 | tf_op jit(solution)/shard_map/ppermute | solution.py:38
  78.6 1.9 %collective-permute-start.19 = (bf16[80,1664]{1,0:T(8,128)(2,1)S(1)}, bf16[80,1664]{1,0:T(8,128)(2,1)S(1)}, u32[]{:S(2)}, u32[]{:S(2)}) collective-permute-start(bf16[80,1664]{1,0:T(8,128)(2,1)S(1)} %get-tuple-element.81), channel_id=1, source_target_pairs={{0,4},{1,3},{2,6},{3,1},{4,0},{5,7},{6,2},{7,5},{8,12},{9,11},{10,... | collective-permute-start | bytes 798728 | tf_op jit(solution)/shard_map/ppermute | solution.py:32
  80.5 0.3 stack_rows.24
  80.8 4.6 %convolution_convert_fusion = bf16[1536,768]{1,0:T(8,128)(2,1)} fusion(bf16[1280,1536]{1,0:T(8,128)(2,1)S(1)} %stack_rows.24, bf16[1280,768]{1,0:T(8,128)(2,1)S(1)} %stack_rows.25), kind=kOutput, calls=%fused_computation | convolution fusion | flops 3021078528 | bytes 8257536 | tf_op jit(solution)/shard_map/dot_general | solution.py:242
  85.4 6.5 %collective-permute-done.20.back = bf16[80,1664]{1,0:T(8,128)(2,1)S(1)} collective-permute-done((bf16[80,1664]{1,0:T(8,128)(2,1)S(1)}, bf16[80,1664]{1,0:T(8,128)(2,1)S(1)}, u32[]{:S(2)}, u32[]{:S(2)}) %collective-permute-start.20) | collective-permute-done | bytes 266272 | tf_op jit(solution)/shard_map/ppermute | solution.py:38
  91.8 1.2 %slots_to_tokens.1 = (bf16[128,1536]{1,0:T(8,128)(2,1)}, f32[1,128]{1,0:T(1,128)}) custom-call(s32[1,128]{1,0:T(1,128)S(1)} %fusion.place, f32[1,128]{1,0:T(1,128)S(1)} %bitcast.30, bf16[80,1664]{1,0:T(8,128)(2,1)S(1)} %get-tuple-element.97.kept, bf16[80,1664]{1,0:T(8,128)(2,1)S(1)} %collective-permute-done.19.got, ...), custom_call_target="tpu_custom_call" | custom-call | tf_op jit(solution)/shard_map/slots_to_tokens/pallas_call | solution.py:128
  (30 shorter events, 0.4 us)
Async XLA Ops:
  3.5 9.1 %collective-permute-start = (bf16[80,1536]{1,0:T(8,128)(2,1)S(1)}, bf16[80,1536]{1,0:T(8,128)(2,1)S(1)}, u32[]{:S(2)}, u32[]{:S(2)}) collective-permute-start(bf16[80,1536]{1,0:T(8,128)(2,1)S(1)} %get-tuple-element.46.refs_0_), channel_id=1, source_target_pairs={{0,4},{1,3},{2,6},{3,1},{4,0},{5,7},{6,2},{7,5},{8,12},{9,11},{10,... | collective-permute-start | bytes 737288 | tf_op jit(solution)/shard_map/ppermute | solution.py:32
  6.5 13.3 %collective-permute-start.2 = (bf16[80,1536]{1,0:T(8,128)(2,1)}, bf16[80,1536]{1,0:T(8,128)(2,1)}, u32[]{:S(2)}, u32[]{:S(2)}) collective-permute-start(bf16[80,1536]{1,0:T(8,128)(2,1)} %get-tuple-element.49), channel_id=1, source_target_pairs={{0,8},{1,9},{2,10},{3,11},{4,12},{5,13},{6,14},{7,15},{8,0},{9,1},... | collective-permute-start | bytes 737288 | tf_op jit(solution)/shard_map/ppermute | solution.py:38
  9.1 1.0 %copy-start.3 = (bf16[128,1536]{1,0:T(8,128)(2,1)S(1)}, bf16[128,1536]{1,0:T(8,128)(2,1)}, u32[]{:S(2)}) copy-start(bf16[128,1536]{1,0:T(8,128)(2,1)} %values.1) | copy-start | bytes 1179652
  12.6 10.7 %copy-start.2 = (bf16[1280,768]{1,0:T(8,128)(2,1)S(1)}, bf16[1280,768]{1,0:T(8,128)(2,1)}, u32[]{:S(2)}) copy-start(bf16[1280,768]{1,0:T(8,128)(2,1)} %param.15) | copy-start | bytes 5898244
  12.6 14.0 %collective-permute-start.1 = (bf16[160,1536]{1,0:T(8,128)(2,1)S(1)}, bf16[160,1536]{1,0:T(8,128)(2,1)S(1)}, u32[]{:S(2)}, u32[]{:S(2)}) collective-permute-start(bf16[160,1536]{1,0:T(8,128)(2,1)S(1)} %stack_rows.13.refs_0_), channel_id=1, source_target_pairs={{0,2},{1,5},{2,0},{3,7},{4,6},{5,1},{6,4},{7,3},{8,10},{9,13},{10,... | collective-permute-start | bytes 1474568 | tf_op jit(solution)/shard_map/ppermute | solution.py:32
  21.4 6.5 %collective-permute-start.4 = (bf16[80,1536]{1,0:T(8,128)(2,1)}, bf16[80,1536]{1,0:T(8,128)(2,1)}, u32[]{:S(2)}, u32[]{:S(2)}) collective-permute-start(bf16[80,1536]{1,0:T(8,128)(2,1)} %pause.2.refs_0_), channel_id=1, source_target_pairs={{0,4},{1,3},{2,6},{3,1},{4,0},{5,7},{6,2},{7,5},{8,12},{9,11},{10,... | collective-permute-start | bytes 737288 | tf_op jit(solution)/shard_map/ppermute | solution.py:32
  26.7 8.1 %collective-permute-start.3 = (bf16[320,1536]{1,0:T(8,128)(2,1)S(1)}, bf16[320,1536]{1,0:T(8,128)(2,1)S(1)}, u32[]{:S(2)}, u32[]{:S(2)}) collective-permute-start(bf16[320,1536]{1,0:T(8,128)(2,1)S(1)} %stack_rows.14.refs_0_), channel_id=1, source_target_pairs={{0,1},{1,0},{2,3},{3,2},{4,5},{5,4},{6,7},{7,6},{8,9},{9,8},{10,11... | collective-permute-start | bytes 2949128 | tf_op jit(solution)/shard_map/ppermute | solution.py:32
  29.1 12.4 %collective-permute-start.6 = (bf16[160,1536]{1,0:T(8,128)(2,1)S(1)}, bf16[160,1536]{1,0:T(8,128)(2,1)S(1)}, u32[]{:S(2)}, u32[]{:S(2)}) collective-permute-start(bf16[160,1536]{1,0:T(8,128)(2,1)S(1)} %stack_rows.15.refs_0_), channel_id=1, source_target_pairs={{0,2},{1,5},{2,0},{3,7},{4,6},{5,1},{6,4},{7,3},{8,10},{9,13},{10,... | collective-permute-start | bytes 1474568 | tf_op jit(solution)/shard_map/ppermute | solution.py:32
  29.9 11.5 %collective-permute-start.7 = (bf16[80,1536]{1,0:T(8,128)(2,1)S(1)}, bf16[80,1536]{1,0:T(8,128)(2,1)S(1)}, u32[]{:S(2)}, u32[]{:S(2)}) collective-permute-start(bf16[80,1536]{1,0:T(8,128)(2,1)S(1)} %get-tuple-element.59.refs_0_), channel_id=1, source_target_pairs={{0,4},{1,3},{2,6},{3,1},{4,0},{5,7},{6,2},{7,5},{8,12},{9,11},{10,... | collective-permute-start | bytes 737288 | tf_op jit(solution)/shard_map/ppermute | solution.py:32
  31.8 9.1 %collective-permute-start.8 = (bf16[40,1536]{1,0:T(8,128)(2,1)S(1)}, bf16[40,1536]{1,0:T(8,128)(2,1)S(1)}, u32[]{:S(2)}, u32[]{:S(2)}) collective-permute-start(bf16[40,1536]{1,0:T(8,128)(2,1)S(1)} %get-tuple-element.99), channel_id=1, source_target_pairs={{0,8},{1,9},{2,10},{3,11},{4,12},{5,13},{6,14},{7,15},{8,0},{9,1},... | collective-permute-start | bytes 368648 | tf_op jit(solution)/shard_map/ppermute | solution.py:38
  34.5 1.7 %copy-start.1 = (bf16[1536,768]{1,0:T(8,128)(2,1)S(1)}, bf16[1536,768]{1,0:T(8,128)(2,1)}, u32[]{:S(2)}) copy-start(bf16[1536,768]{1,0:T(8,128)(2,1)} %w_in.3) | copy-start | bytes 7077892
  34.8 2.1 %copy-start = (bf16[768,1536]{1,0:T(8,128)(2,1)S(1)}, bf16[768,1536]{1,0:T(8,128)(2,1)}, u32[]{:S(2)}) copy-start(bf16[768,1536]{1,0:T(8,128)(2,1)} %w_out.3) | copy-start | bytes 7077892
  40.8 3.0 %collective-permute-start.5 = (bf16[320,1664]{1,0:T(8,128)(2,1)S(1)}, bf16[320,1664]{1,0:T(8,128)(2,1)S(1)}, u32[]{:S(2)}, u32[]{:S(2)}) collective-permute-start(bf16[320,1664]{1,0:T(8,128)(2,1)S(1)} %get-tuple-element.58), channel_id=1, source_target_pairs={{0,1},{1,0},{2,3},{3,2},{4,5},{5,4},{6,7},{7,6},{8,9},{9,8},{10,11... | collective-permute-start | bytes 3194888 | tf_op jit(solution)/shard_map/ppermute | solution.py:32
  41.6 3.9 %collective-permute-start.10 = (bf16[320,1536]{1,0:T(8,128)(2,1)S(1)}, bf16[320,1536]{1,0:T(8,128)(2,1)S(1)}, u32[]{:S(2)}, u32[]{:S(2)}) collective-permute-start(bf16[320,1536]{1,0:T(8,128)(2,1)S(1)} %stack_rows.18.refs_0_), channel_id=1, source_target_pairs={{0,1},{1,0},{2,3},{3,2},{4,5},{5,4},{6,7},{7,6},{8,9},{9,8},{10,11... | collective-permute-start | bytes 2949128 | tf_op jit(solution)/shard_map/ppermute | solution.py:32
  41.7 8.9 %collective-permute-start.11 = (bf16[40,1536]{1,0:T(8,128)(2,1)S(1)}, bf16[40,1536]{1,0:T(8,128)(2,1)S(1)}, u32[]{:S(2)}, u32[]{:S(2)}) collective-permute-start(bf16[40,1536]{1,0:T(8,128)(2,1)S(1)} %get-tuple-element.68), channel_id=1, source_target_pairs={{0,8},{1,9},{2,10},{3,11},{4,12},{5,13},{6,14},{7,15},{8,0},{9,1},... | collective-permute-start | bytes 368648 | tf_op jit(solution)/shard_map/ppermute | solution.py:38
  44.1 9.3 %collective-permute-start.9 = (bf16[160,1664]{1,0:T(8,128)(2,1)S(1)}, bf16[160,1664]{1,0:T(8,128)(2,1)S(1)}, u32[]{:S(2)}, u32[]{:S(2)}) collective-permute-start(bf16[160,1664]{1,0:T(8,128)(2,1)S(1)} %get-tuple-element.88), channel_id=1, source_target_pairs={{0,2},{1,5},{2,0},{3,7},{4,6},{5,1},{6,4},{7,3},{8,10},{9,13},{10,... | collective-permute-start | bytes 1597448 | tf_op jit(solution)/shard_map/ppermute | solution.py:32
  50.7 2.8 %collective-permute-start.13 = (bf16[160,1664]{1,0:T(8,128)(2,1)S(1)}, bf16[160,1664]{1,0:T(8,128)(2,1)S(1)}, u32[]{:S(2)}, u32[]{:S(2)}) collective-permute-start(bf16[160,1664]{1,0:T(8,128)(2,1)S(1)} %get-tuple-element.95), channel_id=1, source_target_pairs={{0,1},{1,0},{2,3},{3,2},{4,5},{5,4},{6,7},{7,6},{8,9},{9,8},{10,11... | collective-permute-start | bytes 1597448 | tf_op jit(solution)/shard_map/ppermute | solution.py:32
  50.8 11.5 %collective-permute-start.15 = (bf16[160,1536]{1,0:T(8,128)(2,1)S(1)}, bf16[160,1536]{1,0:T(8,128)(2,1)S(1)}, u32[]{:S(2)}, u32[]{:S(2)}) collective-permute-start(bf16[160,1536]{1,0:T(8,128)(2,1)S(1)} %stack_rows.17.refs_0_), channel_id=1, source_target_pairs={{0,2},{1,5},{2,0},{3,7},{4,6},{5,1},{6,4},{7,3},{8,10},{9,13},{10,... | collective-permute-start | bytes 1474568 | tf_op jit(solution)/shard_map/ppermute | solution.py:32
  52.7 8.9 %collective-permute-start.16 = (bf16[80,1536]{1,0:T(8,128)(2,1)S(1)}, bf16[80,1536]{1,0:T(8,128)(2,1)S(1)}, u32[]{:S(2)}, u32[]{:S(2)}) collective-permute-start(bf16[80,1536]{1,0:T(8,128)(2,1)S(1)} %maximum_bitcast_fusion.refs_0_), channel_id=1, source_target_pairs={{0,4},{1,3},{2,6},{3,1},{4,0},{5,7},{6,2},{7,5},{8,12},{9,11},{10,... | collective-permute-start | bytes 737288 | tf_op jit(solution)/shard_map/ppermute | solution.py:32
  53.0 2.1 %collective-permute-start.12 = (bf16[160,1664]{1,0:T(8,128)(2,1)S(1)}, bf16[160,1664]{1,0:T(8,128)(2,1)S(1)}, u32[]{:S(2)}, u32[]{:S(2)}) collective-permute-start(bf16[160,1664]{1,0:T(8,128)(2,1)S(1)} %get-tuple-element.94), channel_id=1, source_target_pairs={{0,1},{1,0},{2,3},{3,2},{4,5},{5,4},{6,7},{7,6},{8,9},{9,8},{10,11... | collective-permute-start | bytes 1597448 | tf_op jit(solution)/shard_map/ppermute | solution.py:32
  53.7 14.3 %collective-permute-start.14 = (bf16[160,1664]{1,0:T(8,128)(2,1)S(1)}, bf16[160,1664]{1,0:T(8,128)(2,1)S(1)}, u32[]{:S(2)}, u32[]{:S(2)}) collective-permute-start(bf16[160,1664]{1,0:T(8,128)(2,1)S(1)} %add_convert_fusion.1), channel_id=1, source_target_pairs={{0,2},{1,5},{2,0},{3,7},{4,6},{5,1},{6,4},{7,3},{8,10},{9,13},{10,... | collective-permute-start | bytes 1597448 | tf_op jit(solution)/shard_map/ppermute | solution.py:32
  61.6 14.5 %collective-permute-start.18 = (bf16[160,1536]{1,0:T(8,128)(2,1)S(1)}, bf16[160,1536]{1,0:T(8,128)(2,1)S(1)}, u32[]{:S(2)}, u32[]{:S(2)}) collective-permute-start(bf16[160,1536]{1,0:T(8,128)(2,1)S(1)} %stack_rows.21.refs_0_), channel_id=1, source_target_pairs={{0,2},{1,5},{2,0},{3,7},{4,6},{5,1},{6,4},{7,3},{8,10},{9,13},{10,... | collective-permute-start | bytes 1474568 | tf_op jit(solution)/shard_map/ppermute | solution.py:32
  68.1 8.1 %collective-permute-start.17 = (bf16[80,1664]{1,0:T(8,128)(2,1)S(1)}, bf16[80,1664]{1,0:T(8,128)(2,1)S(1)}, u32[]{:S(2)}, u32[]{:S(2)}) collective-permute-start(bf16[80,1664]{1,0:T(8,128)(2,1)S(1)} %add_convert_fusion.5), channel_id=1, source_target_pairs={{0,4},{1,3},{2,6},{3,1},{4,0},{5,7},{6,2},{7,5},{8,12},{9,11},{10,... | collective-permute-start | bytes 798728 | tf_op jit(solution)/shard_map/ppermute | solution.py:32
  69.5 11.0 %collective-permute-start.21 = (bf16[320,1536]{1,0:T(8,128)(2,1)S(1)}, bf16[320,1536]{1,0:T(8,128)(2,1)S(1)}, u32[]{:S(2)}, u32[]{:S(2)}) collective-permute-start(bf16[320,1536]{1,0:T(8,128)(2,1)S(1)} %stack_rows.22.refs_0_), channel_id=1, source_target_pairs={{0,1},{1,0},{2,3},{3,2},{4,5},{5,4},{6,7},{7,6},{8,9},{9,8},{10,11... | collective-permute-start | bytes 2949128 | tf_op jit(solution)/shard_map/ppermute | solution.py:32
  76.1 4.4 %collective-permute-start.22 = (bf16[320,1536]{1,0:T(8,128)(2,1)S(1)}, bf16[320,1536]{1,0:T(8,128)(2,1)S(1)}, u32[]{:S(2)}, u32[]{:S(2)}) collective-permute-start(bf16[320,1536]{1,0:T(8,128)(2,1)S(1)} %stack_rows.23.refs_2_), channel_id=1, source_target_pairs={{0,1},{1,0},{2,3},{3,2},{4,5},{5,4},{6,7},{7,6},{8,9},{9,8},{10,11... | collective-permute-start | bytes 2949128 | tf_op jit(solution)/shard_map/ppermute | solution.py:32
  76.4 15.5 %collective-permute-start.20 = (bf16[80,1664]{1,0:T(8,128)(2,1)S(1)}, bf16[80,1664]{1,0:T(8,128)(2,1)S(1)}, u32[]{:S(2)}, u32[]{:S(2)}) collective-permute-start(bf16[80,1664]{1,0:T(8,128)(2,1)S(1)} %pause.3), channel_id=1, source_target_pairs={{0,8},{1,9},{2,10},{3,11},{4,12},{5,13},{6,14},{7,15},{8,0},{9,1},... | collective-permute-start | bytes 798728 | tf_op jit(solution)/shard_map/ppermute | solution.py:38
  78.6 13.3 %collective-permute-start.19 = (bf16[80,1664]{1,0:T(8,128)(2,1)S(1)}, bf16[80,1664]{1,0:T(8,128)(2,1)S(1)}, u32[]{:S(2)}, u32[]{:S(2)}) collective-permute-start(bf16[80,1664]{1,0:T(8,128)(2,1)S(1)} %get-tuple-element.81), channel_id=1, source_target_pairs={{0,4},{1,3},{2,6},{3,1},{4,0},{5,7},{6,2},{7,5},{8,12},{9,11},{10,... | collective-permute-start | bytes 798728 | tf_op jit(solution)/shard_map/ppermute | solution.py:32
  80.8 11.1 %copy-start.4 = (f32[128]{0:T(128)S(1)}, f32[128]{0:T(128)}, u32[]{:S(2)}) copy-start(f32[128]{0:T(128)} %param.11) | copy-start | bytes 1540

commit v13 on v11

--- a/solution.py
+++ b/solution.py
@@ -310,19 +310,18 @@
     far_got = meet(far_grad, 0)
     near_four = join(near_two, after(got, far_grad))
     got = meet(near_four, 2)
-    far_two = join(far_grad, after(far_got, near_four), long=True)
+    far_row_a, far_row_b = split_slots(after(far_row, far_grad), experts)
+    far_row_a = cross(far_row_a, 1)
+    far_two = join(far_grad, after(far_got, near_four, far_row_a), long=True)
     far_got = meet(far_two, 1)
 
-    far_row_a, far_row_b = split_slots(after(far_row, far_two), experts)
-    far_row_a = cross(far_row_a, 1)
     row_got = meet(after(near_row, far_two), 0)
     near_grads = join(near_four, after(got, far_two))
     near_hg, near_kept, near_sent = slot_grads(
         near_grads, w_out, w_in, act[:near_count], slope[:near_count]
     )
     near_got = meet(near_sent, 2)
-    far_row_a = after(far_row_a, near_sent)
-    near_row2 = join(near_row, after(row_got, far_row_a))
+    near_row2 = join(near_row, after(row_got, near_sent))
     far_four = join(far_two, after(far_got, near_row2), long=True)
     far_got = meet(far_four, 2)
     far_row_b = cross(after(far_row_b, far_four), 1)

time: 90.7 us -> 90.9 us (level)
  starting transfers between devices: 24.5 us -> 31.5 us
  waiting for transfers between devices: 32.6 us -> 25.8 us
    ppermute x19, waiting for transfers between devices: 24 us -> 16.2 us  [meet(): lax.ppermute(rows, 'expert', [(i, i ^ bits(i % 2)[step]) for i in range(d...]
    ppermute x19, starting transfers between devices: 17.2 us -> 22.7 us  [meet(): lax.ppermute(rows, 'expert', [(i, i ^ bits(i % 2)[step]) for i in range(d...]
    ppermute x4, starting transfers between devices: 7.36 us -> 8.85 us  [shift(): return lax.ppermute(rows, 'expert', pairs)]
    ppermute x4, waiting for transfers between devices: 8.53 us -> 9.64 us  [shift(): return lax.ppermute(rows, 'expert', pairs)]
  transfers between devices with their start and end apart: 23 -> 23, of which waited for: 11 -> 10; matrix products, arithmetic and copies ran while one was open for 12% -> 12% of each run, Pallas kernels for 14% -> 14%
where the time goes in v13:
time: 90.9 us; the launch traced here: 90.6 us
  starting transfers between devices  31.5 us (35%)
  waiting for transfers between devices  25.8 us (28%)
  Pallas kernels  14.3 us (16%)
  matrix products  9.15 us (10%)
  local copies, waits for them, and re-layouts  7.23 us (8%)
  other arithmetic  1.66 us (2%)
  between operations  0.94 us (1%)
    ppermute x19, starting transfers between devices, meet(): lax.ppermute(rows, 'expert', [(i, i ^ bits(i % 2)[step]) for i in range(d...  22.7 us
    ppermute x19, waiting for transfers between devices, meet(): lax.ppermute(rows, 'expert', [(i, i ^ bits(i % 2)[step]) for i in range(d...  16.2 us
    ppermute x4, waiting for transfers between devices, shift(): return lax.ppermute(rows, 'expert', pairs)  9.64 us
    dot_general x2, matrix products, product(): return lax.dot_general(a, b, (dims, ((), ())), preferred_element_type=F32)  9.15 us
    ppermute x4, starting transfers between devices, shift(): return lax.ppermute(rows, 'expert', pairs)  8.85 us
    pallas_call x2, Pallas kernels, slot_grads(): pl.pallas_call(slot_grad_kernel, out_shape=(jax.ShapeDtypeStruct((rows, u...  7.82 us
    unnamed x16, local copies, waits for them, and re-layouts  6.82 us
    pallas_call x1, Pallas kernels, activation(): pl.pallas_call(activation_kernel, grid_spec=pltpu.PrefetchScalarGridSpec(...  3.36 us
  transfers between devices with their start and end apart: 23, of which 10 were waited for; matrix products, arithmetic and copies ran while one was open for 12% of the time, Pallas kernels for 14%

profile of v13, /device:TPU:0, one launch (start us, length us, event | category | flops | bytes accessed | tf_op | source)
XLA Modules:
  0.0 90.6 jit_solution(2841280136367652780)
XLA Ops:
  0.6 0.7 fusion.place
  1.3 1.0 %copy-done.3 = bf16[128,1536]{1,0:T(8,128)(2,1)S(1)} copy-done((bf16[128,1536]{1,0:T(8,128)(2,1)S(1)}, bf16[128,1536]{1,0:T(8,128)(2,1)}, u32[]{:S(2)}) %copy-start.3) | copy-done | bytes 393240
  2.3 0.7 copy-done.5
  3.0 0.4 rows_to_slots.2
  3.4 3.1 %collective-permute-start = (bf16[80,1536]{1,0:T(8,128)(2,1)S(1)}, bf16[80,1536]{1,0:T(8,128)(2,1)S(1)}, u32[]{:S(2)}, u32[]{:S(2)}) collective-permute-start(bf16[80,1536]{1,0:T(8,128)(2,1)S(1)} %get-tuple-element.45.refs_0_), channel_id=1, source_target_pairs={{0,4},{1,3},{2,6},{3,1},{4,0},{5,7},{6,2},{7,5},{8,12},{9,11},{10,... | collective-permute-start | bytes 737288 | tf_op jit(solution)/shard_map/ppermute | solution.py:32
  6.5 2.6 %collective-permute-start.2 = (bf16[80,1536]{1,0:T(8,128)(2,1)S(1)}, bf16[80,1536]{1,0:T(8,128)(2,1)S(1)}, u32[]{:S(2)}, u32[]{:S(2)}) collective-permute-start(bf16[80,1536]{1,0:T(8,128)(2,1)S(1)} %get-tuple-element.48), channel_id=1, source_target_pairs={{0,8},{1,9},{2,10},{3,11},{4,12},{5,13},{6,14},{7,15},{8,0},{9,1},... | collective-permute-start | bytes 737288 | tf_op jit(solution)/shard_map/ppermute | solution.py:38
  9.1 1.0 %copy-done.4 = bf16[128,1536]{1,0:T(8,128)(2,1)S(1)} copy-done((bf16[128,1536]{1,0:T(8,128)(2,1)S(1)}, bf16[128,1536]{1,0:T(8,128)(2,1)}, u32[]{:S(2)}) %copy-start.4) | copy-done | bytes 393240
  10.1 0.7 copy-done.6
  10.7 0.3 rows_to_slots.3
  11.0 0.1 pad_add_fusion.order
  11.1 1.6 %collective-permute-done.refs_1_ = bf16[80,1536]{1,0:T(8,128)(2,1)S(1)} collective-permute-done((bf16[80,1536]{1,0:T(8,128)(2,1)S(1)}, bf16[80,1536]{1,0:T(8,128)(2,1)S(1)}, u32[]{:S(2)}, u32[]{:S(2)}) %collective-permute-start) | collective-permute-done | bytes 245792 | tf_op jit(solution)/shard_map/ppermute | solution.py:32
  12.8 4.4 %collective-permute-start.1 = (bf16[160,1536]{1,0:T(8,128)(2,1)S(1)}, bf16[160,1536]{1,0:T(8,128)(2,1)S(1)}, u32[]{:S(2)}, u32[]{:S(2)}) collective-permute-start(bf16[160,1536]{1,0:T(8,128)(2,1)S(1)} %stack_rows.13.refs_0_), channel_id=1, source_target_pairs={{0,2},{1,5},{2,0},{3,7},{4,6},{5,1},{6,4},{7,3},{8,10},{9,13},{10,... | collective-permute-start | bytes 1474568 | tf_op jit(solution)/shard_map/ppermute | solution.py:32
  17.2 1.5 %copy-done.2 = bf16[1280,768]{1,0:T(8,128)(2,1)S(1)} copy-done((bf16[1280,768]{1,0:T(8,128)(2,1)S(1)}, bf16[1280,768]{1,0:T(8,128)(2,1)}, u32[]{:S(2)}) %copy-start.2) | copy-done | bytes 1966104
  18.7 3.4 %activation.1 = (bf16[16,80,768]{2,1,0:T(8,128)(2,1)S(1)}, bf16[16,80,768]{2,1,0:T(8,128)(2,1)S(1)}) custom-call(s32[16]{0:T(128)S(1)} %pad_add_fusion.order, bf16[16,80,768]{2,1,0:T(8,128)(2,1)S(1)} %bitcast.27), custom_call_target="tpu_custom_call" | custom-call | tf_op jit(solution)/shard_map/activation/pallas_call | solution.py:169
  22.1 0.1 collective-permute-start.4
  22.2 3.0 %collective-permute-start.5 = (bf16[40,1536]{1,0:T(8,128)(2,1)S(1)}, bf16[40,1536]{1,0:T(8,128)(2,1)S(1)}, u32[]{:S(2)}, u32[]{:S(2)}) collective-permute-start(bf16[40,1536]{1,0:T(8,128)(2,1)S(1)} %get-tuple-element.97), channel_id=1, source_target_pairs={{0,8},{1,9},{2,10},{3,11},{4,12},{5,13},{6,14},{7,15},{8,0},{9,1},... | collective-permute-start | bytes 368648 | tf_op jit(solution)/shard_map/ppermute | solution.py:38
  25.2 1.4 %collective-permute-done.1.refs_1_ = bf16[160,1536]{1,0:T(8,128)(2,1)S(1)} collective-permute-done((bf16[160,1536]{1,0:T(8,128)(2,1)S(1)}, bf16[160,1536]{1,0:T(8,128)(2,1)S(1)}, u32[]{:S(2)}, u32[]{:S(2)}) %collective-permute-start.1) | collective-permute-done | bytes 491552 | tf_op jit(solution)/shard_map/ppermute | solution.py:32
  26.6 0.1 stack_rows.14.refs_0_
  26.7 0.1 collective-permute-start.3
  26.8 1.4 %collective-permute-done.5 = bf16[40,1536]{1,0:T(8,128)(2,1)S(1)} collective-permute-done((bf16[40,1536]{1,0:T(8,128)(2,1)S(1)}, bf16[40,1536]{1,0:T(8,128)(2,1)S(1)}, u32[]{:S(2)}, u32[]{:S(2)}) %collective-permute-start.5) | collective-permute-done | bytes 122912 | tf_op jit(solution)/shard_map/ppermute | solution.py:38
  28.2 1.5 %collective-permute-done.4.refs_1_ = bf16[80,1536]{1,0:T(8,128)(2,1)S(1)} collective-permute-done((bf16[80,1536]{1,0:T(8,128)(2,1)S(1)}, bf16[80,1536]{1,0:T(8,128)(2,1)S(1)}, u32[]{:S(2)}, u32[]{:S(2)}) %collective-permute-start.4) | collective-permute-done | bytes 245792 | tf_op jit(solution)/shard_map/ppermute | solution.py:32
  29.7 0.1 collective-permute-start.7
  29.8 2.4 %collective-permute-start.8 = (bf16[80,1536]{1,0:T(8,128)(2,1)S(1)}, bf16[80,1536]{1,0:T(8,128)(2,1)S(1)}, u32[]{:S(2)}, u32[]{:S(2)}) collective-permute-start(bf16[80,1536]{1,0:T(8,128)(2,1)S(1)} %get-tuple-element.60.refs_0_), channel_id=1, source_target_pairs={{0,4},{1,3},{2,6},{3,1},{4,0},{5,7},{6,2},{7,5},{8,12},{9,11},{10,... | collective-permute-start | bytes 737288 | tf_op jit(solution)/shard_map/ppermute | solution.py:32
  32.2 0.3 fusion.3
  32.6 0.1 stack_rows.16.grads.refs_0_
  32.7 1.2 %copy-done.1 = bf16[1536,768]{1,0:T(8,128)(2,1)S(1)} copy-done((bf16[1536,768]{1,0:T(8,128)(2,1)S(1)}, bf16[1536,768]{1,0:T(8,128)(2,1)}, u32[]{:S(2)}) %copy-start.1) | copy-done | bytes 2359320
  33.9 0.8 copy-done
  34.7 3.9 %slot_grads.2 = (bf16[640,768]{1,0:T(8,128)(2,1)S(1)}, bf16[320,1664]{1,0:T(8,128)(2,1)S(1)}, bf16[320,1664]{1,0:T(8,128)(2,1)S(1)}) custom-call(bf16[640,1536]{1,0:T(8,128)(2,1)S(1)} %stack_rows.16.grads.refs_0_, bf16[768,1536]{1,0:T(8,128)(2,1)S(1)} %copy-done, bf16[1536,768]{1,0:T(8,128)(2,1)S(1)} %copy-done.1, bf16[640,768]{1,0:T(8,128)(2,1)S(1)} %bitcast.26, ...), custom_call_target="tpu_custom_call" | custom-call | tf_op jit(solution)/shard_map/slot_grads/pallas_call | solution.py:275
  38.6 0.1 collective-permute-start.6
  38.7 0.1 stack_rows.18.refs_0_
  38.8 0.5 collective-permute-start.10
  39.4 2.6 %collective-permute-start.11 = (bf16[40,1536]{1,0:T(8,128)(2,1)S(1)}, bf16[40,1536]{1,0:T(8,128)(2,1)S(1)}, u32[]{:S(2)}, u32[]{:S(2)}) collective-permute-start(bf16[40,1536]{1,0:T(8,128)(2,1)S(1)} %get-tuple-element.66), channel_id=1, source_target_pairs={{0,8},{1,9},{2,10},{3,11},{4,12},{5,13},{6,14},{7,15},{8,0},{9,1},... | collective-permute-start | bytes 368648 | tf_op jit(solution)/shard_map/ppermute | solution.py:38
  41.9 0.2 add_convert_fusion.2
  42.2 1.4 %collective-permute-start.9 = (bf16[160,1664]{1,0:T(8,128)(2,1)S(1)}, bf16[160,1664]{1,0:T(8,128)(2,1)S(1)}, u32[]{:S(2)}, u32[]{:S(2)}) collective-permute-start(bf16[160,1664]{1,0:T(8,128)(2,1)S(1)} %get-tuple-element.86), channel_id=1, source_target_pairs={{0,2},{1,5},{2,0},{3,7},{4,6},{5,1},{6,4},{7,3},{8,10},{9,13},{10,... | collective-permute-start | bytes 1597448 | tf_op jit(solution)/shard_map/ppermute | solution.py:32
  43.6 0.1 stack_rows.19.grads.refs_1_
  43.8 3.9 %slot_grads.3 = (bf16[640,768]{1,0:T(8,128)(2,1)S(1)}, bf16[320,1664]{1,0:T(8,128)(2,1)S(1)}, bf16[320,1664]{1,0:T(8,128)(2,1)S(1)}) custom-call(bf16[640,1536]{1,0:T(8,128)(2,1)S(1)} %stack_rows.19.grads.refs_1_, bf16[768,1536]{1,0:T(8,128)(2,1)S(1)} %copy-done, bf16[1536,768]{1,0:T(8,128)(2,1)S(1)} %copy-done.1, bf16[640,768]{1,0:T(8,128)(2,1)S(1)} %bitcast.24, ...), custom_call_target="tpu_custom_call" | custom-call | tf_op jit(solution)/shard_map/slot_grads/pallas_call | solution.py:275
  47.7 0.9 %collective-permute-done.11 = bf16[40,1536]{1,0:T(8,128)(2,1)S(1)} collective-permute-done((bf16[40,1536]{1,0:T(8,128)(2,1)S(1)}, bf16[40,1536]{1,0:T(8,128)(2,1)S(1)}, u32[]{:S(2)}, u32[]{:S(2)}) %collective-permute-start.11) | collective-permute-done | bytes 122912 | tf_op jit(solution)/shard_map/ppermute | solution.py:38
  48.6 0.1 fusion.5
  48.7 0.1 collective-permute-start.13
  48.8 1.4 %collective-permute-start.15 = (bf16[160,1536]{1,0:T(8,128)(2,1)S(1)}, bf16[160,1536]{1,0:T(8,128)(2,1)S(1)}, u32[]{:S(2)}, u32[]{:S(2)}) collective-permute-start(bf16[160,1536]{1,0:T(8,128)(2,1)S(1)} %stack_rows.17.refs_0_), channel_id=1, source_target_pairs={{0,2},{1,5},{2,0},{3,7},{4,6},{5,1},{6,4},{7,3},{8,10},{9,13},{10,... | collective-permute-start | bytes 1474568 | tf_op jit(solution)/shard_map/ppermute | solution.py:32
  50.2 0.3 stack_rows.20
  50.5 0.2 collective-permute-start.12
  50.7 0.8 collective-permute-done.9
  51.5 0.1 add_convert_fusion.7
  51.7 0.1 add_convert_fusion.1
  51.8 1.4 %collective-permute-start.14 = (bf16[160,1664]{1,0:T(8,128)(2,1)S(1)}, bf16[160,1664]{1,0:T(8,128)(2,1)S(1)}, u32[]{:S(2)}, u32[]{:S(2)}) collective-permute-start(bf16[160,1664]{1,0:T(8,128)(2,1)S(1)} %add_convert_fusion.1), channel_id=1, source_target_pairs={{0,2},{1,5},{2,0},{3,7},{4,6},{5,1},{6,4},{7,3},{8,10},{9,13},{10,... | collective-permute-start | bytes 1597448 | tf_op jit(solution)/shard_map/ppermute | solution.py:32
  53.2 0.2 add_convert_fusion
  53.4 4.6 %convolution_convert_fusion.1 = bf16[768,1536]{1,0:T(8,128)(2,1)} fusion(bf16[1280,768]{1,0:T(8,128)(2,1)S(1)} %bitcast.28, bf16[1280,1536]{1,0:T(8,128)(2,1)S(1)} %stack_rows.20), kind=kOutput, calls=%fused_computation.1 | convolution fusion | flops 3021078528 | bytes 8257536 | tf_op jit(solution)/shard_map/dot_general | solution.py:250
  57.9 1.2 %collective-permute-done.16.refs_1_ = bf16[80,1536]{1,0:T(8,128)(2,1)S(1)} collective-permute-done((bf16[80,1536]{1,0:T(8,128)(2,1)S(1)}, bf16[80,1536]{1,0:T(8,128)(2,1)S(1)}, u32[]{:S(2)}, u32[]{:S(2)}) %collective-permute-start.16) | collective-permute-done | bytes 245792 | tf_op jit(solution)/shard_map/ppermute | solution.py:32
  59.1 0.7 collective-permute-start.18
  59.9 5.5 %collective-permute-done.14 = bf16[160,1664]{1,0:T(8,128)(2,1)S(1)} collective-permute-done((bf16[160,1664]{1,0:T(8,128)(2,1)S(1)}, bf16[160,1664]{1,0:T(8,128)(2,1)S(1)}, u32[]{:S(2)}, u32[]{:S(2)}) %collective-permute-start.14) | collective-permute-done | bytes 532512 | tf_op jit(solution)/shard_map/ppermute | solution.py:32
  65.5 0.1 add_convert_fusion.5
  65.6 0.6 collective-permute-start.17
  66.2 0.1 stack_rows.25
  66.3 1.6 %collective-permute-start.21 = (bf16[320,1536]{1,0:T(8,128)(2,1)S(1)}, bf16[320,1536]{1,0:T(8,128)(2,1)S(1)}, u32[]{:S(2)}, u32[]{:S(2)}) collective-permute-start(bf16[320,1536]{1,0:T(8,128)(2,1)S(1)} %stack_rows.22.refs_0_), channel_id=1, source_target_pairs={{0,1},{1,0},{2,3},{3,2},{4,5},{5,4},{6,7},{7,6},{8,9},{9,8},{10,11... | collective-permute-start | bytes 2949128 | tf_op jit(solution)/shard_map/ppermute | solution.py:32
  67.9 4.1 %collective-permute-done.18.refs_1_ = bf16[160,1536]{1,0:T(8,128)(2,1)S(1)} collective-permute-done((bf16[160,1536]{1,0:T(8,128)(2,1)S(1)}, bf16[160,1536]{1,0:T(8,128)(2,1)S(1)}, u32[]{:S(2)}, u32[]{:S(2)}) %collective-permute-start.18) | collective-permute-done | bytes 491552 | tf_op jit(solution)/shard_map/ppermute | solution.py:32
  72.0 2.7 %collective-permute-start.22 = (bf16[320,1536]{1,0:T(8,128)(2,1)S(1)}, bf16[320,1536]{1,0:T(8,128)(2,1)S(1)}, u32[]{:S(2)}, u32[]{:S(2)}) collective-permute-start(bf16[320,1536]{1,0:T(8,128)(2,1)S(1)} %stack_rows.23.refs_2_), channel_id=1, source_target_pairs={{0,1},{1,0},{2,3},{3,2},{4,5},{5,4},{6,7},{7,6},{8,9},{9,8},{10,11... | collective-permute-start | bytes 2949128 | tf_op jit(solution)/shard_map/ppermute | solution.py:32
  74.7 0.1 add_convert_fusion.4.rows
  74.9 0.7 collective-permute-start.20
  75.6 1.7 %collective-permute-start.19 = (bf16[80,1664]{1,0:T(8,128)(2,1)S(1)}, bf16[80,1664]{1,0:T(8,128)(2,1)S(1)}, u32[]{:S(2)}, u32[]{:S(2)}) collective-permute-start(bf16[80,1664]{1,0:T(8,128)(2,1)S(1)} %get-tuple-element.79), channel_id=1, source_target_pairs={{0,4},{1,3},{2,6},{3,1},{4,0},{5,7},{6,2},{7,5},{8,12},{9,11},{10,... | collective-permute-start | bytes 798728 | tf_op jit(solution)/shard_map/ppermute | solution.py:32
  77.3 0.3 stack_rows.24
  77.6 4.6 %convolution_convert_fusion = bf16[1536,768]{1,0:T(8,128)(2,1)} fusion(bf16[1280,1536]{1,0:T(8,128)(2,1)S(1)} %stack_rows.24, bf16[1280,768]{1,0:T(8,128)(2,1)S(1)} %stack_rows.25), kind=kOutput, calls=%fused_computation | convolution fusion | flops 3021078528 | bytes 8257536 | tf_op jit(solution)/shard_map/dot_general | solution.py:250
  82.2 7.3 %collective-permute-done.20.back = bf16[80,1664]{1,0:T(8,128)(2,1)S(1)} collective-permute-done((bf16[80,1664]{1,0:T(8,128)(2,1)S(1)}, bf16[80,1664]{1,0:T(8,128)(2,1)S(1)}, u32[]{:S(2)}, u32[]{:S(2)}) %collective-permute-start.20) | collective-permute-done | bytes 266272 | tf_op jit(solution)/shard_map/ppermute | solution.py:38
  89.5 1.2 %slots_to_tokens.1 = (bf16[128,1536]{1,0:T(8,128)(2,1)}, f32[1,128]{1,0:T(1,128)}) custom-call(s32[1,128]{1,0:T(1,128)S(1)} %fusion.place, f32[1,128]{1,0:T(1,128)S(1)} %bitcast.32, bf16[80,1664]{1,0:T(8,128)(2,1)S(1)} %get-tuple-element.95.kept, bf16[80,1664]{1,0:T(8,128)(2,1)S(1)} %collective-permute-done.19.got, ...), custom_call_target="tpu_custom_call" | custom-call | tf_op jit(solution)/shard_map/slots_to_tokens/pallas_call | solution.py:136
  (35 shorter events, 0.4 us)
Async XLA Ops:
  1.3 1.0 %copy-start.3 = (bf16[128,1536]{1,0:T(8,128)(2,1)S(1)}, bf16[128,1536]{1,0:T(8,128)(2,1)}, u32[]{:S(2)}) copy-start(bf16[128,1536]{1,0:T(8,128)(2,1)} %values.2) | copy-start | bytes 1179652
  2.3 0.7 copy-start.5
  3.4 9.4 %collective-permute-start = (bf16[80,1536]{1,0:T(8,128)(2,1)S(1)}, bf16[80,1536]{1,0:T(8,128)(2,1)S(1)}, u32[]{:S(2)}, u32[]{:S(2)}) collective-permute-start(bf16[80,1536]{1,0:T(8,128)(2,1)S(1)} %get-tuple-element.45.refs_0_), channel_id=1, source_target_pairs={{0,4},{1,3},{2,6},{3,1},{4,0},{5,7},{6,2},{7,5},{8,12},{9,11},{10,... | collective-permute-start | bytes 737288 | tf_op jit(solution)/shard_map/ppermute | solution.py:32
  6.5 15.6 %collective-permute-start.2 = (bf16[80,1536]{1,0:T(8,128)(2,1)S(1)}, bf16[80,1536]{1,0:T(8,128)(2,1)S(1)}, u32[]{:S(2)}, u32[]{:S(2)}) collective-permute-start(bf16[80,1536]{1,0:T(8,128)(2,1)S(1)} %get-tuple-element.48), channel_id=1, source_target_pairs={{0,8},{1,9},{2,10},{3,11},{4,12},{5,13},{6,14},{7,15},{8,0},{9,1},... | collective-permute-start | bytes 737288 | tf_op jit(solution)/shard_map/ppermute | solution.py:38
  9.1 1.0 %copy-start.4 = (bf16[128,1536]{1,0:T(8,128)(2,1)S(1)}, bf16[128,1536]{1,0:T(8,128)(2,1)}, u32[]{:S(2)}) copy-start(bf16[128,1536]{1,0:T(8,128)(2,1)} %values.3) | copy-start | bytes 1179652
  10.1 0.7 copy-start.6
  12.8 13.8 %collective-permute-start.1 = (bf16[160,1536]{1,0:T(8,128)(2,1)S(1)}, bf16[160,1536]{1,0:T(8,128)(2,1)S(1)}, u32[]{:S(2)}, u32[]{:S(2)}) collective-permute-start(bf16[160,1536]{1,0:T(8,128)(2,1)S(1)} %stack_rows.13.refs_0_), channel_id=1, source_target_pairs={{0,2},{1,5},{2,0},{3,7},{4,6},{5,1},{6,4},{7,3},{8,10},{9,13},{10,... | collective-permute-start | bytes 1474568 | tf_op jit(solution)/shard_map/ppermute | solution.py:32
  17.2 1.5 %copy-start.2 = (bf16[1280,768]{1,0:T(8,128)(2,1)S(1)}, bf16[1280,768]{1,0:T(8,128)(2,1)}, u32[]{:S(2)}) copy-start(bf16[1280,768]{1,0:T(8,128)(2,1)} %param.15) | copy-start | bytes 5898244
  22.1 7.6 %collective-permute-start.4 = (bf16[80,1536]{1,0:T(8,128)(2,1)S(1)}, bf16[80,1536]{1,0:T(8,128)(2,1)S(1)}, u32[]{:S(2)}, u32[]{:S(2)}) collective-permute-start(bf16[80,1536]{1,0:T(8,128)(2,1)S(1)} %pause.2.refs_0_), channel_id=1, source_target_pairs={{0,4},{1,3},{2,6},{3,1},{4,0},{5,7},{6,2},{7,5},{8,12},{9,11},{10,... | collective-permute-start | bytes 737288 | tf_op jit(solution)/shard_map/ppermute | solution.py:32
  22.2 6.0 %collective-permute-start.5 = (bf16[40,1536]{1,0:T(8,128)(2,1)S(1)}, bf16[40,1536]{1,0:T(8,128)(2,1)S(1)}, u32[]{:S(2)}, u32[]{:S(2)}) collective-permute-start(bf16[40,1536]{1,0:T(8,128)(2,1)S(1)} %get-tuple-element.97), channel_id=1, source_target_pairs={{0,8},{1,9},{2,10},{3,11},{4,12},{5,13},{6,14},{7,15},{8,0},{9,1},... | collective-permute-start | bytes 368648 | tf_op jit(solution)/shard_map/ppermute | solution.py:38
  26.7 5.9 %collective-permute-start.3 = (bf16[320,1536]{1,0:T(8,128)(2,1)S(1)}, bf16[320,1536]{1,0:T(8,128)(2,1)S(1)}, u32[]{:S(2)}, u32[]{:S(2)}) collective-permute-start(bf16[320,1536]{1,0:T(8,128)(2,1)S(1)} %stack_rows.14.refs_0_), channel_id=1, source_target_pairs={{0,1},{1,0},{2,3},{3,2},{4,5},{5,4},{6,7},{7,6},{8,9},{9,8},{10,11... | collective-permute-start | bytes 2949128 | tf_op jit(solution)/shard_map/ppermute | solution.py:32
  29.7 9.0 %collective-permute-start.7 = (bf16[160,1536]{1,0:T(8,128)(2,1)S(1)}, bf16[160,1536]{1,0:T(8,128)(2,1)S(1)}, u32[]{:S(2)}, u32[]{:S(2)}) collective-permute-start(bf16[160,1536]{1,0:T(8,128)(2,1)S(1)} %stack_rows.15.refs_0_), channel_id=1, source_target_pairs={{0,2},{1,5},{2,0},{3,7},{4,6},{5,1},{6,4},{7,3},{8,10},{9,13},{10,... | collective-permute-start | bytes 1474568 | tf_op jit(solution)/shard_map/ppermute | solution.py:32
  29.8 8.9 %collective-permute-start.8 = (bf16[80,1536]{1,0:T(8,128)(2,1)S(1)}, bf16[80,1536]{1,0:T(8,128)(2,1)S(1)}, u32[]{:S(2)}, u32[]{:S(2)}) collective-permute-start(bf16[80,1536]{1,0:T(8,128)(2,1)S(1)} %get-tuple-element.60.refs_0_), channel_id=1, source_target_pairs={{0,4},{1,3},{2,6},{3,1},{4,0},{5,7},{6,2},{7,5},{8,12},{9,11},{10,... | collective-permute-start | bytes 737288 | tf_op jit(solution)/shard_map/ppermute | solution.py:32
  32.2 1.7 %copy-start.1 = (bf16[1536,768]{1,0:T(8,128)(2,1)S(1)}, bf16[1536,768]{1,0:T(8,128)(2,1)}, u32[]{:S(2)}) copy-start(bf16[1536,768]{1,0:T(8,128)(2,1)} %w_in.3) | copy-start | bytes 7077892
  32.5 2.1 %copy-start = (bf16[768,1536]{1,0:T(8,128)(2,1)S(1)}, bf16[768,1536]{1,0:T(8,128)(2,1)}, u32[]{:S(2)}) copy-start(bf16[768,1536]{1,0:T(8,128)(2,1)} %w_out.3) | copy-start | bytes 7077892
  38.6 3.4 %collective-permute-start.6 = (bf16[320,1664]{1,0:T(8,128)(2,1)S(1)}, bf16[320,1664]{1,0:T(8,128)(2,1)S(1)}, u32[]{:S(2)}, u32[]{:S(2)}) collective-permute-start(bf16[320,1664]{1,0:T(8,128)(2,1)S(1)} %get-tuple-element.59), channel_id=1, source_target_pairs={{0,1},{1,0},{2,3},{3,2},{4,5},{5,4},{6,7},{7,6},{8,9},{9,8},{10,11... | collective-permute-start | bytes 3194888 | tf_op jit(solution)/shard_map/ppermute | solution.py:32
  38.8 4.8 %collective-permute-start.10 = (bf16[320,1536]{1,0:T(8,128)(2,1)S(1)}, bf16[320,1536]{1,0:T(8,128)(2,1)S(1)}, u32[]{:S(2)}, u32[]{:S(2)}) collective-permute-start(bf16[320,1536]{1,0:T(8,128)(2,1)S(1)} %stack_rows.18.refs_0_), channel_id=1, source_target_pairs={{0,1},{1,0},{2,3},{3,2},{4,5},{5,4},{6,7},{7,6},{8,9},{9,8},{10,11... | collective-permute-start | bytes 2949128 | tf_op jit(solution)/shard_map/ppermute | solution.py:32
  39.4 9.2 %collective-permute-start.11 = (bf16[40,1536]{1,0:T(8,128)(2,1)S(1)}, bf16[40,1536]{1,0:T(8,128)(2,1)S(1)}, u32[]{:S(2)}, u32[]{:S(2)}) collective-permute-start(bf16[40,1536]{1,0:T(8,128)(2,1)S(1)} %get-tuple-element.66), channel_id=1, source_target_pairs={{0,8},{1,9},{2,10},{3,11},{4,12},{5,13},{6,14},{7,15},{8,0},{9,1},... | collective-permute-start | bytes 368648 | tf_op jit(solution)/shard_map/ppermute | solution.py:38
  42.2 9.3 %collective-permute-start.9 = (bf16[160,1664]{1,0:T(8,128)(2,1)S(1)}, bf16[160,1664]{1,0:T(8,128)(2,1)S(1)}, u32[]{:S(2)}, u32[]{:S(2)}) collective-permute-start(bf16[160,1664]{1,0:T(8,128)(2,1)S(1)} %get-tuple-element.86), channel_id=1, source_target_pairs={{0,2},{1,5},{2,0},{3,7},{4,6},{5,1},{6,4},{7,3},{8,10},{9,13},{10,... | collective-permute-start | bytes 1597448 | tf_op jit(solution)/shard_map/ppermute | solution.py:32
  48.7 3.0 %collective-permute-start.13 = (bf16[160,1664]{1,0:T(8,128)(2,1)S(1)}, bf16[160,1664]{1,0:T(8,128)(2,1)S(1)}, u32[]{:S(2)}, u32[]{:S(2)}) collective-permute-start(bf16[160,1664]{1,0:T(8,128)(2,1)S(1)} %get-tuple-element.93), channel_id=1, source_target_pairs={{0,1},{1,0},{2,3},{3,2},{4,5},{5,4},{6,7},{7,6},{8,9},{9,8},{10,11... | collective-permute-start | bytes 1597448 | tf_op jit(solution)/shard_map/ppermute | solution.py:32
  48.8 11.1 %collective-permute-start.15 = (bf16[160,1536]{1,0:T(8,128)(2,1)S(1)}, bf16[160,1536]{1,0:T(8,128)(2,1)S(1)}, u32[]{:S(2)}, u32[]{:S(2)}) collective-permute-start(bf16[160,1536]{1,0:T(8,128)(2,1)S(1)} %stack_rows.17.refs_0_), channel_id=1, source_target_pairs={{0,2},{1,5},{2,0},{3,7},{4,6},{5,1},{6,4},{7,3},{8,10},{9,13},{10,... | collective-permute-start | bytes 1474568 | tf_op jit(solution)/shard_map/ppermute | solution.py:32
  50.2 8.9 %collective-permute-start.16 = (bf16[80,1536]{1,0:T(8,128)(2,1)S(1)}, bf16[80,1536]{1,0:T(8,128)(2,1)S(1)}, u32[]{:S(2)}, u32[]{:S(2)}) collective-permute-start(bf16[80,1536]{1,0:T(8,128)(2,1)S(1)} %maximum_bitcast_fusion.refs_0_), channel_id=1, source_target_pairs={{0,4},{1,3},{2,6},{3,1},{4,0},{5,7},{6,2},{7,5},{8,12},{9,11},{10,... | collective-permute-start | bytes 737288 | tf_op jit(solution)/shard_map/ppermute | solution.py:32
  50.5 2.8 %collective-permute-start.12 = (bf16[160,1664]{1,0:T(8,128)(2,1)S(1)}, bf16[160,1664]{1,0:T(8,128)(2,1)S(1)}, u32[]{:S(2)}, u32[]{:S(2)}) collective-permute-start(bf16[160,1664]{1,0:T(8,128)(2,1)S(1)} %get-tuple-element.92), channel_id=1, source_target_pairs={{0,1},{1,0},{2,3},{3,2},{4,5},{5,4},{6,7},{7,6},{8,9},{9,8},{10,11... | collective-permute-start | bytes 1597448 | tf_op jit(solution)/shard_map/ppermute | solution.py:32
  51.8 13.7 %collective-permute-start.14 = (bf16[160,1664]{1,0:T(8,128)(2,1)S(1)}, bf16[160,1664]{1,0:T(8,128)(2,1)S(1)}, u32[]{:S(2)}, u32[]{:S(2)}) collective-permute-start(bf16[160,1664]{1,0:T(8,128)(2,1)S(1)} %add_convert_fusion.1), channel_id=1, source_target_pairs={{0,2},{1,5},{2,0},{3,7},{4,6},{5,1},{6,4},{7,3},{8,10},{9,13},{10,... | collective-permute-start | bytes 1597448 | tf_op jit(solution)/shard_map/ppermute | solution.py:32
  59.1 12.8 %collective-permute-start.18 = (bf16[160,1536]{1,0:T(8,128)(2,1)S(1)}, bf16[160,1536]{1,0:T(8,128)(2,1)S(1)}, u32[]{:S(2)}, u32[]{:S(2)}) collective-permute-start(bf16[160,1536]{1,0:T(8,128)(2,1)S(1)} %stack_rows.21.refs_0_), channel_id=1, source_target_pairs={{0,2},{1,5},{2,0},{3,7},{4,6},{5,1},{6,4},{7,3},{8,10},{9,13},{10,... | collective-permute-start | bytes 1474568 | tf_op jit(solution)/shard_map/ppermute | solution.py:32
  65.6 9.2 %collective-permute-start.17 = (bf16[80,1664]{1,0:T(8,128)(2,1)S(1)}, bf16[80,1664]{1,0:T(8,128)(2,1)S(1)}, u32[]{:S(2)}, u32[]{:S(2)}) collective-permute-start(bf16[80,1664]{1,0:T(8,128)(2,1)S(1)} %add_convert_fusion.5), channel_id=1, source_target_pairs={{0,4},{1,3},{2,6},{3,1},{4,0},{5,7},{6,2},{7,5},{8,12},{9,11},{10,... | collective-permute-start | bytes 798728 | tf_op jit(solution)/shard_map/ppermute | solution.py:32
  66.3 11.0 %collective-permute-start.21 = (bf16[320,1536]{1,0:T(8,128)(2,1)S(1)}, bf16[320,1536]{1,0:T(8,128)(2,1)S(1)}, u32[]{:S(2)}, u32[]{:S(2)}) collective-permute-start(bf16[320,1536]{1,0:T(8,128)(2,1)S(1)} %stack_rows.22.refs_0_), channel_id=1, source_target_pairs={{0,1},{1,0},{2,3},{3,2},{4,5},{5,4},{6,7},{7,6},{8,9},{9,8},{10,11... | collective-permute-start | bytes 2949128 | tf_op jit(solution)/shard_map/ppermute | solution.py:32
  72.0 5.3 %collective-permute-start.22 = (bf16[320,1536]{1,0:T(8,128)(2,1)S(1)}, bf16[320,1536]{1,0:T(8,128)(2,1)S(1)}, u32[]{:S(2)}, u32[]{:S(2)}) collective-permute-start(bf16[320,1536]{1,0:T(8,128)(2,1)S(1)} %stack_rows.23.refs_2_), channel_id=1, source_target_pairs={{0,1},{1,0},{2,3},{3,2},{4,5},{5,4},{6,7},{7,6},{8,9},{9,8},{10,11... | collective-permute-start | bytes 2949128 | tf_op jit(solution)/shard_map/ppermute | solution.py:32
  74.9 14.6 %collective-permute-start.20 = (bf16[80,1664]{1,0:T(8,128)(2,1)S(1)}, bf16[80,1664]{1,0:T(8,128)(2,1)S(1)}, u32[]{:S(2)}, u32[]{:S(2)}) collective-permute-start(bf16[80,1664]{1,0:T(8,128)(2,1)S(1)} %pause.3), channel_id=1, source_target_pairs={{0,8},{1,9},{2,10},{3,11},{4,12},{5,13},{6,14},{7,15},{8,0},{9,1},... | collective-permute-start | bytes 798728 | tf_op jit(solution)/shard_map/ppermute | solution.py:38
  75.6 13.9 %collective-permute-start.19 = (bf16[80,1664]{1,0:T(8,128)(2,1)S(1)}, bf16[80,1664]{1,0:T(8,128)(2,1)S(1)}, u32[]{:S(2)}, u32[]{:S(2)}) collective-permute-start(bf16[80,1664]{1,0:T(8,128)(2,1)S(1)} %get-tuple-element.79), channel_id=1, source_target_pairs={{0,4},{1,3},{2,6},{3,1},{4,0},{5,7},{6,2},{7,5},{8,12},{9,11},{10,... | collective-permute-start | bytes 798728 | tf_op jit(solution)/shard_map/ppermute | solution.py:32
  77.6 11.9 %copy-start.7 = (f32[128]{0:T(128)S(1)}, f32[128]{0:T(128)}, u32[]{:S(2)}) copy-start(f32[128]{0:T(128)} %param.11) | copy-start | bytes 1540

commit v14 on v13

--- a/solution.py
+++ b/solution.py
@@ -315,6 +315,7 @@
     far_two = join(far_grad, after(far_got, near_four, far_row_a), long=True)
     far_got = meet(far_two, 1)
 
+    far_row_b = cross(after(far_row_b, far_two), 1)
     row_got = meet(after(near_row, far_two), 0)
     near_grads = join(near_four, after(got, far_two))
     near_hg, near_kept, near_sent = slot_grads(
@@ -322,9 +323,9 @@
     )
     near_got = meet(near_sent, 2)
     near_row2 = join(near_row, after(row_got, near_sent))
-    far_four = join(far_two, after(far_got, near_row2), long=True)
+    far_row_b = after(far_row_b, near_row2)
+    far_four = join(far_two, after(far_got, far_row_b), long=True)
     far_got = meet(far_four, 2)
-    far_row_b = cross(after(far_row_b, far_four), 1)
     near_kept, near_sent = add_halves(near_kept, after(near_got, far_four))
     near_got = meet(near_sent, 1)
     far_grads = join(far_four, after(far_got, near_sent))

time: 90.9 us -> 91.4 us (level)
  waiting for transfers between devices: 25.8 us -> 30.9 us
  starting transfers between devices: 31.5 us -> 26.9 us
    ppermute x19, waiting for transfers between devices: 16.2 us -> 21.3 us  [meet(): lax.ppermute(rows, 'expert', [(i, i ^ bits(i % 2)[step]) for i in range(d...]
    ppermute x19, starting transfers between devices: 22.7 us -> 18.1 us  [meet(): lax.ppermute(rows, 'expert', [(i, i ^ bits(i % 2)[step]) for i in range(d...]
  transfers between devices with their start and end apart: 23 -> 23, of which waited for: 10 -> 12; matrix products, arithmetic and copies ran while one was open for 12% -> 12% of each run, Pallas kernels for 14% -> 14%
where the time goes in v14:
time: 91.4 us; the launch traced here: 91.2 us
  waiting for transfers between devices  30.9 us (34%)
  starting transfers between devices  26.9 us (29%)
  Pallas kernels  14.3 us (16%)
  matrix products  9.15 us (10%)
  local copies, waits for them, and re-layouts  7.23 us (8%)
  other arithmetic  1.66 us (2%)
  between operations  0.96 us (1%)
    ppermute x19, waiting for transfers between devices, meet(): lax.ppermute(rows, 'expert', [(i, i ^ bits(i % 2)[step]) for i in range(d...  21.3 us
    ppermute x19, starting transfers between devices, meet(): lax.ppermute(rows, 'expert', [(i, i ^ bits(i % 2)[step]) for i in range(d...  18.1 us
    ppermute x4, waiting for transfers between devices, shift(): return lax.ppermute(rows, 'expert', pairs)  9.6 us
    dot_general x2, matrix products, product(): return lax.dot_general(a, b, (dims, ((), ())), preferred_element_type=F32)  9.15 us
    ppermute x4, starting transfers between devices, shift(): return lax.ppermute(rows, 'expert', pairs)  8.77 us
    pallas_call x2, Pallas kernels, slot_grads(): pl.pallas_call(slot_grad_kernel, out_shape=(jax.ShapeDtypeStruct((rows, u...  7.82 us
    unnamed x16, local copies, waits for them, and re-layouts  6.82 us
    pallas_call x1, Pallas kernels, activation(): pl.pallas_call(activation_kernel, grid_spec=pltpu.PrefetchScalarGridSpec(...  3.36 us
  transfers between devices with their start and end apart: 23, of which 12 were waited for; matrix products, arithmetic and copies ran while one was open for 12% of the time, Pallas kernels for 14%

profile of v14, /device:TPU:0, one launch (start us, length us, event | category | flops | bytes accessed | tf_op | source)
XLA Modules:
  0.0 91.2 jit_solution(17107498416517300648)
XLA Ops:
  0.6 0.7 fusion.place
  1.3 1.0 %copy-done.3 = bf16[128,1536]{1,0:T(8,128)(2,1)S(1)} copy-done((bf16[128,1536]{1,0:T(8,128)(2,1)S(1)}, bf16[128,1536]{1,0:T(8,128)(2,1)}, u32[]{:S(2)}) %copy-start.3) | copy-done | bytes 393240
  2.3 0.7 copy-done.5
  3.0 0.4 rows_to_slots.2
  3.4 3.1 %collective-permute-start = (bf16[80,1536]{1,0:T(8,128)(2,1)S(1)}, bf16[80,1536]{1,0:T(8,128)(2,1)S(1)}, u32[]{:S(2)}, u32[]{:S(2)}) collective-permute-start(bf16[80,1536]{1,0:T(8,128)(2,1)S(1)} %get-tuple-element.46.refs_0_), channel_id=1, source_target_pairs={{0,4},{1,3},{2,6},{3,1},{4,0},{5,7},{6,2},{7,5},{8,12},{9,11},{10,... | collective-permute-start | bytes 737288 | tf_op jit(solution)/shard_map/ppermute | solution.py:32
  6.5 2.6 %collective-permute-start.2 = (bf16[80,1536]{1,0:T(8,128)(2,1)S(1)}, bf16[80,1536]{1,0:T(8,128)(2,1)S(1)}, u32[]{:S(2)}, u32[]{:S(2)}) collective-permute-start(bf16[80,1536]{1,0:T(8,128)(2,1)S(1)} %get-tuple-element.49), channel_id=1, source_target_pairs={{0,8},{1,9},{2,10},{3,11},{4,12},{5,13},{6,14},{7,15},{8,0},{9,1},... | collective-permute-start | bytes 737288 | tf_op jit(solution)/shard_map/ppermute | solution.py:38
  9.1 1.0 %copy-done.4 = bf16[128,1536]{1,0:T(8,128)(2,1)S(1)} copy-done((bf16[128,1536]{1,0:T(8,128)(2,1)S(1)}, bf16[128,1536]{1,0:T(8,128)(2,1)}, u32[]{:S(2)}) %copy-start.4) | copy-done | bytes 393240
  10.1 0.7 copy-done.6
  10.7 0.3 rows_to_slots.3
  11.0 0.1 pad_add_fusion.order
  11.1 1.6 %collective-permute-done.refs_1_ = bf16[80,1536]{1,0:T(8,128)(2,1)S(1)} collective-permute-done((bf16[80,1536]{1,0:T(8,128)(2,1)S(1)}, bf16[80,1536]{1,0:T(8,128)(2,1)S(1)}, u32[]{:S(2)}, u32[]{:S(2)}) %collective-permute-start) | collective-permute-done | bytes 245792 | tf_op jit(solution)/shard_map/ppermute | solution.py:32
  12.8 4.4 %collective-permute-start.1 = (bf16[160,1536]{1,0:T(8,128)(2,1)S(1)}, bf16[160,1536]{1,0:T(8,128)(2,1)S(1)}, u32[]{:S(2)}, u32[]{:S(2)}) collective-permute-start(bf16[160,1536]{1,0:T(8,128)(2,1)S(1)} %stack_rows.13.refs_0_), channel_id=1, source_target_pairs={{0,2},{1,5},{2,0},{3,7},{4,6},{5,1},{6,4},{7,3},{8,10},{9,13},{10,... | collective-permute-start | bytes 1474568 | tf_op jit(solution)/shard_map/ppermute | solution.py:32
  17.2 1.5 %copy-done.2 = bf16[1280,768]{1,0:T(8,128)(2,1)S(1)} copy-done((bf16[1280,768]{1,0:T(8,128)(2,1)S(1)}, bf16[1280,768]{1,0:T(8,128)(2,1)}, u32[]{:S(2)}) %copy-start.2) | copy-done | bytes 1966104
  18.7 3.4 %activation.1 = (bf16[16,80,768]{2,1,0:T(8,128)(2,1)S(1)}, bf16[16,80,768]{2,1,0:T(8,128)(2,1)S(1)}) custom-call(s32[16]{0:T(128)S(1)} %pad_add_fusion.order, bf16[16,80,768]{2,1,0:T(8,128)(2,1)S(1)} %bitcast.27), custom_call_target="tpu_custom_call" | custom-call | tf_op jit(solution)/shard_map/activation/pallas_call | solution.py:169
  22.1 0.1 collective-permute-start.4
  22.2 3.0 %collective-permute-start.5 = (bf16[40,1536]{1,0:T(8,128)(2,1)S(1)}, bf16[40,1536]{1,0:T(8,128)(2,1)S(1)}, u32[]{:S(2)}, u32[]{:S(2)}) collective-permute-start(bf16[40,1536]{1,0:T(8,128)(2,1)S(1)} %get-tuple-element.99), channel_id=1, source_target_pairs={{0,8},{1,9},{2,10},{3,11},{4,12},{5,13},{6,14},{7,15},{8,0},{9,1},... | collective-permute-start | bytes 368648 | tf_op jit(solution)/shard_map/ppermute | solution.py:38
  25.2 1.4 %collective-permute-done.1.refs_1_ = bf16[160,1536]{1,0:T(8,128)(2,1)S(1)} collective-permute-done((bf16[160,1536]{1,0:T(8,128)(2,1)S(1)}, bf16[160,1536]{1,0:T(8,128)(2,1)S(1)}, u32[]{:S(2)}, u32[]{:S(2)}) %collective-permute-start.1) | collective-permute-done | bytes 491552 | tf_op jit(solution)/shard_map/ppermute | solution.py:32
  26.7 0.1 collective-permute-start.3
  26.8 1.4 %collective-permute-done.5 = bf16[40,1536]{1,0:T(8,128)(2,1)S(1)} collective-permute-done((bf16[40,1536]{1,0:T(8,128)(2,1)S(1)}, bf16[40,1536]{1,0:T(8,128)(2,1)S(1)}, u32[]{:S(2)}, u32[]{:S(2)}) %collective-permute-start.5) | collective-permute-done | bytes 122912 | tf_op jit(solution)/shard_map/ppermute | solution.py:38
  28.2 1.5 %collective-permute-done.4.refs_1_ = bf16[80,1536]{1,0:T(8,128)(2,1)S(1)} collective-permute-done((bf16[80,1536]{1,0:T(8,128)(2,1)S(1)}, bf16[80,1536]{1,0:T(8,128)(2,1)S(1)}, u32[]{:S(2)}, u32[]{:S(2)}) %collective-permute-start.4) | collective-permute-done | bytes 245792 | tf_op jit(solution)/shard_map/ppermute | solution.py:32
  29.7 0.1 collective-permute-start.7
  29.8 1.8 %collective-permute-start.8 = (bf16[40,1536]{1,0:T(8,128)(2,1)S(1)}, bf16[40,1536]{1,0:T(8,128)(2,1)S(1)}, u32[]{:S(2)}, u32[]{:S(2)}) collective-permute-start(bf16[40,1536]{1,0:T(8,128)(2,1)S(1)} %get-tuple-element.61), channel_id=1, source_target_pairs={{0,8},{1,9},{2,10},{3,11},{4,12},{5,13},{6,14},{7,15},{8,0},{9,1},... | collective-permute-start | bytes 368648 | tf_op jit(solution)/shard_map/ppermute | solution.py:38
  31.6 2.4 %collective-permute-start.9 = (bf16[80,1536]{1,0:T(8,128)(2,1)S(1)}, bf16[80,1536]{1,0:T(8,128)(2,1)S(1)}, u32[]{:S(2)}, u32[]{:S(2)}) collective-permute-start(bf16[80,1536]{1,0:T(8,128)(2,1)S(1)} %get-tuple-element.62.refs_0_), channel_id=1, source_target_pairs={{0,4},{1,3},{2,6},{3,1},{4,0},{5,7},{6,2},{7,5},{8,12},{9,11},{10,... | collective-permute-start | bytes 737288 | tf_op jit(solution)/shard_map/ppermute | solution.py:32
  34.1 0.3 fusion.3
  34.4 0.1 stack_rows.16.grads.refs_0_
  34.6 1.2 %copy-done.1 = bf16[1536,768]{1,0:T(8,128)(2,1)S(1)} copy-done((bf16[1536,768]{1,0:T(8,128)(2,1)S(1)}, bf16[1536,768]{1,0:T(8,128)(2,1)}, u32[]{:S(2)}) %copy-start.1) | copy-done | bytes 2359320
  35.7 0.8 copy-done
  36.5 3.9 %slot_grads.2 = (bf16[640,768]{1,0:T(8,128)(2,1)S(1)}, bf16[320,1664]{1,0:T(8,128)(2,1)S(1)}, bf16[320,1664]{1,0:T(8,128)(2,1)S(1)}) custom-call(bf16[640,1536]{1,0:T(8,128)(2,1)S(1)} %stack_rows.16.grads.refs_0_, bf16[768,1536]{1,0:T(8,128)(2,1)S(1)} %copy-done, bf16[1536,768]{1,0:T(8,128)(2,1)S(1)} %copy-done.1, bf16[640,768]{1,0:T(8,128)(2,1)S(1)} %bitcast.26, ...), custom_call_target="tpu_custom_call" | custom-call | tf_op jit(solution)/shard_map/slot_grads/pallas_call | solution.py:275
  40.4 0.1 collective-permute-start.6
  40.6 0.7 collective-permute-done.7.refs_1_
  41.3 0.1 collective-permute-start.11
  41.4 1.8 %collective-permute-done.6 = bf16[320,1664]{1,0:T(8,128)(2,1)S(1)} collective-permute-done((bf16[320,1664]{1,0:T(8,128)(2,1)S(1)}, bf16[320,1664]{1,0:T(8,128)(2,1)S(1)}, u32[]{:S(2)}, u32[]{:S(2)}) %collective-permute-start.6) | collective-permute-done | bytes 1064992 | tf_op jit(solution)/shard_map/ppermute | solution.py:32
  43.2 0.2 add_convert_fusion.2
  43.4 1.7 %collective-permute-start.10 = (bf16[160,1664]{1,0:T(8,128)(2,1)S(1)}, bf16[160,1664]{1,0:T(8,128)(2,1)S(1)}, u32[]{:S(2)}, u32[]{:S(2)}) collective-permute-start(bf16[160,1664]{1,0:T(8,128)(2,1)S(1)} %get-tuple-element.88), channel_id=1, source_target_pairs={{0,2},{1,5},{2,0},{3,7},{4,6},{5,1},{6,4},{7,3},{8,10},{9,13},{10,... | collective-permute-start | bytes 1597448 | tf_op jit(solution)/shard_map/ppermute | solution.py:32
  45.2 0.1 stack_rows.19.grads.refs_1_
  45.3 3.9 %slot_grads.3 = (bf16[640,768]{1,0:T(8,128)(2,1)S(1)}, bf16[320,1664]{1,0:T(8,128)(2,1)S(1)}, bf16[320,1664]{1,0:T(8,128)(2,1)S(1)}) custom-call(bf16[640,1536]{1,0:T(8,128)(2,1)S(1)} %stack_rows.19.grads.refs_1_, bf16[768,1536]{1,0:T(8,128)(2,1)S(1)} %copy-done, bf16[1536,768]{1,0:T(8,128)(2,1)S(1)} %copy-done.1, bf16[640,768]{1,0:T(8,128)(2,1)S(1)} %bitcast.24, ...), custom_call_target="tpu_custom_call" | custom-call | tf_op jit(solution)/shard_map/slot_grads/pallas_call | solution.py:275
  49.3 0.1 fusion.5
  49.4 0.1 collective-permute-start.13
  49.4 1.2 %collective-permute-start.15 = (bf16[160,1536]{1,0:T(8,128)(2,1)S(1)}, bf16[160,1536]{1,0:T(8,128)(2,1)S(1)}, u32[]{:S(2)}, u32[]{:S(2)}) collective-permute-start(bf16[160,1536]{1,0:T(8,128)(2,1)S(1)} %stack_rows.17.refs_0_), channel_id=1, source_target_pairs={{0,2},{1,5},{2,0},{3,7},{4,6},{5,1},{6,4},{7,3},{8,10},{9,13},{10,... | collective-permute-start | bytes 1474568 | tf_op jit(solution)/shard_map/ppermute | solution.py:32
  50.6 0.7 collective-permute-start.16
  51.3 0.3 stack_rows.20
  51.6 0.1 collective-permute-start.12
  51.6 1.3 %collective-permute-done.10 = bf16[160,1664]{1,0:T(8,128)(2,1)S(1)} collective-permute-done((bf16[160,1664]{1,0:T(8,128)(2,1)S(1)}, bf16[160,1664]{1,0:T(8,128)(2,1)S(1)}, u32[]{:S(2)}, u32[]{:S(2)}) %collective-permute-start.10) | collective-permute-done | bytes 532512 | tf_op jit(solution)/shard_map/ppermute | solution.py:32
  53.0 0.1 add_convert_fusion.7
  53.1 0.1 add_convert_fusion.1
  53.2 2.3 %collective-permute-start.14 = (bf16[160,1664]{1,0:T(8,128)(2,1)S(1)}, bf16[160,1664]{1,0:T(8,128)(2,1)S(1)}, u32[]{:S(2)}, u32[]{:S(2)}) collective-permute-start(bf16[160,1664]{1,0:T(8,128)(2,1)S(1)} %add_convert_fusion.1), channel_id=1, source_target_pairs={{0,2},{1,5},{2,0},{3,7},{4,6},{5,1},{6,4},{7,3},{8,10},{9,13},{10,... | collective-permute-start | bytes 1597448 | tf_op jit(solution)/shard_map/ppermute | solution.py:32
  55.5 0.2 add_convert_fusion
  55.7 4.6 %convolution_convert_fusion.1 = bf16[768,1536]{1,0:T(8,128)(2,1)} fusion(bf16[1280,768]{1,0:T(8,128)(2,1)S(1)} %bitcast.28, bf16[1280,1536]{1,0:T(8,128)(2,1)S(1)} %stack_rows.20), kind=kOutput, calls=%fused_computation.1 | convolution fusion | flops 3021078528 | bytes 8257536 | tf_op jit(solution)/shard_map/dot_general | solution.py:250
  60.2 0.3 collective-permute-start.18
  60.5 0.2 collective-permute-done.15.refs_1_
  60.7 5.6 %collective-permute-done.14 = bf16[160,1664]{1,0:T(8,128)(2,1)S(1)} collective-permute-done((bf16[160,1664]{1,0:T(8,128)(2,1)S(1)}, bf16[160,1664]{1,0:T(8,128)(2,1)S(1)}, u32[]{:S(2)}, u32[]{:S(2)}) %collective-permute-start.14) | collective-permute-done | bytes 532512 | tf_op jit(solution)/shard_map/ppermute | solution.py:32
  66.5 0.5 collective-permute-start.17
  66.9 0.1 stack_rows.25
  67.1 0.3 collective-permute-start.21
  67.4 6.8 %collective-permute-done.18.refs_1_ = bf16[160,1536]{1,0:T(8,128)(2,1)S(1)} collective-permute-done((bf16[160,1536]{1,0:T(8,128)(2,1)S(1)}, bf16[160,1536]{1,0:T(8,128)(2,1)S(1)}, u32[]{:S(2)}, u32[]{:S(2)}) %collective-permute-start.18) | collective-permute-done | bytes 491552 | tf_op jit(solution)/shard_map/ppermute | solution.py:32
  74.3 0.1 collective-permute-start.22
  74.4 0.1 add_convert_fusion.4.rows
  74.6 1.4 %collective-permute-start.20 = (bf16[80,1664]{1,0:T(8,128)(2,1)S(1)}, bf16[80,1664]{1,0:T(8,128)(2,1)S(1)}, u32[]{:S(2)}, u32[]{:S(2)}) collective-permute-start(bf16[80,1664]{1,0:T(8,128)(2,1)S(1)} %pause.3), channel_id=1, source_target_pairs={{0,8},{1,9},{2,10},{3,11},{4,12},{5,13},{6,14},{7,15},{8,0},{9,1},... | collective-permute-start | bytes 798728 | tf_op jit(solution)/shard_map/ppermute | solution.py:38
  76.0 0.7 collective-permute-start.19
  76.6 0.3 collective-permute-done.22.refs_3_
  77.0 0.3 stack_rows.24
  77.2 4.6 %convolution_convert_fusion = bf16[1536,768]{1,0:T(8,128)(2,1)} fusion(bf16[1280,1536]{1,0:T(8,128)(2,1)S(1)} %stack_rows.24, bf16[1280,768]{1,0:T(8,128)(2,1)S(1)} %stack_rows.25), kind=kOutput, calls=%fused_computation | convolution fusion | flops 3021078528 | bytes 8257536 | tf_op jit(solution)/shard_map/dot_general | solution.py:250
  81.8 8.2 %collective-permute-done.20.back = bf16[80,1664]{1,0:T(8,128)(2,1)S(1)} collective-permute-done((bf16[80,1664]{1,0:T(8,128)(2,1)S(1)}, bf16[80,1664]{1,0:T(8,128)(2,1)S(1)}, u32[]{:S(2)}, u32[]{:S(2)}) %collective-permute-start.20) | collective-permute-done | bytes 266272 | tf_op jit(solution)/shard_map/ppermute | solution.py:38
  90.0 1.2 %slots_to_tokens.1 = (bf16[128,1536]{1,0:T(8,128)(2,1)}, f32[1,128]{1,0:T(1,128)}) custom-call(s32[1,128]{1,0:T(1,128)S(1)} %fusion.place, f32[1,128]{1,0:T(1,128)S(1)} %bitcast.32, bf16[80,1664]{1,0:T(8,128)(2,1)S(1)} %get-tuple-element.97.kept, bf16[80,1664]{1,0:T(8,128)(2,1)S(1)} %collective-permute-done.19.got, ...), custom_call_target="tpu_custom_call" | custom-call | tf_op jit(solution)/shard_map/slots_to_tokens/pallas_call | solution.py:136
  (35 shorter events, 0.6 us)
Async XLA Ops:
  1.3 1.0 %copy-start.3 = (bf16[128,1536]{1,0:T(8,128)(2,1)S(1)}, bf16[128,1536]{1,0:T(8,128)(2,1)}, u32[]{:S(2)}) copy-start(bf16[128,1536]{1,0:T(8,128)(2,1)} %values.2) | copy-start | bytes 1179652
  2.3 0.7 copy-start.5
  3.4 9.4 %collective-permute-start = (bf16[80,1536]{1,0:T(8,128)(2,1)S(1)}, bf16[80,1536]{1,0:T(8,128)(2,1)S(1)}, u32[]{:S(2)}, u32[]{:S(2)}) collective-permute-start(bf16[80,1536]{1,0:T(8,128)(2,1)S(1)} %get-tuple-element.46.refs_0_), channel_id=1, source_target_pairs={{0,4},{1,3},{2,6},{3,1},{4,0},{5,7},{6,2},{7,5},{8,12},{9,11},{10,... | collective-permute-start | bytes 737288 | tf_op jit(solution)/shard_map/ppermute | solution.py:32
  6.5 15.6 %collective-permute-start.2 = (bf16[80,1536]{1,0:T(8,128)(2,1)S(1)}, bf16[80,1536]{1,0:T(8,128)(2,1)S(1)}, u32[]{:S(2)}, u32[]{:S(2)}) collective-permute-start(bf16[80,1536]{1,0:T(8,128)(2,1)S(1)} %get-tuple-element.49), channel_id=1, source_target_pairs={{0,8},{1,9},{2,10},{3,11},{4,12},{5,13},{6,14},{7,15},{8,0},{9,1},... | collective-permute-start | bytes 737288 | tf_op jit(solution)/shard_map/ppermute | solution.py:38
  9.1 1.0 %copy-start.4 = (bf16[128,1536]{1,0:T(8,128)(2,1)S(1)}, bf16[128,1536]{1,0:T(8,128)(2,1)}, u32[]{:S(2)}) copy-start(bf16[128,1536]{1,0:T(8,128)(2,1)} %values.3) | copy-start | bytes 1179652
  10.1 0.7 copy-start.6
  12.8 13.8 %collective-permute-start.1 = (bf16[160,1536]{1,0:T(8,128)(2,1)S(1)}, bf16[160,1536]{1,0:T(8,128)(2,1)S(1)}, u32[]{:S(2)}, u32[]{:S(2)}) collective-permute-start(bf16[160,1536]{1,0:T(8,128)(2,1)S(1)} %stack_rows.13.refs_0_), channel_id=1, source_target_pairs={{0,2},{1,5},{2,0},{3,7},{4,6},{5,1},{6,4},{7,3},{8,10},{9,13},{10,... | collective-permute-start | bytes 1474568 | tf_op jit(solution)/shard_map/ppermute | solution.py:32
  17.2 1.5 %copy-start.2 = (bf16[1280,768]{1,0:T(8,128)(2,1)S(1)}, bf16[1280,768]{1,0:T(8,128)(2,1)}, u32[]{:S(2)}) copy-start(bf16[1280,768]{1,0:T(8,128)(2,1)} %param.15) | copy-start | bytes 5898244
  22.1 7.6 %collective-permute-start.4 = (bf16[80,1536]{1,0:T(8,128)(2,1)S(1)}, bf16[80,1536]{1,0:T(8,128)(2,1)S(1)}, u32[]{:S(2)}, u32[]{:S(2)}) collective-permute-start(bf16[80,1536]{1,0:T(8,128)(2,1)S(1)} %pause.2.refs_0_), channel_id=1, source_target_pairs={{0,4},{1,3},{2,6},{3,1},{4,0},{5,7},{6,2},{7,5},{8,12},{9,11},{10,... | collective-permute-start | bytes 737288 | tf_op jit(solution)/shard_map/ppermute | solution.py:32
  22.2 6.0 %collective-permute-start.5 = (bf16[40,1536]{1,0:T(8,128)(2,1)S(1)}, bf16[40,1536]{1,0:T(8,128)(2,1)S(1)}, u32[]{:S(2)}, u32[]{:S(2)}) collective-permute-start(bf16[40,1536]{1,0:T(8,128)(2,1)S(1)} %get-tuple-element.99), channel_id=1, source_target_pairs={{0,8},{1,9},{2,10},{3,11},{4,12},{5,13},{6,14},{7,15},{8,0},{9,1},... | collective-permute-start | bytes 368648 | tf_op jit(solution)/shard_map/ppermute | solution.py:38
  26.7 7.7 %collective-permute-start.3 = (bf16[320,1536]{1,0:T(8,128)(2,1)S(1)}, bf16[320,1536]{1,0:T(8,128)(2,1)S(1)}, u32[]{:S(2)}, u32[]{:S(2)}) collective-permute-start(bf16[320,1536]{1,0:T(8,128)(2,1)S(1)} %stack_rows.14.refs_0_), channel_id=1, source_target_pairs={{0,1},{1,0},{2,3},{3,2},{4,5},{5,4},{6,7},{7,6},{8,9},{9,8},{10,11... | collective-permute-start | bytes 2949128 | tf_op jit(solution)/shard_map/ppermute | solution.py:32
  29.7 11.5 %collective-permute-start.7 = (bf16[160,1536]{1,0:T(8,128)(2,1)S(1)}, bf16[160,1536]{1,0:T(8,128)(2,1)S(1)}, u32[]{:S(2)}, u32[]{:S(2)}) collective-permute-start(bf16[160,1536]{1,0:T(8,128)(2,1)S(1)} %stack_rows.15.refs_0_), channel_id=1, source_target_pairs={{0,2},{1,5},{2,0},{3,7},{4,6},{5,1},{6,4},{7,3},{8,10},{9,13},{10,... | collective-permute-start | bytes 1474568 | tf_op jit(solution)/shard_map/ppermute | solution.py:32
  29.8 10.8 %collective-permute-start.8 = (bf16[40,1536]{1,0:T(8,128)(2,1)S(1)}, bf16[40,1536]{1,0:T(8,128)(2,1)S(1)}, u32[]{:S(2)}, u32[]{:S(2)}) collective-permute-start(bf16[40,1536]{1,0:T(8,128)(2,1)S(1)} %get-tuple-element.61), channel_id=1, source_target_pairs={{0,8},{1,9},{2,10},{3,11},{4,12},{5,13},{6,14},{7,15},{8,0},{9,1},... | collective-permute-start | bytes 368648 | tf_op jit(solution)/shard_map/ppermute | solution.py:38
  31.6 8.9 %collective-permute-start.9 = (bf16[80,1536]{1,0:T(8,128)(2,1)S(1)}, bf16[80,1536]{1,0:T(8,128)(2,1)S(1)}, u32[]{:S(2)}, u32[]{:S(2)}) collective-permute-start(bf16[80,1536]{1,0:T(8,128)(2,1)S(1)} %get-tuple-element.62.refs_0_), channel_id=1, source_target_pairs={{0,4},{1,3},{2,6},{3,1},{4,0},{5,7},{6,2},{7,5},{8,12},{9,11},{10,... | collective-permute-start | bytes 737288 | tf_op jit(solution)/shard_map/ppermute | solution.py:32
  34.1 1.7 %copy-start.1 = (bf16[1536,768]{1,0:T(8,128)(2,1)S(1)}, bf16[1536,768]{1,0:T(8,128)(2,1)}, u32[]{:S(2)}) copy-start(bf16[1536,768]{1,0:T(8,128)(2,1)} %w_in.3) | copy-start | bytes 7077892
  34.4 2.1 %copy-start = (bf16[768,1536]{1,0:T(8,128)(2,1)S(1)}, bf16[768,1536]{1,0:T(8,128)(2,1)}, u32[]{:S(2)}) copy-start(bf16[768,1536]{1,0:T(8,128)(2,1)} %w_out.3) | copy-start | bytes 7077892
  40.4 2.7 %collective-permute-start.6 = (bf16[320,1664]{1,0:T(8,128)(2,1)S(1)}, bf16[320,1664]{1,0:T(8,128)(2,1)S(1)}, u32[]{:S(2)}, u32[]{:S(2)}) collective-permute-start(bf16[320,1664]{1,0:T(8,128)(2,1)S(1)} %get-tuple-element.60), channel_id=1, source_target_pairs={{0,1},{1,0},{2,3},{3,2},{4,5},{5,4},{6,7},{7,6},{8,9},{9,8},{10,11... | collective-permute-start | bytes 3194888 | tf_op jit(solution)/shard_map/ppermute | solution.py:32
  41.3 3.9 %collective-permute-start.11 = (bf16[320,1536]{1,0:T(8,128)(2,1)S(1)}, bf16[320,1536]{1,0:T(8,128)(2,1)S(1)}, u32[]{:S(2)}, u32[]{:S(2)}) collective-permute-start(bf16[320,1536]{1,0:T(8,128)(2,1)S(1)} %stack_rows.18.refs_0_), channel_id=1, source_target_pairs={{0,1},{1,0},{2,3},{3,2},{4,5},{5,4},{6,7},{7,6},{8,9},{9,8},{10,11... | collective-permute-start | bytes 2949128 | tf_op jit(solution)/shard_map/ppermute | solution.py:32
  43.4 9.5 %collective-permute-start.10 = (bf16[160,1664]{1,0:T(8,128)(2,1)S(1)}, bf16[160,1664]{1,0:T(8,128)(2,1)S(1)}, u32[]{:S(2)}, u32[]{:S(2)}) collective-permute-start(bf16[160,1664]{1,0:T(8,128)(2,1)S(1)} %get-tuple-element.88), channel_id=1, source_target_pairs={{0,2},{1,5},{2,0},{3,7},{4,6},{5,1},{6,4},{7,3},{8,10},{9,13},{10,... | collective-permute-start | bytes 1597448 | tf_op jit(solution)/shard_map/ppermute | solution.py:32
  49.4 3.7 %collective-permute-start.13 = (bf16[160,1664]{1,0:T(8,128)(2,1)S(1)}, bf16[160,1664]{1,0:T(8,128)(2,1)S(1)}, u32[]{:S(2)}, u32[]{:S(2)}) collective-permute-start(bf16[160,1664]{1,0:T(8,128)(2,1)S(1)} %get-tuple-element.95), channel_id=1, source_target_pairs={{0,1},{1,0},{2,3},{3,2},{4,5},{5,4},{6,7},{7,6},{8,9},{9,8},{10,11... | collective-permute-start | bytes 1597448 | tf_op jit(solution)/shard_map/ppermute | solution.py:32
  49.4 11.2 %collective-permute-start.15 = (bf16[160,1536]{1,0:T(8,128)(2,1)S(1)}, bf16[160,1536]{1,0:T(8,128)(2,1)S(1)}, u32[]{:S(2)}, u32[]{:S(2)}) collective-permute-start(bf16[160,1536]{1,0:T(8,128)(2,1)S(1)} %stack_rows.17.refs_0_), channel_id=1, source_target_pairs={{0,2},{1,5},{2,0},{3,7},{4,6},{5,1},{6,4},{7,3},{8,10},{9,13},{10,... | collective-permute-start | bytes 1474568 | tf_op jit(solution)/shard_map/ppermute | solution.py:32
  50.6 9.6 %collective-permute-start.16 = (bf16[80,1536]{1,0:T(8,128)(2,1)S(1)}, bf16[80,1536]{1,0:T(8,128)(2,1)S(1)}, u32[]{:S(2)}, u32[]{:S(2)}) collective-permute-start(bf16[80,1536]{1,0:T(8,128)(2,1)S(1)} %maximum_bitcast_fusion.refs_0_), channel_id=1, source_target_pairs={{0,4},{1,3},{2,6},{3,1},{4,0},{5,7},{6,2},{7,5},{8,12},{9,11},{10,... | collective-permute-start | bytes 737288 | tf_op jit(solution)/shard_map/ppermute | solution.py:32
  51.6 3.9 %collective-permute-start.12 = (bf16[160,1664]{1,0:T(8,128)(2,1)S(1)}, bf16[160,1664]{1,0:T(8,128)(2,1)S(1)}, u32[]{:S(2)}, u32[]{:S(2)}) collective-permute-start(bf16[160,1664]{1,0:T(8,128)(2,1)S(1)} %get-tuple-element.94), channel_id=1, source_target_pairs={{0,1},{1,0},{2,3},{3,2},{4,5},{5,4},{6,7},{7,6},{8,9},{9,8},{10,11... | collective-permute-start | bytes 1597448 | tf_op jit(solution)/shard_map/ppermute | solution.py:32
  53.2 13.1 %collective-permute-start.14 = (bf16[160,1664]{1,0:T(8,128)(2,1)S(1)}, bf16[160,1664]{1,0:T(8,128)(2,1)S(1)}, u32[]{:S(2)}, u32[]{:S(2)}) collective-permute-start(bf16[160,1664]{1,0:T(8,128)(2,1)S(1)} %add_convert_fusion.1), channel_id=1, source_target_pairs={{0,2},{1,5},{2,0},{3,7},{4,6},{5,1},{6,4},{7,3},{8,10},{9,13},{10,... | collective-permute-start | bytes 1597448 | tf_op jit(solution)/shard_map/ppermute | solution.py:32
  60.2 14.0 %collective-permute-start.18 = (bf16[160,1536]{1,0:T(8,128)(2,1)S(1)}, bf16[160,1536]{1,0:T(8,128)(2,1)S(1)}, u32[]{:S(2)}, u32[]{:S(2)}) collective-permute-start(bf16[160,1536]{1,0:T(8,128)(2,1)S(1)} %stack_rows.21.refs_0_), channel_id=1, source_target_pairs={{0,2},{1,5},{2,0},{3,7},{4,6},{5,1},{6,4},{7,3},{8,10},{9,13},{10,... | collective-permute-start | bytes 1474568 | tf_op jit(solution)/shard_map/ppermute | solution.py:32
  66.5 7.9 %collective-permute-start.17 = (bf16[80,1664]{1,0:T(8,128)(2,1)S(1)}, bf16[80,1664]{1,0:T(8,128)(2,1)S(1)}, u32[]{:S(2)}, u32[]{:S(2)}) collective-permute-start(bf16[80,1664]{1,0:T(8,128)(2,1)S(1)} %add_convert_fusion.5), channel_id=1, source_target_pairs={{0,4},{1,3},{2,6},{3,1},{4,0},{5,7},{6,2},{7,5},{8,12},{9,11},{10,... | collective-permute-start | bytes 798728 | tf_op jit(solution)/shard_map/ppermute | solution.py:32
  67.1 9.6 %collective-permute-start.21 = (bf16[320,1536]{1,0:T(8,128)(2,1)S(1)}, bf16[320,1536]{1,0:T(8,128)(2,1)S(1)}, u32[]{:S(2)}, u32[]{:S(2)}) collective-permute-start(bf16[320,1536]{1,0:T(8,128)(2,1)S(1)} %stack_rows.22.refs_0_), channel_id=1, source_target_pairs={{0,1},{1,0},{2,3},{3,2},{4,5},{5,4},{6,7},{7,6},{8,9},{9,8},{10,11... | collective-permute-start | bytes 2949128 | tf_op jit(solution)/shard_map/ppermute | solution.py:32
  74.3 2.6 %collective-permute-start.22 = (bf16[320,1536]{1,0:T(8,128)(2,1)S(1)}, bf16[320,1536]{1,0:T(8,128)(2,1)S(1)}, u32[]{:S(2)}, u32[]{:S(2)}) collective-permute-start(bf16[320,1536]{1,0:T(8,128)(2,1)S(1)} %stack_rows.23.refs_2_), channel_id=1, source_target_pairs={{0,1},{1,0},{2,3},{3,2},{4,5},{5,4},{6,7},{7,6},{8,9},{9,8},{10,11... | collective-permute-start | bytes 2949128 | tf_op jit(solution)/shard_map/ppermute | solution.py:32
  74.6 15.4 %collective-permute-start.20 = (bf16[80,1664]{1,0:T(8,128)(2,1)S(1)}, bf16[80,1664]{1,0:T(8,128)(2,1)S(1)}, u32[]{:S(2)}, u32[]{:S(2)}) collective-permute-start(bf16[80,1664]{1,0:T(8,128)(2,1)S(1)} %pause.3), channel_id=1, source_target_pairs={{0,8},{1,9},{2,10},{3,11},{4,12},{5,13},{6,14},{7,15},{8,0},{9,1},... | collective-permute-start | bytes 798728 | tf_op jit(solution)/shard_map/ppermute | solution.py:38
  76.0 14.0 %collective-permute-start.19 = (bf16[80,1664]{1,0:T(8,128)(2,1)S(1)}, bf16[80,1664]{1,0:T(8,128)(2,1)S(1)}, u32[]{:S(2)}, u32[]{:S(2)}) collective-permute-start(bf16[80,1664]{1,0:T(8,128)(2,1)S(1)} %get-tuple-element.81), channel_id=1, source_target_pairs={{0,4},{1,3},{2,6},{3,1},{4,0},{5,7},{6,2},{7,5},{8,12},{9,11},{10,... | collective-permute-start | bytes 798728 | tf_op jit(solution)/shard_map/ppermute | solution.py:32
  77.2 12.8 %copy-start.7 = (f32[128]{0:T(128)S(1)}, f32[128]{0:T(128)}, u32[]{:S(2)}) copy-start(f32[128]{0:T(128)} %param.11) | copy-start | bytes 1540

commit v15 on v14

--- a/solution.py
+++ b/solution.py
@@ -328,27 +328,27 @@
     far_got = meet(far_four, 2)
     near_kept, near_sent = add_halves(near_kept, after(near_got, far_four))
     near_got = meet(near_sent, 1)
+    far_row = join_slots(far_row_a, far_row_b, experts)
+    far_row_got = meet(after(far_row, far_four), 0)
     far_grads = join(far_four, after(far_got, near_sent))
 
     far_hg, far_kept, far_sent = slot_grads(
         far_grads, w_out, w_in, act[near_count:], slope[near_count:]
     )
-    far_row = join_slots(far_row_a, after(far_row_b, far_sent), experts)
     far_kept, far_on = halves(far_kept)
-    far_sent = halves(after(far_sent, far_row))
+    far_sent = halves(far_sent)
     far_got, on_got = [meet(x, 2) for x in far_sent]
     row_got = meet(near_row2, 1)
-    far_row_got = meet(far_row, 0)
     near_kept, near_sent = add_halves(near_kept, after(near_got, far_sent[1]))
-    far_sent = add(far_on, after(on_got, near_sent))
+    far_row2 = join(far_row, after(far_row_got, near_sent), long=True)
+    far_sent = add(far_on, after(on_got, far_row2))
     on_got = meet(far_sent, 1)
     far_kept = add(far_kept, after(far_got, far_sent))
     w_out_grad = product(
         after(act, far_kept), join(near_grads, far_grads), ((0,), (0,))
     ).astype(BF16)
-    far_row2 = join(far_row, after(far_row_got, w_out_grad))
-    far_row_got = meet(far_row2, 1)
-    near_row4 = join(near_row2, after(row_got, far_row2))
+    far_row_got = meet(after(far_row2, w_out_grad), 1)
+    near_row4 = join(near_row2, after(row_got, w_out_grad))
     row_got = meet(near_row4, 2)
     far_kept, far_sent = add_halves(far_kept, after(on_got, near_row4))
     far_got = meet(far_sent, 0)

time: 91.4 us -> 94.2 us (1.031)
  waiting for transfers between devices: 30.9 us -> 32.6 us
  starting transfers between devices: 26.9 us -> 28 us
    ppermute x19, waiting for transfers between devices: 21.3 us -> 24.1 us  [meet(): lax.ppermute(rows, 'expert', [(i, i ^ bits(i % 2)[step]) for i in range(d...]
    ppermute x4, waiting for transfers between devices: 9.6 us -> 8.52 us  [shift(): return lax.ppermute(rows, 'expert', pairs)]
  transfers between devices with their start and end apart: 23 -> 23, of which waited for: 12 -> 10; matrix products, arithmetic and copies ran while one was open for 12% -> 11% of each run, Pallas kernels for 14% -> 14%
where the time goes in v15:
time: 94.2 us; the launch traced here: 93.9 us
  waiting for transfers between devices  32.6 us (35%)
  starting transfers between devices  28 us (30%)
  Pallas kernels  14.3 us (15%)
  matrix products  9.15 us (10%)
  local copies, waits for them, and re-layouts  7.23 us (8%)
  other arithmetic  1.63 us (2%)
  between operations  1 us (1%)
    ppermute x19, waiting for transfers between devices, meet(): lax.ppermute(rows, 'expert', [(i, i ^ bits(i % 2)[step]) for i in range(d...  24.1 us
    ppermute x19, starting transfers between devices, meet(): lax.ppermute(rows, 'expert', [(i, i ^ bits(i % 2)[step]) for i in range(d...  18.5 us
    ppermute x4, starting transfers between devices, shift(): return lax.ppermute(rows, 'expert', pairs)  9.45 us
    dot_general x2, matrix products, product(): return lax.dot_general(a, b, (dims, ((), ())), preferred_element_type=F32)  9.15 us
    ppermute x4, waiting for transfers between devices, shift(): return lax.ppermute(rows, 'expert', pairs)  8.52 us
    pallas_call x2, Pallas kernels, slot_grads(): pl.pallas_call(slot_grad_kernel, out_shape=(jax.ShapeDtypeStruct((rows, u...  7.84 us
    unnamed x16, local copies, waits for them, and re-layouts  6.82 us
    pallas_call x1, Pallas kernels, activation(): pl.pallas_call(activation_kernel, grid_spec=pltpu.PrefetchScalarGridSpec(...  3.36 us
  transfers between devices with their start and end apart: 23, of which 10 were waited for; matrix products, arithmetic and copies ran while one was open for 11% of the time, Pallas kernels for 14%

profile of v15, /device:TPU:0, one launch (start us, length us, event | category | flops | bytes accessed | tf_op | source)
XLA Modules:
  0.0 93.9 jit_solution(6972449929991809919)
XLA Ops:
  0.6 0.7 fusion.place
  1.3 1.0 %copy-done.3 = bf16[128,1536]{1,0:T(8,128)(2,1)S(1)} copy-done((bf16[128,1536]{1,0:T(8,128)(2,1)S(1)}, bf16[128,1536]{1,0:T(8,128)(2,1)}, u32[]{:S(2)}) %copy-start.3) | copy-done | bytes 393240
  2.3 0.7 copy-done.5
  3.0 0.4 rows_to_slots.2
  3.4 3.1 %collective-permute-start = (bf16[80,1536]{1,0:T(8,128)(2,1)S(1)}, bf16[80,1536]{1,0:T(8,128)(2,1)S(1)}, u32[]{:S(2)}, u32[]{:S(2)}) collective-permute-start(bf16[80,1536]{1,0:T(8,128)(2,1)S(1)} %get-tuple-element.46.refs_0_), channel_id=1, source_target_pairs={{0,4},{1,3},{2,6},{3,1},{4,0},{5,7},{6,2},{7,5},{8,12},{9,11},{10,... | collective-permute-start | bytes 737288 | tf_op jit(solution)/shard_map/ppermute | solution.py:32
  6.5 2.6 %collective-permute-start.2 = (bf16[80,1536]{1,0:T(8,128)(2,1)S(1)}, bf16[80,1536]{1,0:T(8,128)(2,1)S(1)}, u32[]{:S(2)}, u32[]{:S(2)}) collective-permute-start(bf16[80,1536]{1,0:T(8,128)(2,1)S(1)} %get-tuple-element.49), channel_id=1, source_target_pairs={{0,8},{1,9},{2,10},{3,11},{4,12},{5,13},{6,14},{7,15},{8,0},{9,1},... | collective-permute-start | bytes 737288 | tf_op jit(solution)/shard_map/ppermute | solution.py:38
  9.1 1.0 %copy-done.4 = bf16[128,1536]{1,0:T(8,128)(2,1)S(1)} copy-done((bf16[128,1536]{1,0:T(8,128)(2,1)S(1)}, bf16[128,1536]{1,0:T(8,128)(2,1)}, u32[]{:S(2)}) %copy-start.4) | copy-done | bytes 393240
  10.1 0.7 copy-done.6
  10.7 0.3 rows_to_slots.3
  11.0 0.1 pad_add_fusion.order
  11.1 1.6 %collective-permute-done.refs_1_ = bf16[80,1536]{1,0:T(8,128)(2,1)S(1)} collective-permute-done((bf16[80,1536]{1,0:T(8,128)(2,1)S(1)}, bf16[80,1536]{1,0:T(8,128)(2,1)S(1)}, u32[]{:S(2)}, u32[]{:S(2)}) %collective-permute-start) | collective-permute-done | bytes 245792 | tf_op jit(solution)/shard_map/ppermute | solution.py:32
  12.8 4.4 %collective-permute-start.1 = (bf16[160,1536]{1,0:T(8,128)(2,1)S(1)}, bf16[160,1536]{1,0:T(8,128)(2,1)S(1)}, u32[]{:S(2)}, u32[]{:S(2)}) collective-permute-start(bf16[160,1536]{1,0:T(8,128)(2,1)S(1)} %stack_rows.13.refs_0_), channel_id=1, source_target_pairs={{0,2},{1,5},{2,0},{3,7},{4,6},{5,1},{6,4},{7,3},{8,10},{9,13},{10,... | collective-permute-start | bytes 1474568 | tf_op jit(solution)/shard_map/ppermute | solution.py:32
  17.2 1.5 %copy-done.2 = bf16[1280,768]{1,0:T(8,128)(2,1)S(1)} copy-done((bf16[1280,768]{1,0:T(8,128)(2,1)S(1)}, bf16[1280,768]{1,0:T(8,128)(2,1)}, u32[]{:S(2)}) %copy-start.2) | copy-done | bytes 1966104
  18.7 3.4 %activation.1 = (bf16[16,80,768]{2,1,0:T(8,128)(2,1)S(1)}, bf16[16,80,768]{2,1,0:T(8,128)(2,1)S(1)}) custom-call(s32[16]{0:T(128)S(1)} %pad_add_fusion.order, bf16[16,80,768]{2,1,0:T(8,128)(2,1)S(1)} %bitcast.27), custom_call_target="tpu_custom_call" | custom-call | tf_op jit(solution)/shard_map/activation/pallas_call | solution.py:169
  22.1 0.1 collective-permute-start.4
  22.2 3.0 %collective-permute-start.5 = (bf16[40,1536]{1,0:T(8,128)(2,1)S(1)}, bf16[40,1536]{1,0:T(8,128)(2,1)S(1)}, u32[]{:S(2)}, u32[]{:S(2)}) collective-permute-start(bf16[40,1536]{1,0:T(8,128)(2,1)S(1)} %get-tuple-element.99), channel_id=1, source_target_pairs={{0,8},{1,9},{2,10},{3,11},{4,12},{5,13},{6,14},{7,15},{8,0},{9,1},... | collective-permute-start | bytes 368648 | tf_op jit(solution)/shard_map/ppermute | solution.py:38
  25.2 1.4 %collective-permute-done.1.refs_1_ = bf16[160,1536]{1,0:T(8,128)(2,1)S(1)} collective-permute-done((bf16[160,1536]{1,0:T(8,128)(2,1)S(1)}, bf16[160,1536]{1,0:T(8,128)(2,1)S(1)}, u32[]{:S(2)}, u32[]{:S(2)}) %collective-permute-start.1) | collective-permute-done | bytes 491552 | tf_op jit(solution)/shard_map/ppermute | solution.py:32
  26.7 0.1 collective-permute-start.3
  26.8 1.4 %collective-permute-done.5 = bf16[40,1536]{1,0:T(8,128)(2,1)S(1)} collective-permute-done((bf16[40,1536]{1,0:T(8,128)(2,1)S(1)}, bf16[40,1536]{1,0:T(8,128)(2,1)S(1)}, u32[]{:S(2)}, u32[]{:S(2)}) %collective-permute-start.5) | collective-permute-done | bytes 122912 | tf_op jit(solution)/shard_map/ppermute | solution.py:38
  28.2 1.5 %collective-permute-done.4.refs_1_ = bf16[80,1536]{1,0:T(8,128)(2,1)S(1)} collective-permute-done((bf16[80,1536]{1,0:T(8,128)(2,1)S(1)}, bf16[80,1536]{1,0:T(8,128)(2,1)S(1)}, u32[]{:S(2)}, u32[]{:S(2)}) %collective-permute-start.4) | collective-permute-done | bytes 245792 | tf_op jit(solution)/shard_map/ppermute | solution.py:32
  29.7 0.1 collective-permute-start.7
  29.8 1.8 %collective-permute-start.8 = (bf16[40,1536]{1,0:T(8,128)(2,1)S(1)}, bf16[40,1536]{1,0:T(8,128)(2,1)S(1)}, u32[]{:S(2)}, u32[]{:S(2)}) collective-permute-start(bf16[40,1536]{1,0:T(8,128)(2,1)S(1)} %get-tuple-element.61), channel_id=1, source_target_pairs={{0,8},{1,9},{2,10},{3,11},{4,12},{5,13},{6,14},{7,15},{8,0},{9,1},... | collective-permute-start | bytes 368648 | tf_op jit(solution)/shard_map/ppermute | solution.py:38
  31.6 2.4 %collective-permute-start.9 = (bf16[80,1536]{1,0:T(8,128)(2,1)S(1)}, bf16[80,1536]{1,0:T(8,128)(2,1)S(1)}, u32[]{:S(2)}, u32[]{:S(2)}) collective-permute-start(bf16[80,1536]{1,0:T(8,128)(2,1)S(1)} %get-tuple-element.62.refs_0_), channel_id=1, source_target_pairs={{0,4},{1,3},{2,6},{3,1},{4,0},{5,7},{6,2},{7,5},{8,12},{9,11},{10,... | collective-permute-start | bytes 737288 | tf_op jit(solution)/shard_map/ppermute | solution.py:32
  34.1 0.3 fusion.3
  34.4 0.1 stack_rows.16.grads.refs_0_
  34.6 1.2 %copy-done.1 = bf16[1536,768]{1,0:T(8,128)(2,1)S(1)} copy-done((bf16[1536,768]{1,0:T(8,128)(2,1)S(1)}, bf16[1536,768]{1,0:T(8,128)(2,1)}, u32[]{:S(2)}) %copy-start.1) | copy-done | bytes 2359320
  35.7 0.8 copy-done
  36.5 3.9 %slot_grads.2 = (bf16[640,768]{1,0:T(8,128)(2,1)S(1)}, bf16[320,1664]{1,0:T(8,128)(2,1)S(1)}, bf16[320,1664]{1,0:T(8,128)(2,1)S(1)}) custom-call(bf16[640,1536]{1,0:T(8,128)(2,1)S(1)} %stack_rows.16.grads.refs_0_, bf16[768,1536]{1,0:T(8,128)(2,1)S(1)} %copy-done, bf16[1536,768]{1,0:T(8,128)(2,1)S(1)} %copy-done.1, bf16[640,768]{1,0:T(8,128)(2,1)S(1)} %bitcast.26, ...), custom_call_target="tpu_custom_call" | custom-call | tf_op jit(solution)/shard_map/slot_grads/pallas_call | solution.py:275
  40.5 0.1 collective-permute-start.6
  40.6 0.7 collective-permute-done.7.refs_1_
  41.3 0.1 stack_rows.18.refs_0_
  41.3 0.1 collective-permute-start.11
  41.4 1.5 %collective-permute-start.16 = (bf16[160,1536]{1,0:T(8,128)(2,1)S(1)}, bf16[160,1536]{1,0:T(8,128)(2,1)S(1)}, u32[]{:S(2)}, u32[]{:S(2)}) collective-permute-start(bf16[160,1536]{1,0:T(8,128)(2,1)S(1)} %stack_rows.17.refs_0_), channel_id=1, source_target_pairs={{0,2},{1,5},{2,0},{3,7},{4,6},{5,1},{6,4},{7,3},{8,10},{9,13},{10,... | collective-permute-start | bytes 1474568 | tf_op jit(solution)/shard_map/ppermute | solution.py:32
  42.9 0.3 collective-permute-done.6
  43.2 0.2 add_convert_fusion.2
  43.5 1.7 %collective-permute-start.10 = (bf16[160,1664]{1,0:T(8,128)(2,1)S(1)}, bf16[160,1664]{1,0:T(8,128)(2,1)S(1)}, u32[]{:S(2)}, u32[]{:S(2)}) collective-permute-start(bf16[160,1664]{1,0:T(8,128)(2,1)S(1)} %get-tuple-element.88), channel_id=1, source_target_pairs={{0,2},{1,5},{2,0},{3,7},{4,6},{5,1},{6,4},{7,3},{8,10},{9,13},{10,... | collective-permute-start | bytes 1597448 | tf_op jit(solution)/shard_map/ppermute | solution.py:32
  45.2 0.1 collective-permute-start.14
  45.3 0.1 stack_rows.19.grads.refs_1_
  45.4 0.3 stack_rows.21
  45.7 3.9 %slot_grads.3 = (bf16[640,768]{1,0:T(8,128)(2,1)S(1)}, bf16[320,1664]{1,0:T(8,128)(2,1)S(1)}, bf16[320,1664]{1,0:T(8,128)(2,1)S(1)}) custom-call(bf16[640,1536]{1,0:T(8,128)(2,1)S(1)} %stack_rows.19.grads.refs_1_, bf16[768,1536]{1,0:T(8,128)(2,1)S(1)} %copy-done, bf16[1536,768]{1,0:T(8,128)(2,1)S(1)} %copy-done.1, bf16[640,768]{1,0:T(8,128)(2,1)S(1)} %bitcast.24, ...), custom_call_target="tpu_custom_call" | custom-call | tf_op jit(solution)/shard_map/slot_grads/pallas_call | solution.py:275
  49.6 0.1 fusion.5
  49.7 0.1 collective-permute-start.12
  49.8 0.5 collective-permute-start.13
  50.3 8.3 %collective-permute-done.10 = bf16[160,1664]{1,0:T(8,128)(2,1)S(1)} collective-permute-done((bf16[160,1664]{1,0:T(8,128)(2,1)S(1)}, bf16[160,1664]{1,0:T(8,128)(2,1)S(1)}, u32[]{:S(2)}, u32[]{:S(2)}) %collective-permute-start.10) | collective-permute-done | bytes 532512 | tf_op jit(solution)/shard_map/ppermute | solution.py:32
  58.6 0.1 add_convert_fusion.7
  58.8 0.1 add_convert_fusion.1
  59.0 1.5 %collective-permute-start.15 = (bf16[160,1664]{1,0:T(8,128)(2,1)S(1)}, bf16[160,1664]{1,0:T(8,128)(2,1)S(1)}, u32[]{:S(2)}, u32[]{:S(2)}) collective-permute-start(bf16[160,1664]{1,0:T(8,128)(2,1)S(1)} %add_convert_fusion.1), channel_id=1, source_target_pairs={{0,2},{1,5},{2,0},{3,7},{4,6},{5,1},{6,4},{7,3},{8,10},{9,13},{10,... | collective-permute-start | bytes 1597448 | tf_op jit(solution)/shard_map/ppermute | solution.py:32
  60.5 0.1 add_convert_fusion
  60.6 4.6 %convolution_convert_fusion.1 = bf16[768,1536]{1,0:T(8,128)(2,1)} fusion(bf16[1280,768]{1,0:T(8,128)(2,1)S(1)} %bitcast.28, bf16[1280,1536]{1,0:T(8,128)(2,1)S(1)} %stack_rows.21), kind=kOutput, calls=%fused_computation.1 | convolution fusion | flops 3021078528 | bytes 8257536 | tf_op jit(solution)/shard_map/dot_general | solution.py:250
  65.2 0.6 collective-permute-start.18
  65.9 2.4 %collective-permute-done.15 = bf16[160,1664]{1,0:T(8,128)(2,1)S(1)} collective-permute-done((bf16[160,1664]{1,0:T(8,128)(2,1)S(1)}, bf16[160,1664]{1,0:T(8,128)(2,1)S(1)}, u32[]{:S(2)}, u32[]{:S(2)}) %collective-permute-start.15) | collective-permute-done | bytes 532512 | tf_op jit(solution)/shard_map/ppermute | solution.py:32
  68.3 0.1 add_convert_fusion.5
  68.4 0.6 collective-permute-start.17
  69.0 0.1 stack_rows.25
  69.1 0.1 collective-permute-start.21
  69.2 7.8 %collective-permute-done.18.refs_1_ = bf16[160,1536]{1,0:T(8,128)(2,1)S(1)} collective-permute-done((bf16[160,1536]{1,0:T(8,128)(2,1)S(1)}, bf16[160,1536]{1,0:T(8,128)(2,1)S(1)}, u32[]{:S(2)}, u32[]{:S(2)}) %collective-permute-start.18) | collective-permute-done | bytes 491552 | tf_op jit(solution)/shard_map/ppermute | solution.py:32
  77.1 0.1 collective-permute-start.22
  77.1 0.1 add_convert_fusion.4.rows
  77.3 2.1 %collective-permute-start.20 = (bf16[80,1664]{1,0:T(8,128)(2,1)S(1)}, bf16[80,1664]{1,0:T(8,128)(2,1)S(1)}, u32[]{:S(2)}, u32[]{:S(2)}) collective-permute-start(bf16[80,1664]{1,0:T(8,128)(2,1)S(1)} %pause.3), channel_id=1, source_target_pairs={{0,8},{1,9},{2,10},{3,11},{4,12},{5,13},{6,14},{7,15},{8,0},{9,1},... | collective-permute-start | bytes 798728 | tf_op jit(solution)/shard_map/ppermute | solution.py:38
  79.4 1.4 %collective-permute-start.19 = (bf16[80,1664]{1,0:T(8,128)(2,1)S(1)}, bf16[80,1664]{1,0:T(8,128)(2,1)S(1)}, u32[]{:S(2)}, u32[]{:S(2)}) collective-permute-start(bf16[80,1664]{1,0:T(8,128)(2,1)S(1)} %get-tuple-element.81), channel_id=1, source_target_pairs={{0,4},{1,3},{2,6},{3,1},{4,0},{5,7},{6,2},{7,5},{8,12},{9,11},{10,... | collective-permute-start | bytes 798728 | tf_op jit(solution)/shard_map/ppermute | solution.py:32
  80.8 0.3 stack_rows.24
  81.1 4.6 %convolution_convert_fusion = bf16[1536,768]{1,0:T(8,128)(2,1)} fusion(bf16[1280,1536]{1,0:T(8,128)(2,1)S(1)} %stack_rows.24, bf16[1280,768]{1,0:T(8,128)(2,1)S(1)} %stack_rows.25), kind=kOutput, calls=%fused_computation | convolution fusion | flops 3021078528 | bytes 8257536 | tf_op jit(solution)/shard_map/dot_general | solution.py:250
  85.6 7.1 %collective-permute-done.20.back = bf16[80,1664]{1,0:T(8,128)(2,1)S(1)} collective-permute-done((bf16[80,1664]{1,0:T(8,128)(2,1)S(1)}, bf16[80,1664]{1,0:T(8,128)(2,1)S(1)}, u32[]{:S(2)}, u32[]{:S(2)}) %collective-permute-start.20) | collective-permute-done | bytes 266272 | tf_op jit(solution)/shard_map/ppermute | solution.py:38
  92.8 1.2 %slots_to_tokens.1 = (bf16[128,1536]{1,0:T(8,128)(2,1)}, f32[1,128]{1,0:T(1,128)}) custom-call(s32[1,128]{1,0:T(1,128)S(1)} %fusion.place, f32[1,128]{1,0:T(1,128)S(1)} %bitcast.32, bf16[80,1664]{1,0:T(8,128)(2,1)S(1)} %get-tuple-element.97.kept, bf16[80,1664]{1,0:T(8,128)(2,1)S(1)} %collective-permute-done.19.got, ...), custom_call_target="tpu_custom_call" | custom-call | tf_op jit(solution)/shard_map/slots_to_tokens/pallas_call | solution.py:136
  (35 shorter events, 0.5 us)
Async XLA Ops:
  1.3 1.0 %copy-start.3 = (bf16[128,1536]{1,0:T(8,128)(2,1)S(1)}, bf16[128,1536]{1,0:T(8,128)(2,1)}, u32[]{:S(2)}) copy-start(bf16[128,1536]{1,0:T(8,128)(2,1)} %values.2) | copy-start | bytes 1179652
  2.3 0.7 copy-start.5
  3.4 9.4 %collective-permute-start = (bf16[80,1536]{1,0:T(8,128)(2,1)S(1)}, bf16[80,1536]{1,0:T(8,128)(2,1)S(1)}, u32[]{:S(2)}, u32[]{:S(2)}) collective-permute-start(bf16[80,1536]{1,0:T(8,128)(2,1)S(1)} %get-tuple-element.46.refs_0_), channel_id=1, source_target_pairs={{0,4},{1,3},{2,6},{3,1},{4,0},{5,7},{6,2},{7,5},{8,12},{9,11},{10,... | collective-permute-start | bytes 737288 | tf_op jit(solution)/shard_map/ppermute | solution.py:32
  6.5 15.6 %collective-permute-start.2 = (bf16[80,1536]{1,0:T(8,128)(2,1)S(1)}, bf16[80,1536]{1,0:T(8,128)(2,1)S(1)}, u32[]{:S(2)}, u32[]{:S(2)}) collective-permute-start(bf16[80,1536]{1,0:T(8,128)(2,1)S(1)} %get-tuple-element.49), channel_id=1, source_target_pairs={{0,8},{1,9},{2,10},{3,11},{4,12},{5,13},{6,14},{7,15},{8,0},{9,1},... | collective-permute-start | bytes 737288 | tf_op jit(solution)/shard_map/ppermute | solution.py:38
  9.1 1.0 %copy-start.4 = (bf16[128,1536]{1,0:T(8,128)(2,1)S(1)}, bf16[128,1536]{1,0:T(8,128)(2,1)}, u32[]{:S(2)}) copy-start(bf16[128,1536]{1,0:T(8,128)(2,1)} %values.3) | copy-start | bytes 1179652
  10.1 0.7 copy-start.6
  12.8 13.8 %collective-permute-start.1 = (bf16[160,1536]{1,0:T(8,128)(2,1)S(1)}, bf16[160,1536]{1,0:T(8,128)(2,1)S(1)}, u32[]{:S(2)}, u32[]{:S(2)}) collective-permute-start(bf16[160,1536]{1,0:T(8,128)(2,1)S(1)} %stack_rows.13.refs_0_), channel_id=1, source_target_pairs={{0,2},{1,5},{2,0},{3,7},{4,6},{5,1},{6,4},{7,3},{8,10},{9,13},{10,... | collective-permute-start | bytes 1474568 | tf_op jit(solution)/shard_map/ppermute | solution.py:32
  17.2 1.5 %copy-start.2 = (bf16[1280,768]{1,0:T(8,128)(2,1)S(1)}, bf16[1280,768]{1,0:T(8,128)(2,1)}, u32[]{:S(2)}) copy-start(bf16[1280,768]{1,0:T(8,128)(2,1)} %param.15) | copy-start | bytes 5898244
  22.1 7.6 %collective-permute-start.4 = (bf16[80,1536]{1,0:T(8,128)(2,1)S(1)}, bf16[80,1536]{1,0:T(8,128)(2,1)S(1)}, u32[]{:S(2)}, u32[]{:S(2)}) collective-permute-start(bf16[80,1536]{1,0:T(8,128)(2,1)S(1)} %pause.2.refs_0_), channel_id=1, source_target_pairs={{0,4},{1,3},{2,6},{3,1},{4,0},{5,7},{6,2},{7,5},{8,12},{9,11},{10,... | collective-permute-start | bytes 737288 | tf_op jit(solution)/shard_map/ppermute | solution.py:32
  22.2 6.0 %collective-permute-start.5 = (bf16[40,1536]{1,0:T(8,128)(2,1)S(1)}, bf16[40,1536]{1,0:T(8,128)(2,1)S(1)}, u32[]{:S(2)}, u32[]{:S(2)}) collective-permute-start(bf16[40,1536]{1,0:T(8,128)(2,1)S(1)} %get-tuple-element.99), channel_id=1, source_target_pairs={{0,8},{1,9},{2,10},{3,11},{4,12},{5,13},{6,14},{7,15},{8,0},{9,1},... | collective-permute-start | bytes 368648 | tf_op jit(solution)/shard_map/ppermute | solution.py:38
  26.7 7.7 %collective-permute-start.3 = (bf16[320,1536]{1,0:T(8,128)(2,1)S(1)}, bf16[320,1536]{1,0:T(8,128)(2,1)S(1)}, u32[]{:S(2)}, u32[]{:S(2)}) collective-permute-start(bf16[320,1536]{1,0:T(8,128)(2,1)S(1)} %stack_rows.14.refs_0_), channel_id=1, source_target_pairs={{0,1},{1,0},{2,3},{3,2},{4,5},{5,4},{6,7},{7,6},{8,9},{9,8},{10,11... | collective-permute-start | bytes 2949128 | tf_op jit(solution)/shard_map/ppermute | solution.py:32
  29.7 11.5 %collective-permute-start.7 = (bf16[160,1536]{1,0:T(8,128)(2,1)S(1)}, bf16[160,1536]{1,0:T(8,128)(2,1)S(1)}, u32[]{:S(2)}, u32[]{:S(2)}) collective-permute-start(bf16[160,1536]{1,0:T(8,128)(2,1)S(1)} %stack_rows.15.refs_0_), channel_id=1, source_target_pairs={{0,2},{1,5},{2,0},{3,7},{4,6},{5,1},{6,4},{7,3},{8,10},{9,13},{10,... | collective-permute-start | bytes 1474568 | tf_op jit(solution)/shard_map/ppermute | solution.py:32
  29.8 10.8 %collective-permute-start.8 = (bf16[40,1536]{1,0:T(8,128)(2,1)S(1)}, bf16[40,1536]{1,0:T(8,128)(2,1)S(1)}, u32[]{:S(2)}, u32[]{:S(2)}) collective-permute-start(bf16[40,1536]{1,0:T(8,128)(2,1)S(1)} %get-tuple-element.61), channel_id=1, source_target_pairs={{0,8},{1,9},{2,10},{3,11},{4,12},{5,13},{6,14},{7,15},{8,0},{9,1},... | collective-permute-start | bytes 368648 | tf_op jit(solution)/shard_map/ppermute | solution.py:38
  31.6 8.9 %collective-permute-start.9 = (bf16[80,1536]{1,0:T(8,128)(2,1)S(1)}, bf16[80,1536]{1,0:T(8,128)(2,1)S(1)}, u32[]{:S(2)}, u32[]{:S(2)}) collective-permute-start(bf16[80,1536]{1,0:T(8,128)(2,1)S(1)} %get-tuple-element.62.refs_0_), channel_id=1, source_target_pairs={{0,4},{1,3},{2,6},{3,1},{4,0},{5,7},{6,2},{7,5},{8,12},{9,11},{10,... | collective-permute-start | bytes 737288 | tf_op jit(solution)/shard_map/ppermute | solution.py:32
  34.1 1.7 %copy-start.1 = (bf16[1536,768]{1,0:T(8,128)(2,1)S(1)}, bf16[1536,768]{1,0:T(8,128)(2,1)}, u32[]{:S(2)}) copy-start(bf16[1536,768]{1,0:T(8,128)(2,1)} %w_in.3) | copy-start | bytes 7077892
  34.4 2.1 %copy-start = (bf16[768,1536]{1,0:T(8,128)(2,1)S(1)}, bf16[768,1536]{1,0:T(8,128)(2,1)}, u32[]{:S(2)}) copy-start(bf16[768,1536]{1,0:T(8,128)(2,1)} %w_out.3) | copy-start | bytes 7077892
  40.5 2.7 %collective-permute-start.6 = (bf16[320,1664]{1,0:T(8,128)(2,1)S(1)}, bf16[320,1664]{1,0:T(8,128)(2,1)S(1)}, u32[]{:S(2)}, u32[]{:S(2)}) collective-permute-start(bf16[320,1664]{1,0:T(8,128)(2,1)S(1)} %get-tuple-element.60), channel_id=1, source_target_pairs={{0,1},{1,0},{2,3},{3,2},{4,5},{5,4},{6,7},{7,6},{8,9},{9,8},{10,11... | collective-permute-start | bytes 3194888 | tf_op jit(solution)/shard_map/ppermute | solution.py:32
  41.3 4.0 %collective-permute-start.11 = (bf16[320,1536]{1,0:T(8,128)(2,1)S(1)}, bf16[320,1536]{1,0:T(8,128)(2,1)S(1)}, u32[]{:S(2)}, u32[]{:S(2)}) collective-permute-start(bf16[320,1536]{1,0:T(8,128)(2,1)S(1)} %stack_rows.18.refs_0_), channel_id=1, source_target_pairs={{0,1},{1,0},{2,3},{3,2},{4,5},{5,4},{6,7},{7,6},{8,9},{9,8},{10,11... | collective-permute-start | bytes 2949128 | tf_op jit(solution)/shard_map/ppermute | solution.py:32
  41.4 23.8 %collective-permute-start.16 = (bf16[160,1536]{1,0:T(8,128)(2,1)S(1)}, bf16[160,1536]{1,0:T(8,128)(2,1)S(1)}, u32[]{:S(2)}, u32[]{:S(2)}) collective-permute-start(bf16[160,1536]{1,0:T(8,128)(2,1)S(1)} %stack_rows.17.refs_0_), channel_id=1, source_target_pairs={{0,2},{1,5},{2,0},{3,7},{4,6},{5,1},{6,4},{7,3},{8,10},{9,13},{10,... | collective-permute-start | bytes 1474568 | tf_op jit(solution)/shard_map/ppermute | solution.py:32
  43.5 15.2 %collective-permute-start.10 = (bf16[160,1664]{1,0:T(8,128)(2,1)S(1)}, bf16[160,1664]{1,0:T(8,128)(2,1)S(1)}, u32[]{:S(2)}, u32[]{:S(2)}) collective-permute-start(bf16[160,1664]{1,0:T(8,128)(2,1)S(1)} %get-tuple-element.88), channel_id=1, source_target_pairs={{0,2},{1,5},{2,0},{3,7},{4,6},{5,1},{6,4},{7,3},{8,10},{9,13},{10,... | collective-permute-start | bytes 1597448 | tf_op jit(solution)/shard_map/ppermute | solution.py:32
  45.2 13.6 %collective-permute-start.14 = (bf16[80,1536]{1,0:T(8,128)(2,1)S(1)}, bf16[80,1536]{1,0:T(8,128)(2,1)S(1)}, u32[]{:S(2)}, u32[]{:S(2)}) collective-permute-start(bf16[80,1536]{1,0:T(8,128)(2,1)S(1)} %maximum_bitcast_fusion.refs_0_), channel_id=1, source_target_pairs={{0,4},{1,3},{2,6},{3,1},{4,0},{5,7},{6,2},{7,5},{8,12},{9,11},{10,... | collective-permute-start | bytes 737288 | tf_op jit(solution)/shard_map/ppermute | solution.py:32
  49.7 10.8 %collective-permute-start.12 = (bf16[160,1664]{1,0:T(8,128)(2,1)S(1)}, bf16[160,1664]{1,0:T(8,128)(2,1)S(1)}, u32[]{:S(2)}, u32[]{:S(2)}) collective-permute-start(bf16[160,1664]{1,0:T(8,128)(2,1)S(1)} %get-tuple-element.94), channel_id=1, source_target_pairs={{0,1},{1,0},{2,3},{3,2},{4,5},{5,4},{6,7},{7,6},{8,9},{9,8},{10,11... | collective-permute-start | bytes 1597448 | tf_op jit(solution)/shard_map/ppermute | solution.py:32
  49.8 9.0 %collective-permute-start.13 = (bf16[160,1664]{1,0:T(8,128)(2,1)S(1)}, bf16[160,1664]{1,0:T(8,128)(2,1)S(1)}, u32[]{:S(2)}, u32[]{:S(2)}) collective-permute-start(bf16[160,1664]{1,0:T(8,128)(2,1)S(1)} %get-tuple-element.95), channel_id=1, source_target_pairs={{0,1},{1,0},{2,3},{3,2},{4,5},{5,4},{6,7},{7,6},{8,9},{9,8},{10,11... | collective-permute-start | bytes 1597448 | tf_op jit(solution)/shard_map/ppermute | solution.py:32
  59.0 9.3 %collective-permute-start.15 = (bf16[160,1664]{1,0:T(8,128)(2,1)S(1)}, bf16[160,1664]{1,0:T(8,128)(2,1)S(1)}, u32[]{:S(2)}, u32[]{:S(2)}) collective-permute-start(bf16[160,1664]{1,0:T(8,128)(2,1)S(1)} %add_convert_fusion.1), channel_id=1, source_target_pairs={{0,2},{1,5},{2,0},{3,7},{4,6},{5,1},{6,4},{7,3},{8,10},{9,13},{10,... | collective-permute-start | bytes 1597448 | tf_op jit(solution)/shard_map/ppermute | solution.py:32
  65.2 11.7 %collective-permute-start.18 = (bf16[160,1536]{1,0:T(8,128)(2,1)S(1)}, bf16[160,1536]{1,0:T(8,128)(2,1)S(1)}, u32[]{:S(2)}, u32[]{:S(2)}) collective-permute-start(bf16[160,1536]{1,0:T(8,128)(2,1)S(1)} %stack_rows.20.refs_0_), channel_id=1, source_target_pairs={{0,2},{1,5},{2,0},{3,7},{4,6},{5,1},{6,4},{7,3},{8,10},{9,13},{10,... | collective-permute-start | bytes 1474568 | tf_op jit(solution)/shard_map/ppermute | solution.py:32
  68.4 8.8 %collective-permute-start.17 = (bf16[80,1664]{1,0:T(8,128)(2,1)S(1)}, bf16[80,1664]{1,0:T(8,128)(2,1)S(1)}, u32[]{:S(2)}, u32[]{:S(2)}) collective-permute-start(bf16[80,1664]{1,0:T(8,128)(2,1)S(1)} %add_convert_fusion.5), channel_id=1, source_target_pairs={{0,4},{1,3},{2,6},{3,1},{4,0},{5,7},{6,2},{7,5},{8,12},{9,11},{10,... | collective-permute-start | bytes 798728 | tf_op jit(solution)/shard_map/ppermute | solution.py:32
  69.1 11.7 %collective-permute-start.21 = (bf16[320,1536]{1,0:T(8,128)(2,1)S(1)}, bf16[320,1536]{1,0:T(8,128)(2,1)S(1)}, u32[]{:S(2)}, u32[]{:S(2)}) collective-permute-start(bf16[320,1536]{1,0:T(8,128)(2,1)S(1)} %stack_rows.22.refs_0_), channel_id=1, source_target_pairs={{0,1},{1,0},{2,3},{3,2},{4,5},{5,4},{6,7},{7,6},{8,9},{9,8},{10,11... | collective-permute-start | bytes 2949128 | tf_op jit(solution)/shard_map/ppermute | solution.py:32
  77.1 3.7 %collective-permute-start.22 = (bf16[320,1536]{1,0:T(8,128)(2,1)S(1)}, bf16[320,1536]{1,0:T(8,128)(2,1)S(1)}, u32[]{:S(2)}, u32[]{:S(2)}) collective-permute-start(bf16[320,1536]{1,0:T(8,128)(2,1)S(1)} %stack_rows.23.refs_2_), channel_id=1, source_target_pairs={{0,1},{1,0},{2,3},{3,2},{4,5},{5,4},{6,7},{7,6},{8,9},{9,8},{10,11... | collective-permute-start | bytes 2949128 | tf_op jit(solution)/shard_map/ppermute | solution.py:32
  77.3 15.5 %collective-permute-start.20 = (bf16[80,1664]{1,0:T(8,128)(2,1)S(1)}, bf16[80,1664]{1,0:T(8,128)(2,1)S(1)}, u32[]{:S(2)}, u32[]{:S(2)}) collective-permute-start(bf16[80,1664]{1,0:T(8,128)(2,1)S(1)} %pause.3), channel_id=1, source_target_pairs={{0,8},{1,9},{2,10},{3,11},{4,12},{5,13},{6,14},{7,15},{8,0},{9,1},... | collective-permute-start | bytes 798728 | tf_op jit(solution)/shard_map/ppermute | solution.py:38
  79.4 13.4 %collective-permute-start.19 = (bf16[80,1664]{1,0:T(8,128)(2,1)S(1)}, bf16[80,1664]{1,0:T(8,128)(2,1)S(1)}, u32[]{:S(2)}, u32[]{:S(2)}) collective-permute-start(bf16[80,1664]{1,0:T(8,128)(2,1)S(1)} %get-tuple-element.81), channel_id=1, source_target_pairs={{0,4},{1,3},{2,6},{3,1},{4,0},{5,7},{6,2},{7,5},{8,12},{9,11},{10,... | collective-permute-start | bytes 798728 | tf_op jit(solution)/shard_map/ppermute | solution.py:32
  81.0 11.7 %copy-start.7 = (f32[128]{0:T(128)S(1)}, f32[128]{0:T(128)}, u32[]{:S(2)}) copy-start(f32[128]{0:T(128)} %param.11) | copy-start | bytes 1540
